TPU v7x, 32 devices: a whole 2x2x4 slice. The times are simulated.
32 devices in a mesh: groups: 2 (over x), dp: 8 (over z, y), layer: 2 (over core).
Axes of the slice: x: 2, y: 2, z: 4, core: 2. Of those that a mesh axis runs over, the one named last changes fastest.
Arguments:
- queries: bfloat16 [1024, 16384], P('dp', 'layer'), may hold values from -6 to 6
- documents: bfloat16 [10240, 16384], P(('groups', 'dp'), 'layer'), parts along dimension 0, may hold values from -6 to 6
- counts: int32 [16], P(('groups', 'dp')), parts along dimension 0, may hold values from 160 to 640, as said below
- eigenvalues: float32 [16384], P('layer'), may hold values from 0.05 to 20
Outputs:
- scores: float32 [10240, 384], P(('groups', 'dp', 'layer')), parts along dimension 0
There are 2 independent parts, one for each index of `groups`. A program takes and returns all parts, laid end to end along the dimension named above; an argument that names none is the same for every part. Nothing has to cross between parts.
Inputs may be any that keep to these rules, and one draw needn't show every extreme that they name: `counts`: live document slots of each owner, filled from the first slot; at least one owner is full.
All inputs are finite; a program needn't handle non-finite values.
Results may differ from a plain program's by a relative error of at most 0.0029.
Values may be sent and summed in bfloat16 or wider, within the bound.
No kernel may reach another device: no remote copies, remote signals or barrier semaphores. Data moves between devices by JAX's collectives and lax.ppermute only.
A program may use at most 64 MiB of HBM per device.

v0:
```python
import math

import jax
import jax.numpy as jnp
from jax import lax
from jax.sharding import PartitionSpec as P

L_DIM = 8192
WINDOW = 3


def passed_along(value, axis, by):
    count = lax.axis_size(axis)
    return lax.ppermute(value, axis, [(i, (i + by) % count) for i in range(count)])


def block_scores(doc_rows, block):
    return lax.dot_general(
        doc_rows, block, (((1,), (1,)), ((), ())), preferred_element_type=jnp.float32
    )


def on_device(queries, documents, counts, eigenvalues):
    dim_here = eigenvalues.shape[0]
    blocks = eigenvalues.reshape(dim_here // L_DIM, L_DIM)
    damping = 0.1 * jnp.mean(blocks, axis=1, keepdims=True)
    inverse = (1.0 / (blocks + damping)).reshape(dim_here)
    precond = (queries.astype(jnp.float32) * inverse).astype(jnp.bfloat16)
    factor = 1.0 / math.sqrt(dim_here * lax.axis_size("layer"))
    doc_rows_all = documents.shape[0]
    live = (jnp.arange(doc_rows_all, dtype=jnp.int32) < counts[0]).astype(jnp.float32)
    keep_rows = doc_rows_all // lax.axis_size("layer")
    window_blocks = [precond]
    current = precond
    for step in range(1, WINDOW):
        current = passed_along(current, "dp", 1)
        window_blocks.append(current)
    pieces = []
    for block in window_blocks:

        def one_term(start, count, block=block):
            return block_scores(documents, block) * (factor * live)[:, None]

        pieces.append(
            lax.psum_scatter(
                one_term(jnp.int32(0), keep_rows * lax.axis_size("layer")),
                "layer",
                scatter_dimension=0,
                tiled=True,
            )
        )
    scores = jnp.concatenate(pieces, axis=1)
    return scores


def solution(mesh):
    return jax.shard_map(
        on_device,
        mesh=mesh,
        in_specs=(P("dp", "layer"), P(("groups", "dp"), "layer"), P(("groups", "dp")), P("layer")),
        out_specs=P(("groups", "dp", "layer"), None),
        check_vma=False,
    )
```

profile of v0, /device:TPU:0, one launch (start us, length us, event | category | flops | bytes accessed | tf_op | source)
XLA Modules:
  0.0 135.1 jit_solution(17362350844454661870)
XLA Ops:
  6.5 0.0 reduce-scatter.10.cloned.1.call-start
  6.5 1.4 %reduce_sum.9 = f32[]{:T(128)} reduce(f32[8192]{0:T(1024)} %param.7, f32[]{:T(128)} %constant.10.clone.1), dimensions={0}, to_apply=%region_0.0 | reduce | flops 8191 | bytes 32776 | tf_op jit(solution)/shard_map/reduce_sum | solution.py:26
  8.6 0.8 add_divide_fusion
  9.3 2.0 %multiply_convert_fusion = bf16[128,8192]{1,0:T(8,128)(2,1)S(1)} fusion(bf16[128,8192]{1,0:T(8,128)(2,1)} %param.4, f32[8192]{0:T(1024)S(1)} %add_divide_fusion), kind=kLoop, calls=%fused_computation | loop fusion | flops 3145728 | bytes 4227072 | tf_op jit(solution)/shard_map/convert_element_type | solution.py:28
  11.3 3.0 %collective-permute-start = (bf16[128,8192]{1,0:T(8,128)(2,1)S(1)}, bf16[128,8192]{1,0:T(8,128)(2,1)S(1)}, u32[]{:S(2)}, u32[]{:S(2)}) collective-permute-start(bf16[128,8192]{1,0:T(8,128)(2,1)S(1)} %multiply_convert_fusion), channel_id=1, source_target_pairs={{0,2},{2,4},{4,6},{6,8},{8,10},{10,12},{12,14},{14,0},{1,3},{3,5},... | collective-permute-start | bytes 6291464 | tf_op jit(solution)/shard_map/ppermute | solution.py:14
  14.4 48.7 %collective-permute-done = bf16[128,8192]{1,0:T(8,128)(2,1)S(1)} collective-permute-done((bf16[128,8192]{1,0:T(8,128)(2,1)S(1)}, bf16[128,8192]{1,0:T(8,128)(2,1)S(1)}, u32[]{:S(2)}, u32[]{:S(2)}) %collective-permute-start) | collective-permute-done | bytes 2097184 | tf_op jit(solution)/shard_map/ppermute | solution.py:14
  63.0 0.0 collective-permute-start.1
  63.7 7.4 %fusion.2 = f32[640,128]{0,1:T(8,128)S(1)} fusion(bf16[128,8192]{1,0:T(8,128)(2,1)S(1)} %multiply_convert_fusion, bf16[640,8192]{1,0:T(8,128)(2,1)} %param.5, f32[640]{0:T(1024)S(1)} %fusion.3), kind=kOutput, calls=%fused_computation.6 | convolution fusion | flops 1342259200 | bytes 12913152 | tf_op jit(solution)/shard_map/dot_general | solution.py:18
  71.1 0.9 copy.7
  72.0 0.0 reduce-scatter.10.cloned.1.call-update
  72.0 0.0 reduce-scatter.12.cloned.1.call-start
  72.0 7.3 %fusion.1 = f32[640,128]{0,1:T(8,128)S(1)} fusion(bf16[128,8192]{1,0:T(8,128)(2,1)S(1)} %collective-permute-done, bf16[640,8192]{1,0:T(8,128)(2,1)} %param.5, f32[640]{0:T(1024)S(1)} %fusion.3), kind=kOutput, calls=%fused_computation.4 | convolution fusion | flops 1342259200 | bytes 12913152 | tf_op jit(solution)/shard_map/dot_general | solution.py:18
  79.4 0.9 copy.9
  80.3 0.0 reduce-scatter.12.cloned.1.call-update
  80.3 0.0 reduce-scatter.14.cloned.1.call-start
  80.4 32.3 %collective-permute-done.1 = bf16[128,8192]{1,0:T(8,128)(2,1)} collective-permute-done((bf16[128,8192]{1,0:T(8,128)(2,1)S(1)}, bf16[128,8192]{1,0:T(8,128)(2,1)}, u32[]{:S(2)}, u32[]{:S(2)}) %collective-permute-start.1) | collective-permute-done | bytes 2097184 | tf_op jit(solution)/shard_map/ppermute | solution.py:14
  112.6 8.0 %fusion = f32[640,128]{0,1:T(8,128)S(1)} fusion(bf16[128,8192]{1,0:T(8,128)(2,1)} %collective-permute-done.1, bf16[640,8192]{1,0:T(8,128)(2,1)} %param.5, f32[640]{0:T(1024)S(1)} %fusion.3), kind=kOutput, calls=%fused_computation.2 | convolution fusion | flops 1342259200 | bytes 12913152 | tf_op jit(solution)/shard_map/dot_general | solution.py:18
  120.6 0.9 copy.11
  121.5 0.0 reduce-scatter.14.cloned.1.call-update
  121.5 0.0 reduce-scatter.10.cloned.1.call-done
  121.6 1.0 copy.8
  122.6 0.0 reduce-scatter.12.cloned.1.call-done
  122.6 1.0 copy.10
  123.7 2.8 %reduce-scatter.14.cloned.1.call-done = f32[320,128]{1,0:T(8,128)} async-done(((f32[640,128]{1,0:T(8,128)}), f32[320,128]{1,0:T(8,128)}) %reduce-scatter.14.cloned.1.call-update) | async-done | bytes 163856
  126.5 1.0 copy.12
  127.6 1.0 copy.6
  (2 shorter events, 0.0 us)
Async XLA Ops:
  6.5 115.0 %reduce-scatter.10.cloned.1.call-start = ((), (), s32[]{:S(2)}) async-start(), calls=%async_computation.3 | async-start | bytes 491520
  11.3 51.7 %collective-permute-start = (bf16[128,8192]{1,0:T(8,128)(2,1)S(1)}, bf16[128,8192]{1,0:T(8,128)(2,1)S(1)}, u32[]{:S(2)}, u32[]{:S(2)}) collective-permute-start(bf16[128,8192]{1,0:T(8,128)(2,1)S(1)} %multiply_convert_fusion), channel_id=1, source_target_pairs={{0,2},{2,4},{4,6},{6,8},{8,10},{10,12},{12,14},{14,0},{1,3},{3,5},... | collective-permute-start | bytes 6291464 | tf_op jit(solution)/shard_map/ppermute | solution.py:14
  63.0 49.6 %collective-permute-start.1 = (bf16[128,8192]{1,0:T(8,128)(2,1)S(1)}, bf16[128,8192]{1,0:T(8,128)(2,1)}, u32[]{:S(2)}, u32[]{:S(2)}) collective-permute-start(bf16[128,8192]{1,0:T(8,128)(2,1)S(1)} %collective-permute-done), channel_id=1, source_target_pairs={{0,2},{2,4},{4,6},{6,8},{8,10},{10,12},{12,14},{14,0},{1,3},{3,5},... | collective-permute-start | bytes 6291464 | tf_op jit(solution)/shard_map/ppermute | solution.py:14
  72.0 50.7 %reduce-scatter.12.cloned.1.call-start = ((), (), s32[]{:S(2)}) async-start(), calls=%async_computation.4 | async-start | bytes 491520
  80.3 46.2 %reduce-scatter.14.cloned.1.call-start = ((), (), s32[]{:S(2)}) async-start(), calls=%async_computation.5 | async-start | bytes 491520
Sparse Core Ops, SparseCore 0:
  72.1 9.1 reduce-scatter.9
  83.6 8.9 reduce-scatter.11
  121.7 4.7 reduce-scatter.13
where the time goes:
time: 136 us; the launch traced here: 135 us
  waiting for transfers between devices  83.8 us (62%)
  matrix products  22.7 us (17%)
  between operations  14.5 us (11%)
  local copies, waits for them, and re-layouts  6.84 us (5%)
  other arithmetic  4.18 us (3%)
  starting transfers between devices  3.11 us (2%)
    ppermute x2, waiting for transfers between devices, passed_along(): lax.ppermute(value, axis, [(i, (i + by) % count) for i in range(count)])  80.9 us
    dot_general x3, matrix products, block_scores(): lax.dot_general(doc_rows, block, (((1,), (1,)), ((), ())), preferred_elem...  22.7 us
    unnamed x6, local copies, waits for them, and re-layouts  5.85 us
    ppermute x2, starting transfers between devices, passed_along(): lax.ppermute(value, axis, [(i, (i + by) % count) for i in range(count)])  3.02 us
    unnamed x6, waiting for transfers between devices  2.9 us
  transfers between devices with their start and end apart: 5, of which 3 were waited for; matrix products, arithmetic and copies ran while one was open for 20% of the time, Pallas kernels for 0%

commit v1 on v0

v1 whole, which is shorter than its diff:
```python
import functools
import math

import jax
import jax.numpy as jnp
from jax import lax
from jax.experimental import pallas as pl
from jax.experimental.pallas import tpu as pltpu
from jax.sharding import PartitionSpec as P

L_DIM = 8192
CHUNKS = 8
PHASES = 6


def score_kernel(count, targets, fresh, where_ref, documents, inverse, *refs):
    blocks = max(targets) + 1
    chunks, refs = refs[:count], refs[count:]
    if fresh:
        sums, refs = None, refs
    else:
        sums, refs = refs[0], refs[1:]
    out, rows_buf, sem = refs
    half = documents.shape[0] // 2
    width = chunks[0].shape[1]
    layer = where_ref[count]

    def copies(i):
        column = pl.multiple_of(where_ref[i] * width, width)
        return [
            pltpu.make_async_copy(
                documents.at[
                    pl.ds(pl.multiple_of(row * half, half), half), pl.ds(column, width)
                ],
                rows_buf.at[i, pl.ds(place * half, half), :],
                sem.at[i, place],
            )
            for place, row in enumerate((1 - layer, layer))
        ]

    for i in range(count):
        for copy in copies(i):
            copy.start()
    for b in range(blocks):
        out[b] = jnp.zeros_like(out[b]) if fresh else sums[b]
    for i in range(count):
        for copy in copies(i):
            copy.wait()
        scaled = chunks[i][...].astype(jnp.float32) * inverse[where_ref[i]]
        out[targets[i]] += lax.dot_general(
            rows_buf[i],
            scaled.astype(jnp.bfloat16),
            (((1,), (1,)), ((), ())),
            preferred_element_type=jnp.float32,
        )


def add_scores(documents, inverse, layer, chunks, places, targets, sums=None):
    count = len(chunks)
    blocks = max(targets) + 1
    doc_rows = documents.shape[0]
    rows, width = chunks[0].shape
    where = jnp.stack([jnp.asarray(p, jnp.int32) for p in places] + [layer])
    vmem = pl.BlockSpec(memory_space=pltpu.VMEM)
    operands = [where, documents, inverse, *chunks]
    specs = [pl.BlockSpec(memory_space=pltpu.SMEM), pl.BlockSpec(memory_space=pl.ANY)]
    specs += [vmem] * (1 + count)
    if sums is not None:
        operands.append(sums)
        specs.append(vmem)
    return pl.pallas_call(
        functools.partial(score_kernel, count, targets, sums is None),
        out_shape=jax.ShapeDtypeStruct((blocks, doc_rows, rows), jnp.float32),
        in_specs=specs,
        out_specs=vmem,
        scratch_shapes=[
            pltpu.VMEM((count, doc_rows, width), documents.dtype),
            pltpu.SemaphoreType.DMA((count, 2)),
        ],
        compiler_params=pltpu.CompilerParams(vmem_limit_bytes=40 * 1024 * 1024),
        cost_estimate=pl.CostEstimate(
            flops=2 * count * doc_rows * rows * width,
            bytes_accessed=count * doc_rows * width * 2,
            transcendentals=0,
        ),
    )(*operands)


def on_device(queries, documents, counts, eigenvalues):
    dim_here = eigenvalues.shape[0]
    owners = lax.axis_size("dp")
    rows = queries.shape[0]
    doc_rows = documents.shape[0]
    half = doc_rows // 2
    width = dim_here // CHUNKS
    group, owner, layer = (lax.axis_index(a).astype(jnp.int32) for a in ("groups", "dp", "layer"))
    even = owner % 2 == 0

    def place(k):
        return jnp.where(group == 0, k, CHUNKS - 1 - k).astype(jnp.int32)

    own = [
        lax.dynamic_slice(queries, (0, place(k) * width), (rows, width)) for k in range(PHASES)
    ]
    ahead = [(i, (i + 2) % owners) for i in range(owners)]
    up = [(i, i + 1) for i in range(0, owners, 2)]
    down = [(i + 1, i) for i in range(0, owners, 2)]
    across = [(0, 1), (1, 0)]

    far, near, far_across, near_across = [], [], [], []
    for p in range(PHASES):
        far.append(lax.ppermute(own[p], "dp", ahead))
        if p == 0:
            near.append(lax.ppermute(own[0], "dp", up))
        elif p < PHASES - 1:
            near.append(lax.ppermute(jnp.where(even, own[p], far[p - 1]), "dp", up + down))
        else:
            near.append(lax.ppermute(far[p - 1], "dp", down))
        if p in (1, 3):
            far_across.append(lax.ppermute(far[(p - 1) // 2], "groups", across))
        elif p >= 2:
            k = {2: 0, 4: 1, 5: 2}[p]
            near_across.append(
                lax.ppermute(jnp.where(even, near[k + 1], near[k]), "groups", across)
            )

    blocks = eigenvalues.reshape(dim_here // L_DIM, L_DIM)
    damping = 0.1 * jnp.mean(blocks, axis=1, keepdims=True)
    inverse = (1.0 / (blocks + damping)).reshape(CHUNKS, 1, width)

    run = functools.partial(add_scores, documents, inverse, layer)
    mine0 = run(
        [queries[:, k * width : (k + 1) * width] for k in range(CHUNKS)],
        list(range(CHUNKS)),
        [0] * CHUNKS,
    )
    got0 = lax.ppermute(mine0[0, :half], "layer", across)

    near_k = [jnp.where(even, near[k + 1], near[k]) for k in range(PHASES - 1)]
    first = run(
        [far[0], far[1], far[2], near_k[0], near_k[1], far_across[0], near_across[0]],
        [place(0), place(1), place(2), place(0), place(1), place(CHUNKS - 1), place(CHUNKS - 1)],
        [1, 1, 1, 0, 0, 1, 0],
    )
    second = run(
        [far[3], far[4], near_k[2], near_k[3], far_across[1], near_across[1]],
        [place(3), place(4), place(2), place(3), place(CHUNKS - 2), place(CHUNKS - 2)],
        [1, 1, 0, 0, 1, 0],
        first,
    )
    last = run(
        [far[5], near_k[4], near_across[2]],
        [place(5), place(4), place(CHUNKS - 3)],
        [1, 0, 0],
        second,
    )
    got12 = lax.ppermute(last[:, :half], "layer", across)
    factor = 1.0 / math.sqrt(dim_here * lax.axis_size("layer"))
    doc_index = layer * half + jnp.arange(half, dtype=jnp.int32)
    scale = (factor * (doc_index < counts[0]).astype(jnp.float32))[:, None]
    both = last[:, half:] + got12
    return jnp.concatenate([mine0[0, half:] + got0, both[0], both[1]], axis=1) * scale


def solution(mesh):
    return jax.shard_map(
        on_device,
        mesh=mesh,
        in_specs=(P("dp", "layer"), P(("groups", "dp"), "layer"), P(("groups", "dp")), P("layer")),
        out_specs=P(("groups", "dp", "layer"), None),
        check_vma=False,
    )
```

time: 136 us -> 120 us (0.88)
  waiting for transfers between devices: 83.8 us -> 51.9 us
  Pallas kernels: 0 us -> 24.3 us
  matrix products: 22.7 us -> 0 us
  starting transfers between devices: 3.11 us -> 16.8 us
  between operations: 14.5 us -> 1.61 us
  local copies, waits for them, and re-layouts: 6.84 us -> 13.6 us
  other arithmetic: 4.18 us -> 10.7 us
    ppermute x2 -> x19, waiting for transfers between devices: 80.9 us -> 51.9 us  [the longest x6 35.6 us: on_device(): far.append(lax.ppermute(own[p], 'dp', ahead))]
    pallas_call x0 -> x4, Pallas kernels: none -> 24.3 us  [add_scores(): pl.pallas_call(functools.partial(score_kernel, count, targets, sums is No...]
    dot_general x3 -> x0, matrix products: 22.7 us -> none  [block_scores(): lax.dot_general(doc_rows, block, (((1,), (1,)), ((), ())), preferred_elem...]
    ppermute x2 -> x19, starting transfers between devices: 3.02 us -> 16.8 us  [the longest x4 4.05 us: on_device(): lax.ppermute(jnp.where(even, own[p], far[p - 1]), 'dp', up + down)]
    select_n x0 -> x5, other arithmetic: none -> 9.01 us  [the longest x4 7.09 us: on_device(): jnp.where(even, own[p], far[p - 1])]
    unnamed x6 -> x34, local copies, waits for them, and re-layouts: 5.85 us -> 11.6 us
    unnamed x6 -> x0, waiting for transfers between devices: 2.9 us -> none
    convert_element_type x1 -> x0, other arithmetic: 1.99 us -> none  [on_device(): precond = (queries.astype(jnp.float32) * inverse).astype(jnp.bfloat16)]
  transfers between devices with their start and end apart: 5 -> 19, of which waited for: 3 -> 11; matrix products, arithmetic and copies ran while one was open for 20% -> 4% of each run, Pallas kernels for 0% -> 20%
where the time goes in v1:
time: 120 us; the launch traced here: 119 us
  waiting for transfers between devices  51.9 us (43%)
  Pallas kernels  24.3 us (20%)
  starting transfers between devices  16.8 us (14%)
  local copies, waits for them, and re-layouts  13.6 us (11%)
  other arithmetic  10.7 us (9%)
  between operations  1.61 us (1%)
    ppermute x6, waiting for transfers between devices, on_device(): far.append(lax.ppermute(own[p], 'dp', ahead))  35.6 us
    pallas_call x4, Pallas kernels, add_scores(): pl.pallas_call(functools.partial(score_kernel, count, targets, sums is No...  24.3 us
    unnamed x34, local copies, waits for them, and re-layouts  11.6 us
    ppermute x4, waiting for transfers between devices, on_device(): lax.ppermute(jnp.where(even, own[p], far[p - 1]), 'dp', up + down)  11.2 us
    select_n x4, other arithmetic, on_device(): jnp.where(even, own[p], far[p - 1])  7.09 us
    ppermute x4, starting transfers between devices, on_device(): lax.ppermute(jnp.where(even, own[p], far[p - 1]), 'dp', up + down)  4.05 us
    ppermute x6, starting transfers between devices, on_device(): far.append(lax.ppermute(own[p], 'dp', ahead))  3.15 us
    ppermute x1, starting transfers between devices, on_device(): near.append(lax.ppermute(own[0], 'dp', up))  2.99 us
  transfers between devices with their start and end apart: 19, of which 11 were waited for; matrix products, arithmetic and copies ran while one was open for 4% of the time, Pallas kernels for 20%

profile of v1, /device:TPU:0, one launch (start us, length us, event | category | flops | bytes accessed | tf_op | source)
XLA Modules:
  0.0 118.9 jit_solution(6348739360497660309)
XLA Ops:
  0.0 1.7 %constant_dynamic-slice_fusion = bf16[128,1024]{1,0:T(8,128)(2,1)} fusion(bf16[128,8192]{1,0:T(8,128)(2,1)} %param.4, s32[]{:T(128)S(6)} %select_n.130), kind=kLoop, calls=%fused_computation.19 | loop fusion | bytes 524292 | tf_op jit(solution)/shard_map/dynamic_slice | solution.py:103
  1.7 3.0 %collective-permute-start.12 = (bf16[128,1024]{1,0:T(8,128)(2,1)}, bf16[128,1024]{1,0:T(8,128)(2,1)S(1)}, u32[]{:S(2)}, u32[]{:S(2)}) collective-permute-start(bf16[128,1024]{1,0:T(8,128)(2,1)} %constant_dynamic-slice_fusion), channel_id=1, source_target_pairs={{0,4},{2,6},{4,8},{6,10},{8,12},{10,14},{12,0},{14,2},{1,5},{3,7},... | collective-permute-start | bytes 786440 | tf_op jit(solution)/shard_map/ppermute | solution.py:112
  4.7 8.5 %collective-permute-done.12.refs_0_ = bf16[128,1024]{1,0:T(8,128)(2,1)S(1)} collective-permute-done((bf16[128,1024]{1,0:T(8,128)(2,1)}, bf16[128,1024]{1,0:T(8,128)(2,1)S(1)}, u32[]{:S(2)}, u32[]{:S(2)}) %collective-permute-start.12) | collective-permute-done | bytes 262176 | tf_op jit(solution)/shard_map/ppermute | solution.py:112
  13.2 1.0 broadcast_select_fusion.2
  14.3 9.3 %collective-permute-done.8.refs_1_ = bf16[128,1024]{1,0:T(8,128)(2,1)S(1)} collective-permute-done((bf16[128,1024]{1,0:T(8,128)(2,1)S(1)}, bf16[128,1024]{1,0:T(8,128)(2,1)S(1)}, u32[]{:S(2)}, u32[]{:S(2)}) %collective-permute-start.8) | collective-permute-done | bytes 262176 | tf_op jit(solution)/shard_map/ppermute | solution.py:112
  23.6 3.0 %broadcast_select_fusion.5 = (bf16[128,1024]{1,0:T(8,128)(2,1)S(1)}, bf16[128,1024]{1,0:T(8,128)(2,1)S(1)}, bf16[128,1024]{1,0:T(8,128)(2,1)}, bf16[128,1024]{1,...) fusion(bf16[128,1024]{1,0:T(8,128)(2,1)S(1)} %collective-permut, ...), kind=kLoop, calls=%fused_computation.7 | loop fusion | flops 131072 | bytes 5242885 | tf_op jit(solution)/shard_map/jit(_where)/select_n | solution.py:116
  26.6 8.4 %collective-permute-done.6.refs_2_ = bf16[128,1024]{1,0:T(8,128)(2,1)S(1)} collective-permute-done((bf16[128,1024]{1,0:T(8,128)(2,1)S(1)}, bf16[128,1024]{1,0:T(8,128)(2,1)S(1)}, u32[]{:S(2)}, u32[]{:S(2)}) %collective-permute-start.6) | collective-permute-done | bytes 262176 | tf_op jit(solution)/shard_map/ppermute | solution.py:112
  35.0 1.0 broadcast_select_fusion.6
  36.1 3.0 %collective-permute-start.15 = (bf16[128,1024]{1,0:T(8,128)(2,1)}, bf16[128,1024]{1,0:T(8,128)(2,1)S(1)}, u32[]{:S(2)}, u32[]{:S(2)}) collective-permute-start(bf16[128,1024]{1,0:T(8,128)(2,1)} %constant_dynamic-slice_fusion), channel_id=1, source_target_pairs={{0,2},{4,6},{8,10},{12,14},{1,3},{5,7},{9,11},{13,15},{16,18},{20,... | collective-permute-start | bytes 786440 | tf_op jit(solution)/shard_map/ppermute | solution.py:114
  39.1 5.1 %collective-permute-done.4.refs_0_ = bf16[128,1024]{1,0:T(8,128)(2,1)S(1)} collective-permute-done((bf16[128,1024]{1,0:T(8,128)(2,1)S(1)}, bf16[128,1024]{1,0:T(8,128)(2,1)S(1)}, u32[]{:S(2)}, u32[]{:S(2)}) %collective-permute-start.4) | collective-permute-done | bytes 262176 | tf_op jit(solution)/shard_map/ppermute | solution.py:112
  44.2 2.0 %broadcast_select_fusion.8 = (bf16[128,1024]{1,0:T(8,128)(2,1)S(1)}, bf16[128,1024]{1,0:T(8,128)(2,1)}, bf16[128,1024]{1,0:T(8,128)(2,1)}) fusion(bf16[128,1024]{1,0:T(8,128)(2,1)S(1)} %collective-permute-done.4.refs_0_, pred[]{:T(512)S(6)} %eq.7, bf16[128,8192]{1,0:T(8,128)(2,1)} %param.4, s32[]{:T(128)S(6)} %select_n.115, s32[]{:T(128)S(6)} %select_n.112), kind=kLoop, calls=%fused_computation.10 | loop fusion | flops 131072 | bytes 1572873 | tf_op jit(solution)/shard_map/jit(_where)/select_n | solution.py:116
  46.3 1.1 collective-permute-start.13
  47.4 1.0 collective-permute-start.9
  48.3 1.1 collective-permute-start.7
  49.4 1.0 collective-permute-start.5
  50.3 4.3 %collective-permute-done.2.refs_1_ = bf16[128,1024]{1,0:T(8,128)(2,1)S(1)} collective-permute-done((bf16[128,1024]{1,0:T(8,128)(2,1)}, bf16[128,1024]{1,0:T(8,128)(2,1)S(1)}, u32[]{:S(2)}, u32[]{:S(2)}) %collective-permute-start.2) | collective-permute-done | bytes 262176 | tf_op jit(solution)/shard_map/ppermute | solution.py:112
  54.7 1.3 %collective-permute-start.3 = (bf16[128,1024]{1,0:T(8,128)(2,1)S(1)}, bf16[128,1024]{1,0:T(8,128)(2,1)}, u32[]{:S(2)}, u32[]{:S(2)}) collective-permute-start(bf16[128,1024]{1,0:T(8,128)(2,1)S(1)} %collective-permute-done.2.refs_1_), channel_id=1, source_target_pairs={{2,0},{6,4},{10,8},{14,12},{3,1},{7,5},{11,9},{15,13},{18,16},{22,... | collective-permute-start | bytes 786440 | tf_op jit(solution)/shard_map/ppermute | solution.py:118
  55.9 0.1 pad_add_fusion.where_ref
  56.7 0.6 reduce_sum.9
  57.9 0.1 stack.58.where_ref
  58.0 0.1 stack.62.where_ref
  58.1 0.1 stack.51.where_ref
  58.2 1.1 collective-permute-start.16
  59.4 1.8 %collective-permute-done.9 = bf16[128,1024]{1,0:T(8,128)(2,1)S(1)} collective-permute-done((bf16[128,1024]{1,0:T(8,128)(2,1)S(1)}, bf16[128,1024]{1,0:T(8,128)(2,1)S(1)}, u32[]{:S(2)}, u32[]{:S(2)}) %collective-permute-start.9) | collective-permute-done | bytes 262176 | tf_op jit(solution)/shard_map/ppermute | solution.py:116
  61.1 5.6 %collective-permute-done.7 = bf16[128,1024]{1,0:T(8,128)(2,1)S(1)} collective-permute-done((bf16[128,1024]{1,0:T(8,128)(2,1)S(1)}, bf16[128,1024]{1,0:T(8,128)(2,1)S(1)}, u32[]{:S(2)}, u32[]{:S(2)}) %collective-permute-start.7) | collective-permute-done | bytes 262176 | tf_op jit(solution)/shard_map/ppermute | solution.py:116
  66.8 3.8 %collective-permute-done.5 = bf16[128,1024]{1,0:T(8,128)(2,1)} collective-permute-done((bf16[128,1024]{1,0:T(8,128)(2,1)S(1)}, bf16[128,1024]{1,0:T(8,128)(2,1)}, u32[]{:S(2)}, u32[]{:S(2)}) %collective-permute-start.5) | collective-permute-done | bytes 262176 | tf_op jit(solution)/shard_map/ppermute | solution.py:116
  70.5 2.8 %collective-permute-done.3 = bf16[128,1024]{1,0:T(8,128)(2,1)} collective-permute-done((bf16[128,1024]{1,0:T(8,128)(2,1)S(1)}, bf16[128,1024]{1,0:T(8,128)(2,1)}, u32[]{:S(2)}, u32[]{:S(2)}) %collective-permute-start.3) | collective-permute-done | bytes 262176 | tf_op jit(solution)/shard_map/ppermute | solution.py:118
  73.4 1.9 %broadcast_select_fusion = (bf16[128,1024]{1,0:T(8,128)(2,1)S(1)}, bf16[128,1024]{1,0:T(8,128)(2,1)S(1)}, bf16[128,1024]{1,0:T(8,128)(2,1)}, bf16[128,1024]{1,0:T(8,128)(2,1)}, bf16[128,1024]{1,0:T(8,128)(2,1)}) fusion(bf16[128,1024]{1,0:T(8,128)(2,1)S(1)} %collective-permute-done.13, bf16[128,1024]{1,0:T(8,128)(2,1)S(1)} %collective-permute-done.15, ...), kind=kLoop, calls=%fused_computation.2 | loop fusion | flops 655360 | bytes 2883585 | tf_op jit(solution)/shard_map/jit(_where)/select_n | solution.py:139
  75.3 0.6 collective-permute-start.17
  75.9 4.0 %copy-done = bf16[640,8192]{1,0:T(8,128)(2,1)S(1)} copy-done((bf16[640,8192]{1,0:T(8,128)(2,1)S(1)}, bf16[640,8192]{1,0:T(8,128)(2,1)}, u32[]{:S(2)}) %copy-start) | copy-done | bytes 10485784
  79.9 0.9 copy-done.2
  80.8 0.9 copy-done.3
  81.8 0.9 copy-done.4
  82.7 0.9 copy-done.5
  83.7 0.9 copy-done.6
  84.6 0.9 copy-done.7
  85.6 0.9 copy-done.8
  86.5 0.9 copy-done.9
  87.5 7.6 %shard_map.46 = f32[1,640,128]{2,1,0:T(8,128)S(1)} custom-call(s32[9]{0:T(128)S(1)} %stack.51.where_ref, bf16[640,8192]{1,0:T(8,128)(2,1)S(1)} %copy-done, f32[8,1,1024]{2,1,0:T(1,128)S(1)} %bitcast.22, bf16[128,1024]{1,0:T(8,128)(2,1)S(1)} %copy-done.9, bf16[128,1024]{1,0:T(8,128)(2,1)S(1)} %copy-done.8, bf16[128,1024]{1,0:T(8,128)(2,1)S(1)} %copy-done.7, ...), custom_call_target="tpu_custom_call" | custom-call | flops 1342177280 | bytes 10485760 | tf_op jit(solution)/shard_map/pallas_call | solution.py:71
  95.1 1.5 %collective-permute-start.11 = (bf16[128,1024]{1,0:T(8,128)(2,1)S(1)}, bf16[128,1024]{1,0:T(8,128)(2,1)S(1)}, u32[]{:S(2)}, u32[]{:S(2)}) collective-permute-start(bf16[128,1024]{1,0:T(8,128)(2,1)S(1)} %collective-permute-done.8.refs_1_), channel_id=1, source_target_pairs={{0,16},{16,0},{1,17},{17,1},{2,18},{18,2},{3,19},{19,3},{4,20},{20... | collective-permute-start | bytes 786440 | tf_op jit(solution)/shard_map/ppermute | solution.py:120
  96.6 0.6 collective-permute-start.14
  97.2 1.5 %collective-permute-start.10 = (bf16[128,1024]{1,0:T(8,128)(2,1)}, bf16[128,1024]{1,0:T(8,128)(2,1)S(1)}, u32[]{:S(2)}, u32[]{:S(2)}) collective-permute-start(bf16[128,1024]{1,0:T(8,128)(2,1)} %get-tuple-element.26.refs_2_), channel_id=1, source_target_pairs={{0,16},{16,0},{1,17},{17,1},{2,18},{18,2},{3,19},{19,3},{4,20},{20... | collective-permute-start | bytes 786440 | tf_op jit(solution)/shard_map/ppermute | solution.py:124
  98.8 7.1 %shard_map.47.refs_6_ = f32[2,640,128]{2,1,0:T(8,128)S(1)} custom-call(s32[8]{0:T(128)S(1)} %stack.62.where_ref, bf16[640,8192]{1,0:T(8,128)(2,1)S(1)} %copy-done.1, f32[8,1,1024]{2,1,0:T(1,128)S(1)} %bitcast.23, bf16[128,1024]{1,0:T(8,128)(2,1)S(1)} %collective-permute-done.12.refs_0_, bf16[128,1024]{1,0:T(8,128)(2,1)S(1)} %collective-permute-done.8.refs_1_, ...), custom_call_target="tpu_custom_call" | custom-call | flops 1174405120 | bytes 9175040 | tf_op jit(solution)/shard_map/pallas_call | solution.py:71
  105.9 0.7 collective-permute-done.14.refs_5_
  106.6 6.4 %shard_map.48.refs_3_ = f32[2,640,128]{2,1,0:T(8,128)S(1)} custom-call(s32[7]{0:T(128)S(1)} %stack.58.where_ref, bf16[640,8192]{1,0:T(8,128)(2,1)S(1)} %copy-done.1, f32[8,1,1024]{2,1,0:T(1,128)S(1)} %bitcast.24, bf16[128,1024]{1,0:T(8,128)(2,1)S(1)} %copy-done.12, bf16[128,1024]{1,0:T(8,128)(2,1)S(1)} %copy-done.15, ...), custom_call_target="tpu_custom_call" | custom-call | flops 1006632960 | bytes 7864320 | tf_op jit(solution)/shard_map/pallas_call | solution.py:71
  113.1 3.2 %shard_map.49 = f32[2,640,128]{2,1,0:T(8,128)S(1)} custom-call(s32[4]{0:T(128)S(1)} %pad_add_fusion.where_ref, bf16[640,8192]{1,0:T(8,128)(2,1)S(1)} %copy-done.1, f32[8,1,1024]{2,1,0:T(1,128)S(1)} %bitcast.25, bf16[128,1024]{1,0:T(8,128)(2,1)S(1)} %collective-permute-done.1.refs_0_, bf16[128,1024]{1,0:T(8,128)(2,1)S(1)} %copy-done.10, ...), custom_call_target="tpu_custom_call" | custom-call | flops 503316480 | bytes 3932160 | tf_op jit(solution)/shard_map/pallas_call | solution.py:71
  116.4 1.6 %collective-permute-done.18 = f32[2,320,128]{2,1,0:T(8,128)S(1)} collective-permute-done((f32[2,320,128]{2,1,0:T(8,128)S(1)}, f32[2,320,128]{2,1,0:T(8,128)S(1)}, u32[]{:S(2)}, u32[]{:S(2)}) %collective-permute-start.18) | collective-permute-done | bytes 327712 | tf_op jit(solution)/shard_map/ppermute | solution.py:157
  118.0 0.9 maximum_multiply_fusion
  (47 shorter events, 0.5 us)
Async XLA Ops:
  1.7 11.6 %collective-permute-start.12 = (bf16[128,1024]{1,0:T(8,128)(2,1)}, bf16[128,1024]{1,0:T(8,128)(2,1)S(1)}, u32[]{:S(2)}, u32[]{:S(2)}) collective-permute-start(bf16[128,1024]{1,0:T(8,128)(2,1)} %constant_dynamic-slice_fusion), channel_id=1, source_target_pairs={{0,4},{2,6},{4,8},{6,10},{8,12},{10,14},{12,0},{14,2},{1,5},{3,7},... | collective-permute-start | bytes 786440 | tf_op jit(solution)/shard_map/ppermute | solution.py:112
  14.3 9.3 %collective-permute-start.8 = (bf16[128,1024]{1,0:T(8,128)(2,1)S(1)}, bf16[128,1024]{1,0:T(8,128)(2,1)S(1)}, u32[]{:S(2)}, u32[]{:S(2)}) collective-permute-start(bf16[128,1024]{1,0:T(8,128)(2,1)S(1)} %get-tuple-element.6), channel_id=1, source_target_pairs={{0,4},{2,6},{4,8},{6,10},{8,12},{10,14},{12,0},{14,2},{1,5},{3,7},... | collective-permute-start | bytes 786440 | tf_op jit(solution)/shard_map/ppermute | solution.py:112
  26.6 30.1 %copy-start.16 = (f32[8192]{0:T(1024)S(1)}, f32[8192]{0:T(1024)}, u32[]{:S(2)}) copy-start(f32[8192]{0:T(1024)} %param.7) | copy-start | bytes 98308
  26.6 8.4 %collective-permute-start.6 = (bf16[128,1024]{1,0:T(8,128)(2,1)S(1)}, bf16[128,1024]{1,0:T(8,128)(2,1)S(1)}, u32[]{:S(2)}, u32[]{:S(2)}) collective-permute-start(bf16[128,1024]{1,0:T(8,128)(2,1)S(1)} %get-tuple-element.8), channel_id=1, source_target_pairs={{0,4},{2,6},{4,8},{6,10},{8,12},{10,14},{12,0},{14,2},{1,5},{3,7},... | collective-permute-start | bytes 786440 | tf_op jit(solution)/shard_map/ppermute | solution.py:112
  36.0 8.2 %collective-permute-start.4 = (bf16[128,1024]{1,0:T(8,128)(2,1)S(1)}, bf16[128,1024]{1,0:T(8,128)(2,1)S(1)}, u32[]{:S(2)}, u32[]{:S(2)}) collective-permute-start(bf16[128,1024]{1,0:T(8,128)(2,1)S(1)} %get-tuple-element.10), channel_id=1, source_target_pairs={{0,4},{2,6},{4,8},{6,10},{8,12},{10,14},{12,0},{14,2},{1,5},{3,7},... | collective-permute-start | bytes 786440 | tf_op jit(solution)/shard_map/ppermute | solution.py:112
  36.1 13.3 %collective-permute-start.15 = (bf16[128,1024]{1,0:T(8,128)(2,1)}, bf16[128,1024]{1,0:T(8,128)(2,1)S(1)}, u32[]{:S(2)}, u32[]{:S(2)}) collective-permute-start(bf16[128,1024]{1,0:T(8,128)(2,1)} %constant_dynamic-slice_fusion), channel_id=1, source_target_pairs={{0,2},{4,6},{8,10},{12,14},{1,3},{5,7},{9,11},{13,15},{16,18},{20,... | collective-permute-start | bytes 786440 | tf_op jit(solution)/shard_map/ppermute | solution.py:114
  44.2 31.0 %copy-start.11 = (bf16[128,1024]{1,0:T(8,128)(2,1)}, bf16[128,1024]{1,0:T(8,128)(2,1)S(1)}, u32[]{:S(2)}) copy-start(bf16[128,1024]{1,0:T(8,128)(2,1)S(1)} %collective-permute-done.4.refs_0_) | copy-start | bytes 786436
  46.3 8.4 %collective-permute-start.2 = (bf16[128,1024]{1,0:T(8,128)(2,1)}, bf16[128,1024]{1,0:T(8,128)(2,1)S(1)}, u32[]{:S(2)}, u32[]{:S(2)}) collective-permute-start(bf16[128,1024]{1,0:T(8,128)(2,1)} %get-tuple-element.12), channel_id=1, source_target_pairs={{0,4},{2,6},{4,8},{6,10},{8,12},{10,14},{12,0},{14,2},{1,5},{3,7},... | collective-permute-start | bytes 786440 | tf_op jit(solution)/shard_map/ppermute | solution.py:112
  46.3 12.0 %collective-permute-start.13 = (bf16[128,1024]{1,0:T(8,128)(2,1)S(1)}, bf16[128,1024]{1,0:T(8,128)(2,1)S(1)}, u32[]{:S(2)}, u32[]{:S(2)}) collective-permute-start(bf16[128,1024]{1,0:T(8,128)(2,1)S(1)} %get-tuple-element.5), channel_id=1, source_target_pairs={{0,2},{4,6},{8,10},{12,14},{2,0},{6,4},{10,8},{14,12},{1,3},{5,7},... | collective-permute-start | bytes 786440 | tf_op jit(solution)/shard_map/ppermute | solution.py:116
  47.4 13.8 %collective-permute-start.9 = (bf16[128,1024]{1,0:T(8,128)(2,1)S(1)}, bf16[128,1024]{1,0:T(8,128)(2,1)S(1)}, u32[]{:S(2)}, u32[]{:S(2)}) collective-permute-start(bf16[128,1024]{1,0:T(8,128)(2,1)S(1)} %get-tuple-element.7), channel_id=1, source_target_pairs={{0,2},{4,6},{8,10},{12,14},{2,0},{6,4},{10,8},{14,12},{1,3},{5,7},... | collective-permute-start | bytes 786440 | tf_op jit(solution)/shard_map/ppermute | solution.py:116
  48.3 18.5 %collective-permute-start.7 = (bf16[128,1024]{1,0:T(8,128)(2,1)S(1)}, bf16[128,1024]{1,0:T(8,128)(2,1)S(1)}, u32[]{:S(2)}, u32[]{:S(2)}) collective-permute-start(bf16[128,1024]{1,0:T(8,128)(2,1)S(1)} %get-tuple-element.9), channel_id=1, source_target_pairs={{0,2},{4,6},{8,10},{12,14},{2,0},{6,4},{10,8},{14,12},{1,3},{5,7},... | collective-permute-start | bytes 786440 | tf_op jit(solution)/shard_map/ppermute | solution.py:116
  49.4 21.2 %collective-permute-start.5 = (bf16[128,1024]{1,0:T(8,128)(2,1)S(1)}, bf16[128,1024]{1,0:T(8,128)(2,1)}, u32[]{:S(2)}, u32[]{:S(2)}) collective-permute-start(bf16[128,1024]{1,0:T(8,128)(2,1)S(1)} %get-tuple-element.11), channel_id=1, source_target_pairs={{0,2},{4,6},{8,10},{12,14},{2,0},{6,4},{10,8},{14,12},{1,3},{5,7},... | collective-permute-start | bytes 786440 | tf_op jit(solution)/shard_map/ppermute | solution.py:116
  54.7 21.2 %copy-start.14 = (bf16[128,1024]{1,0:T(8,128)(2,1)}, bf16[128,1024]{1,0:T(8,128)(2,1)S(1)}, u32[]{:S(2)}) copy-start(bf16[128,1024]{1,0:T(8,128)(2,1)S(1)} %collective-permute-done.2.refs_1_) | copy-start | bytes 786436
  54.7 18.7 %collective-permute-start.3 = (bf16[128,1024]{1,0:T(8,128)(2,1)S(1)}, bf16[128,1024]{1,0:T(8,128)(2,1)}, u32[]{:S(2)}, u32[]{:S(2)}) collective-permute-start(bf16[128,1024]{1,0:T(8,128)(2,1)S(1)} %collective-permute-done.2.refs_1_), channel_id=1, source_target_pairs={{2,0},{6,4},{10,8},{14,12},{3,1},{7,5},{11,9},{15,13},{18,16},{22,... | collective-permute-start | bytes 786440 | tf_op jit(solution)/shard_map/ppermute | solution.py:118
  58.2 38.9 %collective-permute-start.16 = (bf16[128,1024]{1,0:T(8,128)(2,1)S(1)}, bf16[128,1024]{1,0:T(8,128)(2,1)S(1)}, u32[]{:S(2)}, u32[]{:S(2)}) collective-permute-start(bf16[128,1024]{1,0:T(8,128)(2,1)S(1)} %collective-permute-done.12.refs_0_), channel_id=1, source_target_pairs={{0,16},{16,0},{1,17},{17,1},{2,18},{18,2},{3,19},{19,3},{4,20},{20... | collective-permute-start | bytes 786440 | tf_op jit(solution)/shard_map/ppermute | solution.py:120
  75.3 23.4 %collective-permute-start.17 = (bf16[128,1024]{1,0:T(8,128)(2,1)S(1)}, bf16[128,1024]{1,0:T(8,128)(2,1)}, u32[]{:S(2)}, u32[]{:S(2)}) collective-permute-start(bf16[128,1024]{1,0:T(8,128)(2,1)S(1)} %get-tuple-element.24.refs_3_), channel_id=1, source_target_pairs={{0,16},{16,0},{1,17},{17,1},{2,18},{18,2},{3,19},{19,3},{4,20},{20... | collective-permute-start | bytes 786440 | tf_op jit(solution)/shard_map/ppermute | solution.py:124
  75.9 4.0 %copy-start = (bf16[640,8192]{1,0:T(8,128)(2,1)S(1)}, bf16[640,8192]{1,0:T(8,128)(2,1)}, u32[]{:S(2)}) copy-start(bf16[640,8192]{1,0:T(8,128)(2,1)} %documents.7) | copy-start | bytes 31457284
  79.9 0.9 copy-start.2
  80.8 0.9 copy-start.3
  81.8 0.9 copy-start.4
  82.7 0.9 copy-start.5
  83.7 0.9 copy-start.6
  84.6 0.9 copy-start.7
  85.6 0.9 copy-start.8
  86.5 0.9 copy-start.9
  87.5 11.3 %copy-start.1 = (bf16[640,8192]{1,0:T(8,128)(2,1)S(1)}, bf16[640,8192]{1,0:T(8,128)(2,1)}, u32[]{:S(2)}) copy-start(bf16[640,8192]{1,0:T(8,128)(2,1)} %documents.7) | copy-start | bytes 31457284
  95.1 10.8 %collective-permute-start.11 = (bf16[128,1024]{1,0:T(8,128)(2,1)S(1)}, bf16[128,1024]{1,0:T(8,128)(2,1)S(1)}, u32[]{:S(2)}, u32[]{:S(2)}) collective-permute-start(bf16[128,1024]{1,0:T(8,128)(2,1)S(1)} %collective-permute-done.8.refs_1_), channel_id=1, source_target_pairs={{0,16},{16,0},{1,17},{17,1},{2,18},{18,2},{3,19},{19,3},{4,20},{20... | collective-permute-start | bytes 786440 | tf_op jit(solution)/shard_map/ppermute | solution.py:120
  96.6 16.4 %collective-permute-start.1 = (bf16[128,1024]{1,0:T(8,128)(2,1)}, bf16[128,1024]{1,0:T(8,128)(2,1)S(1)}, u32[]{:S(2)}, u32[]{:S(2)}) collective-permute-start(bf16[128,1024]{1,0:T(8,128)(2,1)} %get-tuple-element.21), channel_id=1, source_target_pairs={{0,4},{2,6},{4,8},{6,10},{8,12},{10,14},{12,0},{14,2},{1,5},{3,7},... | collective-permute-start | bytes 786440 | tf_op jit(solution)/shard_map/ppermute | solution.py:112
  96.6 10.0 %collective-permute-start.14 = (bf16[128,1024]{1,0:T(8,128)(2,1)S(1)}, bf16[128,1024]{1,0:T(8,128)(2,1)S(1)}, u32[]{:S(2)}, u32[]{:S(2)}) collective-permute-start(bf16[128,1024]{1,0:T(8,128)(2,1)S(1)} %get-tuple-element.25.refs_4_), channel_id=1, source_target_pairs={{0,16},{16,0},{1,17},{17,1},{2,18},{18,2},{3,19},{19,3},{4,20},{20... | collective-permute-start | bytes 786440 | tf_op jit(solution)/shard_map/ppermute | solution.py:124
  97.2 15.8 %collective-permute-start.10 = (bf16[128,1024]{1,0:T(8,128)(2,1)}, bf16[128,1024]{1,0:T(8,128)(2,1)S(1)}, u32[]{:S(2)}, u32[]{:S(2)}) collective-permute-start(bf16[128,1024]{1,0:T(8,128)(2,1)} %get-tuple-element.26.refs_2_), channel_id=1, source_target_pairs={{0,16},{16,0},{1,17},{17,1},{2,18},{18,2},{3,19},{19,3},{4,20},{20... | collective-permute-start | bytes 786440 | tf_op jit(solution)/shard_map/ppermute | solution.py:124
  98.7 7.9 %copy-start.12 = (bf16[128,1024]{1,0:T(8,128)(2,1)S(1)}, bf16[128,1024]{1,0:T(8,128)(2,1)}, u32[]{:S(2)}) copy-start(bf16[128,1024]{1,0:T(8,128)(2,1)} %copy-done.11) | copy-start | bytes 786436
  98.7 7.9 %copy-start.13 = (bf16[128,1024]{1,0:T(8,128)(2,1)S(1)}, bf16[128,1024]{1,0:T(8,128)(2,1)}, u32[]{:S(2)}) copy-start(bf16[128,1024]{1,0:T(8,128)(2,1)} %get-tuple-element.27.refs_3_) | copy-start | bytes 786436
  98.7 7.9 %copy-start.15 = (bf16[128,1024]{1,0:T(8,128)(2,1)S(1)}, bf16[128,1024]{1,0:T(8,128)(2,1)}, u32[]{:S(2)}) copy-start(bf16[128,1024]{1,0:T(8,128)(2,1)} %copy-done.14) | copy-start | bytes 786436
  98.7 17.7 %collective-permute-start = (f32[320,128]{1,0:T(8,128)S(1)}, f32[320,128]{1,0:T(8,128)S(1)}, u32[]{:S(2)}, u32[]{:S(2)}) collective-permute-start(f32[320,128]{1,0:T(8,128)S(1)} %slice_bitcast_fusion.2), channel_id=1, source_target_pairs={{0,1},{1,0},{2,3},{3,2},{4,5},{5,4},{6,7},{7,6},{8,9},{9,8},{10,11... | collective-permute-start | bytes 491528 | tf_op jit(solution)/shard_map/ppermute | solution.py:137
  106.6 6.4 %copy-start.10 = (bf16[128,1024]{1,0:T(8,128)(2,1)S(1)}, bf16[128,1024]{1,0:T(8,128)(2,1)}, u32[]{:S(2)}) copy-start(bf16[128,1024]{1,0:T(8,128)(2,1)} %get-tuple-element.28.refs_1_) | copy-start | bytes 786436
  116.3 1.7 %collective-permute-start.18 = (f32[2,320,128]{2,1,0:T(8,128)S(1)}, f32[2,320,128]{2,1,0:T(8,128)S(1)}, u32[]{:S(2)}, u32[]{:S(2)}) collective-permute-start(f32[2,320,128]{2,1,0:T(8,128)S(1)} %slice.59), channel_id=1, source_target_pairs={{0,1},{1,0},{2,3},{3,2},{4,5},{5,4},{6,7},{7,6},{8,9},{9,8},{10,11... | collective-permute-start | bytes 983048 | tf_op jit(solution)/shard_map/ppermute | solution.py:157

commit v2 on v0

v2 whole, which is shorter than its diff:
```python
import functools
import math

import jax
import jax.numpy as jnp
from jax import lax
from jax.experimental import pallas as pl
from jax.experimental.pallas import tpu as pltpu
from jax.sharding import PartitionSpec as P

L_DIM = 8192
CHUNKS = 8
DIRECT = 6
VMEM = pl.BlockSpec(memory_space=pltpu.VMEM)
SMEM = pl.BlockSpec(memory_space=pltpu.SMEM)
ANY = pl.BlockSpec(memory_space=pl.ANY)
SMALL = pl.CostEstimate(flops=1024, bytes_accessed=1024, transcendentals=0)
PARAMS = pltpu.CompilerParams(vmem_limit_bytes=24 * 1024 * 1024)


def columns_of(k, width):
    place = jnp.where(lax.axis_index("groups") == 0, k, CHUNKS - 1 - k)
    return pl.ds(pl.multiple_of(place * width, width), width)


def document_copies(documents, rows_buf, sem, slot, columns, sides):
    layer = lax.axis_index("layer")
    half = documents.shape[0] // 2
    copies = []
    for at, side in enumerate(sides):
        row = layer if side else 1 - layer
        copies.append(
            pltpu.make_async_copy(
                documents.at[pl.ds(pl.multiple_of(row * half, half), half), columns],
                rows_buf.at[slot, pl.ds(at * half, half), :],
                sem.at[slot, at],
            )
        )
    return copies


def products(rows, block):
    return lax.dot_general(
        rows, block, (((1,), (1,)), ((), ())), preferred_element_type=jnp.float32
    )


def first_kernel(count, queries, *refs):
    outs, sem = refs[:count], refs[count]
    width = outs[0].shape[1]
    copies = [
        pltpu.make_async_copy(queries.at[:, columns_of(k, width)], outs[k], sem.at[k])
        for k in range(count)
    ]
    for copy in copies:
        copy.start()
    for copy in copies:
        copy.wait()


def step_kernel(k, ahead, queries, received, *refs):
    outs, sem = refs[-2 - (ahead is not None) : -1], refs[-1]
    width = received.shape[1]
    even = lax.axis_index("dp") % 2 == 0
    own_copy = pltpu.make_async_copy(queries.at[:, columns_of(k, width)], outs[0], sem.at[0])
    received_copy = pltpu.make_async_copy(received, outs[0], sem.at[0])
    if ahead is not None:
        ahead_copy = pltpu.make_async_copy(
            queries.at[:, columns_of(ahead, width)], outs[1], sem.at[1]
        )
        ahead_copy.start()

    @pl.when(even)
    def _():
        own_copy.start()
        own_copy.wait()

    @pl.when(jnp.logical_not(even))
    def _():
        received_copy.start()
        received_copy.wait()

    if ahead is not None:
        ahead_copy.wait()


def own_kernel(part, held, documents, queries, *refs):
    if part == 0:
        eigenvalues = refs[0]
        theirs, mine, inverse, rows_buf, sem = refs[1 + held :]
    else:
        inverse, theirs_sum, mine_sum = refs[:3]
        theirs, mine, rows_buf, sem = refs[3 + held :]
    half = documents.shape[0] // 2
    count, _, width = rows_buf.shape
    copies = []
    for i in range(count):
        k = part * count + i
        copies.append(
            document_copies(documents, rows_buf, sem, i, pl.ds(k * width, width), (0, 1))
        )
        for copy in copies[i]:
            copy.start()
    if part == 0:
        for start in range(0, eigenvalues.shape[1], L_DIM):
            block = eigenvalues[:, start : start + L_DIM]
            damping = 0.1 * jnp.mean(block, axis=1, keepdims=True)
            inverse[:, start : start + L_DIM] = 1.0 / (block + damping)
    for i in range(count):
        k = part * count + i
        scaled = queries[:, i * width : (i + 1) * width].astype(jnp.float32)
        scaled = (scaled * inverse[:, k * width : (k + 1) * width]).astype(jnp.bfloat16)
        for copy in copies[i]:
            copy.wait()
        term = products(rows_buf[i], scaled)
        if i > 0:
            theirs[...] += term[:half]
            mine[...] += term[half:]
        elif part == 0:
            theirs[...] = term[:half]
            mine[...] = term[half:]
        else:
            theirs[...] = theirs_sum[...] + term[:half]
            mine[...] = mine_sum[...] + term[half:]


def pair_kernel(ks, sides, fresh, documents, inverse, *refs):
    count = len(ks)
    chunks, refs = refs[: 2 * count], refs[2 * count :]
    if not fresh:
        sums = refs[0]
    out, rows_buf, block_buf, sem = refs[-4:]
    half = documents.shape[0] // 2
    first = 0 if 0 in sides else half
    rows, width = chunks[0].shape
    columns = [columns_of(k, width) for k in ks]
    copies = [
        document_copies(documents, rows_buf, sem, i, columns[i], sides) for i in range(count)
    ]
    for pair in copies:
        for copy in pair:
            copy.start()
    for i in range(count):
        for b in range(2):
            scaled = chunks[2 * i + b][...].astype(jnp.float32) * inverse[:, columns[i]]
            block_buf[i, pl.ds(b * rows, rows), :] = scaled.astype(jnp.bfloat16)
        for copy in copies[i]:
            copy.wait()
        term = products(rows_buf[i], block_buf[i])
        if i > 0:
            out[...] += term
        elif fresh:
            out[...] = term
        else:
            out[...] = sums[pl.ds(first, out.shape[0]), :] + term


def final_kernel(factor, counts, mine0, got0, mine, got, out):
    half, rows = mine0.shape
    start = lax.axis_index("layer") * half
    index = start + lax.broadcasted_iota(jnp.int32, (half, 1), 0)
    scale = factor * (index < counts[0]).astype(jnp.float32)
    out[:, :rows] = (mine0[...] + got0[...]) * scale
    out[:, rows:] = (mine[...] + got[...]) * scale


def on_device(queries, documents, counts, eigenvalues):
    rows, dims = queries.shape
    doc_rows = documents.shape[0]
    half = doc_rows // 2
    owners = lax.axis_size("dp")
    width = dims // CHUNKS
    ahead = [(i, (i + 2) % owners) for i in range(owners)]
    pair = [(i, i ^ 1) for i in range(owners)]
    across = [(0, 1), (1, 0)]
    chunk = jax.ShapeDtypeStruct((rows, width), queries.dtype)

    def call(kernel, out_shape, in_specs, out_specs, scratch):
        return pl.pallas_call(
            kernel,
            out_shape=out_shape,
            in_specs=in_specs,
            out_specs=out_specs,
            scratch_shapes=scratch,
            compiler_params=PARAMS,
            cost_estimate=SMALL,
        )

    def step(k, *until):
        ahead_k = k + 2 if k + 2 < DIRECT else None
        outs = 1 if ahead_k is None else 2
        return call(
            functools.partial(step_kernel, k, ahead_k),
            [chunk] * outs,
            [ANY] * (2 + len(until)),
            [ANY] * outs,
            [pltpu.SemaphoreType.DMA((2,))],
        )(queries, far[k], *until)

    def own_scores(part, *operands, until=()):
        half_scores = jax.ShapeDtypeStruct((half, rows), jnp.float32)
        outs = [half_scores] * 2
        if part == 0:
            outs.append(jax.ShapeDtypeStruct((1, dims), jnp.float32))
        return pl.pallas_call(
            functools.partial(own_kernel, part, len(until)),
            out_shape=outs,
            grid=(1,),
            in_specs=[ANY, pl.BlockSpec((rows, dims // 2), lambda i: (0, part))]
            + [VMEM] * len(operands)
            + [ANY] * len(until),
            out_specs=[VMEM] * len(outs),
            scratch_shapes=[
                pltpu.VMEM((CHUNKS // 2, doc_rows, width), documents.dtype),
                pltpu.SemaphoreType.DMA((CHUNKS // 2, 2)),
            ],
            compiler_params=PARAMS,
            cost_estimate=SMALL,
        )(documents, queries, *operands, *until)

    def pair_scores(*ks, sums=None, sides=(0, 1), until=()):
        count = len(ks)
        side_rows = half * len(sides)
        operands = [inverse] + [block[k] for k in ks for block in (near, far)]
        if sums is not None:
            operands.append(sums)
        return call(
            functools.partial(pair_kernel, ks, sides, sums is None),
            jax.ShapeDtypeStruct((side_rows, 2 * rows), jnp.float32),
            [ANY] + [VMEM] * len(operands) + [ANY] * len(until),
            VMEM,
            [
                pltpu.VMEM((count, side_rows, width), documents.dtype),
                pltpu.VMEM((count, 2 * rows, width), documents.dtype),
                pltpu.SemaphoreType.DMA((count, len(sides))),
            ],
        )(documents, *operands, *until)

    far = [None] * CHUNKS
    near = [None] * CHUNKS

    def send_across(block, k, *until):
        sent = lax.optimization_barrier((block[k], *until))[0]
        block[CHUNKS - 1 - k] = lax.ppermute(sent, "groups", across)

    def send(k, outs):
        near[k] = lax.ppermute(outs[0], "dp", pair)
        if len(outs) > 1:
            far[k + 2] = lax.ppermute(outs[1], "dp", ahead)

    for k, to_send in enumerate(
        call(
            functools.partial(first_kernel, 2),
            [chunk] * 2,
            [ANY],
            [ANY] * 2,
            [pltpu.SemaphoreType.DMA((2,))],
        )(queries)
    ):
        far[k] = lax.ppermute(to_send, "dp", ahead)
    theirs0, mine0, inverse = own_scores(0, eigenvalues.reshape(1, dims), until=(to_send,))

    outs = step(0, inverse)
    send(0, outs)
    send_across(far, 0, outs[0])
    theirs0, mine0 = own_scores(1, inverse, theirs0, mine0, until=(outs[0],))

    outs = step(1, theirs0)
    send(1, outs)
    send_across(far, 1, outs[0])
    sums = pair_scores(0, until=(outs[0], far[CHUNKS - 1]))

    outs = step(2, sums)
    send(2, outs)
    send_across(near, 0, outs[0])
    sums = pair_scores(1, sums=sums, until=(outs[0], far[CHUNKS - 2]))

    outs = step(3, sums)
    send(3, outs)
    send_across(near, 1, outs[0])
    sums = pair_scores(2, CHUNKS - 1, sums=sums, until=(outs[0],))

    outs = step(4, sums)
    send(4, outs)
    send_across(near, 2, outs[0])
    sent0 = lax.optimization_barrier((theirs0, outs[0]))[0]
    got0 = lax.ppermute(sent0, "layer", across)
    sums = pair_scores(3, CHUNKS - 2, sums=sums, until=(outs[0],))
    theirs = pair_scores(4, 5, sums=sums, sides=(0,), until=(got0,))
    got = lax.ppermute(theirs, "layer", across)
    mine = pair_scores(4, 5, sums=sums, sides=(1,), until=(theirs,))
    factor = 1.0 / math.sqrt(dims * lax.axis_size("layer"))
    return call(
        functools.partial(final_kernel, factor),
        jax.ShapeDtypeStruct((half, 3 * rows), jnp.float32),
        [SMEM] + [VMEM] * 4,
        VMEM,
        [],
    )(counts, mine0, got0, mine, got)


def solution(mesh):
    return jax.shard_map(
        on_device,
        mesh=mesh,
        in_specs=(P("dp", "layer"), P(("groups", "dp"), "layer"), P(("groups", "dp")), P("layer")),
        out_specs=P(("groups", "dp", "layer"), None),
        check_vma=False,
    )
```

time: 136 us -> 55.3 us (0.41)
  waiting for transfers between devices: 83.8 us -> 12 us
  matrix products: 22.7 us -> 0 us
  Pallas kernels: 0 us -> 17.6 us
  starting transfers between devices: 3.11 us -> 18.1 us
  between operations: 14.5 us -> 0.83 us
  other arithmetic: 4.18 us -> 0 us
    ppermute x2 -> x18, waiting for transfers between devices: 80.9 us -> 12 us  [the longest x5 6.38 us: send_across(): block[CHUNKS - 1 - k] = lax.ppermute(sent, 'groups', across)]
    dot_general x3 -> x0, matrix products: 22.7 us -> none  [block_scores(): lax.dot_general(doc_rows, block, (((1,), (1,)), ((), ())), preferred_elem...]
    pallas_call x0 -> x15, Pallas kernels: none -> 17.6 us  [the longest x6 8.52 us: pair_scores(): call(functools.partial(pair_kernel, ks, sides, sums is None), jax.ShapeDt...]
    ppermute x2 -> x18, starting transfers between devices: 3.02 us -> 18.1 us  [the longest x5 6.26 us: send(): near[k] = lax.ppermute(outs[0], 'dp', pair)]
    unnamed x6 -> x0, waiting for transfers between devices: 2.9 us -> none
    convert_element_type x1 -> x0, other arithmetic: 1.99 us -> none  [on_device(): precond = (queries.astype(jnp.float32) * inverse).astype(jnp.bfloat16)]
    reduce_sum x1 -> x0, other arithmetic: 1.37 us -> none  [on_device(): damping = 0.1 * jnp.mean(blocks, axis=1, keepdims=True)]
    unnamed x6 -> x8, local copies, waits for them, and re-layouts: 5.85 us -> 6.35 us
  transfers between devices with their start and end apart: 5 -> 18, of which waited for: 3 -> 7; matrix products, arithmetic and copies ran while one was open for 20% -> 0% of each run, Pallas kernels for 0% -> 28%
where the time goes in v2:
time: 55.3 us; the launch traced here: 55 us
  starting transfers between devices  18.1 us (33%)
  Pallas kernels  17.6 us (32%)
  waiting for transfers between devices  12 us (22%)
  local copies, waits for them, and re-layouts  6.35 us (11%)
  between operations  0.83 us (2%)
    pallas_call x6, Pallas kernels, pair_scores(): call(functools.partial(pair_kernel, ks, sides, sums is None), jax.ShapeDt...  8.52 us
    pallas_call x2, Pallas kernels, own_scores(): pl.pallas_call(functools.partial(own_kernel, part, len(until)), out_shape...  7.86 us
    ppermute x5, waiting for transfers between devices, send_across(): block[CHUNKS - 1 - k] = lax.ppermute(sent, 'groups', across)  6.38 us
    unnamed x8, local copies, waits for them, and re-layouts  6.35 us
    ppermute x5, starting transfers between devices, send(): near[k] = lax.ppermute(outs[0], 'dp', pair)  6.26 us
    ppermute x5, starting transfers between devices, send_across(): block[CHUNKS - 1 - k] = lax.ppermute(sent, 'groups', across)  5.19 us
    ppermute x2, starting transfers between devices, on_device(): far[k] = lax.ppermute(to_send, 'dp', ahead)  4.65 us
    ppermute x4, waiting for transfers between devices, send(): far[k + 2] = lax.ppermute(outs[1], 'dp', ahead)  3.75 us
  transfers between devices with their start and end apart: 18, of which 7 were waited for; matrix products, arithmetic and copies ran while one was open for 0% of the time, Pallas kernels for 28%

profile of v2, /device:TPU:0, one launch (start us, length us, event | category | flops | bytes accessed | tf_op | source)
XLA Modules:
  0.0 55.0 jit_solution(7427330797913169911)
XLA Ops:
  0.0 1.6 %copy-done.2 = bf16[128,8192]{1,0:T(8,128)(2,1)S(1)} copy-done((bf16[128,8192]{1,0:T(8,128)(2,1)S(1)}, bf16[128,8192]{1,0:T(8,128)(2,1)}, u32[]{:S(2)}) %copy-start.2) | copy-done | bytes 2097176
  1.6 0.1 shard_map.46
  1.7 3.1 %collective-permute-start = (bf16[128,1024]{1,0:T(8,128)(2,1)S(1)}, bf16[128,1024]{1,0:T(8,128)(2,1)S(1)}, u32[]{:S(2)}, u32[]{:S(2)}) collective-permute-start(bf16[128,1024]{1,0:T(8,128)(2,1)S(1)} %get-tuple-element.30), channel_id=1, source_target_pairs={{0,4},{2,6},{4,8},{6,10},{8,12},{10,14},{12,0},{14,2},{1,5},{3,7},... | collective-permute-start | bytes 786440 | tf_op jit(solution)/shard_map/ppermute | solution.py:260
  4.7 1.6 %collective-permute-start.3 = (bf16[128,1024]{1,0:T(8,128)(2,1)S(1)}, bf16[128,1024]{1,0:T(8,128)(2,1)S(1)}, u32[]{:S(2)}, u32[]{:S(2)}) collective-permute-start(bf16[128,1024]{1,0:T(8,128)(2,1)S(1)} %get-tuple-element.26.refs_1_), channel_id=1, source_target_pairs={{0,4},{2,6},{4,8},{6,10},{8,12},{10,14},{12,0},{14,2},{1,5},{3,7},... | collective-permute-start | bytes 786440 | tf_op jit(solution)/shard_map/ppermute | solution.py:260
  6.3 4.0 %copy-done = bf16[640,8192]{1,0:T(8,128)(2,1)S(1)} copy-done((bf16[640,8192]{1,0:T(8,128)(2,1)S(1)}, bf16[640,8192]{1,0:T(8,128)(2,1)}, u32[]{:S(2)}) %copy-start) | copy-done | bytes 10485784
  10.3 0.8 %copy-done.3 = f32[8192]{0:T(1024)S(1)} copy-done((f32[8192]{0:T(1024)S(1)}, f32[8192]{0:T(1024)}, u32[]{:S(2)}) %copy-start.3) | copy-done | bytes 32792
  11.1 4.0 %shard_map.47 = (f32[320,128]{1,0:T(8,128)S(1)}, f32[320,128]{1,0:T(8,128)S(1)}, f32[1,8192]{1,0:T(1,128)S(1)}) custom-call(bf16[640,8192]{1,0:T(8,128)(2,1)S(1)} %copy-done, bf16[128,8192]{1,0:T(8,128)(2,1)S(1)} %copy-done.2, f32[1,8192]{1,0:T(1,128)S(1)} %bitcast.1, bf16[128,1024]{1,0:T(8,128)(2,1)S(1)} %get-tuple-element.26.refs_1_), custom_call_target="tpu_custom_call" | custom-call | flops 1024 | bytes 1024 | tf_op jit(solution)/shard_map/pallas_call | solution.py:205
  15.1 0.0 collective-permute-done.received.refs_1_
  15.1 0.1 shard_map.48
  15.2 1.6 %collective-permute-start.4 = (bf16[128,1024]{1,0:T(8,128)(2,1)S(1)}, bf16[128,1024]{1,0:T(8,128)(2,1)S(1)}, u32[]{:S(2)}, u32[]{:S(2)}) collective-permute-start(bf16[128,1024]{1,0:T(8,128)(2,1)S(1)} %collective-permute-done.received.refs_1_), channel_id=1, source_target_pairs={{0,16},{16,0},{1,17},{17,1},{2,18},{18,2},{3,19},{19,3},{4,20},{20... | collective-permute-start | bytes 786440 | tf_op jit(solution)/shard_map/ppermute | solution.py:244
  16.7 1.5 %collective-permute-start.2 = (bf16[128,1024]{1,0:T(8,128)(2,1)S(1)}, bf16[128,1024]{1,0:T(8,128)(2,1)S(1)}, u32[]{:S(2)}, u32[]{:S(2)}) collective-permute-start(bf16[128,1024]{1,0:T(8,128)(2,1)S(1)} %get-tuple-element.31.refs_3_), channel_id=1, source_target_pairs={{0,2},{2,0},{4,6},{6,4},{8,10},{10,8},{12,14},{14,12},{1,3},{3,1},... | collective-permute-start | bytes 786440 | tf_op jit(solution)/shard_map/ppermute | solution.py:247
  18.2 1.6 %collective-permute-start.1 = (bf16[128,1024]{1,0:T(8,128)(2,1)S(1)}, bf16[128,1024]{1,0:T(8,128)(2,1)S(1)}, u32[]{:S(2)}, u32[]{:S(2)}) collective-permute-start(bf16[128,1024]{1,0:T(8,128)(2,1)S(1)} %get-tuple-element.34), channel_id=1, source_target_pairs={{0,4},{2,6},{4,8},{6,10},{8,12},{10,14},{12,0},{14,2},{1,5},{3,7},... | collective-permute-start | bytes 786440 | tf_op jit(solution)/shard_map/ppermute | solution.py:249
  19.8 3.9 %shard_map.49 = (f32[320,128]{1,0:T(8,128)S(1)}, f32[320,128]{1,0:T(8,128)S(1)}) custom-call(bf16[640,8192]{1,0:T(8,128)(2,1)S(1)} %copy-done.1, bf16[128,8192]{1,0:T(8,128)(2,1)S(1)} %copy-done.2, f32[1,8192]{1,0:T(1,128)S(1)} %get-tuple-element.27.refs_0_.inverse, f32[320,128]{1,0:T(8,128)S(1)} %get-tuple-element.28.refs_1_, ...), custom_call_target="tpu_custom_call" | custom-call | flops 1024 | bytes 1024 | tf_op jit(solution)/shard_map/pallas_call | solution.py:205
  23.7 0.0 collective-permute-done.3.received.refs_1_
  23.7 0.1 shard_map.50
  23.8 0.6 %collective-permute-start.9 = (bf16[128,1024]{1,0:T(8,128)(2,1)S(1)}, bf16[128,1024]{1,0:T(8,128)(2,1)S(1)}, u32[]{:S(2)}, u32[]{:S(2)}) collective-permute-start(bf16[128,1024]{1,0:T(8,128)(2,1)S(1)} %collective-permute-done.3.received.refs_1_), channel_id=1, source_target_pairs={{0,16},{16,0},{1,17},{17,1},{2,18},{18,2},{3,19},{19,3},{4,20},{20... | collective-permute-start | bytes 786440 | tf_op jit(solution)/shard_map/ppermute | solution.py:244
  24.4 0.5 collective-permute-start.8
  24.9 0.0 collective-permute-done.4.refs_3_
  24.9 0.1 collective-permute-start.10
  25.0 0.8 %shard_map.51.refs_0_.refs_2_ = f32[640,256]{1,0:T(8,128)S(1)} custom-call(bf16[640,8192]{1,0:T(8,128)(2,1)S(1)} %copy-done.1, f32[1,8192]{1,0:T(1,128)S(1)} %get-tuple-element.27.refs_0_.inverse, bf16[128,1024]{1,0:T(8,128)(2,1)S(1)} %collective-permute-done.2.refs_0_, bf16[128,1024]{1,0:T(8,128)(2,1)S(1)} %collective-permute-done.received.refs_1_, ...), custom_call_target="tpu_custom_call" | custom-call | flops 1024 | bytes 1024 | tf_op jit(solution)/shard_map/pallas_call | solution.py:227
  25.8 1.2 %collective-permute-done.1.received.refs_1_ = bf16[128,1024]{1,0:T(8,128)(2,1)S(1)} collective-permute-done((bf16[128,1024]{1,0:T(8,128)(2,1)S(1)}, bf16[128,1024]{1,0:T(8,128)(2,1)S(1)}, u32[]{:S(2)}, u32[]{:S(2)}) %collective-permute-start.1) | collective-permute-done | bytes 262176 | tf_op jit(solution)/shard_map/ppermute | solution.py:249
  27.0 0.1 shard_map.52
  27.0 0.6 %collective-permute-start.7 = (bf16[128,1024]{1,0:T(8,128)(2,1)S(1)}, bf16[128,1024]{1,0:T(8,128)(2,1)S(1)}, u32[]{:S(2)}, u32[]{:S(2)}) collective-permute-start(bf16[128,1024]{1,0:T(8,128)(2,1)S(1)} %collective-permute-done.2.refs_0_), channel_id=1, source_target_pairs={{0,16},{16,0},{1,17},{17,1},{2,18},{18,2},{3,19},{19,3},{4,20},{20... | collective-permute-start | bytes 786440 | tf_op jit(solution)/shard_map/ppermute | solution.py:244
  27.6 1.6 %collective-permute-start.6 = (bf16[128,1024]{1,0:T(8,128)(2,1)S(1)}, bf16[128,1024]{1,0:T(8,128)(2,1)S(1)}, u32[]{:S(2)}, u32[]{:S(2)}) collective-permute-start(bf16[128,1024]{1,0:T(8,128)(2,1)S(1)} %get-tuple-element.38.refs_3_), channel_id=1, source_target_pairs={{0,2},{2,0},{4,6},{6,4},{8,10},{10,8},{12,14},{14,12},{1,3},{3,1},... | collective-permute-start | bytes 786440 | tf_op jit(solution)/shard_map/ppermute | solution.py:247
  29.2 3.9 %collective-permute-done.9.refs_4_.refs_3_ = bf16[128,1024]{1,0:T(8,128)(2,1)S(1)} collective-permute-done((bf16[128,1024]{1,0:T(8,128)(2,1)S(1)}, bf16[128,1024]{1,0:T(8,128)(2,1)S(1)}, u32[]{:S(2)}, u32[]{:S(2)}) %collective-permute-start.9) | collective-permute-done | bytes 262176 | tf_op jit(solution)/shard_map/ppermute | solution.py:244
  33.1 0.2 collective-permute-start.5
  33.3 0.2 collective-permute-done.8.refs_0_
  33.6 0.8 %shard_map.53.refs_0_.refs_4_ = f32[640,256]{1,0:T(8,128)S(1)} custom-call(bf16[640,8192]{1,0:T(8,128)(2,1)S(1)} %copy-done.1, f32[1,8192]{1,0:T(1,128)S(1)} %get-tuple-element.27.refs_0_.inverse, bf16[128,1024]{1,0:T(8,128)(2,1)S(1)} %collective-permute-done.8.refs_0_, bf16[128,1024]{1,0:T(8,128)(2,1)S(1)} %collective-permute-done.3.received.refs_1_, ...), custom_call_target="tpu_custom_call" | custom-call | flops 1024 | bytes 1024 | tf_op jit(solution)/shard_map/pallas_call | solution.py:227
  34.4 0.1 shard_map.54
  34.5 1.8 %collective-permute-start.16 = (bf16[128,1024]{1,0:T(8,128)(2,1)S(1)}, bf16[128,1024]{1,0:T(8,128)(2,1)S(1)}, u32[]{:S(2)}, u32[]{:S(2)}) collective-permute-start(bf16[128,1024]{1,0:T(8,128)(2,1)S(1)} %collective-permute-done.8.refs_0_), channel_id=1, source_target_pairs={{0,16},{16,0},{1,17},{17,1},{2,18},{18,2},{3,19},{19,3},{4,20},{20... | collective-permute-start | bytes 786440 | tf_op jit(solution)/shard_map/ppermute | solution.py:244
  36.3 2.5 %collective-permute-start.15 = (bf16[128,1024]{1,0:T(8,128)(2,1)S(1)}, bf16[128,1024]{1,0:T(8,128)(2,1)S(1)}, u32[]{:S(2)}, u32[]{:S(2)}) collective-permute-start(bf16[128,1024]{1,0:T(8,128)(2,1)S(1)} %get-tuple-element.42.refs_5_), channel_id=1, source_target_pairs={{0,2},{2,0},{4,6},{6,4},{8,10},{10,8},{12,14},{14,12},{1,3},{3,1},... | collective-permute-start | bytes 786440 | tf_op jit(solution)/shard_map/ppermute | solution.py:247
  38.9 0.0 collective-permute-done.7.refs_2_
  38.9 0.1 collective-permute-start.14
  39.0 0.0 collective-permute-done.6.refs_0_
  39.0 2.1 %shard_map.55.refs_0_.refs_4_ = f32[640,256]{1,0:T(8,128)S(1)} custom-call(bf16[640,8192]{1,0:T(8,128)(2,1)S(1)} %copy-done.1, f32[1,8192]{1,0:T(1,128)S(1)} %get-tuple-element.27.refs_0_.inverse, bf16[128,1024]{1,0:T(8,128)(2,1)S(1)} %collective-permute-done.6.refs_0_, bf16[128,1024]{1,0:T(8,128)(2,1)S(1)} %collective-permute-done.1.received.refs_1_, ...), custom_call_target="tpu_custom_call" | custom-call | flops 1024 | bytes 1024 | tf_op jit(solution)/shard_map/pallas_call | solution.py:227
  41.1 2.5 %collective-permute-done.5.received.refs_1_ = bf16[128,1024]{1,0:T(8,128)(2,1)S(1)} collective-permute-done((bf16[128,1024]{1,0:T(8,128)(2,1)S(1)}, bf16[128,1024]{1,0:T(8,128)(2,1)S(1)}, u32[]{:S(2)}, u32[]{:S(2)}) %collective-permute-start.5) | collective-permute-done | bytes 262176 | tf_op jit(solution)/shard_map/ppermute | solution.py:249
  43.7 0.6 %collective-permute-start.13 = (bf16[128,1024]{1,0:T(8,128)(2,1)S(1)}, bf16[128,1024]{1,0:T(8,128)(2,1)S(1)}, u32[]{:S(2)}, u32[]{:S(2)}) collective-permute-start(bf16[128,1024]{1,0:T(8,128)(2,1)S(1)} %collective-permute-done.6.refs_0_), channel_id=1, source_target_pairs={{0,16},{16,0},{1,17},{17,1},{2,18},{18,2},{3,19},{19,3},{4,20},{20... | collective-permute-start | bytes 786440 | tf_op jit(solution)/shard_map/ppermute | solution.py:244
  44.3 0.1 collective-permute-start.12
  44.4 1.1 %collective-permute-done.15.refs_0_ = bf16[128,1024]{1,0:T(8,128)(2,1)S(1)} collective-permute-done((bf16[128,1024]{1,0:T(8,128)(2,1)S(1)}, bf16[128,1024]{1,0:T(8,128)(2,1)S(1)}, u32[]{:S(2)}, u32[]{:S(2)}) %collective-permute-start.15) | collective-permute-done | bytes 262176 | tf_op jit(solution)/shard_map/ppermute | solution.py:247
  45.5 2.1 %shard_map.57.refs_4_ = f32[640,256]{1,0:T(8,128)S(1)} custom-call(bf16[640,8192]{1,0:T(8,128)(2,1)S(1)} %copy-done.1, f32[1,8192]{1,0:T(1,128)S(1)} %get-tuple-element.27.refs_0_.inverse, bf16[128,1024]{1,0:T(8,128)(2,1)S(1)} %collective-permute-done.15.refs_0_, bf16[128,1024]{1,0:T(8,128)(2,1)S(1)} %collective-permute-done.10.received.refs_1_, ...), custom_call_target="tpu_custom_call" | custom-call | flops 1024 | bytes 1024 | tf_op jit(solution)/shard_map/pallas_call | solution.py:227
  47.6 0.0 collective-permute-done.14.refs_3_
  47.7 2.5 %collective-permute-done.13.refs_2_ = bf16[128,1024]{1,0:T(8,128)(2,1)S(1)} collective-permute-done((bf16[128,1024]{1,0:T(8,128)(2,1)S(1)}, bf16[128,1024]{1,0:T(8,128)(2,1)S(1)}, u32[]{:S(2)}, u32[]{:S(2)}) %collective-permute-start.13) | collective-permute-done | bytes 262176 | tf_op jit(solution)/shard_map/ppermute | solution.py:244
  50.1 0.5 collective-permute-done.12.refs_0_
  50.7 1.3 %shard_map.58.refs_5_ = f32[320,256]{1,0:T(8,128)S(1)} custom-call(bf16[640,8192]{1,0:T(8,128)(2,1)S(1)} %copy-done.1, f32[1,8192]{1,0:T(1,128)S(1)} %get-tuple-element.27.refs_0_.inverse, bf16[128,1024]{1,0:T(8,128)(2,1)S(1)} %collective-permute-done.12.refs_0_, bf16[128,1024]{1,0:T(8,128)(2,1)S(1)} %collective-permute-done.5.received.refs_1_, ...), custom_call_target="tpu_custom_call" | custom-call | flops 1024 | bytes 1024 | tf_op jit(solution)/shard_map/pallas_call | solution.py:227
  52.0 0.1 collective-permute-start.17
  52.7 1.3 %shard_map.59.mine = f32[320,256]{1,0:T(8,128)S(1)} custom-call(bf16[640,8192]{1,0:T(8,128)(2,1)S(1)} %copy-done.1, f32[1,8192]{1,0:T(1,128)S(1)} %get-tuple-element.27.refs_0_.inverse, bf16[128,1024]{1,0:T(8,128)(2,1)S(1)} %collective-permute-done.12.refs_0_, bf16[128,1024]{1,0:T(8,128)(2,1)S(1)} %collective-permute-done.5.received.refs_1_, ...), custom_call_target="tpu_custom_call" | custom-call | flops 1024 | bytes 1024 | tf_op jit(solution)/shard_map/pallas_call | solution.py:227
  54.1 0.0 collective-permute-done.17.got
  54.1 0.9 %shard_map.60 = f32[320,384]{1,0:T(8,128)} custom-call(s32[1]{0:T(128)S(6)} %copy.5.counts, f32[320,128]{1,0:T(8,128)S(1)} %get-tuple-element.32.mine0, f32[320,128]{1,0:T(8,128)S(1)} %collective-permute-done.11.refs_5_.got0, f32[320,256]{1,0:T(8,128)S(1)} %shard_map.59.mine, f32[320,256]{1,0:T(8,128)S(1)} %collective-permute-done.17.got), custom_call_target="tpu_custom_call" | custom-call | flops 1024 | bytes 1024 | tf_op jit(solution)/shard_map/pallas_call | solution.py:293
  (11 shorter events, 0.1 us)
Async XLA Ops:
  0.0 1.6 %copy-start.2 = (bf16[128,8192]{1,0:T(8,128)(2,1)S(1)}, bf16[128,8192]{1,0:T(8,128)(2,1)}, u32[]{:S(2)}) copy-start(bf16[128,8192]{1,0:T(8,128)(2,1)} %queries.15) | copy-start | bytes 6291460
  1.7 13.4 %collective-permute-start = (bf16[128,1024]{1,0:T(8,128)(2,1)S(1)}, bf16[128,1024]{1,0:T(8,128)(2,1)S(1)}, u32[]{:S(2)}, u32[]{:S(2)}) collective-permute-start(bf16[128,1024]{1,0:T(8,128)(2,1)S(1)} %get-tuple-element.30), channel_id=1, source_target_pairs={{0,4},{2,6},{4,8},{6,10},{8,12},{10,14},{12,0},{14,2},{1,5},{3,7},... | collective-permute-start | bytes 786440 | tf_op jit(solution)/shard_map/ppermute | solution.py:260
  4.7 19.0 %collective-permute-start.3 = (bf16[128,1024]{1,0:T(8,128)(2,1)S(1)}, bf16[128,1024]{1,0:T(8,128)(2,1)S(1)}, u32[]{:S(2)}, u32[]{:S(2)}) collective-permute-start(bf16[128,1024]{1,0:T(8,128)(2,1)S(1)} %get-tuple-element.26.refs_1_), channel_id=1, source_target_pairs={{0,4},{2,6},{4,8},{6,10},{8,12},{10,14},{12,0},{14,2},{1,5},{3,7},... | collective-permute-start | bytes 786440 | tf_op jit(solution)/shard_map/ppermute | solution.py:260
  6.3 4.0 %copy-start = (bf16[640,8192]{1,0:T(8,128)(2,1)S(1)}, bf16[640,8192]{1,0:T(8,128)(2,1)}, u32[]{:S(2)}) copy-start(bf16[640,8192]{1,0:T(8,128)(2,1)} %documents.15) | copy-start | bytes 31457284
  10.3 0.8 %copy-start.3 = (f32[8192]{0:T(1024)S(1)}, f32[8192]{0:T(1024)}, u32[]{:S(2)}) copy-start(f32[8192]{0:T(1024)} %param.7) | copy-start | bytes 98308
  11.1 8.8 %copy-start.1 = (bf16[640,8192]{1,0:T(8,128)(2,1)S(1)}, bf16[640,8192]{1,0:T(8,128)(2,1)}, u32[]{:S(2)}) copy-start(bf16[640,8192]{1,0:T(8,128)(2,1)} %documents.15) | copy-start | bytes 31457284
  15.2 9.7 %collective-permute-start.4 = (bf16[128,1024]{1,0:T(8,128)(2,1)S(1)}, bf16[128,1024]{1,0:T(8,128)(2,1)S(1)}, u32[]{:S(2)}, u32[]{:S(2)}) collective-permute-start(bf16[128,1024]{1,0:T(8,128)(2,1)S(1)} %collective-permute-done.received.refs_1_), channel_id=1, source_target_pairs={{0,16},{16,0},{1,17},{17,1},{2,18},{18,2},{3,19},{19,3},{4,20},{20... | collective-permute-start | bytes 786440 | tf_op jit(solution)/shard_map/ppermute | solution.py:244
  16.7 8.3 %collective-permute-start.2 = (bf16[128,1024]{1,0:T(8,128)(2,1)S(1)}, bf16[128,1024]{1,0:T(8,128)(2,1)S(1)}, u32[]{:S(2)}, u32[]{:S(2)}) collective-permute-start(bf16[128,1024]{1,0:T(8,128)(2,1)S(1)} %get-tuple-element.31.refs_3_), channel_id=1, source_target_pairs={{0,2},{2,0},{4,6},{6,4},{8,10},{10,8},{12,14},{14,12},{1,3},{3,1},... | collective-permute-start | bytes 786440 | tf_op jit(solution)/shard_map/ppermute | solution.py:247
  18.2 8.7 %collective-permute-start.1 = (bf16[128,1024]{1,0:T(8,128)(2,1)S(1)}, bf16[128,1024]{1,0:T(8,128)(2,1)S(1)}, u32[]{:S(2)}, u32[]{:S(2)}) collective-permute-start(bf16[128,1024]{1,0:T(8,128)(2,1)S(1)} %get-tuple-element.34), channel_id=1, source_target_pairs={{0,4},{2,6},{4,8},{6,10},{8,12},{10,14},{12,0},{14,2},{1,5},{3,7},... | collective-permute-start | bytes 786440 | tf_op jit(solution)/shard_map/ppermute | solution.py:249
  23.8 9.3 %collective-permute-start.9 = (bf16[128,1024]{1,0:T(8,128)(2,1)S(1)}, bf16[128,1024]{1,0:T(8,128)(2,1)S(1)}, u32[]{:S(2)}, u32[]{:S(2)}) collective-permute-start(bf16[128,1024]{1,0:T(8,128)(2,1)S(1)} %collective-permute-done.3.received.refs_1_), channel_id=1, source_target_pairs={{0,16},{16,0},{1,17},{17,1},{2,18},{18,2},{3,19},{19,3},{4,20},{20... | collective-permute-start | bytes 786440 | tf_op jit(solution)/shard_map/ppermute | solution.py:244
  24.4 9.2 %collective-permute-start.8 = (bf16[128,1024]{1,0:T(8,128)(2,1)S(1)}, bf16[128,1024]{1,0:T(8,128)(2,1)S(1)}, u32[]{:S(2)}, u32[]{:S(2)}) collective-permute-start(bf16[128,1024]{1,0:T(8,128)(2,1)S(1)} %get-tuple-element.35.refs_2_), channel_id=1, source_target_pairs={{0,2},{2,0},{4,6},{6,4},{8,10},{10,8},{12,14},{14,12},{1,3},{3,1},... | collective-permute-start | bytes 786440 | tf_op jit(solution)/shard_map/ppermute | solution.py:247
  24.9 9.5 %collective-permute-start.10 = (bf16[128,1024]{1,0:T(8,128)(2,1)S(1)}, bf16[128,1024]{1,0:T(8,128)(2,1)S(1)}, u32[]{:S(2)}, u32[]{:S(2)}) collective-permute-start(bf16[128,1024]{1,0:T(8,128)(2,1)S(1)} %get-tuple-element.41), channel_id=1, source_target_pairs={{0,4},{2,6},{4,8},{6,10},{8,12},{10,14},{12,0},{14,2},{1,5},{3,7},... | collective-permute-start | bytes 786440 | tf_op jit(solution)/shard_map/ppermute | solution.py:249
  27.0 11.8 %collective-permute-start.7 = (bf16[128,1024]{1,0:T(8,128)(2,1)S(1)}, bf16[128,1024]{1,0:T(8,128)(2,1)S(1)}, u32[]{:S(2)}, u32[]{:S(2)}) collective-permute-start(bf16[128,1024]{1,0:T(8,128)(2,1)S(1)} %collective-permute-done.2.refs_0_), channel_id=1, source_target_pairs={{0,16},{16,0},{1,17},{17,1},{2,18},{18,2},{3,19},{19,3},{4,20},{20... | collective-permute-start | bytes 786440 | tf_op jit(solution)/shard_map/ppermute | solution.py:244
  27.6 11.3 %collective-permute-start.6 = (bf16[128,1024]{1,0:T(8,128)(2,1)S(1)}, bf16[128,1024]{1,0:T(8,128)(2,1)S(1)}, u32[]{:S(2)}, u32[]{:S(2)}) collective-permute-start(bf16[128,1024]{1,0:T(8,128)(2,1)S(1)} %get-tuple-element.38.refs_3_), channel_id=1, source_target_pairs={{0,2},{2,0},{4,6},{6,4},{8,10},{10,8},{12,14},{14,12},{1,3},{3,1},... | collective-permute-start | bytes 786440 | tf_op jit(solution)/shard_map/ppermute | solution.py:247
  33.1 10.5 %collective-permute-start.5 = (bf16[128,1024]{1,0:T(8,128)(2,1)S(1)}, bf16[128,1024]{1,0:T(8,128)(2,1)S(1)}, u32[]{:S(2)}, u32[]{:S(2)}) collective-permute-start(bf16[128,1024]{1,0:T(8,128)(2,1)S(1)} %get-tuple-element.37), channel_id=1, source_target_pairs={{0,4},{2,6},{4,8},{6,10},{8,12},{10,14},{12,0},{14,2},{1,5},{3,7},... | collective-permute-start | bytes 786440 | tf_op jit(solution)/shard_map/ppermute | solution.py:249
  34.5 9.9 %collective-permute-start.16 = (bf16[128,1024]{1,0:T(8,128)(2,1)S(1)}, bf16[128,1024]{1,0:T(8,128)(2,1)S(1)}, u32[]{:S(2)}, u32[]{:S(2)}) collective-permute-start(bf16[128,1024]{1,0:T(8,128)(2,1)S(1)} %collective-permute-done.8.refs_0_), channel_id=1, source_target_pairs={{0,16},{16,0},{1,17},{17,1},{2,18},{18,2},{3,19},{19,3},{4,20},{20... | collective-permute-start | bytes 786440 | tf_op jit(solution)/shard_map/ppermute | solution.py:244
  36.3 9.2 %collective-permute-start.15 = (bf16[128,1024]{1,0:T(8,128)(2,1)S(1)}, bf16[128,1024]{1,0:T(8,128)(2,1)S(1)}, u32[]{:S(2)}, u32[]{:S(2)}) collective-permute-start(bf16[128,1024]{1,0:T(8,128)(2,1)S(1)} %get-tuple-element.42.refs_5_), channel_id=1, source_target_pairs={{0,2},{2,0},{4,6},{6,4},{8,10},{10,8},{12,14},{14,12},{1,3},{3,1},... | collective-permute-start | bytes 786440 | tf_op jit(solution)/shard_map/ppermute | solution.py:247
  38.9 8.8 %collective-permute-start.14 = (bf16[128,1024]{1,0:T(8,128)(2,1)S(1)}, bf16[128,1024]{1,0:T(8,128)(2,1)S(1)}, u32[]{:S(2)}, u32[]{:S(2)}) collective-permute-start(bf16[128,1024]{1,0:T(8,128)(2,1)S(1)} %get-tuple-element.45), channel_id=1, source_target_pairs={{0,4},{2,6},{4,8},{6,10},{8,12},{10,14},{12,0},{14,2},{1,5},{3,7},... | collective-permute-start | bytes 786440 | tf_op jit(solution)/shard_map/ppermute | solution.py:249
  43.7 6.4 %collective-permute-start.13 = (bf16[128,1024]{1,0:T(8,128)(2,1)S(1)}, bf16[128,1024]{1,0:T(8,128)(2,1)S(1)}, u32[]{:S(2)}, u32[]{:S(2)}) collective-permute-start(bf16[128,1024]{1,0:T(8,128)(2,1)S(1)} %collective-permute-done.6.refs_0_), channel_id=1, source_target_pairs={{0,16},{16,0},{1,17},{17,1},{2,18},{18,2},{3,19},{19,3},{4,20},{20... | collective-permute-start | bytes 786440 | tf_op jit(solution)/shard_map/ppermute | solution.py:244
  44.3 6.4 %collective-permute-start.12 = (bf16[128,1024]{1,0:T(8,128)(2,1)S(1)}, bf16[128,1024]{1,0:T(8,128)(2,1)S(1)}, u32[]{:S(2)}, u32[]{:S(2)}) collective-permute-start(bf16[128,1024]{1,0:T(8,128)(2,1)S(1)} %shard_map.56.refs_5_), channel_id=1, source_target_pairs={{0,2},{2,0},{4,6},{6,4},{8,10},{10,8},{12,14},{14,12},{1,3},{3,1},... | collective-permute-start | bytes 786440 | tf_op jit(solution)/shard_map/ppermute | solution.py:247
  44.4 3.3 %collective-permute-start.11 = (f32[320,128]{1,0:T(8,128)S(1)}, f32[320,128]{1,0:T(8,128)S(1)}, u32[]{:S(2)}, u32[]{:S(2)}) collective-permute-start(f32[320,128]{1,0:T(8,128)S(1)} %get-tuple-element.43.refs_0_), channel_id=1, source_target_pairs={{0,1},{1,0},{2,3},{3,2},{4,5},{5,4},{6,7},{7,6},{8,9},{9,8},{10,11... | collective-permute-start | bytes 491528 | tf_op jit(solution)/shard_map/ppermute | solution.py:287
  52.0 2.1 %collective-permute-start.17 = (f32[320,256]{1,0:T(8,128)S(1)}, f32[320,256]{1,0:T(8,128)S(1)}, u32[]{:S(2)}, u32[]{:S(2)}) collective-permute-start(f32[320,256]{1,0:T(8,128)S(1)} %shard_map.58.refs_5_), channel_id=1, source_target_pairs={{0,1},{1,0},{2,3},{3,2},{4,5},{5,4},{6,7},{7,6},{8,9},{9,8},{10,11... | collective-permute-start | bytes 983048 | tf_op jit(solution)/shard_map/ppermute | solution.py:290

commit v3 on v0

v3 whole, which is shorter than its diff:
```python
import functools
import math

import jax
import jax.numpy as jnp
from jax import lax
from jax.experimental import pallas as pl
from jax.experimental.pallas import tpu as pltpu
from jax.sharding import PartitionSpec as P

L_DIM = 8192
SIZES = (8, 8, 8, 8, 8, 8, 8, 8)
CHUNKS = len(SIZES)
AHEAD = 6
VMEM = pl.BlockSpec(memory_space=pltpu.VMEM)
SMEM = pl.BlockSpec(memory_space=pltpu.SMEM)
HBM = pl.BlockSpec(memory_space=pltpu.HBM)
ANY = pl.BlockSpec(memory_space=pl.ANY)
SMALL = pl.CostEstimate(flops=1024, bytes_accessed=1024, transcendentals=0)
MIB = 1024 * 1024


def width_of(k, dims):
    return SIZES[k] * dims // sum(SIZES)


def columns_of(k, dims):
    unit = dims // sum(SIZES)
    start = jnp.where(
        lax.axis_index("groups") == 0, sum(SIZES[:k]) * unit, sum(SIZES[k + 1 :]) * unit
    )
    return pl.ds(pl.multiple_of(start, unit), width_of(k, dims))


def products(rows, block):
    return lax.dot_general(
        rows, block, (((1,), (1,)), ((), ())), preferred_element_type=jnp.float32
    )


def scale_of(factor, counts, half, side):
    layer = lax.axis_index("layer")
    start = (layer if side else 1 - layer) * half
    index = start + lax.broadcasted_iota(jnp.int32, (half, 1), 0)
    return factor * (index < counts[0]).astype(jnp.float32)


def first_kernel(queries, *refs):
    outs, sem = refs[:2], refs[2]
    dims = queries.shape[1]
    copies = [
        pltpu.make_async_copy(queries.at[:, columns_of(k, dims)], outs[k], sem.at[k])
        for k in range(2)
    ]
    for copy in copies:
        copy.start()
    for copy in copies:
        copy.wait()


def step_kernel(k, ahead, queries, received, *refs):
    outs, sem = refs[-2 - (ahead is not None) : -1], refs[-1]
    dims = queries.shape[1]
    even = lax.axis_index("dp") % 2 == 0
    own_copy = pltpu.make_async_copy(queries.at[:, columns_of(k, dims)], outs[0], sem.at[0])
    received_copy = pltpu.make_async_copy(received, outs[0], sem.at[0])
    if ahead is not None:
        ahead_copy = pltpu.make_async_copy(
            queries.at[:, columns_of(ahead, dims)], outs[1], sem.at[1]
        )
        ahead_copy.start()

    @pl.when(even)
    def _():
        own_copy.start()
        own_copy.wait()

    @pl.when(jnp.logical_not(even))
    def _():
        received_copy.start()
        received_copy.wait()

    if ahead is not None:
        ahead_copy.wait()


def own_kernel(factor, pieces, counts, documents, queries, eigenvalues, *refs):
    theirs, mine, inverse, held, own, doc_sem, own_sem = refs[-7:]
    layer = lax.axis_index("layer")
    half = documents.shape[0] // 2
    dims = documents.shape[1]
    width = dims // pieces
    copies = []
    for i in range(pieces):
        columns = pl.ds(i * width, width)
        copies.append([pltpu.make_async_copy(queries.at[:, columns], own.at[:, columns], own_sem.at[i])])
        for at, row in enumerate((1 - layer, layer)):
            copies[i].append(
                pltpu.make_async_copy(
                    documents.at[pl.ds(pl.multiple_of(row * half, half), half), columns],
                    held.at[pl.ds(at * half, half), columns],
                    doc_sem.at[i, at],
                )
            )
        for copy in copies[i]:
            copy.start()
    for start in range(0, dims, L_DIM):
        block = eigenvalues[:, start : start + L_DIM]
        damping = 0.1 * jnp.mean(block, axis=1, keepdims=True)
        inverse[:, start : start + L_DIM] = 1.0 / (block + damping)
    for i in range(pieces):
        for copy in copies[i]:
            copy.wait()
        columns = slice(i * width, (i + 1) * width)
        scaled = (own[:, columns].astype(jnp.float32) * inverse[:, columns]).astype(jnp.bfloat16)
        for out, rows in ((theirs, slice(0, half)), (mine, slice(half, 2 * half))):
            term = products(held[rows, columns], scaled)
            if i == 0:
                out[...] = term
            else:
                out[...] += term
    theirs[...] *= scale_of(factor, counts, half, 0)
    mine[...] *= scale_of(factor, counts, half, 1)


def pair_kernel(ks, side, factor, fresh, counts, held, inverse, *refs):
    count = len(ks)
    chunks, refs = refs[: 2 * count], refs[2 * count :]
    if not fresh:
        sums = refs[0]
    out, block_buf = refs[-2:]
    dims = held.shape[1]
    first = 0 if side is None else side * out.shape[0]
    rows = chunks[0].shape[0]
    for i, k in enumerate(ks):
        columns = columns_of(k, dims)
        width = width_of(k, dims)
        for b in range(2):
            scaled = chunks[2 * i + b][...].astype(jnp.float32) * inverse[:, columns]
            block_buf[pl.ds(b * rows, rows), :width] = scaled.astype(jnp.bfloat16)
        term = products(held[pl.ds(first, out.shape[0]), columns], block_buf[:, :width])
        if i > 0:
            out[...] += term
        elif fresh:
            out[...] = term
        else:
            out[...] = sums[pl.ds(first, out.shape[0]), :] + term
    if side is not None:
        out[...] *= scale_of(factor, counts, out.shape[0], side)


def final_kernel(mine0, got0, mine, got, out):
    rows = mine0.shape[1]
    out[:, :rows] = mine0[...] + got0[...]
    out[:, rows:] = mine[...] + got[...]


def on_device(queries, documents, counts, eigenvalues):
    rows, dims = queries.shape
    doc_rows = documents.shape[0]
    half = doc_rows // 2
    owners = lax.axis_size("dp")
    factor = 1.0 / math.sqrt(dims * lax.axis_size("layer"))
    ahead = [(i, (i + 2) % owners) for i in range(owners)]
    pair = [(i, i ^ 1) for i in range(owners)]
    across = [(0, 1), (1, 0)]

    def chunk(k):
        return jax.ShapeDtypeStruct((rows, width_of(k, dims)), queries.dtype)

    def scores(count):
        return jax.ShapeDtypeStruct((count, 2 * rows), jnp.float32)

    def call(kernel, out_shape, in_specs, out_specs, scratch, vmem_mib=16):
        return pl.pallas_call(
            kernel,
            out_shape=out_shape,
            in_specs=in_specs,
            out_specs=out_specs,
            scratch_shapes=scratch,
            compiler_params=pltpu.CompilerParams(vmem_limit_bytes=vmem_mib * MIB),
            cost_estimate=SMALL,
        )

    def step(k, *until):
        ahead_k = k + 2 if k + 2 < AHEAD else None
        outs = [chunk(k)] + ([] if ahead_k is None else [chunk(ahead_k)])
        return call(
            functools.partial(step_kernel, k, ahead_k),
            outs,
            [HBM, ANY] + [ANY] * len(until),
            [ANY] * len(outs),
            [pltpu.SemaphoreType.DMA((2,))],
        )(queries, far[k], *until)

    def pair_scores(*ks, sums=None, side=None, until=()):
        operands = [held, inverse] + [block[k] for k in ks for block in (near, far)]
        if sums is not None:
            operands.append(sums)
        return call(
            functools.partial(pair_kernel, ks, side, factor, sums is None),
            scores(doc_rows if side is None else half),
            [SMEM] + [VMEM] * len(operands) + [ANY] * len(until),
            VMEM,
            [pltpu.VMEM((2 * rows, max(width_of(k, dims) for k in ks)), queries.dtype)],
        )(counts, *operands, *until)

    far = [None] * CHUNKS
    near = [None] * CHUNKS

    def send_across(block, k, *until):
        sent = lax.optimization_barrier((block[k], *until))[0]
        block[CHUNKS - 1 - k] = lax.ppermute(sent, "groups", across)

    def send(k, outs):
        near[k] = lax.ppermute(outs[0], "dp", pair)
        if len(outs) > 1:
            far[k + 2] = lax.ppermute(outs[1], "dp", ahead)

    sent = call(
        first_kernel,
        [chunk(0), chunk(1)],
        [HBM],
        [ANY] * 2,
        [pltpu.SemaphoreType.DMA((2,))],
        vmem_mib=60,
    )(queries)
    for k in range(2):
        far[k] = lax.ppermute(sent[k], "dp", ahead)
    pieces = 8
    theirs0, mine0, inverse, held = call(
        functools.partial(own_kernel, factor, pieces),
        [
            jax.ShapeDtypeStruct((half, rows), jnp.float32),
            jax.ShapeDtypeStruct((half, rows), jnp.float32),
            jax.ShapeDtypeStruct((1, dims), jnp.float32),
            jax.ShapeDtypeStruct(documents.shape, documents.dtype),
        ],
        [SMEM, HBM, HBM, VMEM],
        [VMEM] * 4,
        [
            pltpu.VMEM((rows, dims), queries.dtype),
            pltpu.SemaphoreType.DMA((pieces, 2)),
            pltpu.SemaphoreType.DMA((pieces,)),
        ],
        vmem_mib=40,
    )(counts, documents, queries, lax.optimization_barrier((eigenvalues, sent[1]))[0].reshape(1, dims))

    outs = step(0, inverse)
    send(0, outs)
    send_across(far, 0, outs[0])

    outs = step(1)
    send(1, outs)
    send_across(far, 1, outs[0])
    sums = pair_scores(0, until=(outs[0], far[CHUNKS - 1]))

    outs = step(2, sums)
    send(2, outs)
    send_across(near, 0, outs[0])
    sums = pair_scores(1, sums=sums, until=(outs[0], far[CHUNKS - 2]))

    outs = step(3, sums)
    send(3, outs)
    send_across(near, 1, outs[0])
    sums = pair_scores(2, CHUNKS - 1, sums=sums, until=(outs[0],))

    outs = step(4, sums)
    send(4, outs)
    send_across(near, 2, outs[0])
    sent0 = lax.optimization_barrier((theirs0, outs[0]))[0]
    got0 = lax.ppermute(sent0, "layer", across)
    sums = pair_scores(3, CHUNKS - 2, sums=sums, until=(outs[0],))
    theirs = pair_scores(4, 5, sums=sums, side=0, until=(got0,))
    got = lax.ppermute(theirs, "layer", across)
    mine = pair_scores(4, 5, sums=sums, side=1, until=(theirs,))
    return call(final_kernel, jax.ShapeDtypeStruct((half, 3 * rows), jnp.float32), [VMEM] * 4, VMEM, [])(
        mine0, got0, mine, got
    )


def solution(mesh):
    return jax.shard_map(
        on_device,
        mesh=mesh,
        in_specs=(P("dp", "layer"), P(("groups", "dp"), "layer"), P(("groups", "dp")), P("layer")),
        out_specs=P(("groups", "dp", "layer"), None),
        check_vma=False,
    )
```

time: 136 us -> 65.1 us (0.48)
  waiting for transfers between devices: 83.8 us -> 10.4 us
  Pallas kernels: 0 us -> 26.9 us
  matrix products: 22.7 us -> 0 us
  starting transfers between devices: 3.11 us -> 24.4 us
  between operations: 14.5 us -> 0.82 us
  local copies, waits for them, and re-layouts: 6.84 us -> 2.34 us
  other arithmetic: 4.18 us -> 0 us
    ppermute x2 -> x18, waiting for transfers between devices: 80.9 us -> 10.4 us  [the longest x4 4.59 us: send(): far[k + 2] = lax.ppermute(outs[1], 'dp', ahead)]
    pallas_call x0 -> x14, Pallas kernels: none -> 26.9 us  [the longest x1 17 us: on_device(): call(first_kernel, [chunk(0), chunk(1)], [HBM], [ANY] * 2, [pltpu.Semapho...]
    dot_general x3 -> x0, matrix products: 22.7 us -> none  [block_scores(): lax.dot_general(doc_rows, block, (((1,), (1,)), ((), ())), preferred_elem...]
    ppermute x2 -> x18, starting transfers between devices: 3.02 us -> 24.4 us  [the longest x4 7.76 us: send(): far[k + 2] = lax.ppermute(outs[1], 'dp', ahead)]
    unnamed x6 -> x4, local copies, waits for them, and re-layouts: 5.85 us -> 2.34 us
    unnamed x6 -> x0, waiting for transfers between devices: 2.9 us -> none
    convert_element_type x1 -> x0, other arithmetic: 1.99 us -> none  [on_device(): precond = (queries.astype(jnp.float32) * inverse).astype(jnp.bfloat16)]
    reduce_sum x1 -> x0, other arithmetic: 1.37 us -> none  [on_device(): damping = 0.1 * jnp.mean(blocks, axis=1, keepdims=True)]
  transfers between devices with their start and end apart: 5 -> 18, of which waited for: 3 -> 9; matrix products, arithmetic and copies ran while one was open for 20% -> 0% of each run, Pallas kernels for 0% -> 13%
where the time goes in v3:
time: 65.1 us; the launch traced here: 64.8 us
  Pallas kernels  26.9 us (41%)
  starting transfers between devices  24.4 us (37%)
  waiting for transfers between devices  10.4 us (16%)
  local copies, waits for them, and re-layouts  2.34 us (4%)
  between operations  0.82 us (1%)
    pallas_call x1, Pallas kernels, on_device(): call(first_kernel, [chunk(0), chunk(1)], [HBM], [ANY] * 2, [pltpu.Semapho...  17 us
    ppermute x4, starting transfers between devices, send(): far[k + 2] = lax.ppermute(outs[1], 'dp', ahead)  7.76 us
    ppermute x5, starting transfers between devices, send(): near[k] = lax.ppermute(outs[0], 'dp', pair)  7.64 us
    pallas_call x1, Pallas kernels, on_device(): call(functools.partial(own_kernel, factor, pieces), [jax.ShapeDtypeStruct...  4.82 us
    ppermute x2, starting transfers between devices, on_device(): far[k] = lax.ppermute(sent[k], 'dp', ahead)  4.65 us
    ppermute x4, waiting for transfers between devices, send(): far[k + 2] = lax.ppermute(outs[1], 'dp', ahead)  4.59 us
    ppermute x5, starting transfers between devices, send_across(): block[CHUNKS - 1 - k] = lax.ppermute(sent, 'groups', across)  4.26 us
    pallas_call x6, Pallas kernels, pair_scores(): call(functools.partial(pair_kernel, ks, side, factor, sums is None), scor...  4 us
  transfers between devices with their start and end apart: 18, of which 9 were waited for; matrix products, arithmetic and copies ran while one was open for 0% of the time, Pallas kernels for 13%

profile of v3, /device:TPU:0, one launch (start us, length us, event | category | flops | bytes accessed | tf_op | source)
XLA Modules:
  0.0 64.8 jit_solution(587580517329891513)
XLA Ops:
  0.0 17.0 %shard_map.46 = (bf16[128,1024]{1,0:T(8,128)(2,1)}, bf16[128,1024]{1,0:T(8,128)(2,1)}) custom-call(bf16[128,8192]{1,0:T(8,128)(2,1)} %queries.13), custom_call_target="tpu_custom_call" | custom-call | flops 1024 | bytes 1024 | tf_op jit(solution)/shard_map/pallas_call | solution.py:220
  17.0 3.1 %collective-permute-start = (bf16[128,1024]{1,0:T(8,128)(2,1)}, bf16[128,1024]{1,0:T(8,128)(2,1)S(1)}, u32[]{:S(2)}, u32[]{:S(2)}) collective-permute-start(bf16[128,1024]{1,0:T(8,128)(2,1)} %get-tuple-element.30), channel_id=1, source_target_pairs={{0,4},{2,6},{4,8},{6,10},{8,12},{10,14},{12,0},{14,2},{1,5},{3,7},... | collective-permute-start | bytes 786440 | tf_op jit(solution)/shard_map/ppermute | solution.py:229
  20.1 1.6 %collective-permute-start.3 = (bf16[128,1024]{1,0:T(8,128)(2,1)}, bf16[128,1024]{1,0:T(8,128)(2,1)S(1)}, u32[]{:S(2)}, u32[]{:S(2)}) collective-permute-start(bf16[128,1024]{1,0:T(8,128)(2,1)} %get-tuple-element.26), channel_id=1, source_target_pairs={{0,4},{2,6},{4,8},{6,10},{8,12},{10,14},{12,0},{14,2},{1,5},{3,7},... | collective-permute-start | bytes 786440 | tf_op jit(solution)/shard_map/ppermute | solution.py:229
  22.3 0.0 copy-start
  22.3 1.6 %copy-done = bf16[128,8192]{1,0:T(8,128)(2,1)S(1)} copy-done((bf16[128,8192]{1,0:T(8,128)(2,1)S(1)}, bf16[128,8192]{1,0:T(8,128)(2,1)}, u32[]{:S(2)}) %copy-start) | copy-done | bytes 2097176
  23.9 0.8 %copy-done.1 = f32[8192]{0:T(1024)S(1)} copy-done((f32[8192]{0:T(1024)S(1)}, f32[8192]{0:T(1024)}, u32[]{:S(2)}) %copy-start.1) | copy-done | bytes 32792
  24.7 4.8 %shard_map.47 = (f32[320,128]{1,0:T(8,128)S(1)}, f32[320,128]{1,0:T(8,128)S(1)}, f32[1,8192]{1,0:T(1,128)S(1)}, bf16[640,8192]{1,0:T(8,128)(2,1)S(1)}) custom-call(s32[1]{0:T(128)S(6)} %copy.5.counts, bf16[640,8192]{1,0:T(8,128)(2,1)} %documents.1, bf16[128,8192]{1,0:T(8,128)(2,1)S(1)} %copy-done, f32[1,8192]{1,0:T(1,128)S(1)} %bitcast.1), custom_call_target="tpu_custom_call" | custom-call | flops 1024 | bytes 1024 | tf_op jit(solution)/shard_map/pallas_call | solution.py:231
  29.5 0.1 shard_map.48
  29.6 1.7 %collective-permute-start.4 = (bf16[128,1024]{1,0:T(8,128)(2,1)S(1)}, bf16[128,1024]{1,0:T(8,128)(2,1)S(1)}, u32[]{:S(2)}, u32[]{:S(2)}) collective-permute-start(bf16[128,1024]{1,0:T(8,128)(2,1)S(1)} %collective-permute-done.received.refs_1_), channel_id=1, source_target_pairs={{0,16},{16,0},{1,17},{17,1},{2,18},{18,2},{3,19},{19,3},{4,20},{20... | collective-permute-start | bytes 786440 | tf_op jit(solution)/shard_map/ppermute | solution.py:213
  31.3 1.5 %collective-permute-start.2 = (bf16[128,1024]{1,0:T(8,128)(2,1)S(1)}, bf16[128,1024]{1,0:T(8,128)(2,1)S(1)}, u32[]{:S(2)}, u32[]{:S(2)}) collective-permute-start(bf16[128,1024]{1,0:T(8,128)(2,1)S(1)} %get-tuple-element.34), channel_id=1, source_target_pairs={{0,2},{2,0},{4,6},{6,4},{8,10},{10,8},{12,14},{14,12},{1,3},{3,1},... | collective-permute-start | bytes 786440 | tf_op jit(solution)/shard_map/ppermute | solution.py:216
  32.8 1.4 %collective-permute-start.1 = (bf16[128,1024]{1,0:T(8,128)(2,1)S(1)}, bf16[128,1024]{1,0:T(8,128)(2,1)S(1)}, u32[]{:S(2)}, u32[]{:S(2)}) collective-permute-start(bf16[128,1024]{1,0:T(8,128)(2,1)S(1)} %get-tuple-element.32), channel_id=1, source_target_pairs={{0,4},{2,6},{4,8},{6,10},{8,12},{10,14},{12,0},{14,2},{1,5},{3,7},... | collective-permute-start | bytes 786440 | tf_op jit(solution)/shard_map/ppermute | solution.py:218
  34.2 0.0 collective-permute-done.3.received.refs_1_
  34.2 0.1 shard_map.49
  34.3 1.6 %collective-permute-start.9 = (bf16[128,1024]{1,0:T(8,128)(2,1)S(1)}, bf16[128,1024]{1,0:T(8,128)(2,1)S(1)}, u32[]{:S(2)}, u32[]{:S(2)}) collective-permute-start(bf16[128,1024]{1,0:T(8,128)(2,1)S(1)} %collective-permute-done.3.received.refs_1_), channel_id=1, source_target_pairs={{0,16},{16,0},{1,17},{17,1},{2,18},{18,2},{3,19},{19,3},{4,20},{20... | collective-permute-start | bytes 786440 | tf_op jit(solution)/shard_map/ppermute | solution.py:213
  35.9 1.9 %collective-permute-start.8 = (bf16[128,1024]{1,0:T(8,128)(2,1)S(1)}, bf16[128,1024]{1,0:T(8,128)(2,1)S(1)}, u32[]{:S(2)}, u32[]{:S(2)}) collective-permute-start(bf16[128,1024]{1,0:T(8,128)(2,1)S(1)} %get-tuple-element.35.refs_2_), channel_id=1, source_target_pairs={{0,2},{2,0},{4,6},{6,4},{8,10},{10,8},{12,14},{14,12},{1,3},{3,1},... | collective-permute-start | bytes 786440 | tf_op jit(solution)/shard_map/ppermute | solution.py:216
  37.8 0.2 collective-permute-done.4.refs_3_
  38.0 2.5 %collective-permute-start.10 = (bf16[128,1024]{1,0:T(8,128)(2,1)S(1)}, bf16[128,1024]{1,0:T(8,128)(2,1)S(1)}, u32[]{:S(2)}, u32[]{:S(2)}) collective-permute-start(bf16[128,1024]{1,0:T(8,128)(2,1)S(1)} %get-tuple-element.41), channel_id=1, source_target_pairs={{0,4},{2,6},{4,8},{6,10},{8,12},{10,14},{12,0},{14,2},{1,5},{3,7},... | collective-permute-start | bytes 786440 | tf_op jit(solution)/shard_map/ppermute | solution.py:218
  40.5 0.6 shard_map.50.refs_0_.refs_2_
  41.0 1.4 %collective-permute-done.1.received.refs_1_ = bf16[128,1024]{1,0:T(8,128)(2,1)S(1)} collective-permute-done((bf16[128,1024]{1,0:T(8,128)(2,1)S(1)}, bf16[128,1024]{1,0:T(8,128)(2,1)S(1)}, u32[]{:S(2)}, u32[]{:S(2)}) %collective-permute-start.1) | collective-permute-done | bytes 262176 | tf_op jit(solution)/shard_map/ppermute | solution.py:218
  42.5 0.1 shard_map.51
  42.5 0.2 collective-permute-start.7
  42.7 1.5 %collective-permute-start.6 = (bf16[128,1024]{1,0:T(8,128)(2,1)S(1)}, bf16[128,1024]{1,0:T(8,128)(2,1)S(1)}, u32[]{:S(2)}, u32[]{:S(2)}) collective-permute-start(bf16[128,1024]{1,0:T(8,128)(2,1)S(1)} %get-tuple-element.38.refs_3_), channel_id=1, source_target_pairs={{0,2},{2,0},{4,6},{6,4},{8,10},{10,8},{12,14},{14,12},{1,3},{3,1},... | collective-permute-start | bytes 786440 | tf_op jit(solution)/shard_map/ppermute | solution.py:216
  44.2 0.0 collective-permute-done.9.refs_4_.refs_3_
  44.2 1.9 %collective-permute-start.5 = (bf16[128,1024]{1,0:T(8,128)(2,1)S(1)}, bf16[128,1024]{1,0:T(8,128)(2,1)S(1)}, u32[]{:S(2)}, u32[]{:S(2)}) collective-permute-start(bf16[128,1024]{1,0:T(8,128)(2,1)S(1)} %get-tuple-element.37), channel_id=1, source_target_pairs={{0,4},{2,6},{4,8},{6,10},{8,12},{10,14},{12,0},{14,2},{1,5},{3,7},... | collective-permute-start | bytes 786440 | tf_op jit(solution)/shard_map/ppermute | solution.py:218
  46.1 0.0 collective-permute-done.8.refs_0_
  46.1 0.6 shard_map.52.refs_0_.refs_4_
  46.7 0.9 %collective-permute-done.10.received.refs_1_ = bf16[128,1024]{1,0:T(8,128)(2,1)S(1)} collective-permute-done((bf16[128,1024]{1,0:T(8,128)(2,1)S(1)}, bf16[128,1024]{1,0:T(8,128)(2,1)S(1)}, u32[]{:S(2)}, u32[]{:S(2)}) %collective-permute-start.10) | collective-permute-done | bytes 262176 | tf_op jit(solution)/shard_map/ppermute | solution.py:218
  47.5 0.1 shard_map.53
  47.6 0.7 %collective-permute-start.16 = (bf16[128,1024]{1,0:T(8,128)(2,1)S(1)}, bf16[128,1024]{1,0:T(8,128)(2,1)S(1)}, u32[]{:S(2)}, u32[]{:S(2)}) collective-permute-start(bf16[128,1024]{1,0:T(8,128)(2,1)S(1)} %collective-permute-done.8.refs_0_), channel_id=1, source_target_pairs={{0,16},{16,0},{1,17},{17,1},{2,18},{18,2},{3,19},{19,3},{4,20},{20... | collective-permute-start | bytes 786440 | tf_op jit(solution)/shard_map/ppermute | solution.py:213
  48.3 1.5 %collective-permute-start.15 = (bf16[128,1024]{1,0:T(8,128)(2,1)S(1)}, bf16[128,1024]{1,0:T(8,128)(2,1)S(1)}, u32[]{:S(2)}, u32[]{:S(2)}) collective-permute-start(bf16[128,1024]{1,0:T(8,128)(2,1)S(1)} %get-tuple-element.42.refs_5_), channel_id=1, source_target_pairs={{0,2},{2,0},{4,6},{6,4},{8,10},{10,8},{12,14},{14,12},{1,3},{3,1},... | collective-permute-start | bytes 786440 | tf_op jit(solution)/shard_map/ppermute | solution.py:216
  49.8 0.2 collective-permute-done.7.refs_2_
  50.0 2.0 %collective-permute-start.14 = (bf16[128,1024]{1,0:T(8,128)(2,1)S(1)}, bf16[128,1024]{1,0:T(8,128)(2,1)S(1)}, u32[]{:S(2)}, u32[]{:S(2)}) collective-permute-start(bf16[128,1024]{1,0:T(8,128)(2,1)S(1)} %get-tuple-element.45), channel_id=1, source_target_pairs={{0,4},{2,6},{4,8},{6,10},{8,12},{10,14},{12,0},{14,2},{1,5},{3,7},... | collective-permute-start | bytes 786440 | tf_op jit(solution)/shard_map/ppermute | solution.py:218
  52.0 0.0 collective-permute-done.6.refs_0_
  52.0 0.9 %shard_map.54.refs_0_.refs_4_ = f32[640,256]{1,0:T(8,128)S(1)} custom-call(s32[1]{0:T(128)S(6)} %copy.5.counts, bf16[640,8192]{1,0:T(8,128)(2,1)S(1)} %get-tuple-element.33.held, f32[1,8192]{1,0:T(1,128)S(1)} %get-tuple-element.31.refs_0_.inverse, bf16[128,1024]{1,0:T(8,128)(2,1)S(1)} %collective-permute-done.6.refs_0_, ...), custom_call_target="tpu_custom_call" | custom-call | flops 1024 | bytes 1024 | tf_op jit(solution)/shard_map/pallas_call | solution.py:200
  52.9 2.3 %collective-permute-done.5.received.refs_1_ = bf16[128,1024]{1,0:T(8,128)(2,1)S(1)} collective-permute-done((bf16[128,1024]{1,0:T(8,128)(2,1)S(1)}, bf16[128,1024]{1,0:T(8,128)(2,1)S(1)}, u32[]{:S(2)}, u32[]{:S(2)}) %collective-permute-start.5) | collective-permute-done | bytes 262176 | tf_op jit(solution)/shard_map/ppermute | solution.py:218
  55.2 0.1 collective-permute-start.13
  55.3 1.2 %collective-permute-start.12 = (bf16[128,1024]{1,0:T(8,128)(2,1)S(1)}, bf16[128,1024]{1,0:T(8,128)(2,1)S(1)}, u32[]{:S(2)}, u32[]{:S(2)}) collective-permute-start(bf16[128,1024]{1,0:T(8,128)(2,1)S(1)} %shard_map.55.refs_5_), channel_id=1, source_target_pairs={{0,2},{2,0},{4,6},{6,4},{8,10},{10,8},{12,14},{14,12},{1,3},{3,1},... | collective-permute-start | bytes 786440 | tf_op jit(solution)/shard_map/ppermute | solution.py:216
  56.5 0.0 collective-permute-done.16.refs_2_
  56.5 0.0 collective-permute-start.11
  56.5 0.9 %collective-permute-done.15.refs_0_ = bf16[128,1024]{1,0:T(8,128)(2,1)S(1)} collective-permute-done((bf16[128,1024]{1,0:T(8,128)(2,1)S(1)}, bf16[128,1024]{1,0:T(8,128)(2,1)S(1)}, u32[]{:S(2)}, u32[]{:S(2)}) %collective-permute-start.15) | collective-permute-done | bytes 262176 | tf_op jit(solution)/shard_map/ppermute | solution.py:216
  57.5 0.9 %shard_map.56.refs_4_ = f32[640,256]{1,0:T(8,128)S(1)} custom-call(s32[1]{0:T(128)S(6)} %copy.5.counts, bf16[640,8192]{1,0:T(8,128)(2,1)S(1)} %get-tuple-element.33.held, f32[1,8192]{1,0:T(1,128)S(1)} %get-tuple-element.31.refs_0_.inverse, bf16[128,1024]{1,0:T(8,128)(2,1)S(1)} %collective-permute-done.15.refs_0_, ...), custom_call_target="tpu_custom_call" | custom-call | flops 1024 | bytes 1024 | tf_op jit(solution)/shard_map/pallas_call | solution.py:200
  58.4 3.3 %collective-permute-done.13.refs_2_ = bf16[128,1024]{1,0:T(8,128)(2,1)S(1)} collective-permute-done((bf16[128,1024]{1,0:T(8,128)(2,1)S(1)}, bf16[128,1024]{1,0:T(8,128)(2,1)S(1)}, u32[]{:S(2)}, u32[]{:S(2)}) %collective-permute-start.13) | collective-permute-done | bytes 262176 | tf_op jit(solution)/shard_map/ppermute | solution.py:213
  61.7 0.1 collective-permute-done.12.refs_0_
  61.8 0.6 shard_map.57.refs_5_
  62.3 0.1 collective-permute-start.17
  62.4 0.6 shard_map.58.mine
  63.0 1.0 %collective-permute-done.17.got = f32[320,256]{1,0:T(8,128)S(1)} collective-permute-done((f32[320,256]{1,0:T(8,128)S(1)}, f32[320,256]{1,0:T(8,128)S(1)}, u32[]{:S(2)}, u32[]{:S(2)}) %collective-permute-start.17) | collective-permute-done | bytes 327712 | tf_op jit(solution)/shard_map/ppermute | solution.py:275
  64.0 0.8 %shard_map.59 = f32[320,384]{1,0:T(8,128)} custom-call(f32[320,128]{1,0:T(8,128)S(1)} %get-tuple-element.28.mine0, f32[320,128]{1,0:T(8,128)S(1)} %collective-permute-done.11.refs_5_.got0, f32[320,256]{1,0:T(8,128)S(1)} %shard_map.58.mine, f32[320,256]{1,0:T(8,128)S(1)} %collective-permute-done.17.got), custom_call_target="tpu_custom_call" | custom-call | flops 1024 | bytes 1024 | tf_op jit(solution)/shard_map/pallas_call | solution.py:277
  (6 shorter events, 0.0 us)
Async XLA Ops:
  17.0 12.5 %collective-permute-start = (bf16[128,1024]{1,0:T(8,128)(2,1)}, bf16[128,1024]{1,0:T(8,128)(2,1)S(1)}, u32[]{:S(2)}, u32[]{:S(2)}) collective-permute-start(bf16[128,1024]{1,0:T(8,128)(2,1)} %get-tuple-element.30), channel_id=1, source_target_pairs={{0,4},{2,6},{4,8},{6,10},{8,12},{10,14},{12,0},{14,2},{1,5},{3,7},... | collective-permute-start | bytes 786440 | tf_op jit(solution)/shard_map/ppermute | solution.py:229
  20.1 14.2 %collective-permute-start.3 = (bf16[128,1024]{1,0:T(8,128)(2,1)}, bf16[128,1024]{1,0:T(8,128)(2,1)S(1)}, u32[]{:S(2)}, u32[]{:S(2)}) collective-permute-start(bf16[128,1024]{1,0:T(8,128)(2,1)} %get-tuple-element.26), channel_id=1, source_target_pairs={{0,4},{2,6},{4,8},{6,10},{8,12},{10,14},{12,0},{14,2},{1,5},{3,7},... | collective-permute-start | bytes 786440 | tf_op jit(solution)/shard_map/ppermute | solution.py:229
  22.3 1.6 %copy-start = (bf16[128,8192]{1,0:T(8,128)(2,1)S(1)}, bf16[128,8192]{1,0:T(8,128)(2,1)}, u32[]{:S(2)}) copy-start(bf16[128,8192]{1,0:T(8,128)(2,1)} %queries.13) | copy-start | bytes 6291460
  23.9 0.8 %copy-start.1 = (f32[8192]{0:T(1024)S(1)}, f32[8192]{0:T(1024)}, u32[]{:S(2)}) copy-start(f32[8192]{0:T(1024)} %param.7) | copy-start | bytes 98308
  29.6 8.4 %collective-permute-start.4 = (bf16[128,1024]{1,0:T(8,128)(2,1)S(1)}, bf16[128,1024]{1,0:T(8,128)(2,1)S(1)}, u32[]{:S(2)}, u32[]{:S(2)}) collective-permute-start(bf16[128,1024]{1,0:T(8,128)(2,1)S(1)} %collective-permute-done.received.refs_1_), channel_id=1, source_target_pairs={{0,16},{16,0},{1,17},{17,1},{2,18},{18,2},{3,19},{19,3},{4,20},{20... | collective-permute-start | bytes 786440 | tf_op jit(solution)/shard_map/ppermute | solution.py:213
  31.3 9.2 %collective-permute-start.2 = (bf16[128,1024]{1,0:T(8,128)(2,1)S(1)}, bf16[128,1024]{1,0:T(8,128)(2,1)S(1)}, u32[]{:S(2)}, u32[]{:S(2)}) collective-permute-start(bf16[128,1024]{1,0:T(8,128)(2,1)S(1)} %get-tuple-element.34), channel_id=1, source_target_pairs={{0,2},{2,0},{4,6},{6,4},{8,10},{10,8},{12,14},{14,12},{1,3},{3,1},... | collective-permute-start | bytes 786440 | tf_op jit(solution)/shard_map/ppermute | solution.py:216
  32.8 9.6 %collective-permute-start.1 = (bf16[128,1024]{1,0:T(8,128)(2,1)S(1)}, bf16[128,1024]{1,0:T(8,128)(2,1)S(1)}, u32[]{:S(2)}, u32[]{:S(2)}) collective-permute-start(bf16[128,1024]{1,0:T(8,128)(2,1)S(1)} %get-tuple-element.32), channel_id=1, source_target_pairs={{0,4},{2,6},{4,8},{6,10},{8,12},{10,14},{12,0},{14,2},{1,5},{3,7},... | collective-permute-start | bytes 786440 | tf_op jit(solution)/shard_map/ppermute | solution.py:218
  34.3 9.9 %collective-permute-start.9 = (bf16[128,1024]{1,0:T(8,128)(2,1)S(1)}, bf16[128,1024]{1,0:T(8,128)(2,1)S(1)}, u32[]{:S(2)}, u32[]{:S(2)}) collective-permute-start(bf16[128,1024]{1,0:T(8,128)(2,1)S(1)} %collective-permute-done.3.received.refs_1_), channel_id=1, source_target_pairs={{0,16},{16,0},{1,17},{17,1},{2,18},{18,2},{3,19},{19,3},{4,20},{20... | collective-permute-start | bytes 786440 | tf_op jit(solution)/shard_map/ppermute | solution.py:213
  35.9 10.2 %collective-permute-start.8 = (bf16[128,1024]{1,0:T(8,128)(2,1)S(1)}, bf16[128,1024]{1,0:T(8,128)(2,1)S(1)}, u32[]{:S(2)}, u32[]{:S(2)}) collective-permute-start(bf16[128,1024]{1,0:T(8,128)(2,1)S(1)} %get-tuple-element.35.refs_2_), channel_id=1, source_target_pairs={{0,2},{2,0},{4,6},{6,4},{8,10},{10,8},{12,14},{14,12},{1,3},{3,1},... | collective-permute-start | bytes 786440 | tf_op jit(solution)/shard_map/ppermute | solution.py:216
  38.0 9.6 %collective-permute-start.10 = (bf16[128,1024]{1,0:T(8,128)(2,1)S(1)}, bf16[128,1024]{1,0:T(8,128)(2,1)S(1)}, u32[]{:S(2)}, u32[]{:S(2)}) collective-permute-start(bf16[128,1024]{1,0:T(8,128)(2,1)S(1)} %get-tuple-element.41), channel_id=1, source_target_pairs={{0,4},{2,6},{4,8},{6,10},{8,12},{10,14},{12,0},{14,2},{1,5},{3,7},... | collective-permute-start | bytes 786440 | tf_op jit(solution)/shard_map/ppermute | solution.py:218
  42.5 7.5 %collective-permute-start.7 = (bf16[128,1024]{1,0:T(8,128)(2,1)S(1)}, bf16[128,1024]{1,0:T(8,128)(2,1)S(1)}, u32[]{:S(2)}, u32[]{:S(2)}) collective-permute-start(bf16[128,1024]{1,0:T(8,128)(2,1)S(1)} %collective-permute-done.2.refs_0_), channel_id=1, source_target_pairs={{0,16},{16,0},{1,17},{17,1},{2,18},{18,2},{3,19},{19,3},{4,20},{20... | collective-permute-start | bytes 786440 | tf_op jit(solution)/shard_map/ppermute | solution.py:213
  42.7 9.3 %collective-permute-start.6 = (bf16[128,1024]{1,0:T(8,128)(2,1)S(1)}, bf16[128,1024]{1,0:T(8,128)(2,1)S(1)}, u32[]{:S(2)}, u32[]{:S(2)}) collective-permute-start(bf16[128,1024]{1,0:T(8,128)(2,1)S(1)} %get-tuple-element.38.refs_3_), channel_id=1, source_target_pairs={{0,2},{2,0},{4,6},{6,4},{8,10},{10,8},{12,14},{14,12},{1,3},{3,1},... | collective-permute-start | bytes 786440 | tf_op jit(solution)/shard_map/ppermute | solution.py:216
  44.2 11.0 %collective-permute-start.5 = (bf16[128,1024]{1,0:T(8,128)(2,1)S(1)}, bf16[128,1024]{1,0:T(8,128)(2,1)S(1)}, u32[]{:S(2)}, u32[]{:S(2)}) collective-permute-start(bf16[128,1024]{1,0:T(8,128)(2,1)S(1)} %get-tuple-element.37), channel_id=1, source_target_pairs={{0,4},{2,6},{4,8},{6,10},{8,12},{10,14},{12,0},{14,2},{1,5},{3,7},... | collective-permute-start | bytes 786440 | tf_op jit(solution)/shard_map/ppermute | solution.py:218
  47.6 8.9 %collective-permute-start.16 = (bf16[128,1024]{1,0:T(8,128)(2,1)S(1)}, bf16[128,1024]{1,0:T(8,128)(2,1)S(1)}, u32[]{:S(2)}, u32[]{:S(2)}) collective-permute-start(bf16[128,1024]{1,0:T(8,128)(2,1)S(1)} %collective-permute-done.8.refs_0_), channel_id=1, source_target_pairs={{0,16},{16,0},{1,17},{17,1},{2,18},{18,2},{3,19},{19,3},{4,20},{20... | collective-permute-start | bytes 786440 | tf_op jit(solution)/shard_map/ppermute | solution.py:213
  48.3 9.2 %collective-permute-start.15 = (bf16[128,1024]{1,0:T(8,128)(2,1)S(1)}, bf16[128,1024]{1,0:T(8,128)(2,1)S(1)}, u32[]{:S(2)}, u32[]{:S(2)}) collective-permute-start(bf16[128,1024]{1,0:T(8,128)(2,1)S(1)} %get-tuple-element.42.refs_5_), channel_id=1, source_target_pairs={{0,2},{2,0},{4,6},{6,4},{8,10},{10,8},{12,14},{14,12},{1,3},{3,1},... | collective-permute-start | bytes 786440 | tf_op jit(solution)/shard_map/ppermute | solution.py:216
  50.0 8.4 %collective-permute-start.14 = (bf16[128,1024]{1,0:T(8,128)(2,1)S(1)}, bf16[128,1024]{1,0:T(8,128)(2,1)S(1)}, u32[]{:S(2)}, u32[]{:S(2)}) collective-permute-start(bf16[128,1024]{1,0:T(8,128)(2,1)S(1)} %get-tuple-element.45), channel_id=1, source_target_pairs={{0,4},{2,6},{4,8},{6,10},{8,12},{10,14},{12,0},{14,2},{1,5},{3,7},... | collective-permute-start | bytes 786440 | tf_op jit(solution)/shard_map/ppermute | solution.py:218
  55.2 6.4 %collective-permute-start.13 = (bf16[128,1024]{1,0:T(8,128)(2,1)S(1)}, bf16[128,1024]{1,0:T(8,128)(2,1)S(1)}, u32[]{:S(2)}, u32[]{:S(2)}) collective-permute-start(bf16[128,1024]{1,0:T(8,128)(2,1)S(1)} %collective-permute-done.6.refs_0_), channel_id=1, source_target_pairs={{0,16},{16,0},{1,17},{17,1},{2,18},{18,2},{3,19},{19,3},{4,20},{20... | collective-permute-start | bytes 786440 | tf_op jit(solution)/shard_map/ppermute | solution.py:213
  55.3 6.4 %collective-permute-start.12 = (bf16[128,1024]{1,0:T(8,128)(2,1)S(1)}, bf16[128,1024]{1,0:T(8,128)(2,1)S(1)}, u32[]{:S(2)}, u32[]{:S(2)}) collective-permute-start(bf16[128,1024]{1,0:T(8,128)(2,1)S(1)} %shard_map.55.refs_5_), channel_id=1, source_target_pairs={{0,2},{2,0},{4,6},{6,4},{8,10},{10,8},{12,14},{14,12},{1,3},{3,1},... | collective-permute-start | bytes 786440 | tf_op jit(solution)/shard_map/ppermute | solution.py:216
  56.5 1.8 %collective-permute-start.11 = (f32[320,128]{1,0:T(8,128)S(1)}, f32[320,128]{1,0:T(8,128)S(1)}, u32[]{:S(2)}, u32[]{:S(2)}) collective-permute-start(f32[320,128]{1,0:T(8,128)S(1)} %get-tuple-element.43), channel_id=1, source_target_pairs={{0,1},{1,0},{2,3},{3,2},{4,5},{5,4},{6,7},{7,6},{8,9},{9,8},{10,11... | collective-permute-start | bytes 491528 | tf_op jit(solution)/shard_map/ppermute | solution.py:272
  62.3 1.7 %collective-permute-start.17 = (f32[320,256]{1,0:T(8,128)S(1)}, f32[320,256]{1,0:T(8,128)S(1)}, u32[]{:S(2)}, u32[]{:S(2)}) collective-permute-start(f32[320,256]{1,0:T(8,128)S(1)} %shard_map.57.refs_5_), channel_id=1, source_target_pairs={{0,1},{1,0},{2,3},{3,2},{4,5},{5,4},{6,7},{7,6},{8,9},{9,8},{10,11... | collective-permute-start | bytes 983048 | tf_op jit(solution)/shard_map/ppermute | solution.py:275

commit v4 on v0

v4 whole, which is shorter than its diff:
```python
import functools
import math

import jax
import jax.numpy as jnp
from jax import lax
from jax.experimental import pallas as pl
from jax.experimental.pallas import tpu as pltpu
from jax.sharding import PartitionSpec as P

L_DIM = 8192
SIZES = (12, 12, 8, 8, 12, 12)
CHUNKS = len(SIZES)
DIRECT = 5
OWN_MIB = (44, 40)
VMEM = pl.BlockSpec(memory_space=pltpu.VMEM)
SMEM = pl.BlockSpec(memory_space=pltpu.SMEM)
HBM = pl.BlockSpec(memory_space=pltpu.HBM)
ANY = pl.BlockSpec(memory_space=pl.ANY)
COST = pl.CostEstimate(flops=2 * 10**9, bytes_accessed=0, transcendentals=0)
MIB = 1024 * 1024


def width_of(k, dims):
    return SIZES[k] * dims // sum(SIZES)


def columns_of(k, dims, within=None):
    unit = dims // sum(SIZES)
    left, right = sum(SIZES[:k]), sum(SIZES[k + 1 :])
    if within:
        left, right = left % (sum(SIZES) // 2), right % (sum(SIZES) // 2)
    start = jnp.where(lax.axis_index("groups") == 0, left * unit, right * unit)
    return pl.ds(pl.multiple_of(start, unit), width_of(k, dims))


def half_columns(part, dims):
    group = lax.axis_index("groups")
    side = group if part == 0 else 1 - group
    return pl.ds(pl.multiple_of(side * (dims // 2), dims // 2), dims // 2)


def products(rows, block):
    return lax.dot_general(
        rows, block, (((1,), (1,)), ((), ())), preferred_element_type=jnp.float32
    )


def scale_of(factor, counts, half, side):
    layer = lax.axis_index("layer")
    start = (layer if side else 1 - layer) * half
    index = start + lax.broadcasted_iota(jnp.int32, (half, 1), 0)
    return factor * (index < counts[0]).astype(jnp.float32)


def chunk_kernel(ks, queries, *refs):
    outs, sem = refs[-len(ks) - 1 : -1], refs[-1]
    dims = queries.shape[1]
    copies = [
        pltpu.make_async_copy(queries.at[:, columns_of(k, dims)], outs[i], sem.at[i])
        for i, k in enumerate(ks)
    ]
    for copy in copies:
        copy.start()
    for copy in copies:
        copy.wait()


def step_kernel(k, queries, received, *refs):
    out, sem = refs[-2:]
    even = lax.axis_index("dp") % 2 == 0
    own_copy = pltpu.make_async_copy(queries.at[:, columns_of(k, queries.shape[1])], out, sem)
    received_copy = pltpu.make_async_copy(received, out, sem)

    @pl.when(even)
    def _():
        own_copy.start()
        own_copy.wait()

    @pl.when(jnp.logical_not(even))
    def _():
        received_copy.start()
        received_copy.wait()


def own_kernel(part, pieces, documents, queries, *refs):
    if part == 0:
        eigenvalues, sums, held, inverse, sem = refs[0], *refs[-4:]
    else:
        inverse, before, sums, held, sem = refs[0], refs[1], *refs[-3:]
    layer = lax.axis_index("layer")
    half = documents.shape[0] // 2
    dims = documents.shape[1]
    width = dims // 2 // pieces
    first = half_columns(part, dims).start
    copies = []
    for i in range(pieces):
        start = pl.multiple_of(first + i * width, width)
        for at, row in enumerate((1 - layer, layer)):
            copies.append(
                pltpu.make_async_copy(
                    documents.at[pl.ds(pl.multiple_of(row * half, half), half), pl.ds(start, width)],
                    held.at[pl.ds(at * half, half), pl.ds(i * width, width)],
                    sem.at[i, at],
                )
            )
    for copy in copies:
        copy.start()
    if part == 0:
        for start in range(0, dims, L_DIM):
            block = eigenvalues[:, start : start + L_DIM]
            damping = 0.1 * jnp.mean(block, axis=1, keepdims=True)
            inverse[:, start : start + L_DIM] = 1.0 / (block + damping)
    for i in range(pieces):
        columns = pl.ds(pl.multiple_of(first + i * width, width), width)
        scaled = (queries[:, columns].astype(jnp.float32) * inverse[:, columns]).astype(jnp.bfloat16)
        copies[2 * i].wait()
        copies[2 * i + 1].wait()
        term = products(held[:, i * width : (i + 1) * width], scaled)
        if i > 0:
            sums[...] += term
        elif part == 0:
            sums[...] = term
        else:
            sums[...] = before[...] + term


def held_of(k, held):
    return held[0] if k < CHUNKS // 2 else held[1]


def add_pairs(ks, fresh, held, inverse, chunks, sums, out, block_buf):
    dims = inverse.shape[1]
    rows = chunks[0].shape[0]
    for i, k in enumerate(ks):
        width = width_of(k, dims)
        for b in range(2):
            scaled = chunks[2 * i + b][...].astype(jnp.float32) * inverse[:, columns_of(k, dims)]
            block_buf[pl.ds(b * rows, rows), :width] = scaled.astype(jnp.bfloat16)
        term = products(held_of(k, held)[:, columns_of(k, dims, True)], block_buf[:, :width])
        if i > 0:
            out[...] += term
        elif fresh:
            out[...] = term
        else:
            out[...] = sums[...] + term


def one_product(k, rows, held, inverse, chunk):
    dims = inverse.shape[1]
    scaled = chunk[...].astype(jnp.float32) * inverse[:, columns_of(k, dims)]
    return products(held_of(k, held)[rows, columns_of(k, dims, True)], scaled.astype(jnp.bfloat16))


def pair_kernel(ks, fresh, held0, held1, inverse, *refs):
    chunks = refs[: 2 * len(ks)]
    add_pairs(ks, fresh, (held0, held1), inverse, chunks, refs[2 * len(ks)], refs[-2], refs[-1])


def far_kernel(ks, k, factor, counts, held0, held1, inverse, *refs):
    held = held0, held1
    count = 2 * len(ks)
    chunks, (last, sums, own), (near, theirs, mine, total, block_buf) = (
        refs[:count],
        refs[count : count + 3],
        refs[count + 3 :],
    )
    rows = last.shape[0]
    half = mine.shape[0]
    add_pairs(ks, False, held, inverse, chunks, sums, total, block_buf)
    near[...] = total[:, :rows]
    far = total[:, rows:] + one_product(k, slice(None), held, inverse, last)
    for side, out in enumerate((theirs, mine)):
        scale = scale_of(factor, counts, half, side)
        out[:, :rows] = own[side * half : (side + 1) * half] * scale
        out[:, rows:] = far[side * half : (side + 1) * half] * scale


def near_kernel(k, side, factor, counts, held0, held1, inverse, last, near, *refs):
    out = refs[-1]
    half = out.shape[0]
    rows = slice(side * half, (side + 1) * half)
    total = near[rows] + one_product(k, rows, (held0, held1), inverse, last)
    out[...] = total * scale_of(factor, counts, half, side)


def final_kernel(mine, got, mine_near, got_near, out):
    rows = mine_near.shape[1]
    out[:, :rows] = mine[:, :rows] + got[:, :rows]
    out[:, rows : 2 * rows] = mine_near[...] + got_near[...]
    out[:, 2 * rows :] = mine[:, rows:] + got[:, rows:]


def on_device(queries, documents, counts, eigenvalues):
    rows, dims = queries.shape
    doc_rows = documents.shape[0]
    half = doc_rows // 2
    owners = lax.axis_size("dp")
    factor = 1.0 / math.sqrt(dims * lax.axis_size("layer"))
    ahead = [(i, (i + 2) % owners) for i in range(owners)]
    pair = [(i, i ^ 1) for i in range(owners)]
    across = [(0, 1), (1, 0)]

    def chunk(k):
        return jax.ShapeDtypeStruct((rows, width_of(k, dims)), queries.dtype)

    def floats(*shape):
        return jax.ShapeDtypeStruct(shape, jnp.float32)

    def call(kernel, out_shape, in_specs, out_specs, scratch, vmem_mib=16, **options):
        return pl.pallas_call(
            kernel,
            out_shape=out_shape,
            in_specs=in_specs,
            out_specs=out_specs,
            scratch_shapes=scratch,
            compiler_params=pltpu.CompilerParams(vmem_limit_bytes=vmem_mib * MIB),
            cost_estimate=COST,
            **options,
        )

    def own_chunks(*ks, until=(), space=ANY, vmem_mib=16):
        return call(
            functools.partial(chunk_kernel, ks),
            [chunk(k) for k in ks],
            [ANY] * (1 + len(until)),
            [space] * len(ks),
            [pltpu.SemaphoreType.DMA((len(ks),))],
            vmem_mib,
        )(queries, *until)

    def step(k, *until):
        out = call(
            functools.partial(step_kernel, k),
            chunk(k),
            [ANY] * (2 + len(until)),
            ANY,
            [pltpu.SemaphoreType.DMA],
        )(queries, far[k], *until)
        near[k] = lax.ppermute(out, "dp", pair)
        return out

    def send_ahead(k, *until):
        (sent,) = own_chunks(k, until=until)
        far[k] = lax.ppermute(sent, "dp", ahead)
        return sent

    def pair_scores(*ks, sums=None, until=()):
        operands = [*held, inverse] + [block[k] for k in ks for block in (near, far)]
        if sums is not None:
            operands.append(sums)
        return call(
            functools.partial(pair_kernel, ks, sums is None),
            floats(doc_rows, 2 * rows),
            [VMEM] * len(operands) + [ANY] * len(until),
            VMEM,
            [pltpu.VMEM((2 * rows, max(width_of(k, dims) for k in ks)), queries.dtype)],
        )(*operands, *until)

    def send_across(block, k, *until):
        sent = lax.optimization_barrier((block[k], *until))[0]
        block[CHUNKS - 1 - k] = lax.ppermute(sent, "groups", across)

    far = [None] * CHUNKS
    near = [None] * CHUNKS

    sent = own_chunks(0, 1, space=VMEM, vmem_mib=59)
    for k in range(2):
        far[k] = lax.ppermute(sent[k], "dp", ahead)

    def own_scores(part, *operands, until=()):
        pieces = 4
        outs = [
            floats(doc_rows, rows),
            jax.ShapeDtypeStruct((doc_rows, dims // 2), documents.dtype),
            floats(1, dims),
        ][: 3 - part]
        return call(
            functools.partial(own_kernel, part, pieces),
            outs,
            [HBM] + [VMEM] * (1 + len(operands)) + [ANY] * len(until),
            [VMEM] * len(outs),
            [pltpu.SemaphoreType.DMA((pieces, 2))],
            vmem_mib=OWN_MIB[part],
        )(documents, queries, *operands, *until)

    kept = lax.optimization_barrier((eigenvalues, sent[1]))[0].reshape(1, dims)
    own_sums, held0, inverse = own_scores(0, kept)

    out = step(0, inverse)
    out = send_ahead(2, out)
    send_across(far, 0, out)
    own_sums, held1 = own_scores(1, inverse, own_sums, until=(out,))
    held = held0, held1

    out = step(1, own_sums)
    out = send_ahead(3, out)
    send_across(near, 0, out)
    sums = pair_scores(0, until=(out, far[5]))

    out = step(2, sums)
    out = send_ahead(4, out)
    send_across(near, 1, out)
    sums = pair_scores(1, sums=sums, until=(out,))

    out = step(3, sums)
    sums = pair_scores(2, 5, sums=sums, until=(out,))

    operands = [counts, *held, inverse, near[4], far[4], far[3], sums, own_sums]
    near_sums, theirs, mine = call(
        functools.partial(far_kernel, (4,), 3, factor),
        [floats(doc_rows, rows), floats(half, 2 * rows), floats(half, 2 * rows)],
        [SMEM] + [VMEM] * (len(operands) - 1),
        [VMEM] * 3,
        [
            pltpu.VMEM((doc_rows, 2 * rows), jnp.float32),
            pltpu.VMEM((2 * rows, width_of(4, dims)), queries.dtype),
        ],
    )(*operands)
    got = lax.ppermute(theirs, "layer", across)

    def near_scores(side, until):
        return call(
            functools.partial(near_kernel, 3, side, factor),
            floats(half, rows),
            [SMEM] + [VMEM] * 5 + [ANY],
            VMEM,
            [],
        )(counts, *held, inverse, near[3], near_sums, until)

    theirs_near = near_scores(0, theirs)
    got_near = lax.ppermute(theirs_near, "layer", across)
    mine_near = near_scores(1, theirs_near)
    return call(final_kernel, floats(half, 3 * rows), [VMEM] * 4, VMEM, [])(
        mine, got, mine_near, got_near
    )


def solution(mesh):
    return jax.shard_map(
        on_device,
        mesh=mesh,
        in_specs=(P("dp", "layer"), P(("groups", "dp"), "layer"), P(("groups", "dp")), P("layer")),
        out_specs=P(("groups", "dp", "layer"), None),
        check_vma=False,
    )
```

time: 136 us -> 49.9 us (0.37)
  waiting for transfers between devices: 83.8 us -> 14.6 us
  matrix products: 22.7 us -> 0 us
  Pallas kernels: 0 us -> 16.7 us
  starting transfers between devices: 3.11 us -> 17.7 us
  between operations: 14.5 us -> 0.83 us
  local copies, waits for them, and re-layouts: 6.84 us -> 0.01 us
  other arithmetic: 4.18 us -> 0 us
    ppermute x2 -> x14, waiting for transfers between devices: 80.9 us -> 14.6 us  [the longest x4 6.2 us: step(): near[k] = lax.ppermute(out, 'dp', pair)]
    dot_general x3 -> x0, matrix products: 22.7 us -> none  [block_scores(): lax.dot_general(doc_rows, block, (((1,), (1,)), ((), ())), preferred_elem...]
    pallas_call x0 -> x17, Pallas kernels: none -> 16.7 us  [the longest x2 9.12 us: own_scores(): call(functools.partial(own_kernel, part, pieces), outs, [HBM] + [VMEM] *...]
    ppermute x2 -> x14, starting transfers between devices: 3.02 us -> 17.7 us  [the longest x4 7.92 us: step(): near[k] = lax.ppermute(out, 'dp', pair)]
    unnamed x6 -> x4, local copies, waits for them, and re-layouts: 5.85 us -> 0.01 us
    unnamed x6 -> x0, waiting for transfers between devices: 2.9 us -> none
    convert_element_type x1 -> x0, other arithmetic: 1.99 us -> none  [on_device(): precond = (queries.astype(jnp.float32) * inverse).astype(jnp.bfloat16)]
    reduce_sum x1 -> x0, other arithmetic: 1.37 us -> none  [on_device(): damping = 0.1 * jnp.mean(blocks, axis=1, keepdims=True)]
  transfers between devices with their start and end apart: 5 -> 14, of which waited for: 3 -> 7; matrix products, arithmetic and copies ran while one was open for 20% -> 0% of each run, Pallas kernels for 0% -> 27%
where the time goes in v4:
time: 49.9 us; the launch traced here: 49.8 us
  starting transfers between devices  17.7 us (35%)
  Pallas kernels  16.7 us (33%)
  waiting for transfers between devices  14.6 us (29%)
  between operations  0.83 us (2%)
    pallas_call x2, Pallas kernels, own_scores(): call(functools.partial(own_kernel, part, pieces), outs, [HBM] + [VMEM] *...  9.12 us
    ppermute x4, starting transfers between devices, step(): near[k] = lax.ppermute(out, 'dp', pair)  7.92 us
    ppermute x4, waiting for transfers between devices, step(): near[k] = lax.ppermute(out, 'dp', pair)  6.2 us
    ppermute x2, waiting for transfers between devices, on_device(): far[k] = lax.ppermute(sent[k], 'dp', ahead)  5.52 us
    ppermute x2, starting transfers between devices, on_device(): far[k] = lax.ppermute(sent[k], 'dp', ahead)  4.66 us
    ppermute x3, starting transfers between devices, send_across(): block[CHUNKS - 1 - k] = lax.ppermute(sent, 'groups', across)  4.45 us
    pallas_call x3, Pallas kernels, pair_scores(): call(functools.partial(pair_kernel, ks, sums is None), floats(doc_rows, 2...  2.51 us
    pallas_call x4, Pallas kernels, own_chunks(): call(functools.partial(chunk_kernel, ks), [chunk(k) for k in ks], [ANY] *...  2.29 us
  transfers between devices with their start and end apart: 14, of which 7 were waited for; matrix products, arithmetic and copies ran while one was open for 0% of the time, Pallas kernels for 27%

profile of v4, /device:TPU:0, one launch (start us, length us, event | category | flops | bytes accessed | tf_op | source)
XLA Modules:
  0.0 49.8 jit_solution(8060188227541963927)
XLA Ops:
  0.0 0.0 copy-start
  0.0 0.0 copy-start.1
  0.0 2.2 %shard_map.46 = (bf16[128,1536]{1,0:T(8,128)(2,1)}, bf16[128,1536]{1,0:T(8,128)(2,1)}) custom-call(bf16[128,8192]{1,0:T(8,128)(2,1)} %queries.19), custom_call_target="tpu_custom_call" | custom-call | flops 2000000000 | tf_op jit(solution)/shard_map/pallas_call | solution.py:223
  2.2 3.1 %collective-permute-start = (bf16[128,1536]{1,0:T(8,128)(2,1)}, bf16[128,1536]{1,0:T(8,128)(2,1)S(1)}, u32[]{:S(2)}, u32[]{:S(2)}) collective-permute-start(bf16[128,1536]{1,0:T(8,128)(2,1)} %get-tuple-element.24), channel_id=1, source_target_pairs={{0,4},{2,6},{4,8},{6,10},{8,12},{10,14},{12,0},{14,2},{1,5},{3,7},... | collective-permute-start | bytes 1179656 | tf_op jit(solution)/shard_map/ppermute | solution.py:269
  5.2 1.6 %collective-permute-start.1 = (bf16[128,1536]{1,0:T(8,128)(2,1)}, bf16[128,1536]{1,0:T(8,128)(2,1)S(1)}, u32[]{:S(2)}, u32[]{:S(2)}) collective-permute-start(bf16[128,1536]{1,0:T(8,128)(2,1)} %get-tuple-element.19), channel_id=1, source_target_pairs={{0,4},{2,6},{4,8},{6,10},{8,12},{10,14},{12,0},{14,2},{1,5},{3,7},... | collective-permute-start | bytes 1179656 | tf_op jit(solution)/shard_map/ppermute | solution.py:269
  7.5 0.0 copy-done
  7.5 0.0 copy-done.1
  7.5 4.6 %shard_map.47 = (f32[640,128]{1,0:T(8,128)S(1)}, bf16[640,4096]{1,0:T(8,128)(2,1)S(1)}, f32[1,8192]{1,0:T(1,128)S(1)}) custom-call(bf16[640,8192]{1,0:T(8,128)(2,1)} %documents.3, bf16[128,8192]{1,0:T(8,128)(2,1)S(1)} %copy-done, f32[1,8192]{1,0:T(1,128)S(1)} %bitcast.1), custom_call_target="tpu_custom_call" | custom-call | flops 2000000000 | tf_op jit(solution)/shard_map/pallas_call | solution.py:278
  12.1 5.4 %collective-permute-done.received.refs_1_ = bf16[128,1536]{1,0:T(8,128)(2,1)S(1)} collective-permute-done((bf16[128,1536]{1,0:T(8,128)(2,1)}, bf16[128,1536]{1,0:T(8,128)(2,1)S(1)}, u32[]{:S(2)}, u32[]{:S(2)}) %collective-permute-start) | collective-permute-done | bytes 393248 | tf_op jit(solution)/shard_map/ppermute | solution.py:269
  17.5 2.0 %collective-permute-start.4 = (bf16[128,1536]{1,0:T(8,128)(2,1)S(1)}, bf16[128,1536]{1,0:T(8,128)(2,1)S(1)}, u32[]{:S(2)}, u32[]{:S(2)}) collective-permute-start(bf16[128,1536]{1,0:T(8,128)(2,1)S(1)} %shard_map.48.refs_0_), channel_id=1, source_target_pairs={{0,2},{2,0},{4,6},{6,4},{8,10},{10,8},{12,14},{14,12},{1,3},{3,1},... | collective-permute-start | bytes 1179656 | tf_op jit(solution)/shard_map/ppermute | solution.py:240
  19.5 0.1 collective-permute-start.3
  19.6 1.6 %collective-permute-start.5 = (bf16[128,1536]{1,0:T(8,128)(2,1)S(1)}, bf16[128,1536]{1,0:T(8,128)(2,1)S(1)}, u32[]{:S(2)}, u32[]{:S(2)}) collective-permute-start(bf16[128,1536]{1,0:T(8,128)(2,1)S(1)} %collective-permute-done.received.refs_1_), channel_id=1, source_target_pairs={{0,16},{16,0},{1,17},{17,1},{2,18},{18,2},{3,19},{19,3},{4,20},{20... | collective-permute-start | bytes 1179656 | tf_op jit(solution)/shard_map/ppermute | solution.py:262
  21.1 4.6 %shard_map.50 = (f32[640,128]{1,0:T(8,128)S(1)}, bf16[640,4096]{1,0:T(8,128)(2,1)S(1)}) custom-call(bf16[640,8192]{1,0:T(8,128)(2,1)} %documents.3, bf16[128,8192]{1,0:T(8,128)(2,1)S(1)} %copy-done, f32[1,8192]{1,0:T(1,128)S(1)} %get-tuple-element.22.refs_0_.inverse, f32[640,128]{1,0:T(8,128)S(1)} %get-tuple-element.23.refs_1_, ...), custom_call_target="tpu_custom_call" | custom-call | flops 2000000000 | tf_op jit(solution)/shard_map/pallas_call | solution.py:278
  25.7 0.2 collective-permute-done.1.received.refs_1_
  26.0 2.0 %collective-permute-start.2 = (bf16[128,1536]{1,0:T(8,128)(2,1)S(1)}, bf16[128,1536]{1,0:T(8,128)(2,1)S(1)}, u32[]{:S(2)}, u32[]{:S(2)}) collective-permute-start(bf16[128,1536]{1,0:T(8,128)(2,1)S(1)} %shard_map.51.refs_0_), channel_id=1, source_target_pairs={{0,2},{2,0},{4,6},{6,4},{8,10},{10,8},{12,14},{14,12},{1,3},{3,1},... | collective-permute-start | bytes 1179656 | tf_op jit(solution)/shard_map/ppermute | solution.py:240
  27.9 0.0 collective-permute-start.8
  27.9 0.0 collective-permute-done.4.refs_0_
  27.9 1.5 %collective-permute-start.10 = (bf16[128,1536]{1,0:T(8,128)(2,1)S(1)}, bf16[128,1536]{1,0:T(8,128)(2,1)S(1)}, u32[]{:S(2)}, u32[]{:S(2)}) collective-permute-start(bf16[128,1536]{1,0:T(8,128)(2,1)S(1)} %collective-permute-done.4.refs_0_), channel_id=1, source_target_pairs={{0,16},{16,0},{1,17},{17,1},{2,18},{18,2},{3,19},{19,3},{4,20},{20... | collective-permute-start | bytes 1179656 | tf_op jit(solution)/shard_map/ppermute | solution.py:262
  29.4 0.0 collective-permute-done.5.refs_3_
  29.4 0.7 %shard_map.53.refs_0_.refs_2_ = f32[640,256]{1,0:T(8,128)S(1)} custom-call(bf16[640,4096]{1,0:T(8,128)(2,1)S(1)} %get-tuple-element.21.held0, bf16[640,4096]{1,0:T(8,128)(2,1)S(1)} %get-tuple-element.25.held1, f32[1,8192]{1,0:T(1,128)S(1)} %get-tuple-element.22.refs_0_.inverse, bf16[128,1536]{1,0:T(8,128)(2,1)S(1)} %collective-permute-done.4.refs_0_, ...), custom_call_target="tpu_custom_call" | custom-call | flops 2000000000 | tf_op jit(solution)/shard_map/pallas_call | solution.py:252
  30.2 1.0 %collective-permute-done.3.received.refs_1_ = bf16[128,1024]{1,0:T(8,128)(2,1)S(1)} collective-permute-done((bf16[128,1024]{1,0:T(8,128)(2,1)S(1)}, bf16[128,1024]{1,0:T(8,128)(2,1)S(1)}, u32[]{:S(2)}, u32[]{:S(2)}) %collective-permute-start.3) | collective-permute-done | bytes 262176 | tf_op jit(solution)/shard_map/ppermute | solution.py:245
  31.2 0.1 shard_map.55.refs_3_
  31.3 2.1 %collective-permute-start.9 = (bf16[128,1024]{1,0:T(8,128)(2,1)S(1)}, bf16[128,1024]{1,0:T(8,128)(2,1)S(1)}, u32[]{:S(2)}, u32[]{:S(2)}) collective-permute-start(bf16[128,1024]{1,0:T(8,128)(2,1)S(1)} %shard_map.54.refs_0_), channel_id=1, source_target_pairs={{0,2},{2,0},{4,6},{6,4},{8,10},{10,8},{12,14},{14,12},{1,3},{3,1},... | collective-permute-start | bytes 786440 | tf_op jit(solution)/shard_map/ppermute | solution.py:240
  33.4 0.0 collective-permute-start.7
  33.4 4.7 %collective-permute-done.2.refs_0_ = bf16[128,1536]{1,0:T(8,128)(2,1)S(1)} collective-permute-done((bf16[128,1536]{1,0:T(8,128)(2,1)S(1)}, bf16[128,1536]{1,0:T(8,128)(2,1)S(1)}, u32[]{:S(2)}, u32[]{:S(2)}) %collective-permute-start.2) | collective-permute-done | bytes 393248 | tf_op jit(solution)/shard_map/ppermute | solution.py:240
  38.1 1.4 %collective-permute-start.6 = (bf16[128,1536]{1,0:T(8,128)(2,1)S(1)}, bf16[128,1536]{1,0:T(8,128)(2,1)S(1)}, u32[]{:S(2)}, u32[]{:S(2)}) collective-permute-start(bf16[128,1536]{1,0:T(8,128)(2,1)S(1)} %collective-permute-done.2.refs_0_), channel_id=1, source_target_pairs={{0,16},{16,0},{1,17},{17,1},{2,18},{18,2},{3,19},{19,3},{4,20},{20... | collective-permute-start | bytes 1179656 | tf_op jit(solution)/shard_map/ppermute | solution.py:262
  39.5 0.7 %shard_map.56.refs_0_.refs_4_ = f32[640,256]{1,0:T(8,128)S(1)} custom-call(bf16[640,4096]{1,0:T(8,128)(2,1)S(1)} %get-tuple-element.21.held0, bf16[640,4096]{1,0:T(8,128)(2,1)S(1)} %get-tuple-element.25.held1, f32[1,8192]{1,0:T(1,128)S(1)} %get-tuple-element.22.refs_0_.inverse, bf16[128,1536]{1,0:T(8,128)(2,1)S(1)} %collective-permute-done.2.refs_0_, ...), custom_call_target="tpu_custom_call" | custom-call | flops 2000000000 | tf_op jit(solution)/shard_map/pallas_call | solution.py:252
  40.2 0.0 collective-permute-done.8.received.refs_2_
  40.2 0.1 shard_map.57.refs_5_
  40.3 1.9 %collective-permute-start.12 = (bf16[128,1024]{1,0:T(8,128)(2,1)S(1)}, bf16[128,1024]{1,0:T(8,128)(2,1)S(1)}, u32[]{:S(2)}, u32[]{:S(2)}) collective-permute-start(bf16[128,1024]{1,0:T(8,128)(2,1)S(1)} %shard_map.57.refs_5_), channel_id=1, source_target_pairs={{0,2},{2,0},{4,6},{6,4},{8,10},{10,8},{12,14},{14,12},{1,3},{3,1},... | collective-permute-start | bytes 786440 | tf_op jit(solution)/shard_map/ppermute | solution.py:240
  42.2 1.5 %collective-permute-done.9.refs_0_ = bf16[128,1024]{1,0:T(8,128)(2,1)S(1)} collective-permute-done((bf16[128,1024]{1,0:T(8,128)(2,1)S(1)}, bf16[128,1024]{1,0:T(8,128)(2,1)S(1)}, u32[]{:S(2)}, u32[]{:S(2)}) %collective-permute-start.9) | collective-permute-done | bytes 262176 | tf_op jit(solution)/shard_map/ppermute | solution.py:240
  43.7 0.0 collective-permute-done.10.refs_2_
  43.7 1.1 %shard_map.58.refs_3_ = f32[640,256]{1,0:T(8,128)S(1)} custom-call(bf16[640,4096]{1,0:T(8,128)(2,1)S(1)} %get-tuple-element.21.held0, bf16[640,4096]{1,0:T(8,128)(2,1)S(1)} %get-tuple-element.25.held1, f32[1,8192]{1,0:T(1,128)S(1)} %get-tuple-element.22.refs_0_.inverse, bf16[128,1024]{1,0:T(8,128)(2,1)S(1)} %collective-permute-done.9.refs_0_, ...), custom_call_target="tpu_custom_call" | custom-call | flops 2000000000 | tf_op jit(solution)/shard_map/pallas_call | solution.py:252
  44.8 1.1 %collective-permute-done.6.refs_0_ = bf16[128,1536]{1,0:T(8,128)(2,1)S(1)} collective-permute-done((bf16[128,1536]{1,0:T(8,128)(2,1)S(1)}, bf16[128,1536]{1,0:T(8,128)(2,1)S(1)}, u32[]{:S(2)}, u32[]{:S(2)}) %collective-permute-start.6) | collective-permute-done | bytes 393248 | tf_op jit(solution)/shard_map/ppermute | solution.py:262
  45.9 0.0 collective-permute-done.7.refs_1_
  45.9 1.1 %shard_map.59 = (f32[640,128]{1,0:T(8,128)S(1)}, f32[320,256]{1,0:T(8,128)S(1)}, f32[320,256]{1,0:T(8,128)S(1)}) custom-call(s32[1]{0:T(128)S(6)} %copy.5.counts, bf16[640,4096]{1,0:T(8,128)(2,1)S(1)} %get-tuple-element.21.held0, bf16[640,4096]{1,0:T(8,128)(2,1)S(1)} %get-tuple-element.25.held1, f32[1,8192]{1,0:T(1,128)S(1)} %get-tuple-element.22.refs_0_.inverse, ...), custom_call_target="tpu_custom_call" | custom-call | flops 2000000000 | tf_op jit(solution)/shard_map/pallas_call | solution.py:310
  46.9 0.1 collective-permute-start.11
  47.0 0.0 collective-permute-done.12.last
  47.0 0.4 shard_map.60.refs_0_
  47.4 0.5 %collective-permute-start.13 = (f32[320,128]{1,0:T(8,128)S(1)}, f32[320,128]{1,0:T(8,128)S(1)}, u32[]{:S(2)}, u32[]{:S(2)}) collective-permute-start(f32[320,128]{1,0:T(8,128)S(1)} %shard_map.60.refs_0_), channel_id=1, source_target_pairs={{0,1},{1,0},{2,3},{3,2},{4,5},{5,4},{6,7},{7,6},{8,9},{9,8},{10,11... | collective-permute-start | bytes 491528 | tf_op jit(solution)/shard_map/ppermute | solution.py:332
  47.9 0.3 shard_map.61.mine_near
  48.3 0.7 %collective-permute-done.13.got_near = f32[320,128]{1,0:T(8,128)S(1)} collective-permute-done((f32[320,128]{1,0:T(8,128)S(1)}, f32[320,128]{1,0:T(8,128)S(1)}, u32[]{:S(2)}, u32[]{:S(2)}) %collective-permute-start.13) | collective-permute-done | bytes 163872 | tf_op jit(solution)/shard_map/ppermute | solution.py:332
  48.9 0.0 collective-permute-done.11.got
  48.9 0.8 %shard_map.62 = f32[320,384]{1,0:T(8,128)} custom-call(f32[320,256]{1,0:T(8,128)S(1)} %get-tuple-element.30.mine, f32[320,256]{1,0:T(8,128)S(1)} %collective-permute-done.11.got, f32[320,128]{1,0:T(8,128)S(1)} %shard_map.61.mine_near, f32[320,128]{1,0:T(8,128)S(1)} %collective-permute-done.13.got_near), custom_call_target="tpu_custom_call" | custom-call | flops 2000000000 | tf_op jit(solution)/shard_map/pallas_call | solution.py:334
  (5 shorter events, 0.2 us)
Async XLA Ops:
  0.0 7.5 %copy-start = (bf16[128,8192]{1,0:T(8,128)(2,1)S(1)}, bf16[128,8192]{1,0:T(8,128)(2,1)}, u32[]{:S(2)}) copy-start(bf16[128,8192]{1,0:T(8,128)(2,1)} %queries.19) | copy-start | bytes 6291460
  0.0 7.5 %copy-start.1 = (f32[8192]{0:T(1024)S(1)}, f32[8192]{0:T(1024)}, u32[]{:S(2)}) copy-start(f32[8192]{0:T(1024)} %param.7) | copy-start | bytes 98308
  2.2 15.3 %collective-permute-start = (bf16[128,1536]{1,0:T(8,128)(2,1)}, bf16[128,1536]{1,0:T(8,128)(2,1)S(1)}, u32[]{:S(2)}, u32[]{:S(2)}) collective-permute-start(bf16[128,1536]{1,0:T(8,128)(2,1)} %get-tuple-element.24), channel_id=1, source_target_pairs={{0,4},{2,6},{4,8},{6,10},{8,12},{10,14},{12,0},{14,2},{1,5},{3,7},... | collective-permute-start | bytes 1179656 | tf_op jit(solution)/shard_map/ppermute | solution.py:269
  5.2 20.6 %collective-permute-start.1 = (bf16[128,1536]{1,0:T(8,128)(2,1)}, bf16[128,1536]{1,0:T(8,128)(2,1)S(1)}, u32[]{:S(2)}, u32[]{:S(2)}) collective-permute-start(bf16[128,1536]{1,0:T(8,128)(2,1)} %get-tuple-element.19), channel_id=1, source_target_pairs={{0,4},{2,6},{4,8},{6,10},{8,12},{10,14},{12,0},{14,2},{1,5},{3,7},... | collective-permute-start | bytes 1179656 | tf_op jit(solution)/shard_map/ppermute | solution.py:269
  17.5 10.5 %collective-permute-start.4 = (bf16[128,1536]{1,0:T(8,128)(2,1)S(1)}, bf16[128,1536]{1,0:T(8,128)(2,1)S(1)}, u32[]{:S(2)}, u32[]{:S(2)}) collective-permute-start(bf16[128,1536]{1,0:T(8,128)(2,1)S(1)} %shard_map.48.refs_0_), channel_id=1, source_target_pairs={{0,2},{2,0},{4,6},{6,4},{8,10},{10,8},{12,14},{14,12},{1,3},{3,1},... | collective-permute-start | bytes 1179656 | tf_op jit(solution)/shard_map/ppermute | solution.py:240
  19.5 11.7 %collective-permute-start.3 = (bf16[128,1024]{1,0:T(8,128)(2,1)S(1)}, bf16[128,1024]{1,0:T(8,128)(2,1)S(1)}, u32[]{:S(2)}, u32[]{:S(2)}) collective-permute-start(bf16[128,1024]{1,0:T(8,128)(2,1)S(1)} %shard_map.49.refs_2_), channel_id=1, source_target_pairs={{0,4},{2,6},{4,8},{6,10},{8,12},{10,14},{12,0},{14,2},{1,5},{3,7},... | collective-permute-start | bytes 786440 | tf_op jit(solution)/shard_map/ppermute | solution.py:245
  19.6 9.9 %collective-permute-start.5 = (bf16[128,1536]{1,0:T(8,128)(2,1)S(1)}, bf16[128,1536]{1,0:T(8,128)(2,1)S(1)}, u32[]{:S(2)}, u32[]{:S(2)}) collective-permute-start(bf16[128,1536]{1,0:T(8,128)(2,1)S(1)} %collective-permute-done.received.refs_1_), channel_id=1, source_target_pairs={{0,16},{16,0},{1,17},{17,1},{2,18},{18,2},{3,19},{19,3},{4,20},{20... | collective-permute-start | bytes 1179656 | tf_op jit(solution)/shard_map/ppermute | solution.py:262
  26.0 12.1 %collective-permute-start.2 = (bf16[128,1536]{1,0:T(8,128)(2,1)S(1)}, bf16[128,1536]{1,0:T(8,128)(2,1)S(1)}, u32[]{:S(2)}, u32[]{:S(2)}) collective-permute-start(bf16[128,1536]{1,0:T(8,128)(2,1)S(1)} %shard_map.51.refs_0_), channel_id=1, source_target_pairs={{0,2},{2,0},{4,6},{6,4},{8,10},{10,8},{12,14},{14,12},{1,3},{3,1},... | collective-permute-start | bytes 1179656 | tf_op jit(solution)/shard_map/ppermute | solution.py:240
  27.9 12.3 %collective-permute-start.8 = (bf16[128,1024]{1,0:T(8,128)(2,1)S(1)}, bf16[128,1024]{1,0:T(8,128)(2,1)S(1)}, u32[]{:S(2)}, u32[]{:S(2)}) collective-permute-start(bf16[128,1024]{1,0:T(8,128)(2,1)S(1)} %shard_map.52.refs_2_), channel_id=1, source_target_pairs={{0,4},{2,6},{4,8},{6,10},{8,12},{10,14},{12,0},{14,2},{1,5},{3,7},... | collective-permute-start | bytes 786440 | tf_op jit(solution)/shard_map/ppermute | solution.py:245
  27.9 15.8 %collective-permute-start.10 = (bf16[128,1536]{1,0:T(8,128)(2,1)S(1)}, bf16[128,1536]{1,0:T(8,128)(2,1)S(1)}, u32[]{:S(2)}, u32[]{:S(2)}) collective-permute-start(bf16[128,1536]{1,0:T(8,128)(2,1)S(1)} %collective-permute-done.4.refs_0_), channel_id=1, source_target_pairs={{0,16},{16,0},{1,17},{17,1},{2,18},{18,2},{3,19},{19,3},{4,20},{20... | collective-permute-start | bytes 1179656 | tf_op jit(solution)/shard_map/ppermute | solution.py:262
  31.3 12.4 %collective-permute-start.9 = (bf16[128,1024]{1,0:T(8,128)(2,1)S(1)}, bf16[128,1024]{1,0:T(8,128)(2,1)S(1)}, u32[]{:S(2)}, u32[]{:S(2)}) collective-permute-start(bf16[128,1024]{1,0:T(8,128)(2,1)S(1)} %shard_map.54.refs_0_), channel_id=1, source_target_pairs={{0,2},{2,0},{4,6},{6,4},{8,10},{10,8},{12,14},{14,12},{1,3},{3,1},... | collective-permute-start | bytes 786440 | tf_op jit(solution)/shard_map/ppermute | solution.py:240
  33.4 12.4 %collective-permute-start.7 = (bf16[128,1536]{1,0:T(8,128)(2,1)S(1)}, bf16[128,1536]{1,0:T(8,128)(2,1)S(1)}, u32[]{:S(2)}, u32[]{:S(2)}) collective-permute-start(bf16[128,1536]{1,0:T(8,128)(2,1)S(1)} %shard_map.55.refs_3_), channel_id=1, source_target_pairs={{0,4},{2,6},{4,8},{6,10},{8,12},{10,14},{12,0},{14,2},{1,5},{3,7},... | collective-permute-start | bytes 1179656 | tf_op jit(solution)/shard_map/ppermute | solution.py:245
  38.1 7.8 %collective-permute-start.6 = (bf16[128,1536]{1,0:T(8,128)(2,1)S(1)}, bf16[128,1536]{1,0:T(8,128)(2,1)S(1)}, u32[]{:S(2)}, u32[]{:S(2)}) collective-permute-start(bf16[128,1536]{1,0:T(8,128)(2,1)S(1)} %collective-permute-done.2.refs_0_), channel_id=1, source_target_pairs={{0,16},{16,0},{1,17},{17,1},{2,18},{18,2},{3,19},{19,3},{4,20},{20... | collective-permute-start | bytes 1179656 | tf_op jit(solution)/shard_map/ppermute | solution.py:262
  40.3 6.7 %collective-permute-start.12 = (bf16[128,1024]{1,0:T(8,128)(2,1)S(1)}, bf16[128,1024]{1,0:T(8,128)(2,1)S(1)}, u32[]{:S(2)}, u32[]{:S(2)}) collective-permute-start(bf16[128,1024]{1,0:T(8,128)(2,1)S(1)} %shard_map.57.refs_5_), channel_id=1, source_target_pairs={{0,2},{2,0},{4,6},{6,4},{8,10},{10,8},{12,14},{14,12},{1,3},{3,1},... | collective-permute-start | bytes 786440 | tf_op jit(solution)/shard_map/ppermute | solution.py:240
  46.9 2.0 %collective-permute-start.11 = (f32[320,256]{1,0:T(8,128)S(1)}, f32[320,256]{1,0:T(8,128)S(1)}, u32[]{:S(2)}, u32[]{:S(2)}) collective-permute-start(f32[320,256]{1,0:T(8,128)S(1)} %get-tuple-element.31.refs_0_), channel_id=1, source_target_pairs={{0,1},{1,0},{2,3},{3,2},{4,5},{5,4},{6,7},{7,6},{8,9},{9,8},{10,11... | collective-permute-start | bytes 983048 | tf_op jit(solution)/shard_map/ppermute | solution.py:320
  47.4 1.6 %collective-permute-start.13 = (f32[320,128]{1,0:T(8,128)S(1)}, f32[320,128]{1,0:T(8,128)S(1)}, u32[]{:S(2)}, u32[]{:S(2)}) collective-permute-start(f32[320,128]{1,0:T(8,128)S(1)} %shard_map.60.refs_0_), channel_id=1, source_target_pairs={{0,1},{1,0},{2,3},{3,2},{4,5},{5,4},{6,7},{7,6},{8,9},{9,8},{10,11... | collective-permute-start | bytes 491528 | tf_op jit(solution)/shard_map/ppermute | solution.py:332

commit v5 on v4

--- a/solution.py
+++ b/solution.py
@@ -17,7 +17,7 @@
 SMEM = pl.BlockSpec(memory_space=pltpu.SMEM)
 HBM = pl.BlockSpec(memory_space=pltpu.HBM)
 ANY = pl.BlockSpec(memory_space=pl.ANY)
-COST = pl.CostEstimate(flops=2 * 10**9, bytes_accessed=0, transcendentals=0)
+COST = pl.CostEstimate(flops=16 * 10**8, bytes_accessed=0, transcendentals=0)
 MIB = 1024 * 1024
 
 
@@ -83,11 +83,12 @@
         received_copy.wait()
 
 
-def own_kernel(part, pieces, documents, queries, *refs):
+def own_kernel(part, pieces, factor, counts, documents, queries, *refs):
     if part == 0:
-        eigenvalues, sums, held, inverse, sem = refs[0], *refs[-4:]
+        eigenvalues, theirs, mine, held, inverse, sem = refs[0], *refs[-5:]
+        before = None
     else:
-        inverse, before, sums, held, sem = refs[0], refs[1], *refs[-3:]
+        inverse, before, theirs, mine, held, sem = refs[0], refs[1:3], *refs[-4:]
     layer = lax.axis_index("layer")
     half = documents.shape[0] // 2
     dims = documents.shape[1]
@@ -114,81 +115,54 @@
     for i in range(pieces):
         columns = pl.ds(pl.multiple_of(first + i * width, width), width)
         scaled = (queries[:, columns].astype(jnp.float32) * inverse[:, columns]).astype(jnp.bfloat16)
-        copies[2 * i].wait()
-        copies[2 * i + 1].wait()
-        term = products(held[:, i * width : (i + 1) * width], scaled)
-        if i > 0:
-            sums[...] += term
-        elif part == 0:
-            sums[...] = term
-        else:
-            sums[...] = before[...] + term
+        for side, out in enumerate((theirs, mine)):
+            copies[2 * i + side].wait()
+            term = products(
+                held[side * half : (side + 1) * half, i * width : (i + 1) * width], scaled
+            )
+            if i > 0:
+                out[...] += term
+            elif part == 0:
+                out[...] = term
+            else:
+                out[...] = before[side][...] + term
+    if part == 1:
+        theirs[...] *= scale_of(factor, counts, half, 0)
+        mine[...] *= scale_of(factor, counts, half, 1)
 
 
 def held_of(k, held):
     return held[0] if k < CHUNKS // 2 else held[1]
 
 
-def add_pairs(ks, fresh, held, inverse, chunks, sums, out, block_buf):
+def pair_kernel(ks, side, factor, fresh, counts, held0, held1, inverse, *refs):
+    count = len(ks)
+    chunks, out, block_buf = refs[: 2 * count], refs[-2], refs[-1]
     dims = inverse.shape[1]
+    size = out.shape[0]
+    first = 0 if side is None else side * size
     rows = chunks[0].shape[0]
     for i, k in enumerate(ks):
         width = width_of(k, dims)
         for b in range(2):
             scaled = chunks[2 * i + b][...].astype(jnp.float32) * inverse[:, columns_of(k, dims)]
             block_buf[pl.ds(b * rows, rows), :width] = scaled.astype(jnp.bfloat16)
-        term = products(held_of(k, held)[:, columns_of(k, dims, True)], block_buf[:, :width])
+        held = held_of(k, (held0, held1))
+        term = products(held[first : first + size, columns_of(k, dims, True)], block_buf[:, :width])
         if i > 0:
             out[...] += term
         elif fresh:
             out[...] = term
         else:
-            out[...] = sums[...] + term
-
-
-def one_product(k, rows, held, inverse, chunk):
-    dims = inverse.shape[1]
-    scaled = chunk[...].astype(jnp.float32) * inverse[:, columns_of(k, dims)]
-    return products(held_of(k, held)[rows, columns_of(k, dims, True)], scaled.astype(jnp.bfloat16))
-
-
-def pair_kernel(ks, fresh, held0, held1, inverse, *refs):
-    chunks = refs[: 2 * len(ks)]
-    add_pairs(ks, fresh, (held0, held1), inverse, chunks, refs[2 * len(ks)], refs[-2], refs[-1])
-
-
-def far_kernel(ks, k, factor, counts, held0, held1, inverse, *refs):
-    held = held0, held1
-    count = 2 * len(ks)
-    chunks, (last, sums, own), (near, theirs, mine, total, block_buf) = (
-        refs[:count],
-        refs[count : count + 3],
-        refs[count + 3 :],
-    )
-    rows = last.shape[0]
-    half = mine.shape[0]
-    add_pairs(ks, False, held, inverse, chunks, sums, total, block_buf)
-    near[...] = total[:, :rows]
-    far = total[:, rows:] + one_product(k, slice(None), held, inverse, last)
-    for side, out in enumerate((theirs, mine)):
-        scale = scale_of(factor, counts, half, side)
-        out[:, :rows] = own[side * half : (side + 1) * half] * scale
-        out[:, rows:] = far[side * half : (side + 1) * half] * scale
-
-
-def near_kernel(k, side, factor, counts, held0, held1, inverse, last, near, *refs):
-    out = refs[-1]
-    half = out.shape[0]
-    rows = slice(side * half, (side + 1) * half)
-    total = near[rows] + one_product(k, rows, (held0, held1), inverse, last)
-    out[...] = total * scale_of(factor, counts, half, side)
-
-
-def final_kernel(mine, got, mine_near, got_near, out):
-    rows = mine_near.shape[1]
-    out[:, :rows] = mine[:, :rows] + got[:, :rows]
-    out[:, rows : 2 * rows] = mine_near[...] + got_near[...]
-    out[:, 2 * rows :] = mine[:, rows:] + got[:, rows:]
+            out[...] = refs[2 * count][first : first + size] + term
+    if side is not None:
+        out[...] *= scale_of(factor, counts, size, side)
+
+
+def final_kernel(mine0, got0, mine, got, out):
+    rows = mine0.shape[1]
+    out[:, :rows] = mine0[...] + got0[...]
+    out[:, rows:] = mine[...] + got[...]
 
 
 def on_device(queries, documents, counts, eigenvalues):
@@ -245,17 +219,17 @@
         far[k] = lax.ppermute(sent, "dp", ahead)
         return sent
 
-    def pair_scores(*ks, sums=None, until=()):
+    def pair_scores(*ks, sums=None, side=None, until=()):
         operands = [*held, inverse] + [block[k] for k in ks for block in (near, far)]
         if sums is not None:
             operands.append(sums)
         return call(
-            functools.partial(pair_kernel, ks, sums is None),
-            floats(doc_rows, 2 * rows),
-            [VMEM] * len(operands) + [ANY] * len(until),
+            functools.partial(pair_kernel, ks, side, factor, sums is None),
+            floats(doc_rows if side is None else half, 2 * rows),
+            [SMEM] + [VMEM] * len(operands) + [ANY] * len(until),
             VMEM,
             [pltpu.VMEM((2 * rows, max(width_of(k, dims) for k in ks)), queries.dtype)],
-        )(*operands, *until)
+        )(counts, *operands, *until)
 
     def send_across(block, k, *until):
         sent = lax.optimization_barrier((block[k], *until))[0]
@@ -264,36 +238,37 @@
     far = [None] * CHUNKS
     near = [None] * CHUNKS
 
-    sent = own_chunks(0, 1, space=VMEM, vmem_mib=59)
+    sent = own_chunks(0, 1, space=VMEM, vmem_mib=53)
     for k in range(2):
         far[k] = lax.ppermute(sent[k], "dp", ahead)
 
     def own_scores(part, *operands, until=()):
         pieces = 4
         outs = [
-            floats(doc_rows, rows),
+            floats(half, rows),
+            floats(half, rows),
             jax.ShapeDtypeStruct((doc_rows, dims // 2), documents.dtype),
             floats(1, dims),
-        ][: 3 - part]
+        ][: 4 - part]
         return call(
-            functools.partial(own_kernel, part, pieces),
+            functools.partial(own_kernel, part, pieces, factor),
             outs,
-            [HBM] + [VMEM] * (1 + len(operands)) + [ANY] * len(until),
+            [SMEM, HBM] + [VMEM] * (1 + len(operands)) + [ANY] * len(until),
             [VMEM] * len(outs),
             [pltpu.SemaphoreType.DMA((pieces, 2))],
             vmem_mib=OWN_MIB[part],
-        )(documents, queries, *operands, *until)
+        )(counts, documents, queries, *operands, *until)
 
     kept = lax.optimization_barrier((eigenvalues, sent[1]))[0].reshape(1, dims)
-    own_sums, held0, inverse = own_scores(0, kept)
+    theirs0, mine0, held0, inverse = own_scores(0, kept)
 
     out = step(0, inverse)
     out = send_ahead(2, out)
     send_across(far, 0, out)
-    own_sums, held1 = own_scores(1, inverse, own_sums, until=(out,))
+    theirs0, mine0, held1 = own_scores(1, inverse, theirs0, mine0, until=(out,))
     held = held0, held1
 
-    out = step(1, own_sums)
+    out = step(1, theirs0)
     out = send_ahead(3, out)
     send_across(near, 0, out)
     sums = pair_scores(0, until=(out, far[5]))
@@ -304,36 +279,12 @@
     sums = pair_scores(1, sums=sums, until=(out,))
 
     out = step(3, sums)
+    got0 = lax.ppermute(lax.optimization_barrier((theirs0, out))[0], "layer", across)
     sums = pair_scores(2, 5, sums=sums, until=(out,))
-
-    operands = [counts, *held, inverse, near[4], far[4], far[3], sums, own_sums]
-    near_sums, theirs, mine = call(
-        functools.partial(far_kernel, (4,), 3, factor),
-        [floats(doc_rows, rows), floats(half, 2 * rows), floats(half, 2 * rows)],
-        [SMEM] + [VMEM] * (len(operands) - 1),
-        [VMEM] * 3,
-        [
-            pltpu.VMEM((doc_rows, 2 * rows), jnp.float32),
-            pltpu.VMEM((2 * rows, width_of(4, dims)), queries.dtype),
-        ],
-    )(*operands)
+    theirs = pair_scores(3, 4, sums=sums, side=0, until=(got0,))
     got = lax.ppermute(theirs, "layer", across)
-
-    def near_scores(side, until):
-        return call(
-            functools.partial(near_kernel, 3, side, factor),
-            floats(half, rows),
-            [SMEM] + [VMEM] * 5 + [ANY],
-            VMEM,
-            [],
-        )(counts, *held, inverse, near[3], near_sums, until)
-
-    theirs_near = near_scores(0, theirs)
-    got_near = lax.ppermute(theirs_near, "layer", across)
-    mine_near = near_scores(1, theirs_near)
-    return call(final_kernel, floats(half, 3 * rows), [VMEM] * 4, VMEM, [])(
-        mine, got, mine_near, got_near
-    )
+    mine = pair_scores(3, 4, sums=sums, side=1, until=(theirs,))
+    return call(final_kernel, floats(half, 3 * rows), [VMEM] * 4, VMEM, [])(mine0, got0, mine, got)
 
 
 def solution(mesh):

time: 49.9 us -> 48.9 us (0.980)
  Pallas kernels: 16.7 us -> 15.2 us
  waiting for transfers between devices: 14.6 us -> 15.4 us
    ppermute x4, waiting for transfers between devices: 6.2 us -> 7.74 us  [step(): near[k] = lax.ppermute(out, 'dp', pair)]
    ppermute x3, waiting for transfers between devices: 1.09 us -> 0.01 us  [send_across(): block[CHUNKS - 1 - k] = lax.ppermute(sent, 'groups', across)]
    ppermute x1, waiting for transfers between devices: 0.01 us -> 0.96 us  [on_device(): got = lax.ppermute(theirs, 'layer', across)]
    pallas_call x4, Pallas kernels: 2.29 us -> 1.38 us  [own_chunks(): call(functools.partial(chunk_kernel, ks), [chunk(k) for k in ks], [ANY] *...]
    pallas_call x8 -> x7, Pallas kernels: 13.4 us -> 12.8 us  [the longest x2 8.97 us: own_scores(): call(functools.partial(own_kernel, part, pieces, factor), outs, [SMEM, HB...]
    ppermute x1, starting transfers between devices: 0.54 us -> 0.01 us  [on_device(): lax.ppermute(lax.optimization_barrier((theirs0, out))[0], 'layer', across)]
  transfers between devices with their start and end apart: 14 -> 14, of which waited for: 7 -> 8; matrix products, arithmetic and copies ran while one was open for 0% -> 0% of each run, Pallas kernels for 27% -> 25%
where the time goes in v5:
time: 48.9 us; the launch traced here: 48.8 us
  starting transfers between devices  17.4 us (36%)
  waiting for transfers between devices  15.4 us (31%)
  Pallas kernels  15.2 us (31%)
  between operations  0.85 us (2%)
    pallas_call x2, Pallas kernels, own_scores(): call(functools.partial(own_kernel, part, pieces, factor), outs, [SMEM, HB...  8.97 us
    ppermute x4, starting transfers between devices, step(): near[k] = lax.ppermute(out, 'dp', pair)  7.96 us
    ppermute x4, waiting for transfers between devices, step(): near[k] = lax.ppermute(out, 'dp', pair)  7.74 us
    ppermute x2, waiting for transfers between devices, on_device(): far[k] = lax.ppermute(sent[k], 'dp', ahead)  5.47 us
    ppermute x2, starting transfers between devices, on_device(): far[k] = lax.ppermute(sent[k], 'dp', ahead)  4.65 us
    ppermute x3, starting transfers between devices, send_across(): block[CHUNKS - 1 - k] = lax.ppermute(sent, 'groups', across)  4.54 us
    pallas_call x5, Pallas kernels, pair_scores(): call(functools.partial(pair_kernel, ks, side, factor, sums is None), floa...  3.8 us
    pallas_call x4, Pallas kernels, own_chunks(): call(functools.partial(chunk_kernel, ks), [chunk(k) for k in ks], [ANY] *...  1.38 us
  transfers between devices with their start and end apart: 14, of which 8 were waited for; matrix products, arithmetic and copies ran while one was open for 0% of the time, Pallas kernels for 25%

profile of v5, /device:TPU:0, one launch (start us, length us, event | category | flops | bytes accessed | tf_op | source)
XLA Modules:
  0.0 48.8 jit_solution(15730385205751605258)
XLA Ops:
  0.0 0.0 copy-start
  0.0 0.0 copy-start.1
  0.0 1.3 %shard_map.46 = (bf16[128,1536]{1,0:T(8,128)(2,1)S(1)}, bf16[128,1536]{1,0:T(8,128)(2,1)S(1)}) custom-call(bf16[128,8192]{1,0:T(8,128)(2,1)} %queries.19), custom_call_target="tpu_custom_call" | custom-call | flops 1600000000 | tf_op jit(solution)/shard_map/pallas_call | solution.py:197
  1.3 3.1 %collective-permute-start = (bf16[128,1536]{1,0:T(8,128)(2,1)S(1)}, bf16[128,1536]{1,0:T(8,128)(2,1)S(1)}, u32[]{:S(2)}, u32[]{:S(2)}) collective-permute-start(bf16[128,1536]{1,0:T(8,128)(2,1)S(1)} %get-tuple-element.24), channel_id=1, source_target_pairs={{0,4},{2,6},{4,8},{6,10},{8,12},{10,14},{12,0},{14,2},{1,5},{3,7},... | collective-permute-start | bytes 1179656 | tf_op jit(solution)/shard_map/ppermute | solution.py:243
  4.4 1.6 %collective-permute-start.1 = (bf16[128,1536]{1,0:T(8,128)(2,1)S(1)}, bf16[128,1536]{1,0:T(8,128)(2,1)S(1)}, u32[]{:S(2)}, u32[]{:S(2)}) collective-permute-start(bf16[128,1536]{1,0:T(8,128)(2,1)S(1)} %get-tuple-element.19), channel_id=1, source_target_pairs={{0,4},{2,6},{4,8},{6,10},{8,12},{10,14},{12,0},{14,2},{1,5},{3,7},... | collective-permute-start | bytes 1179656 | tf_op jit(solution)/shard_map/ppermute | solution.py:243
  6.6 0.0 copy-done
  6.6 0.0 copy-done.1
  6.6 4.5 %shard_map.47 = (f32[320,128]{1,0:T(8,128)S(1)}, f32[320,128]{1,0:T(8,128)S(1)}, bf16[640,4096]{1,0:T(8,128)(2,1)S(1)}, f32[1,8192]{1,0:T(1,128)S(1)}) custom-call(s32[1]{0:T(128)S(6)} %copy.5.counts, bf16[640,8192]{1,0:T(8,128)(2,1)} %documents.3, bf16[128,8192]{1,0:T(8,128)(2,1)S(1)} %copy-done, f32[1,8192]{1,0:T(1,128)S(1)} %bitcast.1), custom_call_target="tpu_custom_call" | custom-call | flops 1600000000 | tf_op jit(solution)/shard_map/pallas_call | solution.py:253
  11.1 5.2 %collective-permute-done.received.refs_1_ = bf16[128,1536]{1,0:T(8,128)(2,1)S(1)} collective-permute-done((bf16[128,1536]{1,0:T(8,128)(2,1)S(1)}, bf16[128,1536]{1,0:T(8,128)(2,1)S(1)}, u32[]{:S(2)}, u32[]{:S(2)}) %collective-permute-start) | collective-permute-done | bytes 393248 | tf_op jit(solution)/shard_map/ppermute | solution.py:243
  16.4 2.0 %collective-permute-start.4 = (bf16[128,1536]{1,0:T(8,128)(2,1)S(1)}, bf16[128,1536]{1,0:T(8,128)(2,1)S(1)}, u32[]{:S(2)}, u32[]{:S(2)}) collective-permute-start(bf16[128,1536]{1,0:T(8,128)(2,1)S(1)} %shard_map.48.refs_0_), channel_id=1, source_target_pairs={{0,2},{2,0},{4,6},{6,4},{8,10},{10,8},{12,14},{14,12},{1,3},{3,1},... | collective-permute-start | bytes 1179656 | tf_op jit(solution)/shard_map/ppermute | solution.py:214
  18.4 0.1 collective-permute-start.6
  18.5 1.6 %collective-permute-start.5 = (bf16[128,1536]{1,0:T(8,128)(2,1)S(1)}, bf16[128,1536]{1,0:T(8,128)(2,1)S(1)}, u32[]{:S(2)}, u32[]{:S(2)}) collective-permute-start(bf16[128,1536]{1,0:T(8,128)(2,1)S(1)} %collective-permute-done.received.refs_1_), channel_id=1, source_target_pairs={{0,16},{16,0},{1,17},{17,1},{2,18},{18,2},{3,19},{19,3},{4,20},{20... | collective-permute-start | bytes 1179656 | tf_op jit(solution)/shard_map/ppermute | solution.py:236
  20.0 4.5 %shard_map.50 = (f32[320,128]{1,0:T(8,128)S(1)}, f32[320,128]{1,0:T(8,128)S(1)}, bf16[640,4096]{1,0:T(8,128)(2,1)S(1)}) custom-call(s32[1]{0:T(128)S(6)} %copy.5.counts, bf16[640,8192]{1,0:T(8,128)(2,1)} %documents.3, bf16[128,8192]{1,0:T(8,128)(2,1)S(1)} %copy-done, f32[1,8192]{1,0:T(1,128)S(1)} %get-tuple-element.21.refs_0_.inverse, ...), custom_call_target="tpu_custom_call" | custom-call | flops 1600000000 | tf_op jit(solution)/shard_map/pallas_call | solution.py:253
  24.5 0.2 collective-permute-done.1.received.refs_1_
  24.8 2.0 %collective-permute-start.3 = (bf16[128,1536]{1,0:T(8,128)(2,1)S(1)}, bf16[128,1536]{1,0:T(8,128)(2,1)S(1)}, u32[]{:S(2)}, u32[]{:S(2)}) collective-permute-start(bf16[128,1536]{1,0:T(8,128)(2,1)S(1)} %shard_map.51.refs_0_), channel_id=1, source_target_pairs={{0,2},{2,0},{4,6},{6,4},{8,10},{10,8},{12,14},{14,12},{1,3},{3,1},... | collective-permute-start | bytes 1179656 | tf_op jit(solution)/shard_map/ppermute | solution.py:214
  26.8 0.1 collective-permute-start.2
  26.9 0.0 collective-permute-done.4.refs_0_
  26.9 1.6 %collective-permute-start.12 = (bf16[128,1536]{1,0:T(8,128)(2,1)S(1)}, bf16[128,1536]{1,0:T(8,128)(2,1)S(1)}, u32[]{:S(2)}, u32[]{:S(2)}) collective-permute-start(bf16[128,1536]{1,0:T(8,128)(2,1)S(1)} %collective-permute-done.4.refs_0_), channel_id=1, source_target_pairs={{0,16},{16,0},{1,17},{17,1},{2,18},{18,2},{3,19},{19,3},{4,20},{20... | collective-permute-start | bytes 1179656 | tf_op jit(solution)/shard_map/ppermute | solution.py:236
  28.5 0.0 collective-permute-done.5.refs_3_
  28.5 0.7 %shard_map.53.refs_0_.refs_2_ = f32[640,256]{1,0:T(8,128)S(1)} custom-call(s32[1]{0:T(128)S(6)} %copy.5.counts, bf16[640,4096]{1,0:T(8,128)(2,1)S(1)} %get-tuple-element.27.held0, bf16[640,4096]{1,0:T(8,128)(2,1)S(1)} %get-tuple-element.28.held1, f32[1,8192]{1,0:T(1,128)S(1)} %get-tuple-element.21.refs_0_.inverse, ...), custom_call_target="tpu_custom_call" | custom-call | flops 1600000000 | tf_op jit(solution)/shard_map/pallas_call | solution.py:226
  29.2 0.9 %collective-permute-done.6.received.refs_1_ = bf16[128,1024]{1,0:T(8,128)(2,1)S(1)} collective-permute-done((bf16[128,1024]{1,0:T(8,128)(2,1)S(1)}, bf16[128,1024]{1,0:T(8,128)(2,1)S(1)}, u32[]{:S(2)}, u32[]{:S(2)}) %collective-permute-start.6) | collective-permute-done | bytes 262176 | tf_op jit(solution)/shard_map/ppermute | solution.py:219
  30.1 2.1 %collective-permute-start.11 = (bf16[128,1024]{1,0:T(8,128)(2,1)S(1)}, bf16[128,1024]{1,0:T(8,128)(2,1)S(1)}, u32[]{:S(2)}, u32[]{:S(2)}) collective-permute-start(bf16[128,1024]{1,0:T(8,128)(2,1)S(1)} %shard_map.54.refs_0_), channel_id=1, source_target_pairs={{0,2},{2,0},{4,6},{6,4},{8,10},{10,8},{12,14},{14,12},{1,3},{3,1},... | collective-permute-start | bytes 786440 | tf_op jit(solution)/shard_map/ppermute | solution.py:214
  32.3 0.1 collective-permute-start.10
  32.4 4.6 %collective-permute-done.3.refs_0_ = bf16[128,1536]{1,0:T(8,128)(2,1)S(1)} collective-permute-done((bf16[128,1536]{1,0:T(8,128)(2,1)S(1)}, bf16[128,1536]{1,0:T(8,128)(2,1)S(1)}, u32[]{:S(2)}, u32[]{:S(2)}) %collective-permute-start.3) | collective-permute-done | bytes 393248 | tf_op jit(solution)/shard_map/ppermute | solution.py:214
  36.9 1.4 %collective-permute-start.9 = (bf16[128,1536]{1,0:T(8,128)(2,1)S(1)}, bf16[128,1536]{1,0:T(8,128)(2,1)S(1)}, u32[]{:S(2)}, u32[]{:S(2)}) collective-permute-start(bf16[128,1536]{1,0:T(8,128)(2,1)S(1)} %collective-permute-done.3.refs_0_), channel_id=1, source_target_pairs={{0,16},{16,0},{1,17},{17,1},{2,18},{18,2},{3,19},{19,3},{4,20},{20... | collective-permute-start | bytes 1179656 | tf_op jit(solution)/shard_map/ppermute | solution.py:236
  38.4 0.7 %shard_map.56.refs_0_.refs_4_ = f32[640,256]{1,0:T(8,128)S(1)} custom-call(s32[1]{0:T(128)S(6)} %copy.5.counts, bf16[640,4096]{1,0:T(8,128)(2,1)S(1)} %get-tuple-element.27.held0, bf16[640,4096]{1,0:T(8,128)(2,1)S(1)} %get-tuple-element.28.held1, f32[1,8192]{1,0:T(1,128)S(1)} %get-tuple-element.21.refs_0_.inverse, ...), custom_call_target="tpu_custom_call" | custom-call | flops 1600000000 | tf_op jit(solution)/shard_map/pallas_call | solution.py:226
  39.1 0.0 collective-permute-done.2.received.refs_1_
  39.1 0.1 shard_map.57.refs_5_
  39.2 1.9 %collective-permute-start.8 = (bf16[128,1024]{1,0:T(8,128)(2,1)S(1)}, bf16[128,1024]{1,0:T(8,128)(2,1)S(1)}, u32[]{:S(2)}, u32[]{:S(2)}) collective-permute-start(bf16[128,1024]{1,0:T(8,128)(2,1)S(1)} %shard_map.57.refs_5_), channel_id=1, source_target_pairs={{0,2},{2,0},{4,6},{6,4},{8,10},{10,8},{12,14},{14,12},{1,3},{3,1},... | collective-permute-start | bytes 786440 | tf_op jit(solution)/shard_map/ppermute | solution.py:214
  41.0 1.5 %collective-permute-done.11.refs_0_ = bf16[128,1024]{1,0:T(8,128)(2,1)S(1)} collective-permute-done((bf16[128,1024]{1,0:T(8,128)(2,1)S(1)}, bf16[128,1024]{1,0:T(8,128)(2,1)S(1)}, u32[]{:S(2)}, u32[]{:S(2)}) %collective-permute-start.11) | collective-permute-done | bytes 262176 | tf_op jit(solution)/shard_map/ppermute | solution.py:214
  42.6 0.0 collective-permute-start.7
  42.6 0.0 collective-permute-done.12.refs_2_
  42.6 1.1 %shard_map.58.refs_4_ = f32[640,256]{1,0:T(8,128)S(1)} custom-call(s32[1]{0:T(128)S(6)} %copy.5.counts, bf16[640,4096]{1,0:T(8,128)(2,1)S(1)} %get-tuple-element.27.held0, bf16[640,4096]{1,0:T(8,128)(2,1)S(1)} %get-tuple-element.28.held1, f32[1,8192]{1,0:T(1,128)S(1)} %get-tuple-element.21.refs_0_.inverse, ...), custom_call_target="tpu_custom_call" | custom-call | flops 1600000000 | tf_op jit(solution)/shard_map/pallas_call | solution.py:226
  43.6 0.3 collective-permute-done.7.refs_5_.got0
  44.0 1.7 %collective-permute-done.8.refs_0_ = bf16[128,1024]{1,0:T(8,128)(2,1)S(1)} collective-permute-done((bf16[128,1024]{1,0:T(8,128)(2,1)S(1)}, bf16[128,1024]{1,0:T(8,128)(2,1)S(1)}, u32[]{:S(2)}, u32[]{:S(2)}) %collective-permute-start.8) | collective-permute-done | bytes 262176 | tf_op jit(solution)/shard_map/ppermute | solution.py:214
  45.6 0.0 collective-permute-done.9.refs_2_
  45.6 0.0 collective-permute-done.10.refs_3_
  45.6 0.6 %shard_map.59.refs_5_ = f32[320,256]{1,0:T(8,128)S(1)} custom-call(s32[1]{0:T(128)S(6)} %copy.5.counts, bf16[640,4096]{1,0:T(8,128)(2,1)S(1)} %get-tuple-element.27.held0, bf16[640,4096]{1,0:T(8,128)(2,1)S(1)} %get-tuple-element.28.held1, f32[1,8192]{1,0:T(1,128)S(1)} %get-tuple-element.21.refs_0_.inverse, ...), custom_call_target="tpu_custom_call" | custom-call | flops 1600000000 | tf_op jit(solution)/shard_map/pallas_call | solution.py:226
  46.3 0.1 collective-permute-start.13
  46.3 0.6 %shard_map.60.mine = f32[320,256]{1,0:T(8,128)S(1)} custom-call(s32[1]{0:T(128)S(6)} %copy.5.counts, bf16[640,4096]{1,0:T(8,128)(2,1)S(1)} %get-tuple-element.27.held0, bf16[640,4096]{1,0:T(8,128)(2,1)S(1)} %get-tuple-element.28.held1, f32[1,8192]{1,0:T(1,128)S(1)} %get-tuple-element.21.refs_0_.inverse, ...), custom_call_target="tpu_custom_call" | custom-call | flops 1600000000 | tf_op jit(solution)/shard_map/pallas_call | solution.py:226
  47.0 1.0 %collective-permute-done.13.got = f32[320,256]{1,0:T(8,128)S(1)} collective-permute-done((f32[320,256]{1,0:T(8,128)S(1)}, f32[320,256]{1,0:T(8,128)S(1)}, u32[]{:S(2)}, u32[]{:S(2)}) %collective-permute-start.13) | collective-permute-done | bytes 327712 | tf_op jit(solution)/shard_map/ppermute | solution.py:285
  48.0 0.8 %shard_map.61 = f32[320,384]{1,0:T(8,128)} custom-call(f32[320,128]{1,0:T(8,128)S(1)} %get-tuple-element.25.mine0, f32[320,128]{1,0:T(8,128)S(1)} %collective-permute-done.7.refs_5_.got0, f32[320,256]{1,0:T(8,128)S(1)} %shard_map.60.mine, f32[320,256]{1,0:T(8,128)S(1)} %collective-permute-done.13.got), custom_call_target="tpu_custom_call" | custom-call | flops 1600000000 | tf_op jit(solution)/shard_map/pallas_call | solution.py:287
  (6 shorter events, 0.2 us)
Async XLA Ops:
  0.0 6.6 %copy-start = (bf16[128,8192]{1,0:T(8,128)(2,1)S(1)}, bf16[128,8192]{1,0:T(8,128)(2,1)}, u32[]{:S(2)}) copy-start(bf16[128,8192]{1,0:T(8,128)(2,1)} %queries.19) | copy-start | bytes 6291460
  0.0 6.6 %copy-start.1 = (f32[8192]{0:T(1024)S(1)}, f32[8192]{0:T(1024)}, u32[]{:S(2)}) copy-start(f32[8192]{0:T(1024)} %param.7) | copy-start | bytes 98308
  1.3 15.0 %collective-permute-start = (bf16[128,1536]{1,0:T(8,128)(2,1)S(1)}, bf16[128,1536]{1,0:T(8,128)(2,1)S(1)}, u32[]{:S(2)}, u32[]{:S(2)}) collective-permute-start(bf16[128,1536]{1,0:T(8,128)(2,1)S(1)} %get-tuple-element.24), channel_id=1, source_target_pairs={{0,4},{2,6},{4,8},{6,10},{8,12},{10,14},{12,0},{14,2},{1,5},{3,7},... | collective-permute-start | bytes 1179656 | tf_op jit(solution)/shard_map/ppermute | solution.py:243
  4.4 20.4 %collective-permute-start.1 = (bf16[128,1536]{1,0:T(8,128)(2,1)S(1)}, bf16[128,1536]{1,0:T(8,128)(2,1)S(1)}, u32[]{:S(2)}, u32[]{:S(2)}) collective-permute-start(bf16[128,1536]{1,0:T(8,128)(2,1)S(1)} %get-tuple-element.19), channel_id=1, source_target_pairs={{0,4},{2,6},{4,8},{6,10},{8,12},{10,14},{12,0},{14,2},{1,5},{3,7},... | collective-permute-start | bytes 1179656 | tf_op jit(solution)/shard_map/ppermute | solution.py:243
  16.4 10.5 %collective-permute-start.4 = (bf16[128,1536]{1,0:T(8,128)(2,1)S(1)}, bf16[128,1536]{1,0:T(8,128)(2,1)S(1)}, u32[]{:S(2)}, u32[]{:S(2)}) collective-permute-start(bf16[128,1536]{1,0:T(8,128)(2,1)S(1)} %shard_map.48.refs_0_), channel_id=1, source_target_pairs={{0,2},{2,0},{4,6},{6,4},{8,10},{10,8},{12,14},{14,12},{1,3},{3,1},... | collective-permute-start | bytes 1179656 | tf_op jit(solution)/shard_map/ppermute | solution.py:214
  18.4 11.7 %collective-permute-start.6 = (bf16[128,1024]{1,0:T(8,128)(2,1)S(1)}, bf16[128,1024]{1,0:T(8,128)(2,1)S(1)}, u32[]{:S(2)}, u32[]{:S(2)}) collective-permute-start(bf16[128,1024]{1,0:T(8,128)(2,1)S(1)} %shard_map.49.refs_3_), channel_id=1, source_target_pairs={{0,4},{2,6},{4,8},{6,10},{8,12},{10,14},{12,0},{14,2},{1,5},{3,7},... | collective-permute-start | bytes 786440 | tf_op jit(solution)/shard_map/ppermute | solution.py:219
  18.5 10.0 %collective-permute-start.5 = (bf16[128,1536]{1,0:T(8,128)(2,1)S(1)}, bf16[128,1536]{1,0:T(8,128)(2,1)S(1)}, u32[]{:S(2)}, u32[]{:S(2)}) collective-permute-start(bf16[128,1536]{1,0:T(8,128)(2,1)S(1)} %collective-permute-done.received.refs_1_), channel_id=1, source_target_pairs={{0,16},{16,0},{1,17},{17,1},{2,18},{18,2},{3,19},{19,3},{4,20},{20... | collective-permute-start | bytes 1179656 | tf_op jit(solution)/shard_map/ppermute | solution.py:236
  24.8 12.1 %collective-permute-start.3 = (bf16[128,1536]{1,0:T(8,128)(2,1)S(1)}, bf16[128,1536]{1,0:T(8,128)(2,1)S(1)}, u32[]{:S(2)}, u32[]{:S(2)}) collective-permute-start(bf16[128,1536]{1,0:T(8,128)(2,1)S(1)} %shard_map.51.refs_0_), channel_id=1, source_target_pairs={{0,2},{2,0},{4,6},{6,4},{8,10},{10,8},{12,14},{14,12},{1,3},{3,1},... | collective-permute-start | bytes 1179656 | tf_op jit(solution)/shard_map/ppermute | solution.py:214
  26.8 12.3 %collective-permute-start.2 = (bf16[128,1024]{1,0:T(8,128)(2,1)S(1)}, bf16[128,1024]{1,0:T(8,128)(2,1)S(1)}, u32[]{:S(2)}, u32[]{:S(2)}) collective-permute-start(bf16[128,1024]{1,0:T(8,128)(2,1)S(1)} %shard_map.52.refs_2_), channel_id=1, source_target_pairs={{0,4},{2,6},{4,8},{6,10},{8,12},{10,14},{12,0},{14,2},{1,5},{3,7},... | collective-permute-start | bytes 786440 | tf_op jit(solution)/shard_map/ppermute | solution.py:219
  26.9 15.7 %collective-permute-start.12 = (bf16[128,1536]{1,0:T(8,128)(2,1)S(1)}, bf16[128,1536]{1,0:T(8,128)(2,1)S(1)}, u32[]{:S(2)}, u32[]{:S(2)}) collective-permute-start(bf16[128,1536]{1,0:T(8,128)(2,1)S(1)} %collective-permute-done.4.refs_0_), channel_id=1, source_target_pairs={{0,16},{16,0},{1,17},{17,1},{2,18},{18,2},{3,19},{19,3},{4,20},{20... | collective-permute-start | bytes 1179656 | tf_op jit(solution)/shard_map/ppermute | solution.py:236
  30.1 12.4 %collective-permute-start.11 = (bf16[128,1024]{1,0:T(8,128)(2,1)S(1)}, bf16[128,1024]{1,0:T(8,128)(2,1)S(1)}, u32[]{:S(2)}, u32[]{:S(2)}) collective-permute-start(bf16[128,1024]{1,0:T(8,128)(2,1)S(1)} %shard_map.54.refs_0_), channel_id=1, source_target_pairs={{0,2},{2,0},{4,6},{6,4},{8,10},{10,8},{12,14},{14,12},{1,3},{3,1},... | collective-permute-start | bytes 786440 | tf_op jit(solution)/shard_map/ppermute | solution.py:214
  32.3 13.3 %collective-permute-start.10 = (bf16[128,1536]{1,0:T(8,128)(2,1)S(1)}, bf16[128,1536]{1,0:T(8,128)(2,1)S(1)}, u32[]{:S(2)}, u32[]{:S(2)}) collective-permute-start(bf16[128,1536]{1,0:T(8,128)(2,1)S(1)} %shard_map.55.refs_3_), channel_id=1, source_target_pairs={{0,4},{2,6},{4,8},{6,10},{8,12},{10,14},{12,0},{14,2},{1,5},{3,7},... | collective-permute-start | bytes 1179656 | tf_op jit(solution)/shard_map/ppermute | solution.py:219
  36.9 8.7 %collective-permute-start.9 = (bf16[128,1536]{1,0:T(8,128)(2,1)S(1)}, bf16[128,1536]{1,0:T(8,128)(2,1)S(1)}, u32[]{:S(2)}, u32[]{:S(2)}) collective-permute-start(bf16[128,1536]{1,0:T(8,128)(2,1)S(1)} %collective-permute-done.3.refs_0_), channel_id=1, source_target_pairs={{0,16},{16,0},{1,17},{17,1},{2,18},{18,2},{3,19},{19,3},{4,20},{20... | collective-permute-start | bytes 1179656 | tf_op jit(solution)/shard_map/ppermute | solution.py:236
  39.2 6.4 %collective-permute-start.8 = (bf16[128,1024]{1,0:T(8,128)(2,1)S(1)}, bf16[128,1024]{1,0:T(8,128)(2,1)S(1)}, u32[]{:S(2)}, u32[]{:S(2)}) collective-permute-start(bf16[128,1024]{1,0:T(8,128)(2,1)S(1)} %shard_map.57.refs_5_), channel_id=1, source_target_pairs={{0,2},{2,0},{4,6},{6,4},{8,10},{10,8},{12,14},{14,12},{1,3},{3,1},... | collective-permute-start | bytes 786440 | tf_op jit(solution)/shard_map/ppermute | solution.py:214
  42.6 1.4 %collective-permute-start.7 = (f32[320,128]{1,0:T(8,128)S(1)}, f32[320,128]{1,0:T(8,128)S(1)}, u32[]{:S(2)}, u32[]{:S(2)}) collective-permute-start(f32[320,128]{1,0:T(8,128)S(1)} %get-tuple-element.30.refs_0_), channel_id=1, source_target_pairs={{0,1},{1,0},{2,3},{3,2},{4,5},{5,4},{6,7},{7,6},{8,9},{9,8},{10,11... | collective-permute-start | bytes 491528 | tf_op jit(solution)/shard_map/ppermute | solution.py:282
  46.3 1.7 %collective-permute-start.13 = (f32[320,256]{1,0:T(8,128)S(1)}, f32[320,256]{1,0:T(8,128)S(1)}, u32[]{:S(2)}, u32[]{:S(2)}) collective-permute-start(f32[320,256]{1,0:T(8,128)S(1)} %shard_map.59.refs_5_), channel_id=1, source_target_pairs={{0,1},{1,0},{2,3},{3,2},{4,5},{5,4},{6,7},{7,6},{8,9},{9,8},{10,11... | collective-permute-start | bytes 983048 | tf_op jit(solution)/shard_map/ppermute | solution.py:285

commit v6 on v5

--- a/solution.py
+++ b/solution.py
@@ -9,15 +9,16 @@
 from jax.sharding import PartitionSpec as P
 
 L_DIM = 8192
-SIZES = (12, 12, 8, 8, 12, 12)
+SIZES = (11, 13, 8, 8, 13, 11)
 CHUNKS = len(SIZES)
 DIRECT = 5
+PARTS = 4
 OWN_MIB = (44, 40)
 VMEM = pl.BlockSpec(memory_space=pltpu.VMEM)
 SMEM = pl.BlockSpec(memory_space=pltpu.SMEM)
 HBM = pl.BlockSpec(memory_space=pltpu.HBM)
 ANY = pl.BlockSpec(memory_space=pl.ANY)
-COST = pl.CostEstimate(flops=16 * 10**8, bytes_accessed=0, transcendentals=0)
+COST = pl.CostEstimate(flops=18*10**8, bytes_accessed=0, transcendentals=0)
 MIB = 1024 * 1024
 
 
@@ -53,12 +54,20 @@
     return factor * (index < counts[0]).astype(jnp.float32)
 
 
+def row_parts(rows, parts):
+    size = rows // parts
+    return [pl.ds(i * size, size) for i in range(parts)]
+
+
 def chunk_kernel(ks, queries, *refs):
     outs, sem = refs[-len(ks) - 1 : -1], refs[-1]
-    dims = queries.shape[1]
+    rows, dims = queries.shape
     copies = [
-        pltpu.make_async_copy(queries.at[:, columns_of(k, dims)], outs[i], sem.at[i])
+        pltpu.make_async_copy(
+            queries.at[part, columns_of(k, dims)], outs[i].at[part], sem.at[i, p]
+        )
         for i, k in enumerate(ks)
+        for p, part in enumerate(row_parts(rows, PARTS))
     ]
     for copy in copies:
         copy.start()
@@ -94,19 +103,24 @@
     dims = documents.shape[1]
     width = dims // 2 // pieces
     first = half_columns(part, dims).start
-    copies = []
+    size = half // PARTS
+    copies = {}
     for i in range(pieces):
         start = pl.multiple_of(first + i * width, width)
-        for at, row in enumerate((1 - layer, layer)):
-            copies.append(
+        for side, row in enumerate((1 - layer, layer)):
+            copies[i, side] = [
                 pltpu.make_async_copy(
-                    documents.at[pl.ds(pl.multiple_of(row * half, half), half), pl.ds(start, width)],
-                    held.at[pl.ds(at * half, half), pl.ds(i * width, width)],
-                    sem.at[i, at],
+                    documents.at[
+                        pl.ds(pl.multiple_of(row * half + p * size, size), size),
+                        pl.ds(start, width),
+                    ],
+                    held.at[pl.ds(side * half + p * size, size), pl.ds(i * width, width)],
+                    sem.at[i, side, p],
                 )
-            )
-    for copy in copies:
-        copy.start()
+                for p in range(PARTS)
+            ]
+            for copy in copies[i, side]:
+                copy.start()
     if part == 0:
         for start in range(0, dims, L_DIM):
             block = eigenvalues[:, start : start + L_DIM]
@@ -116,7 +130,8 @@
         columns = pl.ds(pl.multiple_of(first + i * width, width), width)
         scaled = (queries[:, columns].astype(jnp.float32) * inverse[:, columns]).astype(jnp.bfloat16)
         for side, out in enumerate((theirs, mine)):
-            copies[2 * i + side].wait()
+            for copy in copies[i, side]:
+                copy.wait()
             term = products(
                 held[side * half : (side + 1) * half, i * width : (i + 1) * width], scaled
             )
@@ -159,10 +174,16 @@
         out[...] *= scale_of(factor, counts, size, side)
 
 
-def final_kernel(mine0, got0, mine, got, out):
-    rows = mine0.shape[1]
-    out[:, :rows] = mine0[...] + got0[...]
-    out[:, rows:] = mine[...] + got[...]
+def final_kernel(mine0, got0, mine, got, out, buf, sem):
+    half, rows = mine0.shape
+    copies = []
+    for p, part in enumerate(row_parts(half, PARTS)):
+        buf[part, :rows] = mine0[part, :] + got0[part, :]
+        buf[part, rows:] = mine[part, :] + got[part, :]
+        copies.append(pltpu.make_async_copy(buf.at[part], out.at[part], sem.at[p]))
+        copies[p].start()
+    for copy in copies:
+        copy.wait()
 
 
 def on_device(queries, documents, counts, eigenvalues):
@@ -199,7 +220,7 @@
             [chunk(k) for k in ks],
             [ANY] * (1 + len(until)),
             [space] * len(ks),
-            [pltpu.SemaphoreType.DMA((len(ks),))],
+            [pltpu.SemaphoreType.DMA((len(ks), PARTS))],
             vmem_mib,
         )(queries, *until)
 
@@ -255,7 +276,7 @@
             outs,
             [SMEM, HBM] + [VMEM] * (1 + len(operands)) + [ANY] * len(until),
             [VMEM] * len(outs),
-            [pltpu.SemaphoreType.DMA((pieces, 2))],
+            [pltpu.SemaphoreType.DMA((pieces, 2, PARTS))],
             vmem_mib=OWN_MIB[part],
         )(counts, documents, queries, *operands, *until)
 
@@ -281,10 +302,17 @@
     out = step(3, sums)
     got0 = lax.ppermute(lax.optimization_barrier((theirs0, out))[0], "layer", across)
     sums = pair_scores(2, 5, sums=sums, until=(out,))
-    theirs = pair_scores(3, 4, sums=sums, side=0, until=(got0,))
+    sums = pair_scores(4, sums=sums, until=(got0,))
+    theirs = pair_scores(3, sums=sums, side=0)
     got = lax.ppermute(theirs, "layer", across)
-    mine = pair_scores(3, 4, sums=sums, side=1, until=(theirs,))
-    return call(final_kernel, floats(half, 3 * rows), [VMEM] * 4, VMEM, [])(mine0, got0, mine, got)
+    mine = pair_scores(3, sums=sums, side=1, until=(theirs,))
+    return call(
+        final_kernel,
+        floats(half, 3 * rows),
+        [VMEM] * 4,
+        HBM,
+        [pltpu.VMEM((half, 3 * rows), jnp.float32), pltpu.SemaphoreType.DMA((PARTS,))],
+    )(mine0, got0, mine, got)
 
 
 def solution(mesh):

time: 48.9 us -> 49.9 us (1.020)
  Pallas kernels: 15.2 us -> 16.7 us
  waiting for transfers between devices: 15.4 us -> 14.6 us
    ppermute x4, waiting for transfers between devices: 7.74 us -> 6.54 us  [step(): near[k] = lax.ppermute(out, 'dp', pair)]
    ppermute x3, waiting for transfers between devices: 0.01 us -> 1.12 us  [send_across(): block[CHUNKS - 1 - k] = lax.ppermute(sent, 'groups', across)]
    ppermute x2, waiting for transfers between devices: 5.47 us -> 4.79 us  [on_device(): far[k] = lax.ppermute(sent[k], 'dp', ahead)]
    pallas_call x2, Pallas kernels: 8.97 us -> 9.6 us  [own_scores(): call(functools.partial(own_kernel, part, pieces, factor), outs, [SMEM, HB...]
    pallas_call x5 -> x6, Pallas kernels: 3.8 us -> 4.25 us  [pair_scores(): call(functools.partial(pair_kernel, ks, side, factor, sums is None), floa...]
  transfers between devices with their start and end apart: 14 -> 14, of which waited for: 8 -> 9; matrix products, arithmetic and copies ran while one was open for 0% -> 0% of each run, Pallas kernels for 25% -> 28%
where the time goes in v6:
time: 49.9 us; the launch traced here: 49.8 us
  starting transfers between devices  17.7 us (35%)
  Pallas kernels  16.7 us (33%)
  waiting for transfers between devices  14.6 us (29%)
  between operations  0.85 us (2%)
    pallas_call x2, Pallas kernels, own_scores(): call(functools.partial(own_kernel, part, pieces, factor), outs, [SMEM, HB...  9.6 us
    ppermute x4, starting transfers between devices, step(): near[k] = lax.ppermute(out, 'dp', pair)  7.98 us
    ppermute x4, waiting for transfers between devices, step(): near[k] = lax.ppermute(out, 'dp', pair)  6.54 us
    ppermute x3, starting transfers between devices, send_across(): block[CHUNKS - 1 - k] = lax.ppermute(sent, 'groups', across)  4.85 us
    ppermute x2, waiting for transfers between devices, on_device(): far[k] = lax.ppermute(sent[k], 'dp', ahead)  4.79 us
    ppermute x2, starting transfers between devices, on_device(): far[k] = lax.ppermute(sent[k], 'dp', ahead)  4.65 us
    pallas_call x6, Pallas kernels, pair_scores(): call(functools.partial(pair_kernel, ks, side, factor, sums is None), floa...  4.25 us
    pallas_call x4, Pallas kernels, own_chunks(): call(functools.partial(chunk_kernel, ks), [chunk(k) for k in ks], [ANY] *...  1.84 us
  transfers between devices with their start and end apart: 14, of which 9 were waited for; matrix products, arithmetic and copies ran while one was open for 0% of the time, Pallas kernels for 28%

profile of v6, /device:TPU:0, one launch (start us, length us, event | category | flops | bytes accessed | tf_op | source)
XLA Modules:
  0.0 49.8 jit_solution(7886870085212981189)
XLA Ops:
  0.0 0.0 copy-start
  0.0 0.0 copy-start.1
  0.0 1.4 %shard_map.46 = (bf16[128,1408]{1,0:T(8,128)(2,1)S(1)}, bf16[128,1664]{1,0:T(8,128)(2,1)S(1)}) custom-call(bf16[128,8192]{1,0:T(8,128)(2,1)} %queries.19), custom_call_target="tpu_custom_call" | custom-call | flops 1800000000 | tf_op jit(solution)/shard_map/pallas_call | solution.py:218
  1.4 3.1 %collective-permute-start = (bf16[128,1408]{1,0:T(8,128)(2,1)S(1)}, bf16[128,1408]{1,0:T(8,128)(2,1)S(1)}, u32[]{:S(2)}, u32[]{:S(2)}) collective-permute-start(bf16[128,1408]{1,0:T(8,128)(2,1)S(1)} %get-tuple-element.24), channel_id=1, source_target_pairs={{0,4},{2,6},{4,8},{6,10},{8,12},{10,14},{12,0},{14,2},{1,5},{3,7},... | collective-permute-start | bytes 1081352 | tf_op jit(solution)/shard_map/ppermute | solution.py:264
  4.5 1.6 %collective-permute-start.1 = (bf16[128,1664]{1,0:T(8,128)(2,1)S(1)}, bf16[128,1664]{1,0:T(8,128)(2,1)S(1)}, u32[]{:S(2)}, u32[]{:S(2)}) collective-permute-start(bf16[128,1664]{1,0:T(8,128)(2,1)S(1)} %get-tuple-element.19), channel_id=1, source_target_pairs={{0,4},{2,6},{4,8},{6,10},{8,12},{10,14},{12,0},{14,2},{1,5},{3,7},... | collective-permute-start | bytes 1277960 | tf_op jit(solution)/shard_map/ppermute | solution.py:264
  6.7 0.0 copy-done
  6.8 0.0 copy-done.1
  6.8 4.8 %shard_map.47 = (f32[320,128]{1,0:T(8,128)S(1)}, f32[320,128]{1,0:T(8,128)S(1)}, bf16[640,4096]{1,0:T(8,128)(2,1)S(1)}, f32[1,8192]{1,0:T(1,128)S(1)}) custom-call(s32[1]{0:T(128)S(6)} %copy.5.counts, bf16[640,8192]{1,0:T(8,128)(2,1)} %documents.3, bf16[128,8192]{1,0:T(8,128)(2,1)S(1)} %copy-done, f32[1,8192]{1,0:T(1,128)S(1)} %bitcast.1), custom_call_target="tpu_custom_call" | custom-call | flops 1800000000 | tf_op jit(solution)/shard_map/pallas_call | solution.py:274
  11.6 4.2 %collective-permute-done.received.refs_1_ = bf16[128,1408]{1,0:T(8,128)(2,1)S(1)} collective-permute-done((bf16[128,1408]{1,0:T(8,128)(2,1)S(1)}, bf16[128,1408]{1,0:T(8,128)(2,1)S(1)}, u32[]{:S(2)}, u32[]{:S(2)}) %collective-permute-start) | collective-permute-done | bytes 360480 | tf_op jit(solution)/shard_map/ppermute | solution.py:264
  15.8 1.9 %collective-permute-start.4 = (bf16[128,1408]{1,0:T(8,128)(2,1)S(1)}, bf16[128,1408]{1,0:T(8,128)(2,1)S(1)}, u32[]{:S(2)}, u32[]{:S(2)}) collective-permute-start(bf16[128,1408]{1,0:T(8,128)(2,1)S(1)} %shard_map.48.refs_0_), channel_id=1, source_target_pairs={{0,2},{2,0},{4,6},{6,4},{8,10},{10,8},{12,14},{14,12},{1,3},{3,1},... | collective-permute-start | bytes 1081352 | tf_op jit(solution)/shard_map/ppermute | solution.py:235
  17.8 0.1 shard_map.49.refs_3_
  17.9 0.1 collective-permute-start.6
  18.0 1.6 %collective-permute-start.5 = (bf16[128,1408]{1,0:T(8,128)(2,1)S(1)}, bf16[128,1408]{1,0:T(8,128)(2,1)S(1)}, u32[]{:S(2)}, u32[]{:S(2)}) collective-permute-start(bf16[128,1408]{1,0:T(8,128)(2,1)S(1)} %collective-permute-done.received.refs_1_), channel_id=1, source_target_pairs={{0,16},{16,0},{1,17},{17,1},{2,18},{18,2},{3,19},{19,3},{4,20},{20... | collective-permute-start | bytes 1081352 | tf_op jit(solution)/shard_map/ppermute | solution.py:257
  19.5 4.8 %shard_map.50 = (f32[320,128]{1,0:T(8,128)S(1)}, f32[320,128]{1,0:T(8,128)S(1)}, bf16[640,4096]{1,0:T(8,128)(2,1)S(1)}) custom-call(s32[1]{0:T(128)S(6)} %copy.5.counts, bf16[640,8192]{1,0:T(8,128)(2,1)} %documents.3, bf16[128,8192]{1,0:T(8,128)(2,1)S(1)} %copy-done, f32[1,8192]{1,0:T(1,128)S(1)} %get-tuple-element.21.refs_0_.inverse, ...), custom_call_target="tpu_custom_call" | custom-call | flops 1800000000 | tf_op jit(solution)/shard_map/pallas_call | solution.py:274
  24.3 0.6 %collective-permute-done.1.received.refs_1_ = bf16[128,1664]{1,0:T(8,128)(2,1)S(1)} collective-permute-done((bf16[128,1664]{1,0:T(8,128)(2,1)S(1)}, bf16[128,1664]{1,0:T(8,128)(2,1)S(1)}, u32[]{:S(2)}, u32[]{:S(2)}) %collective-permute-start.1) | collective-permute-done | bytes 426016 | tf_op jit(solution)/shard_map/ppermute | solution.py:264
  24.9 0.1 shard_map.51.refs_0_
  25.0 2.0 %collective-permute-start.3 = (bf16[128,1664]{1,0:T(8,128)(2,1)S(1)}, bf16[128,1664]{1,0:T(8,128)(2,1)S(1)}, u32[]{:S(2)}, u32[]{:S(2)}) collective-permute-start(bf16[128,1664]{1,0:T(8,128)(2,1)S(1)} %shard_map.51.refs_0_), channel_id=1, source_target_pairs={{0,2},{2,0},{4,6},{6,4},{8,10},{10,8},{12,14},{14,12},{1,3},{3,1},... | collective-permute-start | bytes 1277960 | tf_op jit(solution)/shard_map/ppermute | solution.py:235
  27.0 0.1 shard_map.52.refs_2_
  27.1 0.1 collective-permute-start.2
  27.2 0.0 collective-permute-done.4.refs_0_
  27.2 1.6 %collective-permute-start.12 = (bf16[128,1408]{1,0:T(8,128)(2,1)S(1)}, bf16[128,1408]{1,0:T(8,128)(2,1)S(1)}, u32[]{:S(2)}, u32[]{:S(2)}) collective-permute-start(bf16[128,1408]{1,0:T(8,128)(2,1)S(1)} %collective-permute-done.4.refs_0_), channel_id=1, source_target_pairs={{0,16},{16,0},{1,17},{17,1},{2,18},{18,2},{3,19},{19,3},{4,20},{20... | collective-permute-start | bytes 1081352 | tf_op jit(solution)/shard_map/ppermute | solution.py:257
  28.7 0.0 collective-permute-done.5.refs_3_
  28.7 0.7 %shard_map.53.refs_0_.refs_2_ = f32[640,256]{1,0:T(8,128)S(1)} custom-call(s32[1]{0:T(128)S(6)} %copy.5.counts, bf16[640,4096]{1,0:T(8,128)(2,1)S(1)} %get-tuple-element.27.held0, bf16[640,4096]{1,0:T(8,128)(2,1)S(1)} %get-tuple-element.28.held1, f32[1,8192]{1,0:T(1,128)S(1)} %get-tuple-element.21.refs_0_.inverse, ...), custom_call_target="tpu_custom_call" | custom-call | flops 1800000000 | tf_op jit(solution)/shard_map/pallas_call | solution.py:247
  29.5 0.6 %collective-permute-done.6.received.refs_1_ = bf16[128,1024]{1,0:T(8,128)(2,1)S(1)} collective-permute-done((bf16[128,1024]{1,0:T(8,128)(2,1)S(1)}, bf16[128,1024]{1,0:T(8,128)(2,1)S(1)}, u32[]{:S(2)}, u32[]{:S(2)}) %collective-permute-start.6) | collective-permute-done | bytes 262176 | tf_op jit(solution)/shard_map/ppermute | solution.py:240
  30.1 0.2 shard_map.55.refs_3_
  30.3 2.3 %collective-permute-start.11 = (bf16[128,1024]{1,0:T(8,128)(2,1)S(1)}, bf16[128,1024]{1,0:T(8,128)(2,1)S(1)}, u32[]{:S(2)}, u32[]{:S(2)}) collective-permute-start(bf16[128,1024]{1,0:T(8,128)(2,1)S(1)} %shard_map.54.refs_0_), channel_id=1, source_target_pairs={{0,2},{2,0},{4,6},{6,4},{8,10},{10,8},{12,14},{14,12},{1,3},{3,1},... | collective-permute-start | bytes 786440 | tf_op jit(solution)/shard_map/ppermute | solution.py:235
  32.6 0.0 collective-permute-start.10
  32.6 5.2 %collective-permute-done.3.refs_0_ = bf16[128,1664]{1,0:T(8,128)(2,1)S(1)} collective-permute-done((bf16[128,1664]{1,0:T(8,128)(2,1)S(1)}, bf16[128,1664]{1,0:T(8,128)(2,1)S(1)}, u32[]{:S(2)}, u32[]{:S(2)}) %collective-permute-start.3) | collective-permute-done | bytes 426016 | tf_op jit(solution)/shard_map/ppermute | solution.py:235
  37.8 1.7 %collective-permute-start.9 = (bf16[128,1664]{1,0:T(8,128)(2,1)S(1)}, bf16[128,1664]{1,0:T(8,128)(2,1)S(1)}, u32[]{:S(2)}, u32[]{:S(2)}) collective-permute-start(bf16[128,1664]{1,0:T(8,128)(2,1)S(1)} %collective-permute-done.3.refs_0_), channel_id=1, source_target_pairs={{0,16},{16,0},{1,17},{17,1},{2,18},{18,2},{3,19},{19,3},{4,20},{20... | collective-permute-start | bytes 1277960 | tf_op jit(solution)/shard_map/ppermute | solution.py:257
  39.5 0.8 %shard_map.56.refs_0_.refs_4_ = f32[640,256]{1,0:T(8,128)S(1)} custom-call(s32[1]{0:T(128)S(6)} %copy.5.counts, bf16[640,4096]{1,0:T(8,128)(2,1)S(1)} %get-tuple-element.27.held0, bf16[640,4096]{1,0:T(8,128)(2,1)S(1)} %get-tuple-element.28.held1, f32[1,8192]{1,0:T(1,128)S(1)} %get-tuple-element.21.refs_0_.inverse, ...), custom_call_target="tpu_custom_call" | custom-call | flops 1800000000 | tf_op jit(solution)/shard_map/pallas_call | solution.py:247
  40.4 0.0 collective-permute-done.2.received.refs_1_
  40.4 0.1 shard_map.57.refs_5_
  40.4 1.8 %collective-permute-start.8 = (bf16[128,1024]{1,0:T(8,128)(2,1)S(1)}, bf16[128,1024]{1,0:T(8,128)(2,1)S(1)}, u32[]{:S(2)}, u32[]{:S(2)}) collective-permute-start(bf16[128,1024]{1,0:T(8,128)(2,1)S(1)} %shard_map.57.refs_5_), channel_id=1, source_target_pairs={{0,2},{2,0},{4,6},{6,4},{8,10},{10,8},{12,14},{14,12},{1,3},{3,1},... | collective-permute-start | bytes 786440 | tf_op jit(solution)/shard_map/ppermute | solution.py:235
  42.2 1.2 %collective-permute-done.11.refs_0_ = bf16[128,1024]{1,0:T(8,128)(2,1)S(1)} collective-permute-done((bf16[128,1024]{1,0:T(8,128)(2,1)S(1)}, bf16[128,1024]{1,0:T(8,128)(2,1)S(1)}, u32[]{:S(2)}, u32[]{:S(2)}) %collective-permute-start.11) | collective-permute-done | bytes 262176 | tf_op jit(solution)/shard_map/ppermute | solution.py:235
  43.4 0.0 collective-permute-start.7
  43.4 0.0 collective-permute-done.12.refs_2_
  43.4 1.1 %shard_map.58.refs_2_ = f32[640,256]{1,0:T(8,128)S(1)} custom-call(s32[1]{0:T(128)S(6)} %copy.5.counts, bf16[640,4096]{1,0:T(8,128)(2,1)S(1)} %get-tuple-element.27.held0, bf16[640,4096]{1,0:T(8,128)(2,1)S(1)} %get-tuple-element.28.held1, f32[1,8192]{1,0:T(1,128)S(1)} %get-tuple-element.21.refs_0_.inverse, ...), custom_call_target="tpu_custom_call" | custom-call | flops 1800000000 | tf_op jit(solution)/shard_map/pallas_call | solution.py:247
  44.5 0.3 collective-permute-done.7.refs_3_.got0
  44.8 0.0 collective-permute-done.10.refs_1_
  44.8 1.1 %collective-permute-done.9.refs_0_ = bf16[128,1664]{1,0:T(8,128)(2,1)S(1)} collective-permute-done((bf16[128,1664]{1,0:T(8,128)(2,1)S(1)}, bf16[128,1664]{1,0:T(8,128)(2,1)S(1)}, u32[]{:S(2)}, u32[]{:S(2)}) %collective-permute-start.9) | collective-permute-done | bytes 426016 | tf_op jit(solution)/shard_map/ppermute | solution.py:257
  45.9 0.8 %shard_map.59.refs_2_ = f32[640,256]{1,0:T(8,128)S(1)} custom-call(s32[1]{0:T(128)S(6)} %copy.5.counts, bf16[640,4096]{1,0:T(8,128)(2,1)S(1)} %get-tuple-element.27.held0, bf16[640,4096]{1,0:T(8,128)(2,1)S(1)} %get-tuple-element.28.held1, f32[1,8192]{1,0:T(1,128)S(1)} %get-tuple-element.21.refs_0_.inverse, ...), custom_call_target="tpu_custom_call" | custom-call | flops 1800000000 | tf_op jit(solution)/shard_map/pallas_call | solution.py:247
  46.7 0.1 collective-permute-done.8.refs_0_
  46.9 0.4 shard_map.60.refs_3_
  47.3 0.1 collective-permute-start.13
  47.3 0.4 shard_map.61.mine
  47.7 1.2 %collective-permute-done.13.got = f32[320,256]{1,0:T(8,128)S(1)} collective-permute-done((f32[320,256]{1,0:T(8,128)S(1)}, f32[320,256]{1,0:T(8,128)S(1)}, u32[]{:S(2)}, u32[]{:S(2)}) %collective-permute-start.13) | collective-permute-done | bytes 327712 | tf_op jit(solution)/shard_map/ppermute | solution.py:307
  49.0 0.8 %shard_map.62 = f32[320,384]{1,0:T(8,128)} custom-call(f32[320,128]{1,0:T(8,128)S(1)} %get-tuple-element.25.mine0, f32[320,128]{1,0:T(8,128)S(1)} %collective-permute-done.7.refs_3_.got0, f32[320,256]{1,0:T(8,128)S(1)} %shard_map.61.mine, f32[320,256]{1,0:T(8,128)S(1)} %collective-permute-done.13.got), custom_call_target="tpu_custom_call" | custom-call | flops 1800000000 | tf_op jit(solution)/shard_map/pallas_call | solution.py:309
  (2 shorter events, 0.1 us)
Async XLA Ops:
  0.0 6.7 %copy-start = (bf16[128,8192]{1,0:T(8,128)(2,1)S(1)}, bf16[128,8192]{1,0:T(8,128)(2,1)}, u32[]{:S(2)}) copy-start(bf16[128,8192]{1,0:T(8,128)(2,1)} %queries.19) | copy-start | bytes 6291460
  0.0 6.7 %copy-start.1 = (f32[8192]{0:T(1024)S(1)}, f32[8192]{0:T(1024)}, u32[]{:S(2)}) copy-start(f32[8192]{0:T(1024)} %param.7) | copy-start | bytes 98308
  1.4 14.3 %collective-permute-start = (bf16[128,1408]{1,0:T(8,128)(2,1)S(1)}, bf16[128,1408]{1,0:T(8,128)(2,1)S(1)}, u32[]{:S(2)}, u32[]{:S(2)}) collective-permute-start(bf16[128,1408]{1,0:T(8,128)(2,1)S(1)} %get-tuple-element.24), channel_id=1, source_target_pairs={{0,4},{2,6},{4,8},{6,10},{8,12},{10,14},{12,0},{14,2},{1,5},{3,7},... | collective-permute-start | bytes 1081352 | tf_op jit(solution)/shard_map/ppermute | solution.py:264
  4.5 20.4 %collective-permute-start.1 = (bf16[128,1664]{1,0:T(8,128)(2,1)S(1)}, bf16[128,1664]{1,0:T(8,128)(2,1)S(1)}, u32[]{:S(2)}, u32[]{:S(2)}) collective-permute-start(bf16[128,1664]{1,0:T(8,128)(2,1)S(1)} %get-tuple-element.19), channel_id=1, source_target_pairs={{0,4},{2,6},{4,8},{6,10},{8,12},{10,14},{12,0},{14,2},{1,5},{3,7},... | collective-permute-start | bytes 1277960 | tf_op jit(solution)/shard_map/ppermute | solution.py:264
  15.8 11.3 %collective-permute-start.4 = (bf16[128,1408]{1,0:T(8,128)(2,1)S(1)}, bf16[128,1408]{1,0:T(8,128)(2,1)S(1)}, u32[]{:S(2)}, u32[]{:S(2)}) collective-permute-start(bf16[128,1408]{1,0:T(8,128)(2,1)S(1)} %shard_map.48.refs_0_), channel_id=1, source_target_pairs={{0,2},{2,0},{4,6},{6,4},{8,10},{10,8},{12,14},{14,12},{1,3},{3,1},... | collective-permute-start | bytes 1081352 | tf_op jit(solution)/shard_map/ppermute | solution.py:235
  17.9 12.2 %collective-permute-start.6 = (bf16[128,1024]{1,0:T(8,128)(2,1)S(1)}, bf16[128,1024]{1,0:T(8,128)(2,1)S(1)}, u32[]{:S(2)}, u32[]{:S(2)}) collective-permute-start(bf16[128,1024]{1,0:T(8,128)(2,1)S(1)} %shard_map.49.refs_3_), channel_id=1, source_target_pairs={{0,4},{2,6},{4,8},{6,10},{8,12},{10,14},{12,0},{14,2},{1,5},{3,7},... | collective-permute-start | bytes 786440 | tf_op jit(solution)/shard_map/ppermute | solution.py:240
  18.0 10.8 %collective-permute-start.5 = (bf16[128,1408]{1,0:T(8,128)(2,1)S(1)}, bf16[128,1408]{1,0:T(8,128)(2,1)S(1)}, u32[]{:S(2)}, u32[]{:S(2)}) collective-permute-start(bf16[128,1408]{1,0:T(8,128)(2,1)S(1)} %collective-permute-done.received.refs_1_), channel_id=1, source_target_pairs={{0,16},{16,0},{1,17},{17,1},{2,18},{18,2},{3,19},{19,3},{4,20},{20... | collective-permute-start | bytes 1081352 | tf_op jit(solution)/shard_map/ppermute | solution.py:257
  25.0 12.8 %collective-permute-start.3 = (bf16[128,1664]{1,0:T(8,128)(2,1)S(1)}, bf16[128,1664]{1,0:T(8,128)(2,1)S(1)}, u32[]{:S(2)}, u32[]{:S(2)}) collective-permute-start(bf16[128,1664]{1,0:T(8,128)(2,1)S(1)} %shard_map.51.refs_0_), channel_id=1, source_target_pairs={{0,2},{2,0},{4,6},{6,4},{8,10},{10,8},{12,14},{14,12},{1,3},{3,1},... | collective-permute-start | bytes 1277960 | tf_op jit(solution)/shard_map/ppermute | solution.py:235
  27.1 13.3 %collective-permute-start.2 = (bf16[128,1024]{1,0:T(8,128)(2,1)S(1)}, bf16[128,1024]{1,0:T(8,128)(2,1)S(1)}, u32[]{:S(2)}, u32[]{:S(2)}) collective-permute-start(bf16[128,1024]{1,0:T(8,128)(2,1)S(1)} %shard_map.52.refs_2_), channel_id=1, source_target_pairs={{0,4},{2,6},{4,8},{6,10},{8,12},{10,14},{12,0},{14,2},{1,5},{3,7},... | collective-permute-start | bytes 786440 | tf_op jit(solution)/shard_map/ppermute | solution.py:240
  27.2 16.2 %collective-permute-start.12 = (bf16[128,1408]{1,0:T(8,128)(2,1)S(1)}, bf16[128,1408]{1,0:T(8,128)(2,1)S(1)}, u32[]{:S(2)}, u32[]{:S(2)}) collective-permute-start(bf16[128,1408]{1,0:T(8,128)(2,1)S(1)} %collective-permute-done.4.refs_0_), channel_id=1, source_target_pairs={{0,16},{16,0},{1,17},{17,1},{2,18},{18,2},{3,19},{19,3},{4,20},{20... | collective-permute-start | bytes 1081352 | tf_op jit(solution)/shard_map/ppermute | solution.py:257
  30.3 13.1 %collective-permute-start.11 = (bf16[128,1024]{1,0:T(8,128)(2,1)S(1)}, bf16[128,1024]{1,0:T(8,128)(2,1)S(1)}, u32[]{:S(2)}, u32[]{:S(2)}) collective-permute-start(bf16[128,1024]{1,0:T(8,128)(2,1)S(1)} %shard_map.54.refs_0_), channel_id=1, source_target_pairs={{0,2},{2,0},{4,6},{6,4},{8,10},{10,8},{12,14},{14,12},{1,3},{3,1},... | collective-permute-start | bytes 786440 | tf_op jit(solution)/shard_map/ppermute | solution.py:235
  32.6 12.2 %collective-permute-start.10 = (bf16[128,1664]{1,0:T(8,128)(2,1)S(1)}, bf16[128,1664]{1,0:T(8,128)(2,1)S(1)}, u32[]{:S(2)}, u32[]{:S(2)}) collective-permute-start(bf16[128,1664]{1,0:T(8,128)(2,1)S(1)} %shard_map.55.refs_3_), channel_id=1, source_target_pairs={{0,4},{2,6},{4,8},{6,10},{8,12},{10,14},{12,0},{14,2},{1,5},{3,7},... | collective-permute-start | bytes 1277960 | tf_op jit(solution)/shard_map/ppermute | solution.py:240
  37.8 8.1 %collective-permute-start.9 = (bf16[128,1664]{1,0:T(8,128)(2,1)S(1)}, bf16[128,1664]{1,0:T(8,128)(2,1)S(1)}, u32[]{:S(2)}, u32[]{:S(2)}) collective-permute-start(bf16[128,1664]{1,0:T(8,128)(2,1)S(1)} %collective-permute-done.3.refs_0_), channel_id=1, source_target_pairs={{0,16},{16,0},{1,17},{17,1},{2,18},{18,2},{3,19},{19,3},{4,20},{20... | collective-permute-start | bytes 1277960 | tf_op jit(solution)/shard_map/ppermute | solution.py:257
  40.4 6.4 %collective-permute-start.8 = (bf16[128,1024]{1,0:T(8,128)(2,1)S(1)}, bf16[128,1024]{1,0:T(8,128)(2,1)S(1)}, u32[]{:S(2)}, u32[]{:S(2)}) collective-permute-start(bf16[128,1024]{1,0:T(8,128)(2,1)S(1)} %shard_map.57.refs_5_), channel_id=1, source_target_pairs={{0,2},{2,0},{4,6},{6,4},{8,10},{10,8},{12,14},{14,12},{1,3},{3,1},... | collective-permute-start | bytes 786440 | tf_op jit(solution)/shard_map/ppermute | solution.py:235
  43.4 1.4 %collective-permute-start.7 = (f32[320,128]{1,0:T(8,128)S(1)}, f32[320,128]{1,0:T(8,128)S(1)}, u32[]{:S(2)}, u32[]{:S(2)}) collective-permute-start(f32[320,128]{1,0:T(8,128)S(1)} %get-tuple-element.30.refs_0_), channel_id=1, source_target_pairs={{0,1},{1,0},{2,3},{3,2},{4,5},{5,4},{6,7},{7,6},{8,9},{9,8},{10,11... | collective-permute-start | bytes 491528 | tf_op jit(solution)/shard_map/ppermute | solution.py:303
  47.3 1.7 %collective-permute-start.13 = (f32[320,256]{1,0:T(8,128)S(1)}, f32[320,256]{1,0:T(8,128)S(1)}, u32[]{:S(2)}, u32[]{:S(2)}) collective-permute-start(f32[320,256]{1,0:T(8,128)S(1)} %shard_map.60.refs_3_), channel_id=1, source_target_pairs={{0,1},{1,0},{2,3},{3,2},{4,5},{5,4},{6,7},{7,6},{8,9},{9,8},{10,11... | collective-permute-start | bytes 983048 | tf_op jit(solution)/shard_map/ppermute | solution.py:307

commit v7 on v5

--- a/solution.py
+++ b/solution.py
@@ -13,11 +13,12 @@
 CHUNKS = len(SIZES)
 DIRECT = 5
 OWN_MIB = (44, 40)
+TILE = 4
 VMEM = pl.BlockSpec(memory_space=pltpu.VMEM)
 SMEM = pl.BlockSpec(memory_space=pltpu.SMEM)
 HBM = pl.BlockSpec(memory_space=pltpu.HBM)
 ANY = pl.BlockSpec(memory_space=pl.ANY)
-COST = pl.CostEstimate(flops=16 * 10**8, bytes_accessed=0, transcendentals=0)
+COST = pl.CostEstimate(flops=16*10**8, bytes_accessed=0, transcendentals=0)
 MIB = 1024 * 1024
 
 
@@ -83,52 +84,57 @@
         received_copy.wait()
 
 
-def own_kernel(part, pieces, factor, counts, documents, queries, *refs):
+def tile_of(dims):
+    return TILE * dims // sum(SIZES)
+
+
+def own_kernel(part, factor, counts, documents, queries, *refs):
     if part == 0:
-        eigenvalues, theirs, mine, held, inverse, sem = refs[0], *refs[-5:]
-        before = None
+        eigenvalues, sums, held, inverse, sem = refs[0], *refs[-4:]
     else:
-        inverse, before, theirs, mine, held, sem = refs[0], refs[1:3], *refs[-4:]
+        inverse, before, theirs, mine, held, sums, sem = refs[0], refs[1], *refs[-5:]
     layer = lax.axis_index("layer")
     half = documents.shape[0] // 2
     dims = documents.shape[1]
-    width = dims // 2 // pieces
+    tile = tile_of(dims)
     first = half_columns(part, dims).start
-    copies = []
-    for i in range(pieces):
-        start = pl.multiple_of(first + i * width, width)
-        for at, row in enumerate((1 - layer, layer)):
-            copies.append(
-                pltpu.make_async_copy(
-                    documents.at[pl.ds(pl.multiple_of(row * half, half), half), pl.ds(start, width)],
-                    held.at[pl.ds(at * half, half), pl.ds(i * width, width)],
-                    sem.at[i, at],
-                )
+
+    def copies(i):
+        start = pl.multiple_of(first + i * tile, tile)
+        return [
+            pltpu.make_async_copy(
+                documents.at[pl.ds(pl.multiple_of(row * half, half), half), pl.ds(start, tile)],
+                held.at[pl.ds(side * half, half), pl.ds(pl.multiple_of(i * tile, tile), tile)],
+                sem.at[i, side],
             )
-    for copy in copies:
-        copy.start()
+            for side, row in enumerate((1 - layer, layer))
+        ]
+
+    @pl.loop(0, dims // 2 // tile)
+    def _(i):
+        for copy in copies(i):
+            copy.start()
+
     if part == 0:
         for start in range(0, dims, L_DIM):
             block = eigenvalues[:, start : start + L_DIM]
             damping = 0.1 * jnp.mean(block, axis=1, keepdims=True)
             inverse[:, start : start + L_DIM] = 1.0 / (block + damping)
-    for i in range(pieces):
-        columns = pl.ds(pl.multiple_of(first + i * width, width), width)
+        sums[...] = jnp.zeros_like(sums)
+    else:
+        sums[...] = before[...]
+
+    @pl.loop(0, dims // 2 // tile)
+    def _(i):
+        columns = pl.ds(pl.multiple_of(first + i * tile, tile), tile)
         scaled = (queries[:, columns].astype(jnp.float32) * inverse[:, columns]).astype(jnp.bfloat16)
-        for side, out in enumerate((theirs, mine)):
-            copies[2 * i + side].wait()
-            term = products(
-                held[side * half : (side + 1) * half, i * width : (i + 1) * width], scaled
-            )
-            if i > 0:
-                out[...] += term
-            elif part == 0:
-                out[...] = term
-            else:
-                out[...] = before[side][...] + term
+        for copy in copies(i):
+            copy.wait()
+        sums[...] += products(held[:, pl.ds(pl.multiple_of(i * tile, tile), tile)], scaled)
+
     if part == 1:
-        theirs[...] *= scale_of(factor, counts, half, 0)
-        mine[...] *= scale_of(factor, counts, half, 1)
+        theirs[...] = sums[:half] * scale_of(factor, counts, half, 0)
+        mine[...] = sums[half:] * scale_of(factor, counts, half, 1)
 
 
 def held_of(k, held):
@@ -136,25 +142,29 @@
 
 
 def pair_kernel(ks, side, factor, fresh, counts, held0, held1, inverse, *refs):
-    count = len(ks)
-    chunks, out, block_buf = refs[: 2 * count], refs[-2], refs[-1]
+    chunks, out, block = refs[: 2 * len(ks)], refs[-2], refs[-1]
     dims = inverse.shape[1]
+    tile = tile_of(dims)
     size = out.shape[0]
     first = 0 if side is None else side * size
     rows = chunks[0].shape[0]
+    out[...] = jnp.zeros_like(out) if fresh else refs[2 * len(ks)][first : first + size]
     for i, k in enumerate(ks):
-        width = width_of(k, dims)
-        for b in range(2):
-            scaled = chunks[2 * i + b][...].astype(jnp.float32) * inverse[:, columns_of(k, dims)]
-            block_buf[pl.ds(b * rows, rows), :width] = scaled.astype(jnp.bfloat16)
         held = held_of(k, (held0, held1))
-        term = products(held[first : first + size, columns_of(k, dims, True)], block_buf[:, :width])
-        if i > 0:
-            out[...] += term
-        elif fresh:
-            out[...] = term
-        else:
-            out[...] = refs[2 * count][first : first + size] + term
+        at, held_at = columns_of(k, dims).start, columns_of(k, dims, True).start
+
+        @pl.loop(0, width_of(k, dims) // tile)
+        def _(t, i=i, held=held, at=at, held_at=held_at):
+            shift = t * tile
+            scale = inverse[:, pl.ds(pl.multiple_of(at + shift, tile), tile)]
+            for b in range(2):
+                chunk = chunks[2 * i + b][:, pl.ds(pl.multiple_of(shift, tile), tile)]
+                block[b * rows : (b + 1) * rows, :] = (chunk.astype(jnp.float32) * scale).astype(
+                    jnp.bfloat16
+                )
+            columns = pl.ds(pl.multiple_of(held_at + shift, tile), tile)
+            out[...] += products(held[first : first + size, columns], block[...])
+
     if side is not None:
         out[...] *= scale_of(factor, counts, size, side)
 
@@ -228,7 +238,7 @@
             floats(doc_rows if side is None else half, 2 * rows),
             [SMEM] + [VMEM] * len(operands) + [ANY] * len(until),
             VMEM,
-            [pltpu.VMEM((2 * rows, max(width_of(k, dims) for k in ks)), queries.dtype)],
+            [pltpu.VMEM((2 * rows, tile_of(dims)), queries.dtype)],
         )(counts, *operands, *until)
 
     def send_across(block, k, *until):
@@ -243,29 +253,30 @@
         far[k] = lax.ppermute(sent[k], "dp", ahead)
 
     def own_scores(part, *operands, until=()):
-        pieces = 4
-        outs = [
-            floats(half, rows),
-            floats(half, rows),
-            jax.ShapeDtypeStruct((doc_rows, dims // 2), documents.dtype),
-            floats(1, dims),
-        ][: 4 - part]
+        sums = floats(doc_rows, rows)
+        keep = jax.ShapeDtypeStruct((doc_rows, dims // 2), documents.dtype)
+        semaphores = pltpu.SemaphoreType.DMA((dims // 2 // tile_of(dims), 2))
+        if part == 0:
+            outs, scratch = [sums, keep, floats(1, dims)], [semaphores]
+        else:
+            outs = [floats(half, rows), floats(half, rows), keep]
+            scratch = [pltpu.VMEM(sums.shape, sums.dtype), semaphores]
         return call(
-            functools.partial(own_kernel, part, pieces, factor),
+            functools.partial(own_kernel, part, factor),
             outs,
             [SMEM, HBM] + [VMEM] * (1 + len(operands)) + [ANY] * len(until),
-            [VMEM] * len(outs),
-            [pltpu.SemaphoreType.DMA((pieces, 2))],
+            [VMEM] * 3,
+            scratch,
             vmem_mib=OWN_MIB[part],
         )(counts, documents, queries, *operands, *until)
 
     kept = lax.optimization_barrier((eigenvalues, sent[1]))[0].reshape(1, dims)
-    theirs0, mine0, held0, inverse = own_scores(0, kept)
+    own_sums, held0, inverse = own_scores(0, kept)
 
     out = step(0, inverse)
     out = send_ahead(2, out)
     send_across(far, 0, out)
-    theirs0, mine0, held1 = own_scores(1, inverse, theirs0, mine0, until=(out,))
+    theirs0, mine0, held1 = own_scores(1, inverse, own_sums, until=(out,))
     held = held0, held1
 
     out = step(1, theirs0)

time: 48.9 us -> 50.2 us (1.027)
  Pallas kernels: 15.2 us -> 17.8 us
  waiting for transfers between devices: 15.4 us -> 14 us
    pallas_call x5, Pallas kernels: 3.8 us -> 7.2 us  [pair_scores(): call(functools.partial(pair_kernel, ks, side, factor, sums is None), floa...]
    ppermute x1, waiting for transfers between devices: 0.96 us -> 0.11 us  [on_device(): got = lax.ppermute(theirs, 'layer', across)]
    pallas_call x2, Pallas kernels: 8.97 us -> 8.23 us  [own_scores(): call(functools.partial(own_kernel, part, factor), outs, [SMEM, HBM] + [VM...]
    ppermute x2, waiting for transfers between devices: 5.47 us -> 6.21 us  [on_device(): far[k] = lax.ppermute(sent[k], 'dp', ahead)]
    ppermute x4, waiting for transfers between devices: 7.74 us -> 7.2 us  [step(): near[k] = lax.ppermute(out, 'dp', pair)]
  transfers between devices with their start and end apart: 14 -> 14, of which waited for: 8 -> 7; matrix products, arithmetic and copies ran while one was open for 0% -> 0% of each run, Pallas kernels for 25% -> 28%
where the time goes in v7:
time: 50.2 us; the launch traced here: 50.1 us
  Pallas kernels  17.8 us (35%)
  starting transfers between devices  17.4 us (35%)
  waiting for transfers between devices  14 us (28%)
  between operations  0.85 us (2%)
    pallas_call x2, Pallas kernels, own_scores(): call(functools.partial(own_kernel, part, factor), outs, [SMEM, HBM] + [VM...  8.23 us
    ppermute x4, starting transfers between devices, step(): near[k] = lax.ppermute(out, 'dp', pair)  7.95 us
    ppermute x4, waiting for transfers between devices, step(): near[k] = lax.ppermute(out, 'dp', pair)  7.2 us
    pallas_call x5, Pallas kernels, pair_scores(): call(functools.partial(pair_kernel, ks, side, factor, sums is None), floa...  7.2 us
    ppermute x2, waiting for transfers between devices, on_device(): far[k] = lax.ppermute(sent[k], 'dp', ahead)  6.21 us
    ppermute x2, starting transfers between devices, on_device(): far[k] = lax.ppermute(sent[k], 'dp', ahead)  4.65 us
    ppermute x3, starting transfers between devices, send_across(): block[CHUNKS - 1 - k] = lax.ppermute(sent, 'groups', across)  4.54 us
    pallas_call x4, Pallas kernels, own_chunks(): call(functools.partial(chunk_kernel, ks), [chunk(k) for k in ks], [ANY] *...  1.38 us
  transfers between devices with their start and end apart: 14, of which 7 were waited for; matrix products, arithmetic and copies ran while one was open for 0% of the time, Pallas kernels for 28%

profile of v7, /device:TPU:0, one launch (start us, length us, event | category | flops | bytes accessed | tf_op | source)
XLA Modules:
  0.0 50.1 jit_solution(2431559497578877115)
XLA Ops:
  0.0 0.0 copy-start
  0.0 0.0 copy-start.1
  0.0 1.3 %shard_map.46 = (bf16[128,1536]{1,0:T(8,128)(2,1)S(1)}, bf16[128,1536]{1,0:T(8,128)(2,1)S(1)}) custom-call(bf16[128,8192]{1,0:T(8,128)(2,1)} %queries.19), custom_call_target="tpu_custom_call" | custom-call | flops 1600000000 | tf_op jit(solution)/shard_map/pallas_call | solution.py:207
  1.3 3.1 %collective-permute-start = (bf16[128,1536]{1,0:T(8,128)(2,1)S(1)}, bf16[128,1536]{1,0:T(8,128)(2,1)S(1)}, u32[]{:S(2)}, u32[]{:S(2)}) collective-permute-start(bf16[128,1536]{1,0:T(8,128)(2,1)S(1)} %get-tuple-element.22), channel_id=1, source_target_pairs={{0,4},{2,6},{4,8},{6,10},{8,12},{10,14},{12,0},{14,2},{1,5},{3,7},... | collective-permute-start | bytes 1179656 | tf_op jit(solution)/shard_map/ppermute | solution.py:253
  4.4 1.6 %collective-permute-start.1 = (bf16[128,1536]{1,0:T(8,128)(2,1)S(1)}, bf16[128,1536]{1,0:T(8,128)(2,1)S(1)}, u32[]{:S(2)}, u32[]{:S(2)}) collective-permute-start(bf16[128,1536]{1,0:T(8,128)(2,1)S(1)} %get-tuple-element.18), channel_id=1, source_target_pairs={{0,4},{2,6},{4,8},{6,10},{8,12},{10,14},{12,0},{14,2},{1,5},{3,7},... | collective-permute-start | bytes 1179656 | tf_op jit(solution)/shard_map/ppermute | solution.py:253
  6.6 0.0 copy-done
  6.6 0.0 copy-done.1
  6.6 4.1 %shard_map.47 = (f32[640,128]{1,0:T(8,128)S(1)}, bf16[640,4096]{1,0:T(8,128)(2,1)S(1)}, f32[1,8192]{1,0:T(1,128)S(1)}) custom-call(s32[1]{0:T(128)S(6)} %copy.5.counts, bf16[640,8192]{1,0:T(8,128)(2,1)} %documents.3, bf16[128,8192]{1,0:T(8,128)(2,1)S(1)} %copy-done, f32[1,8192]{1,0:T(1,128)S(1)} %bitcast.1), custom_call_target="tpu_custom_call" | custom-call | flops 1600000000 | tf_op jit(solution)/shard_map/pallas_call | solution.py:264
  10.7 5.6 %collective-permute-done.received.refs_1_ = bf16[128,1536]{1,0:T(8,128)(2,1)S(1)} collective-permute-done((bf16[128,1536]{1,0:T(8,128)(2,1)S(1)}, bf16[128,1536]{1,0:T(8,128)(2,1)S(1)}, u32[]{:S(2)}, u32[]{:S(2)}) %collective-permute-start) | collective-permute-done | bytes 393248 | tf_op jit(solution)/shard_map/ppermute | solution.py:253
  16.4 2.0 %collective-permute-start.4 = (bf16[128,1536]{1,0:T(8,128)(2,1)S(1)}, bf16[128,1536]{1,0:T(8,128)(2,1)S(1)}, u32[]{:S(2)}, u32[]{:S(2)}) collective-permute-start(bf16[128,1536]{1,0:T(8,128)(2,1)S(1)} %shard_map.48.refs_0_), channel_id=1, source_target_pairs={{0,2},{2,0},{4,6},{6,4},{8,10},{10,8},{12,14},{14,12},{1,3},{3,1},... | collective-permute-start | bytes 1179656 | tf_op jit(solution)/shard_map/ppermute | solution.py:224
  18.4 0.1 collective-permute-start.6
  18.5 1.6 %collective-permute-start.5 = (bf16[128,1536]{1,0:T(8,128)(2,1)S(1)}, bf16[128,1536]{1,0:T(8,128)(2,1)S(1)}, u32[]{:S(2)}, u32[]{:S(2)}) collective-permute-start(bf16[128,1536]{1,0:T(8,128)(2,1)S(1)} %collective-permute-done.received.refs_1_), channel_id=1, source_target_pairs={{0,16},{16,0},{1,17},{17,1},{2,18},{18,2},{3,19},{19,3},{4,20},{20... | collective-permute-start | bytes 1179656 | tf_op jit(solution)/shard_map/ppermute | solution.py:246
  20.0 4.1 %shard_map.50 = (f32[320,128]{1,0:T(8,128)S(1)}, f32[320,128]{1,0:T(8,128)S(1)}, bf16[640,4096]{1,0:T(8,128)(2,1)S(1)}) custom-call(s32[1]{0:T(128)S(6)} %copy.5.counts, bf16[640,8192]{1,0:T(8,128)(2,1)} %documents.3, bf16[128,8192]{1,0:T(8,128)(2,1)S(1)} %copy-done, f32[1,8192]{1,0:T(1,128)S(1)} %get-tuple-element.20.refs_0_.inverse, ...), custom_call_target="tpu_custom_call" | custom-call | flops 1600000000 | tf_op jit(solution)/shard_map/pallas_call | solution.py:264
  24.2 0.6 %collective-permute-done.1.received.refs_1_ = bf16[128,1536]{1,0:T(8,128)(2,1)S(1)} collective-permute-done((bf16[128,1536]{1,0:T(8,128)(2,1)S(1)}, bf16[128,1536]{1,0:T(8,128)(2,1)S(1)}, u32[]{:S(2)}, u32[]{:S(2)}) %collective-permute-start.1) | collective-permute-done | bytes 393248 | tf_op jit(solution)/shard_map/ppermute | solution.py:253
  24.8 2.0 %collective-permute-start.3 = (bf16[128,1536]{1,0:T(8,128)(2,1)S(1)}, bf16[128,1536]{1,0:T(8,128)(2,1)S(1)}, u32[]{:S(2)}, u32[]{:S(2)}) collective-permute-start(bf16[128,1536]{1,0:T(8,128)(2,1)S(1)} %shard_map.51.refs_0_), channel_id=1, source_target_pairs={{0,2},{2,0},{4,6},{6,4},{8,10},{10,8},{12,14},{14,12},{1,3},{3,1},... | collective-permute-start | bytes 1179656 | tf_op jit(solution)/shard_map/ppermute | solution.py:224
  26.8 0.1 collective-permute-start.2
  26.9 0.0 collective-permute-done.4.refs_0_
  26.9 1.6 %collective-permute-start.12 = (bf16[128,1536]{1,0:T(8,128)(2,1)S(1)}, bf16[128,1536]{1,0:T(8,128)(2,1)S(1)}, u32[]{:S(2)}, u32[]{:S(2)}) collective-permute-start(bf16[128,1536]{1,0:T(8,128)(2,1)S(1)} %collective-permute-done.4.refs_0_), channel_id=1, source_target_pairs={{0,16},{16,0},{1,17},{17,1},{2,18},{18,2},{3,19},{19,3},{4,20},{20... | collective-permute-start | bytes 1179656 | tf_op jit(solution)/shard_map/ppermute | solution.py:246
  28.5 0.0 collective-permute-done.5.refs_3_
  28.5 1.2 %shard_map.53.refs_0_.refs_2_ = f32[640,256]{1,0:T(8,128)S(1)} custom-call(s32[1]{0:T(128)S(6)} %copy.5.counts, bf16[640,4096]{1,0:T(8,128)(2,1)S(1)} %get-tuple-element.25.held0, bf16[640,4096]{1,0:T(8,128)(2,1)S(1)} %get-tuple-element.26.held1, f32[1,8192]{1,0:T(1,128)S(1)} %get-tuple-element.20.refs_0_.inverse, ...), custom_call_target="tpu_custom_call" | custom-call | flops 1600000000 | tf_op jit(solution)/shard_map/pallas_call | solution.py:236
  29.6 0.5 collective-permute-done.6.received.refs_1_
  30.1 2.1 %collective-permute-start.11 = (bf16[128,1024]{1,0:T(8,128)(2,1)S(1)}, bf16[128,1024]{1,0:T(8,128)(2,1)S(1)}, u32[]{:S(2)}, u32[]{:S(2)}) collective-permute-start(bf16[128,1024]{1,0:T(8,128)(2,1)S(1)} %shard_map.54.refs_0_), channel_id=1, source_target_pairs={{0,2},{2,0},{4,6},{6,4},{8,10},{10,8},{12,14},{14,12},{1,3},{3,1},... | collective-permute-start | bytes 786440 | tf_op jit(solution)/shard_map/ppermute | solution.py:224
  32.3 0.1 collective-permute-start.10
  32.4 4.6 %collective-permute-done.3.refs_0_ = bf16[128,1536]{1,0:T(8,128)(2,1)S(1)} collective-permute-done((bf16[128,1536]{1,0:T(8,128)(2,1)S(1)}, bf16[128,1536]{1,0:T(8,128)(2,1)S(1)}, u32[]{:S(2)}, u32[]{:S(2)}) %collective-permute-start.3) | collective-permute-done | bytes 393248 | tf_op jit(solution)/shard_map/ppermute | solution.py:224
  36.9 1.4 %collective-permute-start.9 = (bf16[128,1536]{1,0:T(8,128)(2,1)S(1)}, bf16[128,1536]{1,0:T(8,128)(2,1)S(1)}, u32[]{:S(2)}, u32[]{:S(2)}) collective-permute-start(bf16[128,1536]{1,0:T(8,128)(2,1)S(1)} %collective-permute-done.3.refs_0_), channel_id=1, source_target_pairs={{0,16},{16,0},{1,17},{17,1},{2,18},{18,2},{3,19},{19,3},{4,20},{20... | collective-permute-start | bytes 1179656 | tf_op jit(solution)/shard_map/ppermute | solution.py:246
  38.4 1.2 %shard_map.56.refs_0_.refs_4_ = f32[640,256]{1,0:T(8,128)S(1)} custom-call(s32[1]{0:T(128)S(6)} %copy.5.counts, bf16[640,4096]{1,0:T(8,128)(2,1)S(1)} %get-tuple-element.25.held0, bf16[640,4096]{1,0:T(8,128)(2,1)S(1)} %get-tuple-element.26.held1, f32[1,8192]{1,0:T(1,128)S(1)} %get-tuple-element.20.refs_0_.inverse, ...), custom_call_target="tpu_custom_call" | custom-call | flops 1600000000 | tf_op jit(solution)/shard_map/pallas_call | solution.py:236
  39.5 0.0 collective-permute-done.2.received.refs_1_
  39.5 0.1 shard_map.57.refs_5_
  39.6 1.9 %collective-permute-start.8 = (bf16[128,1024]{1,0:T(8,128)(2,1)S(1)}, bf16[128,1024]{1,0:T(8,128)(2,1)S(1)}, u32[]{:S(2)}, u32[]{:S(2)}) collective-permute-start(bf16[128,1024]{1,0:T(8,128)(2,1)S(1)} %shard_map.57.refs_5_), channel_id=1, source_target_pairs={{0,2},{2,0},{4,6},{6,4},{8,10},{10,8},{12,14},{14,12},{1,3},{3,1},... | collective-permute-start | bytes 786440 | tf_op jit(solution)/shard_map/ppermute | solution.py:224
  41.5 1.1 %collective-permute-done.11.refs_0_ = bf16[128,1024]{1,0:T(8,128)(2,1)S(1)} collective-permute-done((bf16[128,1024]{1,0:T(8,128)(2,1)S(1)}, bf16[128,1024]{1,0:T(8,128)(2,1)S(1)}, u32[]{:S(2)}, u32[]{:S(2)}) %collective-permute-start.11) | collective-permute-done | bytes 262176 | tf_op jit(solution)/shard_map/ppermute | solution.py:224
  42.6 0.0 collective-permute-start.7
  42.6 0.0 collective-permute-done.12.refs_2_
  42.6 1.9 %shard_map.58.refs_4_ = f32[640,256]{1,0:T(8,128)S(1)} custom-call(s32[1]{0:T(128)S(6)} %copy.5.counts, bf16[640,4096]{1,0:T(8,128)(2,1)S(1)} %get-tuple-element.25.held0, bf16[640,4096]{1,0:T(8,128)(2,1)S(1)} %get-tuple-element.26.held1, f32[1,8192]{1,0:T(1,128)S(1)} %get-tuple-element.20.refs_0_.inverse, ...), custom_call_target="tpu_custom_call" | custom-call | flops 1600000000 | tf_op jit(solution)/shard_map/pallas_call | solution.py:236
  44.5 0.0 collective-permute-done.7.refs_5_.got0
  44.5 1.5 %collective-permute-done.8.refs_0_ = bf16[128,1024]{1,0:T(8,128)(2,1)S(1)} collective-permute-done((bf16[128,1024]{1,0:T(8,128)(2,1)S(1)}, bf16[128,1024]{1,0:T(8,128)(2,1)S(1)}, u32[]{:S(2)}, u32[]{:S(2)}) %collective-permute-start.8) | collective-permute-done | bytes 262176 | tf_op jit(solution)/shard_map/ppermute | solution.py:224
  46.0 0.0 collective-permute-done.9.refs_2_
  46.0 0.0 collective-permute-done.10.refs_3_
  46.0 1.5 %shard_map.59.refs_5_ = f32[320,256]{1,0:T(8,128)S(1)} custom-call(s32[1]{0:T(128)S(6)} %copy.5.counts, bf16[640,4096]{1,0:T(8,128)(2,1)S(1)} %get-tuple-element.25.held0, bf16[640,4096]{1,0:T(8,128)(2,1)S(1)} %get-tuple-element.26.held1, f32[1,8192]{1,0:T(1,128)S(1)} %get-tuple-element.20.refs_0_.inverse, ...), custom_call_target="tpu_custom_call" | custom-call | flops 1600000000 | tf_op jit(solution)/shard_map/pallas_call | solution.py:236
  47.5 0.1 collective-permute-start.13
  47.6 1.5 %shard_map.60.mine = f32[320,256]{1,0:T(8,128)S(1)} custom-call(s32[1]{0:T(128)S(6)} %copy.5.counts, bf16[640,4096]{1,0:T(8,128)(2,1)S(1)} %get-tuple-element.25.held0, bf16[640,4096]{1,0:T(8,128)(2,1)S(1)} %get-tuple-element.26.held1, f32[1,8192]{1,0:T(1,128)S(1)} %get-tuple-element.20.refs_0_.inverse, ...), custom_call_target="tpu_custom_call" | custom-call | flops 1600000000 | tf_op jit(solution)/shard_map/pallas_call | solution.py:236
  49.1 0.1 collective-permute-done.13.got
  49.2 0.8 %shard_map.61 = f32[320,384]{1,0:T(8,128)} custom-call(f32[320,128]{1,0:T(8,128)S(1)} %get-tuple-element.23.mine0, f32[320,128]{1,0:T(8,128)S(1)} %collective-permute-done.7.refs_5_.got0, f32[320,256]{1,0:T(8,128)S(1)} %shard_map.60.mine, f32[320,256]{1,0:T(8,128)S(1)} %collective-permute-done.13.got), custom_call_target="tpu_custom_call" | custom-call | flops 1600000000 | tf_op jit(solution)/shard_map/pallas_call | solution.py:298
  (6 shorter events, 0.2 us)
Async XLA Ops:
  0.0 6.6 %copy-start = (bf16[128,8192]{1,0:T(8,128)(2,1)S(1)}, bf16[128,8192]{1,0:T(8,128)(2,1)}, u32[]{:S(2)}) copy-start(bf16[128,8192]{1,0:T(8,128)(2,1)} %queries.19) | copy-start | bytes 6291460
  0.0 6.6 %copy-start.1 = (f32[8192]{0:T(1024)S(1)}, f32[8192]{0:T(1024)}, u32[]{:S(2)}) copy-start(f32[8192]{0:T(1024)} %param.7) | copy-start | bytes 98308
  1.3 15.0 %collective-permute-start = (bf16[128,1536]{1,0:T(8,128)(2,1)S(1)}, bf16[128,1536]{1,0:T(8,128)(2,1)S(1)}, u32[]{:S(2)}, u32[]{:S(2)}) collective-permute-start(bf16[128,1536]{1,0:T(8,128)(2,1)S(1)} %get-tuple-element.22), channel_id=1, source_target_pairs={{0,4},{2,6},{4,8},{6,10},{8,12},{10,14},{12,0},{14,2},{1,5},{3,7},... | collective-permute-start | bytes 1179656 | tf_op jit(solution)/shard_map/ppermute | solution.py:253
  4.4 20.4 %collective-permute-start.1 = (bf16[128,1536]{1,0:T(8,128)(2,1)S(1)}, bf16[128,1536]{1,0:T(8,128)(2,1)S(1)}, u32[]{:S(2)}, u32[]{:S(2)}) collective-permute-start(bf16[128,1536]{1,0:T(8,128)(2,1)S(1)} %get-tuple-element.18), channel_id=1, source_target_pairs={{0,4},{2,6},{4,8},{6,10},{8,12},{10,14},{12,0},{14,2},{1,5},{3,7},... | collective-permute-start | bytes 1179656 | tf_op jit(solution)/shard_map/ppermute | solution.py:253
  16.4 10.5 %collective-permute-start.4 = (bf16[128,1536]{1,0:T(8,128)(2,1)S(1)}, bf16[128,1536]{1,0:T(8,128)(2,1)S(1)}, u32[]{:S(2)}, u32[]{:S(2)}) collective-permute-start(bf16[128,1536]{1,0:T(8,128)(2,1)S(1)} %shard_map.48.refs_0_), channel_id=1, source_target_pairs={{0,2},{2,0},{4,6},{6,4},{8,10},{10,8},{12,14},{14,12},{1,3},{3,1},... | collective-permute-start | bytes 1179656 | tf_op jit(solution)/shard_map/ppermute | solution.py:224
  18.4 11.7 %collective-permute-start.6 = (bf16[128,1024]{1,0:T(8,128)(2,1)S(1)}, bf16[128,1024]{1,0:T(8,128)(2,1)S(1)}, u32[]{:S(2)}, u32[]{:S(2)}) collective-permute-start(bf16[128,1024]{1,0:T(8,128)(2,1)S(1)} %shard_map.49.refs_2_), channel_id=1, source_target_pairs={{0,4},{2,6},{4,8},{6,10},{8,12},{10,14},{12,0},{14,2},{1,5},{3,7},... | collective-permute-start | bytes 786440 | tf_op jit(solution)/shard_map/ppermute | solution.py:229
  18.5 10.0 %collective-permute-start.5 = (bf16[128,1536]{1,0:T(8,128)(2,1)S(1)}, bf16[128,1536]{1,0:T(8,128)(2,1)S(1)}, u32[]{:S(2)}, u32[]{:S(2)}) collective-permute-start(bf16[128,1536]{1,0:T(8,128)(2,1)S(1)} %collective-permute-done.received.refs_1_), channel_id=1, source_target_pairs={{0,16},{16,0},{1,17},{17,1},{2,18},{18,2},{3,19},{19,3},{4,20},{20... | collective-permute-start | bytes 1179656 | tf_op jit(solution)/shard_map/ppermute | solution.py:246
  24.8 12.1 %collective-permute-start.3 = (bf16[128,1536]{1,0:T(8,128)(2,1)S(1)}, bf16[128,1536]{1,0:T(8,128)(2,1)S(1)}, u32[]{:S(2)}, u32[]{:S(2)}) collective-permute-start(bf16[128,1536]{1,0:T(8,128)(2,1)S(1)} %shard_map.51.refs_0_), channel_id=1, source_target_pairs={{0,2},{2,0},{4,6},{6,4},{8,10},{10,8},{12,14},{14,12},{1,3},{3,1},... | collective-permute-start | bytes 1179656 | tf_op jit(solution)/shard_map/ppermute | solution.py:224
  26.8 12.7 %collective-permute-start.2 = (bf16[128,1024]{1,0:T(8,128)(2,1)S(1)}, bf16[128,1024]{1,0:T(8,128)(2,1)S(1)}, u32[]{:S(2)}, u32[]{:S(2)}) collective-permute-start(bf16[128,1024]{1,0:T(8,128)(2,1)S(1)} %shard_map.52.refs_2_), channel_id=1, source_target_pairs={{0,4},{2,6},{4,8},{6,10},{8,12},{10,14},{12,0},{14,2},{1,5},{3,7},... | collective-permute-start | bytes 786440 | tf_op jit(solution)/shard_map/ppermute | solution.py:229
  26.9 15.7 %collective-permute-start.12 = (bf16[128,1536]{1,0:T(8,128)(2,1)S(1)}, bf16[128,1536]{1,0:T(8,128)(2,1)S(1)}, u32[]{:S(2)}, u32[]{:S(2)}) collective-permute-start(bf16[128,1536]{1,0:T(8,128)(2,1)S(1)} %collective-permute-done.4.refs_0_), channel_id=1, source_target_pairs={{0,16},{16,0},{1,17},{17,1},{2,18},{18,2},{3,19},{19,3},{4,20},{20... | collective-permute-start | bytes 1179656 | tf_op jit(solution)/shard_map/ppermute | solution.py:246
  30.1 12.4 %collective-permute-start.11 = (bf16[128,1024]{1,0:T(8,128)(2,1)S(1)}, bf16[128,1024]{1,0:T(8,128)(2,1)S(1)}, u32[]{:S(2)}, u32[]{:S(2)}) collective-permute-start(bf16[128,1024]{1,0:T(8,128)(2,1)S(1)} %shard_map.54.refs_0_), channel_id=1, source_target_pairs={{0,2},{2,0},{4,6},{6,4},{8,10},{10,8},{12,14},{14,12},{1,3},{3,1},... | collective-permute-start | bytes 786440 | tf_op jit(solution)/shard_map/ppermute | solution.py:224
  32.3 13.7 %collective-permute-start.10 = (bf16[128,1536]{1,0:T(8,128)(2,1)S(1)}, bf16[128,1536]{1,0:T(8,128)(2,1)S(1)}, u32[]{:S(2)}, u32[]{:S(2)}) collective-permute-start(bf16[128,1536]{1,0:T(8,128)(2,1)S(1)} %shard_map.55.refs_3_), channel_id=1, source_target_pairs={{0,4},{2,6},{4,8},{6,10},{8,12},{10,14},{12,0},{14,2},{1,5},{3,7},... | collective-permute-start | bytes 1179656 | tf_op jit(solution)/shard_map/ppermute | solution.py:229
  36.9 9.1 %collective-permute-start.9 = (bf16[128,1536]{1,0:T(8,128)(2,1)S(1)}, bf16[128,1536]{1,0:T(8,128)(2,1)S(1)}, u32[]{:S(2)}, u32[]{:S(2)}) collective-permute-start(bf16[128,1536]{1,0:T(8,128)(2,1)S(1)} %collective-permute-done.3.refs_0_), channel_id=1, source_target_pairs={{0,16},{16,0},{1,17},{17,1},{2,18},{18,2},{3,19},{19,3},{4,20},{20... | collective-permute-start | bytes 1179656 | tf_op jit(solution)/shard_map/ppermute | solution.py:246
  39.6 6.4 %collective-permute-start.8 = (bf16[128,1024]{1,0:T(8,128)(2,1)S(1)}, bf16[128,1024]{1,0:T(8,128)(2,1)S(1)}, u32[]{:S(2)}, u32[]{:S(2)}) collective-permute-start(bf16[128,1024]{1,0:T(8,128)(2,1)S(1)} %shard_map.57.refs_5_), channel_id=1, source_target_pairs={{0,2},{2,0},{4,6},{6,4},{8,10},{10,8},{12,14},{14,12},{1,3},{3,1},... | collective-permute-start | bytes 786440 | tf_op jit(solution)/shard_map/ppermute | solution.py:224
  42.6 1.9 %collective-permute-start.7 = (f32[320,128]{1,0:T(8,128)S(1)}, f32[320,128]{1,0:T(8,128)S(1)}, u32[]{:S(2)}, u32[]{:S(2)}) collective-permute-start(f32[320,128]{1,0:T(8,128)S(1)} %get-tuple-element.28.refs_0_), channel_id=1, source_target_pairs={{0,1},{1,0},{2,3},{3,2},{4,5},{5,4},{6,7},{7,6},{8,9},{9,8},{10,11... | collective-permute-start | bytes 491528 | tf_op jit(solution)/shard_map/ppermute | solution.py:293
  47.5 1.7 %collective-permute-start.13 = (f32[320,256]{1,0:T(8,128)S(1)}, f32[320,256]{1,0:T(8,128)S(1)}, u32[]{:S(2)}, u32[]{:S(2)}) collective-permute-start(f32[320,256]{1,0:T(8,128)S(1)} %shard_map.59.refs_5_), channel_id=1, source_target_pairs={{0,1},{1,0},{2,3},{3,2},{4,5},{5,4},{6,7},{7,6},{8,9},{9,8},{10,11... | collective-permute-start | bytes 983048 | tf_op jit(solution)/shard_map/ppermute | solution.py:296

commit v8 on v5

v8 whole, which is shorter than its diff:
```python
import functools
import math

import jax
import jax.numpy as jnp
from jax import lax
from jax.experimental import pallas as pl
from jax.experimental.pallas import tpu as pltpu
from jax.sharding import PartitionSpec as P

L_DIM = 8192
SIZES = (8, 8, 8, 8, 8, 8, 8, 8)
CHUNKS = len(SIZES)
DIRECT = 6
VMEM = pl.BlockSpec(memory_space=pltpu.VMEM)
SMEM = pl.BlockSpec(memory_space=pltpu.SMEM)
HBM = pl.BlockSpec(memory_space=pltpu.HBM)
ANY = pl.BlockSpec(memory_space=pl.ANY)
PACE = 16 * 10**8
FIRST = 10**10
MIB = 1024 * 1024


def width_of(k, dims):
    return SIZES[k] * dims // sum(SIZES)


def columns_of(k, dims):
    unit = dims // sum(SIZES)
    left, right = sum(SIZES[:k]) * unit, sum(SIZES[k + 1 :]) * unit
    start = jnp.where(lax.axis_index("groups") == 0, left, right)
    return pl.ds(pl.multiple_of(start, unit), width_of(k, dims))


def products(rows, block):
    return lax.dot_general(
        rows, block, (((1,), (1,)), ((), ())), preferred_element_type=jnp.float32
    )


def scale_of(factor, counts, half, side):
    layer = lax.axis_index("layer")
    start = (layer if side else 1 - layer) * half
    index = start + lax.broadcasted_iota(jnp.int32, (half, 1), 0)
    return factor * (index < counts[0]).astype(jnp.float32)


def chunk_kernel(ks, queries, *refs):
    outs, sem = refs[-len(ks) - 1 : -1], refs[-1]
    dims = queries.shape[1]
    copies = [
        pltpu.make_async_copy(queries.at[:, columns_of(k, dims)], outs[i], sem.at[i])
        for i, k in enumerate(ks)
    ]
    for copy in copies:
        copy.start()
    for copy in copies:
        copy.wait()


def step_kernel(k, queries, received, *refs):
    out, sem = refs[-2:]
    even = lax.axis_index("dp") % 2 == 0
    own_copy = pltpu.make_async_copy(queries.at[:, columns_of(k, queries.shape[1])], out, sem)
    received_copy = pltpu.make_async_copy(received, out, sem)

    @pl.when(even)
    def _():
        own_copy.start()
        own_copy.wait()

    @pl.when(jnp.logical_not(even))
    def _():
        received_copy.start()
        received_copy.wait()


def own_kernel(pieces, factor, counts, documents, queries, eigenvalues, *refs):
    theirs, mine, held, inverse, sem = refs
    layer = lax.axis_index("layer")
    half = documents.shape[0] // 2
    dims = documents.shape[1]
    width = dims // pieces
    copies = {}
    for i in range(pieces):
        columns = pl.ds(i * width, width)
        for side, row in enumerate((1 - layer, layer)):
            copies[i, side] = pltpu.make_async_copy(
                documents.at[pl.ds(pl.multiple_of(row * half, half), half), columns],
                held.at[pl.ds(side * half, half), columns],
                sem.at[i, side],
            )
            copies[i, side].start()
    for start in range(0, dims, L_DIM):
        block = eigenvalues[:, start : start + L_DIM]
        damping = 0.1 * jnp.mean(block, axis=1, keepdims=True)
        inverse[:, start : start + L_DIM] = 1.0 / (block + damping)
    for i in range(pieces):
        columns = slice(i * width, (i + 1) * width)
        scaled = (queries[:, columns].astype(jnp.float32) * inverse[:, columns]).astype(jnp.bfloat16)
        for side, out in enumerate((theirs, mine)):
            copies[i, side].wait()
            term = products(held[side * half : (side + 1) * half, columns], scaled)
            if i == 0:
                out[...] = term
            else:
                out[...] += term
    theirs[...] *= scale_of(factor, counts, half, 0)
    mine[...] *= scale_of(factor, counts, half, 1)


def pair_kernel(ks, side, factor, fresh, counts, held, inverse, *refs):
    count = len(ks)
    chunks, out, block_buf = refs[: 2 * count], refs[-2], refs[-1]
    dims = inverse.shape[1]
    size = out.shape[0]
    first = 0 if side is None else side * size
    rows = chunks[0].shape[0]
    for i, k in enumerate(ks):
        columns = columns_of(k, dims)
        width = width_of(k, dims)
        for b in range(2):
            scaled = chunks[2 * i + b][...].astype(jnp.float32) * inverse[:, columns]
            block_buf[pl.ds(b * rows, rows), :width] = scaled.astype(jnp.bfloat16)
        term = products(held[first : first + size, columns], block_buf[:, :width])
        if i > 0:
            out[...] += term
        elif fresh:
            out[...] = term
        else:
            out[...] = refs[2 * count][first : first + size] + term
    if side is not None:
        out[...] *= scale_of(factor, counts, size, side)


def final_kernel(mine0, got0, mine, got, out):
    rows = mine0.shape[1]
    out[:, :rows] = mine0[...] + got0[...]
    out[:, rows:] = mine[...] + got[...]


def on_device(queries, documents, counts, eigenvalues):
    rows, dims = queries.shape
    doc_rows = documents.shape[0]
    half = doc_rows // 2
    owners = lax.axis_size("dp")
    factor = 1.0 / math.sqrt(dims * lax.axis_size("layer"))
    ahead = [(i, (i + 2) % owners) for i in range(owners)]
    pair = [(i, i ^ 1) for i in range(owners)]
    across = [(0, 1), (1, 0)]

    def chunk(k):
        return jax.ShapeDtypeStruct((rows, width_of(k, dims)), queries.dtype)

    def floats(*shape):
        return jax.ShapeDtypeStruct(shape, jnp.float32)

    def call(kernel, out_shape, in_specs, out_specs, scratch, vmem_mib=16, flops=PACE):
        return pl.pallas_call(
            kernel,
            out_shape=out_shape,
            in_specs=in_specs,
            out_specs=out_specs,
            scratch_shapes=scratch,
            compiler_params=pltpu.CompilerParams(vmem_limit_bytes=vmem_mib * MIB),
            cost_estimate=pl.CostEstimate(flops=flops, bytes_accessed=0, transcendentals=0),
        )

    def own_chunks(*ks, until=(), space=ANY, **options):
        return call(
            functools.partial(chunk_kernel, ks),
            [chunk(k) for k in ks],
            [ANY] * (1 + len(until)),
            [space] * len(ks),
            [pltpu.SemaphoreType.DMA((len(ks),))],
            **options,
        )(queries, *until)

    def step(k, *until):
        out = call(
            functools.partial(step_kernel, k),
            chunk(k),
            [ANY] * (2 + len(until)),
            ANY,
            [pltpu.SemaphoreType.DMA],
        )(queries, far[k], *until)
        near[k] = lax.ppermute(out, "dp", pair)
        return out

    def send_ahead(k, *until):
        (sent,) = own_chunks(k, until=until)
        far[k] = lax.ppermute(sent, "dp", ahead)
        return sent

    def pair_scores(*ks, sums=None, side=None, until=()):
        operands = [held, inverse] + [block[k] for k in ks for block in (near, far)]
        if sums is not None:
            operands.append(sums)
        return call(
            functools.partial(pair_kernel, ks, side, factor, sums is None),
            floats(doc_rows if side is None else half, 2 * rows),
            [SMEM] + [VMEM] * len(operands) + [ANY] * len(until),
            VMEM,
            [pltpu.VMEM((2 * rows, max(width_of(k, dims) for k in ks)), queries.dtype)],
        )(counts, *operands, *until)

    def send_across(block, k, *until):
        sent = lax.optimization_barrier((block[k], *until))[0]
        block[CHUNKS - 1 - k] = lax.ppermute(sent, "groups", across)

    far = [None] * CHUNKS
    near = [None] * CHUNKS

    sent = own_chunks(0, 1, space=VMEM, vmem_mib=53, flops=FIRST)
    for k in range(2):
        far[k] = lax.ppermute(sent[k], "dp", ahead)

    kept = lax.optimization_barrier((eigenvalues, sent[1]))[0].reshape(1, dims)
    pieces = 8
    theirs0, mine0, held, inverse = call(
        functools.partial(own_kernel, pieces, factor),
        [
            floats(half, rows),
            floats(half, rows),
            jax.ShapeDtypeStruct(documents.shape, documents.dtype),
            floats(1, dims),
        ],
        [SMEM, HBM, VMEM, VMEM],
        [VMEM] * 4,
        [pltpu.SemaphoreType.DMA((pieces, 2))],
        vmem_mib=40,
    )(counts, documents, queries, kept)

    out = step(0, inverse)
    out = send_ahead(2, out)
    send_across(far, 0, out)

    out = step(1, out)
    out = send_ahead(3, out)
    send_across(far, 1, out)
    sums = pair_scores(0, until=(out, far[7]))

    out = step(2, sums)
    out = send_ahead(4, out)
    send_across(near, 0, out)
    sums = pair_scores(1, sums=sums, until=(out, far[6]))

    out = step(3, sums)
    out = send_ahead(5, out)
    send_across(near, 1, out)
    sums = pair_scores(2, 7, sums=sums, until=(out,))

    out = step(4, sums)
    send_across(near, 2, out)
    got0 = lax.ppermute(lax.optimization_barrier((theirs0, out))[0], "layer", across)
    sums = pair_scores(3, 6, sums=sums, until=(out,))
    theirs = pair_scores(4, 5, sums=sums, side=0, until=(got0,))
    got = lax.ppermute(theirs, "layer", across)
    mine = pair_scores(4, 5, sums=sums, side=1, until=(theirs,))
    return call(final_kernel, floats(half, 3 * rows), [VMEM] * 4, VMEM, [])(mine0, got0, mine, got)


def solution(mesh):
    return jax.shard_map(
        on_device,
        mesh=mesh,
        in_specs=(P("dp", "layer"), P(("groups", "dp"), "layer"), P(("groups", "dp")), P("layer")),
        out_specs=P(("groups", "dp", "layer"), None),
        check_vma=False,
    )
```

time: 48.9 us -> 50.2 us (1.027)
  starting transfers between devices: 17.4 us -> 22.3 us
  waiting for transfers between devices: 15.4 us -> 12.9 us
  Pallas kernels: 15.2 us -> 14 us
    ppermute x3 -> x5, waiting for transfers between devices: 0.01 us -> 7.16 us  [send_across(): block[CHUNKS - 1 - k] = lax.ppermute(sent, 'groups', across)]
    ppermute x2, waiting for transfers between devices: 5.47 us -> 0.01 us  [on_device(): far[k] = lax.ppermute(sent[k], 'dp', ahead)]
    ppermute x3 -> x4, starting transfers between devices: 0.18 us -> 4.97 us  [send_ahead(): far[k] = lax.ppermute(sent, 'dp', ahead)]
    ppermute x4 -> x5, waiting for transfers between devices: 7.74 us -> 4.15 us  [step(): near[k] = lax.ppermute(out, 'dp', pair)]
    ppermute x3 -> x5, starting transfers between devices: 4.54 us -> 7.81 us  [send_across(): block[CHUNKS - 1 - k] = lax.ppermute(sent, 'groups', across)]
    ppermute x4 -> x5, starting transfers between devices: 7.96 us -> 4.77 us  [step(): near[k] = lax.ppermute(out, 'dp', pair)]
    pallas_call x2 -> x1, Pallas kernels: 8.97 us -> 7.69 us  [on_device(): call(functools.partial(own_kernel, pieces, factor), [floats(half, rows),...]
    pallas_call x5 -> x6, Pallas kernels: 3.8 us -> 4.01 us  [pair_scores(): call(functools.partial(pair_kernel, ks, side, factor, sums is None), floa...]
  transfers between devices with their start and end apart: 14 -> 18, of which waited for: 8 -> 11; matrix products, arithmetic and copies ran while one was open for 0% -> 0% of each run, Pallas kernels for 25% -> 23%
where the time goes in v8:
time: 50.2 us; the launch traced here: 50 us
  starting transfers between devices  22.3 us (44%)
  Pallas kernels  14 us (28%)
  waiting for transfers between devices  12.9 us (26%)
  between operations  0.86 us (2%)
    ppermute x5, starting transfers between devices, send_across(): block[CHUNKS - 1 - k] = lax.ppermute(sent, 'groups', across)  7.81 us
    pallas_call x1, Pallas kernels, on_device(): call(functools.partial(own_kernel, pieces, factor), [floats(half, rows),...  7.69 us
    ppermute x5, waiting for transfers between devices, send_across(): block[CHUNKS - 1 - k] = lax.ppermute(sent, 'groups', across)  7.16 us
    ppermute x4, starting transfers between devices, send_ahead(): far[k] = lax.ppermute(sent, 'dp', ahead)  4.97 us
    ppermute x5, starting transfers between devices, step(): near[k] = lax.ppermute(out, 'dp', pair)  4.77 us
    ppermute x2, starting transfers between devices, on_device(): far[k] = lax.ppermute(sent[k], 'dp', ahead)  4.65 us
    ppermute x5, waiting for transfers between devices, step(): near[k] = lax.ppermute(out, 'dp', pair)  4.15 us
    pallas_call x6, Pallas kernels, pair_scores(): call(functools.partial(pair_kernel, ks, side, factor, sums is None), floa...  4.01 us
  transfers between devices with their start and end apart: 18, of which 11 were waited for; matrix products, arithmetic and copies ran while one was open for 0% of the time, Pallas kernels for 23%

profile of v8, /device:TPU:0, one launch (start us, length us, event | category | flops | bytes accessed | tf_op | source)
XLA Modules:
  0.0 50.0 jit_solution(18276544960010790424)
XLA Ops:
  0.0 1.2 %shard_map.46 = (bf16[128,1024]{1,0:T(8,128)(2,1)S(1)}, bf16[128,1024]{1,0:T(8,128)(2,1)S(1)}) custom-call(bf16[128,8192]{1,0:T(8,128)(2,1)} %queries.21), custom_call_target="tpu_custom_call" | custom-call | flops 10000000000 | tf_op jit(solution)/shard_map/pallas_call | solution.py:170
  1.2 3.1 %collective-permute-start = (bf16[128,1024]{1,0:T(8,128)(2,1)S(1)}, bf16[128,1024]{1,0:T(8,128)(2,1)S(1)}, u32[]{:S(2)}, u32[]{:S(2)}) collective-permute-start(bf16[128,1024]{1,0:T(8,128)(2,1)S(1)} %get-tuple-element.22), channel_id=1, source_target_pairs={{0,4},{2,6},{4,8},{6,10},{8,12},{10,14},{12,0},{14,2},{1,5},{3,7},... | collective-permute-start | bytes 786440 | tf_op jit(solution)/shard_map/ppermute | solution.py:216
  4.3 1.6 %collective-permute-start.3 = (bf16[128,1024]{1,0:T(8,128)(2,1)S(1)}, bf16[128,1024]{1,0:T(8,128)(2,1)S(1)}, u32[]{:S(2)}, u32[]{:S(2)}) collective-permute-start(bf16[128,1024]{1,0:T(8,128)(2,1)S(1)} %get-tuple-element.18), channel_id=1, source_target_pairs={{0,4},{2,6},{4,8},{6,10},{8,12},{10,14},{12,0},{14,2},{1,5},{3,7},... | collective-permute-start | bytes 786440 | tf_op jit(solution)/shard_map/ppermute | solution.py:216
  6.5 0.0 copy-done
  6.5 7.7 %shard_map.47 = (f32[320,128]{1,0:T(8,128)S(1)}, f32[320,128]{1,0:T(8,128)S(1)}, bf16[640,8192]{1,0:T(8,128)(2,1)S(1)}, f32[1,8192]{1,0:T(1,128)S(1)}) custom-call(s32[1]{0:T(128)S(6)} %copy.5.counts, bf16[640,8192]{1,0:T(8,128)(2,1)} %documents.1, bf16[128,8192]{1,0:T(8,128)(2,1)S(1)} %copy-done, f32[1,8192]{1,0:T(1,128)S(1)} %bitcast.1), custom_call_target="tpu_custom_call" | custom-call | flops 1600000000 | tf_op jit(solution)/shard_map/pallas_call | solution.py:220
  14.2 0.0 collective-permute-done.received.refs_1_
  14.2 0.1 shard_map.48.refs_0_
  14.3 1.6 %collective-permute-start.2 = (bf16[128,1024]{1,0:T(8,128)(2,1)S(1)}, bf16[128,1024]{1,0:T(8,128)(2,1)S(1)}, u32[]{:S(2)}, u32[]{:S(2)}) collective-permute-start(bf16[128,1024]{1,0:T(8,128)(2,1)S(1)} %shard_map.48.refs_0_), channel_id=1, source_target_pairs={{0,2},{2,0},{4,6},{6,4},{8,10},{10,8},{12,14},{14,12},{1,3},{3,1},... | collective-permute-start | bytes 786440 | tf_op jit(solution)/shard_map/ppermute | solution.py:187
  15.9 1.6 %collective-permute-start.1 = (bf16[128,1024]{1,0:T(8,128)(2,1)S(1)}, bf16[128,1024]{1,0:T(8,128)(2,1)S(1)}, u32[]{:S(2)}, u32[]{:S(2)}) collective-permute-start(bf16[128,1024]{1,0:T(8,128)(2,1)S(1)} %shard_map.49.refs_0_), channel_id=1, source_target_pairs={{0,4},{2,6},{4,8},{6,10},{8,12},{10,14},{12,0},{14,2},{1,5},{3,7},... | collective-permute-start | bytes 786440 | tf_op jit(solution)/shard_map/ppermute | solution.py:192
  17.6 1.5 %collective-permute-start.4 = (bf16[128,1024]{1,0:T(8,128)(2,1)S(1)}, bf16[128,1024]{1,0:T(8,128)(2,1)S(1)}, u32[]{:S(2)}, u32[]{:S(2)}) collective-permute-start(bf16[128,1024]{1,0:T(8,128)(2,1)S(1)} %collective-permute-done.received.refs_1_), channel_id=1, source_target_pairs={{0,16},{16,0},{1,17},{17,1},{2,18},{18,2},{3,19},{19,3},{4,20},{20... | collective-permute-start | bytes 786440 | tf_op jit(solution)/shard_map/ppermute | solution.py:209
  19.0 0.0 collective-permute-done.3.received.refs_1_
  19.1 0.8 %collective-permute-start.8 = (bf16[128,1024]{1,0:T(8,128)(2,1)S(1)}, bf16[128,1024]{1,0:T(8,128)(2,1)S(1)}, u32[]{:S(2)}, u32[]{:S(2)}) collective-permute-start(bf16[128,1024]{1,0:T(8,128)(2,1)S(1)} %shard_map.50.refs_0_), channel_id=1, source_target_pairs={{0,2},{2,0},{4,6},{6,4},{8,10},{10,8},{12,14},{14,12},{1,3},{3,1},... | collective-permute-start | bytes 786440 | tf_op jit(solution)/shard_map/ppermute | solution.py:187
  19.9 0.1 collective-permute-start.10
  20.0 3.5 %collective-permute-done.2.refs_0_ = bf16[128,1024]{1,0:T(8,128)(2,1)S(1)} collective-permute-done((bf16[128,1024]{1,0:T(8,128)(2,1)S(1)}, bf16[128,1024]{1,0:T(8,128)(2,1)S(1)}, u32[]{:S(2)}, u32[]{:S(2)}) %collective-permute-start.2) | collective-permute-done | bytes 262176 | tf_op jit(solution)/shard_map/ppermute | solution.py:187
  23.4 1.7 %collective-permute-start.9 = (bf16[128,1024]{1,0:T(8,128)(2,1)S(1)}, bf16[128,1024]{1,0:T(8,128)(2,1)S(1)}, u32[]{:S(2)}, u32[]{:S(2)}) collective-permute-start(bf16[128,1024]{1,0:T(8,128)(2,1)S(1)} %collective-permute-done.3.received.refs_1_), channel_id=1, source_target_pairs={{0,16},{16,0},{1,17},{17,1},{2,18},{18,2},{3,19},{19,3},{4,20},{20... | collective-permute-start | bytes 786440 | tf_op jit(solution)/shard_map/ppermute | solution.py:209
  25.1 1.0 %collective-permute-done.4.refs_3_ = bf16[128,1024]{1,0:T(8,128)(2,1)S(1)} collective-permute-done((bf16[128,1024]{1,0:T(8,128)(2,1)S(1)}, bf16[128,1024]{1,0:T(8,128)(2,1)S(1)}, u32[]{:S(2)}, u32[]{:S(2)}) %collective-permute-start.4) | collective-permute-done | bytes 262176 | tf_op jit(solution)/shard_map/ppermute | solution.py:209
  26.1 0.6 %shard_map.52.refs_0_.refs_2_ = f32[640,256]{1,0:T(8,128)S(1)} custom-call(s32[1]{0:T(128)S(6)} %copy.5.counts, bf16[640,8192]{1,0:T(8,128)(2,1)S(1)} %get-tuple-element.24.held, f32[1,8192]{1,0:T(1,128)S(1)} %get-tuple-element.23.refs_0_.inverse, bf16[128,1024]{1,0:T(8,128)(2,1)S(1)} %collective-permute-done.2.refs_0_, ...), custom_call_target="tpu_custom_call" | custom-call | flops 1600000000 | tf_op jit(solution)/shard_map/pallas_call | solution.py:199
  26.7 0.1 collective-permute-done.1.received.refs_1_
  26.8 0.5 collective-permute-start.6
  27.4 1.6 %collective-permute-start.5 = (bf16[128,1024]{1,0:T(8,128)(2,1)S(1)}, bf16[128,1024]{1,0:T(8,128)(2,1)S(1)}, u32[]{:S(2)}, u32[]{:S(2)}) collective-permute-start(bf16[128,1024]{1,0:T(8,128)(2,1)S(1)} %shard_map.54.refs_3_), channel_id=1, source_target_pairs={{0,4},{2,6},{4,8},{6,10},{8,12},{10,14},{12,0},{14,2},{1,5},{3,7},... | collective-permute-start | bytes 786440 | tf_op jit(solution)/shard_map/ppermute | solution.py:192
  29.0 0.1 collective-permute-done.8.refs_0_
  29.0 1.6 %collective-permute-start.7 = (bf16[128,1024]{1,0:T(8,128)(2,1)S(1)}, bf16[128,1024]{1,0:T(8,128)(2,1)S(1)}, u32[]{:S(2)}, u32[]{:S(2)}) collective-permute-start(bf16[128,1024]{1,0:T(8,128)(2,1)S(1)} %collective-permute-done.2.refs_0_), channel_id=1, source_target_pairs={{0,16},{16,0},{1,17},{17,1},{2,18},{18,2},{3,19},{19,3},{4,20},{20... | collective-permute-start | bytes 786440 | tf_op jit(solution)/shard_map/ppermute | solution.py:209
  30.6 0.9 %collective-permute-done.9.refs_4_.refs_3_ = bf16[128,1024]{1,0:T(8,128)(2,1)S(1)} collective-permute-done((bf16[128,1024]{1,0:T(8,128)(2,1)S(1)}, bf16[128,1024]{1,0:T(8,128)(2,1)S(1)}, u32[]{:S(2)}, u32[]{:S(2)}) %collective-permute-start.9) | collective-permute-done | bytes 262176 | tf_op jit(solution)/shard_map/ppermute | solution.py:209
  31.5 0.6 %shard_map.55.refs_0_.refs_4_ = f32[640,256]{1,0:T(8,128)S(1)} custom-call(s32[1]{0:T(128)S(6)} %copy.5.counts, bf16[640,8192]{1,0:T(8,128)(2,1)S(1)} %get-tuple-element.24.held, f32[1,8192]{1,0:T(1,128)S(1)} %get-tuple-element.23.refs_0_.inverse, bf16[128,1024]{1,0:T(8,128)(2,1)S(1)} %collective-permute-done.8.refs_0_, ...), custom_call_target="tpu_custom_call" | custom-call | flops 1600000000 | tf_op jit(solution)/shard_map/pallas_call | solution.py:199
  32.1 0.3 collective-permute-done.10.received.refs_1_
  32.5 1.3 %collective-permute-start.15 = (bf16[128,1024]{1,0:T(8,128)(2,1)S(1)}, bf16[128,1024]{1,0:T(8,128)(2,1)S(1)}, u32[]{:S(2)}, u32[]{:S(2)}) collective-permute-start(bf16[128,1024]{1,0:T(8,128)(2,1)S(1)} %shard_map.56.refs_0_), channel_id=1, source_target_pairs={{0,2},{2,0},{4,6},{6,4},{8,10},{10,8},{12,14},{14,12},{1,3},{3,1},... | collective-permute-start | bytes 786440 | tf_op jit(solution)/shard_map/ppermute | solution.py:187
  33.8 1.6 %collective-permute-start.14 = (bf16[128,1024]{1,0:T(8,128)(2,1)S(1)}, bf16[128,1024]{1,0:T(8,128)(2,1)S(1)}, u32[]{:S(2)}, u32[]{:S(2)}) collective-permute-start(bf16[128,1024]{1,0:T(8,128)(2,1)S(1)} %shard_map.57.refs_5_), channel_id=1, source_target_pairs={{0,4},{2,6},{4,8},{6,10},{8,12},{10,14},{12,0},{14,2},{1,5},{3,7},... | collective-permute-start | bytes 786440 | tf_op jit(solution)/shard_map/ppermute | solution.py:192
  35.4 0.0 collective-permute-done.6.refs_0_
  35.4 1.5 %collective-permute-start.16 = (bf16[128,1024]{1,0:T(8,128)(2,1)S(1)}, bf16[128,1024]{1,0:T(8,128)(2,1)S(1)}, u32[]{:S(2)}, u32[]{:S(2)}) collective-permute-start(bf16[128,1024]{1,0:T(8,128)(2,1)S(1)} %collective-permute-done.8.refs_0_), channel_id=1, source_target_pairs={{0,16},{16,0},{1,17},{17,1},{2,18},{18,2},{3,19},{19,3},{4,20},{20... | collective-permute-start | bytes 786440 | tf_op jit(solution)/shard_map/ppermute | solution.py:209
  36.9 1.4 %collective-permute-done.7.refs_2_ = bf16[128,1024]{1,0:T(8,128)(2,1)S(1)} collective-permute-done((bf16[128,1024]{1,0:T(8,128)(2,1)S(1)}, bf16[128,1024]{1,0:T(8,128)(2,1)S(1)}, u32[]{:S(2)}, u32[]{:S(2)}) %collective-permute-start.7) | collective-permute-done | bytes 262176 | tf_op jit(solution)/shard_map/ppermute | solution.py:209
  38.3 0.9 %shard_map.58.refs_0_.refs_4_ = f32[640,256]{1,0:T(8,128)S(1)} custom-call(s32[1]{0:T(128)S(6)} %copy.5.counts, bf16[640,8192]{1,0:T(8,128)(2,1)S(1)} %get-tuple-element.24.held, f32[1,8192]{1,0:T(1,128)S(1)} %get-tuple-element.23.refs_0_.inverse, bf16[128,1024]{1,0:T(8,128)(2,1)S(1)} %collective-permute-done.6.refs_0_, ...), custom_call_target="tpu_custom_call" | custom-call | flops 1600000000 | tf_op jit(solution)/shard_map/pallas_call | solution.py:199
  39.2 0.0 collective-permute-done.5.received.refs_1_
  39.2 0.1 shard_map.59.refs_5_
  39.3 0.7 %collective-permute-start.12 = (bf16[128,1024]{1,0:T(8,128)(2,1)S(1)}, bf16[128,1024]{1,0:T(8,128)(2,1)S(1)}, u32[]{:S(2)}, u32[]{:S(2)}) collective-permute-start(bf16[128,1024]{1,0:T(8,128)(2,1)S(1)} %shard_map.59.refs_5_), channel_id=1, source_target_pairs={{0,2},{2,0},{4,6},{6,4},{8,10},{10,8},{12,14},{14,12},{1,3},{3,1},... | collective-permute-start | bytes 786440 | tf_op jit(solution)/shard_map/ppermute | solution.py:187
  39.9 1.6 %collective-permute-start.13 = (bf16[128,1024]{1,0:T(8,128)(2,1)S(1)}, bf16[128,1024]{1,0:T(8,128)(2,1)S(1)}, u32[]{:S(2)}, u32[]{:S(2)}) collective-permute-start(bf16[128,1024]{1,0:T(8,128)(2,1)S(1)} %collective-permute-done.6.refs_0_), channel_id=1, source_target_pairs={{0,16},{16,0},{1,17},{17,1},{2,18},{18,2},{3,19},{19,3},{4,20},{20... | collective-permute-start | bytes 786440 | tf_op jit(solution)/shard_map/ppermute | solution.py:209
  41.5 0.0 collective-permute-done.15.refs_0_
  41.5 0.0 collective-permute-start.11
  41.5 2.6 %collective-permute-done.16.refs_2_ = bf16[128,1024]{1,0:T(8,128)(2,1)S(1)} collective-permute-done((bf16[128,1024]{1,0:T(8,128)(2,1)S(1)}, bf16[128,1024]{1,0:T(8,128)(2,1)S(1)}, u32[]{:S(2)}, u32[]{:S(2)}) %collective-permute-start.16) | collective-permute-done | bytes 262176 | tf_op jit(solution)/shard_map/ppermute | solution.py:209
  44.1 0.9 %shard_map.60.refs_4_ = f32[640,256]{1,0:T(8,128)S(1)} custom-call(s32[1]{0:T(128)S(6)} %copy.5.counts, bf16[640,8192]{1,0:T(8,128)(2,1)S(1)} %get-tuple-element.24.held, f32[1,8192]{1,0:T(1,128)S(1)} %get-tuple-element.23.refs_0_.inverse, bf16[128,1024]{1,0:T(8,128)(2,1)S(1)} %collective-permute-done.15.refs_0_, ...), custom_call_target="tpu_custom_call" | custom-call | flops 1600000000 | tf_op jit(solution)/shard_map/pallas_call | solution.py:199
  45.0 0.0 collective-permute-done.14.refs_3_
  45.1 0.0 collective-permute-done.11.refs_5_.got0
  45.1 0.6 %collective-permute-done.12.refs_0_ = bf16[128,1024]{1,0:T(8,128)(2,1)S(1)} collective-permute-done((bf16[128,1024]{1,0:T(8,128)(2,1)S(1)}, bf16[128,1024]{1,0:T(8,128)(2,1)S(1)}, u32[]{:S(2)}, u32[]{:S(2)}) %collective-permute-start.12) | collective-permute-done | bytes 262176 | tf_op jit(solution)/shard_map/ppermute | solution.py:187
  45.7 1.2 %collective-permute-done.13.refs_2_ = bf16[128,1024]{1,0:T(8,128)(2,1)S(1)} collective-permute-done((bf16[128,1024]{1,0:T(8,128)(2,1)S(1)}, bf16[128,1024]{1,0:T(8,128)(2,1)S(1)}, u32[]{:S(2)}, u32[]{:S(2)}) %collective-permute-start.13) | collective-permute-done | bytes 262176 | tf_op jit(solution)/shard_map/ppermute | solution.py:209
  47.0 0.6 %shard_map.61.refs_5_ = f32[320,256]{1,0:T(8,128)S(1)} custom-call(s32[1]{0:T(128)S(6)} %copy.5.counts, bf16[640,8192]{1,0:T(8,128)(2,1)S(1)} %get-tuple-element.24.held, f32[1,8192]{1,0:T(1,128)S(1)} %get-tuple-element.23.refs_0_.inverse, bf16[128,1024]{1,0:T(8,128)(2,1)S(1)} %collective-permute-done.12.refs_0_, ...), custom_call_target="tpu_custom_call" | custom-call | flops 1600000000 | tf_op jit(solution)/shard_map/pallas_call | solution.py:199
  47.5 0.1 collective-permute-start.17
  47.6 0.6 %shard_map.62.mine = f32[320,256]{1,0:T(8,128)S(1)} custom-call(s32[1]{0:T(128)S(6)} %copy.5.counts, bf16[640,8192]{1,0:T(8,128)(2,1)S(1)} %get-tuple-element.24.held, f32[1,8192]{1,0:T(1,128)S(1)} %get-tuple-element.23.refs_0_.inverse, bf16[128,1024]{1,0:T(8,128)(2,1)S(1)} %collective-permute-done.12.refs_0_, ...), custom_call_target="tpu_custom_call" | custom-call | flops 1600000000 | tf_op jit(solution)/shard_map/pallas_call | solution.py:199
  48.2 1.1 %collective-permute-done.17.got = f32[320,256]{1,0:T(8,128)S(1)} collective-permute-done((f32[320,256]{1,0:T(8,128)S(1)}, f32[320,256]{1,0:T(8,128)S(1)}, u32[]{:S(2)}, u32[]{:S(2)}) %collective-permute-start.17) | collective-permute-done | bytes 327712 | tf_op jit(solution)/shard_map/ppermute | solution.py:258
  49.2 0.8 %shard_map.63 = f32[320,384]{1,0:T(8,128)} custom-call(f32[320,128]{1,0:T(8,128)S(1)} %get-tuple-element.20.mine0, f32[320,128]{1,0:T(8,128)S(1)} %collective-permute-done.11.refs_5_.got0, f32[320,256]{1,0:T(8,128)S(1)} %shard_map.62.mine, f32[320,256]{1,0:T(8,128)S(1)} %collective-permute-done.17.got), custom_call_target="tpu_custom_call" | custom-call | flops 1600000000 | tf_op jit(solution)/shard_map/pallas_call | solution.py:260
  (10 shorter events, 0.2 us)
Async XLA Ops:
  0.0 6.5 %copy-start = (bf16[128,8192]{1,0:T(8,128)(2,1)S(1)}, bf16[128,8192]{1,0:T(8,128)(2,1)}, u32[]{:S(2)}) copy-start(bf16[128,8192]{1,0:T(8,128)(2,1)} %queries.21) | copy-start | bytes 6291460
  0.0 6.5 %copy-start.1 = (f32[8192]{0:T(1024)S(1)}, f32[8192]{0:T(1024)}, u32[]{:S(2)}) copy-start(f32[8192]{0:T(1024)} %param.7) | copy-start | bytes 98308
  1.2 13.0 %collective-permute-start = (bf16[128,1024]{1,0:T(8,128)(2,1)S(1)}, bf16[128,1024]{1,0:T(8,128)(2,1)S(1)}, u32[]{:S(2)}, u32[]{:S(2)}) collective-permute-start(bf16[128,1024]{1,0:T(8,128)(2,1)S(1)} %get-tuple-element.22), channel_id=1, source_target_pairs={{0,4},{2,6},{4,8},{6,10},{8,12},{10,14},{12,0},{14,2},{1,5},{3,7},... | collective-permute-start | bytes 786440 | tf_op jit(solution)/shard_map/ppermute | solution.py:216
  4.3 14.8 %collective-permute-start.3 = (bf16[128,1024]{1,0:T(8,128)(2,1)S(1)}, bf16[128,1024]{1,0:T(8,128)(2,1)S(1)}, u32[]{:S(2)}, u32[]{:S(2)}) collective-permute-start(bf16[128,1024]{1,0:T(8,128)(2,1)S(1)} %get-tuple-element.18), channel_id=1, source_target_pairs={{0,4},{2,6},{4,8},{6,10},{8,12},{10,14},{12,0},{14,2},{1,5},{3,7},... | collective-permute-start | bytes 786440 | tf_op jit(solution)/shard_map/ppermute | solution.py:216
  14.3 9.1 %collective-permute-start.2 = (bf16[128,1024]{1,0:T(8,128)(2,1)S(1)}, bf16[128,1024]{1,0:T(8,128)(2,1)S(1)}, u32[]{:S(2)}, u32[]{:S(2)}) collective-permute-start(bf16[128,1024]{1,0:T(8,128)(2,1)S(1)} %shard_map.48.refs_0_), channel_id=1, source_target_pairs={{0,2},{2,0},{4,6},{6,4},{8,10},{10,8},{12,14},{14,12},{1,3},{3,1},... | collective-permute-start | bytes 786440 | tf_op jit(solution)/shard_map/ppermute | solution.py:187
  15.9 10.9 %collective-permute-start.1 = (bf16[128,1024]{1,0:T(8,128)(2,1)S(1)}, bf16[128,1024]{1,0:T(8,128)(2,1)S(1)}, u32[]{:S(2)}, u32[]{:S(2)}) collective-permute-start(bf16[128,1024]{1,0:T(8,128)(2,1)S(1)} %shard_map.49.refs_0_), channel_id=1, source_target_pairs={{0,4},{2,6},{4,8},{6,10},{8,12},{10,14},{12,0},{14,2},{1,5},{3,7},... | collective-permute-start | bytes 786440 | tf_op jit(solution)/shard_map/ppermute | solution.py:192
  17.6 8.5 %collective-permute-start.4 = (bf16[128,1024]{1,0:T(8,128)(2,1)S(1)}, bf16[128,1024]{1,0:T(8,128)(2,1)S(1)}, u32[]{:S(2)}, u32[]{:S(2)}) collective-permute-start(bf16[128,1024]{1,0:T(8,128)(2,1)S(1)} %collective-permute-done.received.refs_1_), channel_id=1, source_target_pairs={{0,16},{16,0},{1,17},{17,1},{2,18},{18,2},{3,19},{19,3},{4,20},{20... | collective-permute-start | bytes 786440 | tf_op jit(solution)/shard_map/ppermute | solution.py:209
  19.1 10.0 %collective-permute-start.8 = (bf16[128,1024]{1,0:T(8,128)(2,1)S(1)}, bf16[128,1024]{1,0:T(8,128)(2,1)S(1)}, u32[]{:S(2)}, u32[]{:S(2)}) collective-permute-start(bf16[128,1024]{1,0:T(8,128)(2,1)S(1)} %shard_map.50.refs_0_), channel_id=1, source_target_pairs={{0,2},{2,0},{4,6},{6,4},{8,10},{10,8},{12,14},{14,12},{1,3},{3,1},... | collective-permute-start | bytes 786440 | tf_op jit(solution)/shard_map/ppermute | solution.py:187
  19.9 12.5 %collective-permute-start.10 = (bf16[128,1024]{1,0:T(8,128)(2,1)S(1)}, bf16[128,1024]{1,0:T(8,128)(2,1)S(1)}, u32[]{:S(2)}, u32[]{:S(2)}) collective-permute-start(bf16[128,1024]{1,0:T(8,128)(2,1)S(1)} %shard_map.51.refs_2_), channel_id=1, source_target_pairs={{0,4},{2,6},{4,8},{6,10},{8,12},{10,14},{12,0},{14,2},{1,5},{3,7},... | collective-permute-start | bytes 786440 | tf_op jit(solution)/shard_map/ppermute | solution.py:192
  23.4 8.1 %collective-permute-start.9 = (bf16[128,1024]{1,0:T(8,128)(2,1)S(1)}, bf16[128,1024]{1,0:T(8,128)(2,1)S(1)}, u32[]{:S(2)}, u32[]{:S(2)}) collective-permute-start(bf16[128,1024]{1,0:T(8,128)(2,1)S(1)} %collective-permute-done.3.received.refs_1_), channel_id=1, source_target_pairs={{0,16},{16,0},{1,17},{17,1},{2,18},{18,2},{3,19},{19,3},{4,20},{20... | collective-permute-start | bytes 786440 | tf_op jit(solution)/shard_map/ppermute | solution.py:209
  26.8 8.6 %collective-permute-start.6 = (bf16[128,1024]{1,0:T(8,128)(2,1)S(1)}, bf16[128,1024]{1,0:T(8,128)(2,1)S(1)}, u32[]{:S(2)}, u32[]{:S(2)}) collective-permute-start(bf16[128,1024]{1,0:T(8,128)(2,1)S(1)} %shard_map.53.refs_0_), channel_id=1, source_target_pairs={{0,2},{2,0},{4,6},{6,4},{8,10},{10,8},{12,14},{14,12},{1,3},{3,1},... | collective-permute-start | bytes 786440 | tf_op jit(solution)/shard_map/ppermute | solution.py:187
  27.4 11.8 %collective-permute-start.5 = (bf16[128,1024]{1,0:T(8,128)(2,1)S(1)}, bf16[128,1024]{1,0:T(8,128)(2,1)S(1)}, u32[]{:S(2)}, u32[]{:S(2)}) collective-permute-start(bf16[128,1024]{1,0:T(8,128)(2,1)S(1)} %shard_map.54.refs_3_), channel_id=1, source_target_pairs={{0,4},{2,6},{4,8},{6,10},{8,12},{10,14},{12,0},{14,2},{1,5},{3,7},... | collective-permute-start | bytes 786440 | tf_op jit(solution)/shard_map/ppermute | solution.py:192
  29.0 9.2 %collective-permute-start.7 = (bf16[128,1024]{1,0:T(8,128)(2,1)S(1)}, bf16[128,1024]{1,0:T(8,128)(2,1)S(1)}, u32[]{:S(2)}, u32[]{:S(2)}) collective-permute-start(bf16[128,1024]{1,0:T(8,128)(2,1)S(1)} %collective-permute-done.2.refs_0_), channel_id=1, source_target_pairs={{0,16},{16,0},{1,17},{17,1},{2,18},{18,2},{3,19},{19,3},{4,20},{20... | collective-permute-start | bytes 786440 | tf_op jit(solution)/shard_map/ppermute | solution.py:209
  32.5 9.1 %collective-permute-start.15 = (bf16[128,1024]{1,0:T(8,128)(2,1)S(1)}, bf16[128,1024]{1,0:T(8,128)(2,1)S(1)}, u32[]{:S(2)}, u32[]{:S(2)}) collective-permute-start(bf16[128,1024]{1,0:T(8,128)(2,1)S(1)} %shard_map.56.refs_0_), channel_id=1, source_target_pairs={{0,2},{2,0},{4,6},{6,4},{8,10},{10,8},{12,14},{14,12},{1,3},{3,1},... | collective-permute-start | bytes 786440 | tf_op jit(solution)/shard_map/ppermute | solution.py:187
  33.8 11.3 %collective-permute-start.14 = (bf16[128,1024]{1,0:T(8,128)(2,1)S(1)}, bf16[128,1024]{1,0:T(8,128)(2,1)S(1)}, u32[]{:S(2)}, u32[]{:S(2)}) collective-permute-start(bf16[128,1024]{1,0:T(8,128)(2,1)S(1)} %shard_map.57.refs_5_), channel_id=1, source_target_pairs={{0,4},{2,6},{4,8},{6,10},{8,12},{10,14},{12,0},{14,2},{1,5},{3,7},... | collective-permute-start | bytes 786440 | tf_op jit(solution)/shard_map/ppermute | solution.py:192
  35.4 8.7 %collective-permute-start.16 = (bf16[128,1024]{1,0:T(8,128)(2,1)S(1)}, bf16[128,1024]{1,0:T(8,128)(2,1)S(1)}, u32[]{:S(2)}, u32[]{:S(2)}) collective-permute-start(bf16[128,1024]{1,0:T(8,128)(2,1)S(1)} %collective-permute-done.8.refs_0_), channel_id=1, source_target_pairs={{0,16},{16,0},{1,17},{17,1},{2,18},{18,2},{3,19},{19,3},{4,20},{20... | collective-permute-start | bytes 786440 | tf_op jit(solution)/shard_map/ppermute | solution.py:209
  39.3 6.4 %collective-permute-start.12 = (bf16[128,1024]{1,0:T(8,128)(2,1)S(1)}, bf16[128,1024]{1,0:T(8,128)(2,1)S(1)}, u32[]{:S(2)}, u32[]{:S(2)}) collective-permute-start(bf16[128,1024]{1,0:T(8,128)(2,1)S(1)} %shard_map.59.refs_5_), channel_id=1, source_target_pairs={{0,2},{2,0},{4,6},{6,4},{8,10},{10,8},{12,14},{14,12},{1,3},{3,1},... | collective-permute-start | bytes 786440 | tf_op jit(solution)/shard_map/ppermute | solution.py:187
  39.9 7.0 %collective-permute-start.13 = (bf16[128,1024]{1,0:T(8,128)(2,1)S(1)}, bf16[128,1024]{1,0:T(8,128)(2,1)S(1)}, u32[]{:S(2)}, u32[]{:S(2)}) collective-permute-start(bf16[128,1024]{1,0:T(8,128)(2,1)S(1)} %collective-permute-done.6.refs_0_), channel_id=1, source_target_pairs={{0,16},{16,0},{1,17},{17,1},{2,18},{18,2},{3,19},{19,3},{4,20},{20... | collective-permute-start | bytes 786440 | tf_op jit(solution)/shard_map/ppermute | solution.py:209
  41.5 3.5 %collective-permute-start.11 = (f32[320,128]{1,0:T(8,128)S(1)}, f32[320,128]{1,0:T(8,128)S(1)}, u32[]{:S(2)}, u32[]{:S(2)}) collective-permute-start(f32[320,128]{1,0:T(8,128)S(1)} %get-tuple-element.28), channel_id=1, source_target_pairs={{0,1},{1,0},{2,3},{3,2},{4,5},{5,4},{6,7},{7,6},{8,9},{9,8},{10,11... | collective-permute-start | bytes 491528 | tf_op jit(solution)/shard_map/ppermute | solution.py:255
  47.5 1.7 %collective-permute-start.17 = (f32[320,256]{1,0:T(8,128)S(1)}, f32[320,256]{1,0:T(8,128)S(1)}, u32[]{:S(2)}, u32[]{:S(2)}) collective-permute-start(f32[320,256]{1,0:T(8,128)S(1)} %shard_map.61.refs_5_), channel_id=1, source_target_pairs={{0,1},{1,0},{2,3},{3,2},{4,5},{5,4},{6,7},{7,6},{8,9},{9,8},{10,11... | collective-permute-start | bytes 983048 | tf_op jit(solution)/shard_map/ppermute | solution.py:258

commit v9 on v5

--- a/solution.py
+++ b/solution.py
@@ -17,7 +17,8 @@
 SMEM = pl.BlockSpec(memory_space=pltpu.SMEM)
 HBM = pl.BlockSpec(memory_space=pltpu.HBM)
 ANY = pl.BlockSpec(memory_space=pl.ANY)
-COST = pl.CostEstimate(flops=16 * 10**8, bytes_accessed=0, transcendentals=0)
+PACE = 16 * 10**8
+FIRST = 1024
 MIB = 1024 * 1024
 
 
@@ -115,8 +116,9 @@
     for i in range(pieces):
         columns = pl.ds(pl.multiple_of(first + i * width, width), width)
         scaled = (queries[:, columns].astype(jnp.float32) * inverse[:, columns]).astype(jnp.bfloat16)
+        copies[2 * i].wait()
+        copies[2 * i + 1].wait()
         for side, out in enumerate((theirs, mine)):
-            copies[2 * i + side].wait()
             term = products(
                 held[side * half : (side + 1) * half, i * width : (i + 1) * width], scaled
             )
@@ -181,7 +183,7 @@
     def floats(*shape):
         return jax.ShapeDtypeStruct(shape, jnp.float32)
 
-    def call(kernel, out_shape, in_specs, out_specs, scratch, vmem_mib=16, **options):
+    def call(kernel, out_shape, in_specs, out_specs, scratch, vmem_mib=16, flops=PACE):
         return pl.pallas_call(
             kernel,
             out_shape=out_shape,
@@ -189,18 +191,17 @@
             out_specs=out_specs,
             scratch_shapes=scratch,
             compiler_params=pltpu.CompilerParams(vmem_limit_bytes=vmem_mib * MIB),
-            cost_estimate=COST,
-            **options,
+            cost_estimate=pl.CostEstimate(flops=flops, bytes_accessed=0, transcendentals=0),
         )
 
-    def own_chunks(*ks, until=(), space=ANY, vmem_mib=16):
+    def own_chunks(*ks, until=(), space=ANY, **options):
         return call(
             functools.partial(chunk_kernel, ks),
             [chunk(k) for k in ks],
             [ANY] * (1 + len(until)),
             [space] * len(ks),
             [pltpu.SemaphoreType.DMA((len(ks),))],
-            vmem_mib,
+            **options,
         )(queries, *until)
 
     def step(k, *until):
@@ -238,7 +239,7 @@
     far = [None] * CHUNKS
     near = [None] * CHUNKS
 
-    sent = own_chunks(0, 1, space=VMEM, vmem_mib=53)
+    sent = own_chunks(0, 1, space=VMEM, vmem_mib=53, flops=FIRST)
     for k in range(2):
         far[k] = lax.ppermute(sent[k], "dp", ahead)
 

time: 48.9 us -> 48.9 us (level)
  Pallas kernels: 15.2 us -> 12.4 us
  local copies, waits for them, and re-layouts: 0.01 us -> 2.35 us
    pallas_call x2, Pallas kernels: 8.97 us -> 6.38 us  [own_scores(): call(functools.partial(own_kernel, part, pieces, factor), outs, [SMEM, HB...]
    unnamed x4 -> x6, local copies, waits for them, and re-layouts: 0.01 us -> 2.35 us
  transfers between devices with their start and end apart: 14 -> 14, of which waited for: 8 -> 8; matrix products, arithmetic and copies ran while one was open for 0% -> 0% of each run, Pallas kernels for 25% -> 20%
where the time goes in v9:
time: 48.9 us; the launch traced here: 48.6 us
  starting transfers between devices  17.4 us (36%)
  waiting for transfers between devices  15.6 us (32%)
  Pallas kernels  12.4 us (25%)
  local copies, waits for them, and re-layouts  2.35 us (5%)
  between operations  0.84 us (2%)
    ppermute x4, starting transfers between devices, step(): near[k] = lax.ppermute(out, 'dp', pair)  7.96 us
    ppermute x4, waiting for transfers between devices, step(): near[k] = lax.ppermute(out, 'dp', pair)  7.73 us
    pallas_call x2, Pallas kernels, own_scores(): call(functools.partial(own_kernel, part, pieces, factor), outs, [SMEM, HB...  6.38 us
    ppermute x2, waiting for transfers between devices, on_device(): far[k] = lax.ppermute(sent[k], 'dp', ahead)  5.72 us
    ppermute x2, starting transfers between devices, on_device(): far[k] = lax.ppermute(sent[k], 'dp', ahead)  4.65 us
    ppermute x3, starting transfers between devices, send_across(): block[CHUNKS - 1 - k] = lax.ppermute(sent, 'groups', across)  4.54 us
    pallas_call x5, Pallas kernels, pair_scores(): call(functools.partial(pair_kernel, ks, side, factor, sums is None), floa...  3.79 us
    unnamed x6, local copies, waits for them, and re-layouts  2.35 us
  transfers between devices with their start and end apart: 14, of which 8 were waited for; matrix products, arithmetic and copies ran while one was open for 0% of the time, Pallas kernels for 20%

profile of v9, /device:TPU:0, one launch (start us, length us, event | category | flops | bytes accessed | tf_op | source)
XLA Modules:
  0.0 48.6 jit_solution(12577560870571719523)
XLA Ops:
  0.0 1.1 %shard_map.46 = (bf16[128,1536]{1,0:T(8,128)(2,1)S(1)}, bf16[128,1536]{1,0:T(8,128)(2,1)S(1)}) custom-call(bf16[128,8192]{1,0:T(8,128)(2,1)} %queries.19), custom_call_target="tpu_custom_call" | custom-call | flops 1024 | tf_op jit(solution)/shard_map/pallas_call | solution.py:198
  1.1 3.1 %collective-permute-start = (bf16[128,1536]{1,0:T(8,128)(2,1)S(1)}, bf16[128,1536]{1,0:T(8,128)(2,1)S(1)}, u32[]{:S(2)}, u32[]{:S(2)}) collective-permute-start(bf16[128,1536]{1,0:T(8,128)(2,1)S(1)} %get-tuple-element.24), channel_id=1, source_target_pairs={{0,4},{2,6},{4,8},{6,10},{8,12},{10,14},{12,0},{14,2},{1,5},{3,7},... | collective-permute-start | bytes 1179656 | tf_op jit(solution)/shard_map/ppermute | solution.py:244
  4.2 1.6 %collective-permute-start.1 = (bf16[128,1536]{1,0:T(8,128)(2,1)S(1)}, bf16[128,1536]{1,0:T(8,128)(2,1)S(1)}, u32[]{:S(2)}, u32[]{:S(2)}) collective-permute-start(bf16[128,1536]{1,0:T(8,128)(2,1)S(1)} %get-tuple-element.19), channel_id=1, source_target_pairs={{0,4},{2,6},{4,8},{6,10},{8,12},{10,14},{12,0},{14,2},{1,5},{3,7},... | collective-permute-start | bytes 1179656 | tf_op jit(solution)/shard_map/ppermute | solution.py:244
  6.4 0.0 copy-start
  6.5 1.6 %copy-done = bf16[128,8192]{1,0:T(8,128)(2,1)S(1)} copy-done((bf16[128,8192]{1,0:T(8,128)(2,1)S(1)}, bf16[128,8192]{1,0:T(8,128)(2,1)}, u32[]{:S(2)}) %copy-start) | copy-done | bytes 2097176
  8.0 0.0 copy-start.2
  8.0 0.8 %copy-done.2 = f32[8192]{0:T(1024)S(1)} copy-done((f32[8192]{0:T(1024)S(1)}, f32[8192]{0:T(1024)}, u32[]{:S(2)}) %copy-start.2) | copy-done | bytes 32792
  8.8 3.2 %shard_map.47 = (f32[320,128]{1,0:T(8,128)S(1)}, f32[320,128]{1,0:T(8,128)S(1)}, bf16[640,4096]{1,0:T(8,128)(2,1)S(1)}, f32[1,8192]{1,0:T(1,128)S(1)}) custom-call(s32[1]{0:T(128)S(6)} %copy.5.counts, bf16[640,8192]{1,0:T(8,128)(2,1)} %documents.3, bf16[128,8192]{1,0:T(8,128)(2,1)S(1)} %copy-done, f32[1,8192]{1,0:T(1,128)S(1)} %bitcast.1), custom_call_target="tpu_custom_call" | custom-call | flops 1600000000 | tf_op jit(solution)/shard_map/pallas_call | solution.py:254
  12.0 4.2 %collective-permute-done.received.refs_1_ = bf16[128,1536]{1,0:T(8,128)(2,1)S(1)} collective-permute-done((bf16[128,1536]{1,0:T(8,128)(2,1)S(1)}, bf16[128,1536]{1,0:T(8,128)(2,1)S(1)}, u32[]{:S(2)}, u32[]{:S(2)}) %collective-permute-start) | collective-permute-done | bytes 393248 | tf_op jit(solution)/shard_map/ppermute | solution.py:244
  16.2 0.0 copy-start.1
  16.2 2.0 %collective-permute-start.4 = (bf16[128,1536]{1,0:T(8,128)(2,1)S(1)}, bf16[128,1536]{1,0:T(8,128)(2,1)S(1)}, u32[]{:S(2)}, u32[]{:S(2)}) collective-permute-start(bf16[128,1536]{1,0:T(8,128)(2,1)S(1)} %shard_map.48.refs_0_), channel_id=1, source_target_pairs={{0,2},{2,0},{4,6},{6,4},{8,10},{10,8},{12,14},{14,12},{1,3},{3,1},... | collective-permute-start | bytes 1179656 | tf_op jit(solution)/shard_map/ppermute | solution.py:215
  18.3 0.1 collective-permute-start.6
  18.3 1.6 %collective-permute-start.5 = (bf16[128,1536]{1,0:T(8,128)(2,1)S(1)}, bf16[128,1536]{1,0:T(8,128)(2,1)S(1)}, u32[]{:S(2)}, u32[]{:S(2)}) collective-permute-start(bf16[128,1536]{1,0:T(8,128)(2,1)S(1)} %collective-permute-done.received.refs_1_), channel_id=1, source_target_pairs={{0,16},{16,0},{1,17},{17,1},{2,18},{18,2},{3,19},{19,3},{4,20},{20... | collective-permute-start | bytes 1179656 | tf_op jit(solution)/shard_map/ppermute | solution.py:237
  19.9 0.0 copy-done.1
  19.9 3.2 %shard_map.50 = (f32[320,128]{1,0:T(8,128)S(1)}, f32[320,128]{1,0:T(8,128)S(1)}, bf16[640,4096]{1,0:T(8,128)(2,1)S(1)}) custom-call(s32[1]{0:T(128)S(6)} %copy.5.counts, bf16[640,8192]{1,0:T(8,128)(2,1)} %documents.3, bf16[128,8192]{1,0:T(8,128)(2,1)S(1)} %copy-done.1, f32[1,8192]{1,0:T(1,128)S(1)} %get-tuple-element.21.refs_0_.inverse, ...), custom_call_target="tpu_custom_call" | custom-call | flops 1600000000 | tf_op jit(solution)/shard_map/pallas_call | solution.py:254
  23.1 1.5 %collective-permute-done.1.received.refs_1_ = bf16[128,1536]{1,0:T(8,128)(2,1)S(1)} collective-permute-done((bf16[128,1536]{1,0:T(8,128)(2,1)S(1)}, bf16[128,1536]{1,0:T(8,128)(2,1)S(1)}, u32[]{:S(2)}, u32[]{:S(2)}) %collective-permute-start.1) | collective-permute-done | bytes 393248 | tf_op jit(solution)/shard_map/ppermute | solution.py:244
  24.7 2.0 %collective-permute-start.3 = (bf16[128,1536]{1,0:T(8,128)(2,1)S(1)}, bf16[128,1536]{1,0:T(8,128)(2,1)S(1)}, u32[]{:S(2)}, u32[]{:S(2)}) collective-permute-start(bf16[128,1536]{1,0:T(8,128)(2,1)S(1)} %shard_map.51.refs_0_), channel_id=1, source_target_pairs={{0,2},{2,0},{4,6},{6,4},{8,10},{10,8},{12,14},{14,12},{1,3},{3,1},... | collective-permute-start | bytes 1179656 | tf_op jit(solution)/shard_map/ppermute | solution.py:215
  26.7 0.1 collective-permute-start.2
  26.7 0.0 collective-permute-done.4.refs_0_
  26.8 1.6 %collective-permute-start.12 = (bf16[128,1536]{1,0:T(8,128)(2,1)S(1)}, bf16[128,1536]{1,0:T(8,128)(2,1)S(1)}, u32[]{:S(2)}, u32[]{:S(2)}) collective-permute-start(bf16[128,1536]{1,0:T(8,128)(2,1)S(1)} %collective-permute-done.4.refs_0_), channel_id=1, source_target_pairs={{0,16},{16,0},{1,17},{17,1},{2,18},{18,2},{3,19},{19,3},{4,20},{20... | collective-permute-start | bytes 1179656 | tf_op jit(solution)/shard_map/ppermute | solution.py:237
  28.3 0.0 collective-permute-done.5.refs_3_
  28.3 0.7 %shard_map.53.refs_0_.refs_2_ = f32[640,256]{1,0:T(8,128)S(1)} custom-call(s32[1]{0:T(128)S(6)} %copy.5.counts, bf16[640,4096]{1,0:T(8,128)(2,1)S(1)} %get-tuple-element.27.held0, bf16[640,4096]{1,0:T(8,128)(2,1)S(1)} %get-tuple-element.28.held1, f32[1,8192]{1,0:T(1,128)S(1)} %get-tuple-element.21.refs_0_.inverse, ...), custom_call_target="tpu_custom_call" | custom-call | flops 1600000000 | tf_op jit(solution)/shard_map/pallas_call | solution.py:227
  29.0 0.9 %collective-permute-done.6.received.refs_1_ = bf16[128,1024]{1,0:T(8,128)(2,1)S(1)} collective-permute-done((bf16[128,1024]{1,0:T(8,128)(2,1)S(1)}, bf16[128,1024]{1,0:T(8,128)(2,1)S(1)}, u32[]{:S(2)}, u32[]{:S(2)}) %collective-permute-start.6) | collective-permute-done | bytes 262176 | tf_op jit(solution)/shard_map/ppermute | solution.py:220
  30.0 2.1 %collective-permute-start.11 = (bf16[128,1024]{1,0:T(8,128)(2,1)S(1)}, bf16[128,1024]{1,0:T(8,128)(2,1)S(1)}, u32[]{:S(2)}, u32[]{:S(2)}) collective-permute-start(bf16[128,1024]{1,0:T(8,128)(2,1)S(1)} %shard_map.54.refs_0_), channel_id=1, source_target_pairs={{0,2},{2,0},{4,6},{6,4},{8,10},{10,8},{12,14},{14,12},{1,3},{3,1},... | collective-permute-start | bytes 786440 | tf_op jit(solution)/shard_map/ppermute | solution.py:215
  32.2 0.1 collective-permute-start.10
  32.2 4.6 %collective-permute-done.3.refs_0_ = bf16[128,1536]{1,0:T(8,128)(2,1)S(1)} collective-permute-done((bf16[128,1536]{1,0:T(8,128)(2,1)S(1)}, bf16[128,1536]{1,0:T(8,128)(2,1)S(1)}, u32[]{:S(2)}, u32[]{:S(2)}) %collective-permute-start.3) | collective-permute-done | bytes 393248 | tf_op jit(solution)/shard_map/ppermute | solution.py:215
  36.8 1.4 %collective-permute-start.9 = (bf16[128,1536]{1,0:T(8,128)(2,1)S(1)}, bf16[128,1536]{1,0:T(8,128)(2,1)S(1)}, u32[]{:S(2)}, u32[]{:S(2)}) collective-permute-start(bf16[128,1536]{1,0:T(8,128)(2,1)S(1)} %collective-permute-done.3.refs_0_), channel_id=1, source_target_pairs={{0,16},{16,0},{1,17},{17,1},{2,18},{18,2},{3,19},{19,3},{4,20},{20... | collective-permute-start | bytes 1179656 | tf_op jit(solution)/shard_map/ppermute | solution.py:237
  38.2 0.7 %shard_map.56.refs_0_.refs_4_ = f32[640,256]{1,0:T(8,128)S(1)} custom-call(s32[1]{0:T(128)S(6)} %copy.5.counts, bf16[640,4096]{1,0:T(8,128)(2,1)S(1)} %get-tuple-element.27.held0, bf16[640,4096]{1,0:T(8,128)(2,1)S(1)} %get-tuple-element.28.held1, f32[1,8192]{1,0:T(1,128)S(1)} %get-tuple-element.21.refs_0_.inverse, ...), custom_call_target="tpu_custom_call" | custom-call | flops 1600000000 | tf_op jit(solution)/shard_map/pallas_call | solution.py:227
  38.9 0.0 collective-permute-done.2.received.refs_1_
  39.0 0.1 shard_map.57.refs_5_
  39.0 1.9 %collective-permute-start.8 = (bf16[128,1024]{1,0:T(8,128)(2,1)S(1)}, bf16[128,1024]{1,0:T(8,128)(2,1)S(1)}, u32[]{:S(2)}, u32[]{:S(2)}) collective-permute-start(bf16[128,1024]{1,0:T(8,128)(2,1)S(1)} %shard_map.57.refs_5_), channel_id=1, source_target_pairs={{0,2},{2,0},{4,6},{6,4},{8,10},{10,8},{12,14},{14,12},{1,3},{3,1},... | collective-permute-start | bytes 786440 | tf_op jit(solution)/shard_map/ppermute | solution.py:215
  40.9 1.5 %collective-permute-done.11.refs_0_ = bf16[128,1024]{1,0:T(8,128)(2,1)S(1)} collective-permute-done((bf16[128,1024]{1,0:T(8,128)(2,1)S(1)}, bf16[128,1024]{1,0:T(8,128)(2,1)S(1)}, u32[]{:S(2)}, u32[]{:S(2)}) %collective-permute-start.11) | collective-permute-done | bytes 262176 | tf_op jit(solution)/shard_map/ppermute | solution.py:215
  42.4 0.0 collective-permute-start.7
  42.4 0.0 collective-permute-done.12.refs_2_
  42.4 1.1 %shard_map.58.refs_4_ = f32[640,256]{1,0:T(8,128)S(1)} custom-call(s32[1]{0:T(128)S(6)} %copy.5.counts, bf16[640,4096]{1,0:T(8,128)(2,1)S(1)} %get-tuple-element.27.held0, bf16[640,4096]{1,0:T(8,128)(2,1)S(1)} %get-tuple-element.28.held1, f32[1,8192]{1,0:T(1,128)S(1)} %get-tuple-element.21.refs_0_.inverse, ...), custom_call_target="tpu_custom_call" | custom-call | flops 1600000000 | tf_op jit(solution)/shard_map/pallas_call | solution.py:227
  43.5 0.3 collective-permute-done.7.refs_5_.got0
  43.8 1.7 %collective-permute-done.8.refs_0_ = bf16[128,1024]{1,0:T(8,128)(2,1)S(1)} collective-permute-done((bf16[128,1024]{1,0:T(8,128)(2,1)S(1)}, bf16[128,1024]{1,0:T(8,128)(2,1)S(1)}, u32[]{:S(2)}, u32[]{:S(2)}) %collective-permute-start.8) | collective-permute-done | bytes 262176 | tf_op jit(solution)/shard_map/ppermute | solution.py:215
  45.5 0.0 collective-permute-done.9.refs_2_
  45.5 0.0 collective-permute-done.10.refs_3_
  45.5 0.6 %shard_map.59.refs_5_ = f32[320,256]{1,0:T(8,128)S(1)} custom-call(s32[1]{0:T(128)S(6)} %copy.5.counts, bf16[640,4096]{1,0:T(8,128)(2,1)S(1)} %get-tuple-element.27.held0, bf16[640,4096]{1,0:T(8,128)(2,1)S(1)} %get-tuple-element.28.held1, f32[1,8192]{1,0:T(1,128)S(1)} %get-tuple-element.21.refs_0_.inverse, ...), custom_call_target="tpu_custom_call" | custom-call | flops 1600000000 | tf_op jit(solution)/shard_map/pallas_call | solution.py:227
  46.1 0.1 collective-permute-start.13
  46.2 0.6 %shard_map.60.mine = f32[320,256]{1,0:T(8,128)S(1)} custom-call(s32[1]{0:T(128)S(6)} %copy.5.counts, bf16[640,4096]{1,0:T(8,128)(2,1)S(1)} %get-tuple-element.27.held0, bf16[640,4096]{1,0:T(8,128)(2,1)S(1)} %get-tuple-element.28.held1, f32[1,8192]{1,0:T(1,128)S(1)} %get-tuple-element.21.refs_0_.inverse, ...), custom_call_target="tpu_custom_call" | custom-call | flops 1600000000 | tf_op jit(solution)/shard_map/pallas_call | solution.py:227
  46.8 1.0 %collective-permute-done.13.got = f32[320,256]{1,0:T(8,128)S(1)} collective-permute-done((f32[320,256]{1,0:T(8,128)S(1)}, f32[320,256]{1,0:T(8,128)S(1)}, u32[]{:S(2)}, u32[]{:S(2)}) %collective-permute-start.13) | collective-permute-done | bytes 327712 | tf_op jit(solution)/shard_map/ppermute | solution.py:286
  47.8 0.8 %shard_map.61 = f32[320,384]{1,0:T(8,128)} custom-call(f32[320,128]{1,0:T(8,128)S(1)} %get-tuple-element.25.mine0, f32[320,128]{1,0:T(8,128)S(1)} %collective-permute-done.7.refs_5_.got0, f32[320,256]{1,0:T(8,128)S(1)} %shard_map.60.mine, f32[320,256]{1,0:T(8,128)S(1)} %collective-permute-done.13.got), custom_call_target="tpu_custom_call" | custom-call | flops 1600000000 | tf_op jit(solution)/shard_map/pallas_call | solution.py:288
  (6 shorter events, 0.2 us)
Async XLA Ops:
  1.1 15.0 %collective-permute-start = (bf16[128,1536]{1,0:T(8,128)(2,1)S(1)}, bf16[128,1536]{1,0:T(8,128)(2,1)S(1)}, u32[]{:S(2)}, u32[]{:S(2)}) collective-permute-start(bf16[128,1536]{1,0:T(8,128)(2,1)S(1)} %get-tuple-element.24), channel_id=1, source_target_pairs={{0,4},{2,6},{4,8},{6,10},{8,12},{10,14},{12,0},{14,2},{1,5},{3,7},... | collective-permute-start | bytes 1179656 | tf_op jit(solution)/shard_map/ppermute | solution.py:244
  4.2 20.4 %collective-permute-start.1 = (bf16[128,1536]{1,0:T(8,128)(2,1)S(1)}, bf16[128,1536]{1,0:T(8,128)(2,1)S(1)}, u32[]{:S(2)}, u32[]{:S(2)}) collective-permute-start(bf16[128,1536]{1,0:T(8,128)(2,1)S(1)} %get-tuple-element.19), channel_id=1, source_target_pairs={{0,4},{2,6},{4,8},{6,10},{8,12},{10,14},{12,0},{14,2},{1,5},{3,7},... | collective-permute-start | bytes 1179656 | tf_op jit(solution)/shard_map/ppermute | solution.py:244
  6.4 1.6 %copy-start = (bf16[128,8192]{1,0:T(8,128)(2,1)S(1)}, bf16[128,8192]{1,0:T(8,128)(2,1)}, u32[]{:S(2)}) copy-start(bf16[128,8192]{1,0:T(8,128)(2,1)} %queries.19) | copy-start | bytes 6291460
  8.0 0.8 %copy-start.2 = (f32[8192]{0:T(1024)S(1)}, f32[8192]{0:T(1024)}, u32[]{:S(2)}) copy-start(f32[8192]{0:T(1024)} %param.7) | copy-start | bytes 98308
  16.2 3.7 %copy-start.1 = (bf16[128,8192]{1,0:T(8,128)(2,1)S(1)}, bf16[128,8192]{1,0:T(8,128)(2,1)}, u32[]{:S(2)}) copy-start(bf16[128,8192]{1,0:T(8,128)(2,1)} %queries.19) | copy-start | bytes 6291460
  16.2 10.5 %collective-permute-start.4 = (bf16[128,1536]{1,0:T(8,128)(2,1)S(1)}, bf16[128,1536]{1,0:T(8,128)(2,1)S(1)}, u32[]{:S(2)}, u32[]{:S(2)}) collective-permute-start(bf16[128,1536]{1,0:T(8,128)(2,1)S(1)} %shard_map.48.refs_0_), channel_id=1, source_target_pairs={{0,2},{2,0},{4,6},{6,4},{8,10},{10,8},{12,14},{14,12},{1,3},{3,1},... | collective-permute-start | bytes 1179656 | tf_op jit(solution)/shard_map/ppermute | solution.py:215
  18.3 11.7 %collective-permute-start.6 = (bf16[128,1024]{1,0:T(8,128)(2,1)S(1)}, bf16[128,1024]{1,0:T(8,128)(2,1)S(1)}, u32[]{:S(2)}, u32[]{:S(2)}) collective-permute-start(bf16[128,1024]{1,0:T(8,128)(2,1)S(1)} %shard_map.49.refs_3_), channel_id=1, source_target_pairs={{0,4},{2,6},{4,8},{6,10},{8,12},{10,14},{12,0},{14,2},{1,5},{3,7},... | collective-permute-start | bytes 786440 | tf_op jit(solution)/shard_map/ppermute | solution.py:220
  18.3 10.0 %collective-permute-start.5 = (bf16[128,1536]{1,0:T(8,128)(2,1)S(1)}, bf16[128,1536]{1,0:T(8,128)(2,1)S(1)}, u32[]{:S(2)}, u32[]{:S(2)}) collective-permute-start(bf16[128,1536]{1,0:T(8,128)(2,1)S(1)} %collective-permute-done.received.refs_1_), channel_id=1, source_target_pairs={{0,16},{16,0},{1,17},{17,1},{2,18},{18,2},{3,19},{19,3},{4,20},{20... | collective-permute-start | bytes 1179656 | tf_op jit(solution)/shard_map/ppermute | solution.py:237
  24.7 12.1 %collective-permute-start.3 = (bf16[128,1536]{1,0:T(8,128)(2,1)S(1)}, bf16[128,1536]{1,0:T(8,128)(2,1)S(1)}, u32[]{:S(2)}, u32[]{:S(2)}) collective-permute-start(bf16[128,1536]{1,0:T(8,128)(2,1)S(1)} %shard_map.51.refs_0_), channel_id=1, source_target_pairs={{0,2},{2,0},{4,6},{6,4},{8,10},{10,8},{12,14},{14,12},{1,3},{3,1},... | collective-permute-start | bytes 1179656 | tf_op jit(solution)/shard_map/ppermute | solution.py:215
  26.7 12.3 %collective-permute-start.2 = (bf16[128,1024]{1,0:T(8,128)(2,1)S(1)}, bf16[128,1024]{1,0:T(8,128)(2,1)S(1)}, u32[]{:S(2)}, u32[]{:S(2)}) collective-permute-start(bf16[128,1024]{1,0:T(8,128)(2,1)S(1)} %shard_map.52.refs_2_), channel_id=1, source_target_pairs={{0,4},{2,6},{4,8},{6,10},{8,12},{10,14},{12,0},{14,2},{1,5},{3,7},... | collective-permute-start | bytes 786440 | tf_op jit(solution)/shard_map/ppermute | solution.py:220
  26.8 15.7 %collective-permute-start.12 = (bf16[128,1536]{1,0:T(8,128)(2,1)S(1)}, bf16[128,1536]{1,0:T(8,128)(2,1)S(1)}, u32[]{:S(2)}, u32[]{:S(2)}) collective-permute-start(bf16[128,1536]{1,0:T(8,128)(2,1)S(1)} %collective-permute-done.4.refs_0_), channel_id=1, source_target_pairs={{0,16},{16,0},{1,17},{17,1},{2,18},{18,2},{3,19},{19,3},{4,20},{20... | collective-permute-start | bytes 1179656 | tf_op jit(solution)/shard_map/ppermute | solution.py:237
  30.0 12.4 %collective-permute-start.11 = (bf16[128,1024]{1,0:T(8,128)(2,1)S(1)}, bf16[128,1024]{1,0:T(8,128)(2,1)S(1)}, u32[]{:S(2)}, u32[]{:S(2)}) collective-permute-start(bf16[128,1024]{1,0:T(8,128)(2,1)S(1)} %shard_map.54.refs_0_), channel_id=1, source_target_pairs={{0,2},{2,0},{4,6},{6,4},{8,10},{10,8},{12,14},{14,12},{1,3},{3,1},... | collective-permute-start | bytes 786440 | tf_op jit(solution)/shard_map/ppermute | solution.py:215
  32.2 13.3 %collective-permute-start.10 = (bf16[128,1536]{1,0:T(8,128)(2,1)S(1)}, bf16[128,1536]{1,0:T(8,128)(2,1)S(1)}, u32[]{:S(2)}, u32[]{:S(2)}) collective-permute-start(bf16[128,1536]{1,0:T(8,128)(2,1)S(1)} %shard_map.55.refs_3_), channel_id=1, source_target_pairs={{0,4},{2,6},{4,8},{6,10},{8,12},{10,14},{12,0},{14,2},{1,5},{3,7},... | collective-permute-start | bytes 1179656 | tf_op jit(solution)/shard_map/ppermute | solution.py:220
  36.8 8.7 %collective-permute-start.9 = (bf16[128,1536]{1,0:T(8,128)(2,1)S(1)}, bf16[128,1536]{1,0:T(8,128)(2,1)S(1)}, u32[]{:S(2)}, u32[]{:S(2)}) collective-permute-start(bf16[128,1536]{1,0:T(8,128)(2,1)S(1)} %collective-permute-done.3.refs_0_), channel_id=1, source_target_pairs={{0,16},{16,0},{1,17},{17,1},{2,18},{18,2},{3,19},{19,3},{4,20},{20... | collective-permute-start | bytes 1179656 | tf_op jit(solution)/shard_map/ppermute | solution.py:237
  39.0 6.4 %collective-permute-start.8 = (bf16[128,1024]{1,0:T(8,128)(2,1)S(1)}, bf16[128,1024]{1,0:T(8,128)(2,1)S(1)}, u32[]{:S(2)}, u32[]{:S(2)}) collective-permute-start(bf16[128,1024]{1,0:T(8,128)(2,1)S(1)} %shard_map.57.refs_5_), channel_id=1, source_target_pairs={{0,2},{2,0},{4,6},{6,4},{8,10},{10,8},{12,14},{14,12},{1,3},{3,1},... | collective-permute-start | bytes 786440 | tf_op jit(solution)/shard_map/ppermute | solution.py:215
  42.4 1.4 %collective-permute-start.7 = (f32[320,128]{1,0:T(8,128)S(1)}, f32[320,128]{1,0:T(8,128)S(1)}, u32[]{:S(2)}, u32[]{:S(2)}) collective-permute-start(f32[320,128]{1,0:T(8,128)S(1)} %get-tuple-element.30.refs_0_), channel_id=1, source_target_pairs={{0,1},{1,0},{2,3},{3,2},{4,5},{5,4},{6,7},{7,6},{8,9},{9,8},{10,11... | collective-permute-start | bytes 491528 | tf_op jit(solution)/shard_map/ppermute | solution.py:283
  46.1 1.7 %collective-permute-start.13 = (f32[320,256]{1,0:T(8,128)S(1)}, f32[320,256]{1,0:T(8,128)S(1)}, u32[]{:S(2)}, u32[]{:S(2)}) collective-permute-start(f32[320,256]{1,0:T(8,128)S(1)} %shard_map.59.refs_5_), channel_id=1, source_target_pairs={{0,1},{1,0},{2,3},{3,2},{4,5},{5,4},{6,7},{7,6},{8,9},{9,8},{10,11... | collective-permute-start | bytes 983048 | tf_op jit(solution)/shard_map/ppermute | solution.py:286

commit v10 on v9

--- a/solution.py
+++ b/solution.py
@@ -137,12 +137,16 @@
     return held[0] if k < CHUNKS // 2 else held[1]
 
 
-def pair_kernel(ks, side, factor, fresh, counts, held0, held1, inverse, *refs):
+def one_product(k, rows, held, inverse, chunk):
+    dims = inverse.shape[1]
+    scaled = chunk[...].astype(jnp.float32) * inverse[:, columns_of(k, dims)]
+    return products(held_of(k, held)[rows, columns_of(k, dims, True)], scaled.astype(jnp.bfloat16))
+
+
+def pair_kernel(ks, alone, fresh, held0, held1, inverse, *refs):
     count = len(ks)
     chunks, out, block_buf = refs[: 2 * count], refs[-2], refs[-1]
     dims = inverse.shape[1]
-    size = out.shape[0]
-    first = 0 if side is None else side * size
     rows = chunks[0].shape[0]
     for i, k in enumerate(ks):
         width = width_of(k, dims)
@@ -150,21 +154,48 @@
             scaled = chunks[2 * i + b][...].astype(jnp.float32) * inverse[:, columns_of(k, dims)]
             block_buf[pl.ds(b * rows, rows), :width] = scaled.astype(jnp.bfloat16)
         held = held_of(k, (held0, held1))
-        term = products(held[first : first + size, columns_of(k, dims, True)], block_buf[:, :width])
+        term = products(held[:, columns_of(k, dims, True)], block_buf[:, :width])
         if i > 0:
             out[...] += term
         elif fresh:
             out[...] = term
         else:
-            out[...] = refs[2 * count][first : first + size] + term
-    if side is not None:
-        out[...] *= scale_of(factor, counts, size, side)
-
-
-def final_kernel(mine0, got0, mine, got, out):
-    rows = mine0.shape[1]
-    out[:, :rows] = mine0[...] + got0[...]
-    out[:, rows:] = mine[...] + got[...]
+            out[...] = refs[2 * count][...] + term
+    if alone is not None:
+        out[:, rows:] += one_product(
+            alone, slice(None), (held0, held1), inverse, refs[2 * count + 1 - fresh]
+        )
+
+
+def far_kernel(k, factor, counts, held0, held1, inverse, near, far, sums, *outs):
+    near_out, theirs, mine, block = outs
+    dims = inverse.shape[1]
+    rows = near.shape[0]
+    half = mine.shape[0]
+    held = held_of(k, (held0, held1))
+    for b, chunk in enumerate((near, far)):
+        scaled = chunk[...].astype(jnp.float32) * inverse[:, columns_of(k, dims)]
+        block[b * rows : (b + 1) * rows, :] = scaled.astype(jnp.bfloat16)
+    for side, out in enumerate((theirs, mine)):
+        part = slice(side * half, (side + 1) * half)
+        total = sums[part] + products(held[part, columns_of(k, dims, True)], block[...])
+        near_out[part] = total[:, :rows]
+        out[...] = total[:, rows:] * scale_of(factor, counts, half, side)
+
+
+def near_kernel(k, side, factor, counts, held0, held1, inverse, last, near, *refs):
+    out = refs[-1]
+    half = out.shape[0]
+    part = slice(side * half, (side + 1) * half)
+    total = near[part] + one_product(k, part, (held0, held1), inverse, last)
+    out[...] = total * scale_of(factor, counts, half, side)
+
+
+def final_kernel(*refs):
+    terms, out = refs[:-1], refs[-1]
+    rows = terms[0].shape[1]
+    for i in range(3):
+        out[:, i * rows : (i + 1) * rows] = terms[2 * i][...] + terms[2 * i + 1][...]
 
 
 def on_device(queries, documents, counts, eigenvalues):
@@ -220,17 +251,19 @@
         far[k] = lax.ppermute(sent, "dp", ahead)
         return sent
 
-    def pair_scores(*ks, sums=None, side=None, until=()):
+    def pair_scores(*ks, sums=None, alone=None, until=()):
         operands = [*held, inverse] + [block[k] for k in ks for block in (near, far)]
         if sums is not None:
             operands.append(sums)
+        if alone is not None:
+            operands.append(far[alone])
         return call(
-            functools.partial(pair_kernel, ks, side, factor, sums is None),
-            floats(doc_rows if side is None else half, 2 * rows),
-            [SMEM] + [VMEM] * len(operands) + [ANY] * len(until),
+            functools.partial(pair_kernel, ks, alone, sums is None),
+            floats(doc_rows, 2 * rows),
+            [VMEM] * len(operands) + [ANY] * len(until),
             VMEM,
             [pltpu.VMEM((2 * rows, max(width_of(k, dims) for k in ks)), queries.dtype)],
-        )(counts, *operands, *until)
+        )(*operands, *until)
 
     def send_across(block, k, *until):
         sent = lax.optimization_barrier((block[k], *until))[0]
@@ -281,11 +314,31 @@
 
     out = step(3, sums)
     got0 = lax.ppermute(lax.optimization_barrier((theirs0, out))[0], "layer", across)
-    sums = pair_scores(2, 5, sums=sums, until=(out,))
-    theirs = pair_scores(3, 4, sums=sums, side=0, until=(got0,))
-    got = lax.ppermute(theirs, "layer", across)
-    mine = pair_scores(3, 4, sums=sums, side=1, until=(theirs,))
-    return call(final_kernel, floats(half, 3 * rows), [VMEM] * 4, VMEM, [])(mine0, got0, mine, got)
+    sums = pair_scores(2, 5, sums=sums, alone=3, until=(out,))
+    near_sums, theirs_far, mine_far = call(
+        functools.partial(far_kernel, 4, factor),
+        [floats(doc_rows, rows), floats(half, rows), floats(half, rows)],
+        [SMEM] + [VMEM] * 6,
+        [VMEM] * 3,
+        [pltpu.VMEM((2 * rows, width_of(4, dims)), queries.dtype)],
+    )(counts, *held, inverse, near[4], far[4], sums)
+    got_far = lax.ppermute(theirs_far, "layer", across)
+
+    def near_scores(side, *until):
+        return call(
+            functools.partial(near_kernel, 3, side, factor),
+            floats(half, rows),
+            [SMEM] + [VMEM] * 5 + [ANY] * len(until),
+            VMEM,
+            [],
+        )(counts, *held, inverse, near[3], near_sums, *until)
+
+    theirs_near = near_scores(0, got0, got_far)
+    got_near = lax.ppermute(theirs_near, "layer", across)
+    mine_near = near_scores(1, theirs_near)
+    return call(final_kernel, floats(half, 3 * rows), [VMEM] * 6, VMEM, [])(
+        mine0, got0, mine_near, got_near, mine_far, got_far
+    )
 
 
 def solution(mesh):

time: 48.9 us -> 49.6 us (1.014)
  Pallas kernels: 12.4 us -> 12.9 us
    ppermute x4, waiting for transfers between devices: 7.73 us -> 6.15 us  [step(): near[k] = lax.ppermute(out, 'dp', pair)]
    ppermute x1 -> x2, waiting for transfers between devices: 0.96 us -> 2.21 us  [the longest x1 1.3 us: on_device(): got_far = lax.ppermute(theirs_far, 'layer', across)]
    ppermute x3, waiting for transfers between devices: 0.01 us -> 0.73 us  [send_across(): block[CHUNKS - 1 - k] = lax.ppermute(sent, 'groups', across)]
    pallas_call x6 -> x7, Pallas kernels: 4.62 us -> 5.08 us  [the longest x3 2.87 us: pair_scores(): call(functools.partial(pair_kernel, ks, alone, sums is None), floats(doc_...]
  transfers between devices with their start and end apart: 14 -> 15, of which waited for: 8 -> 9; matrix products, arithmetic and copies ran while one was open for 0% -> 0% of each run, Pallas kernels for 20% -> 21%
where the time goes in v10:
time: 49.6 us; the launch traced here: 49.4 us
  starting transfers between devices  17.6 us (35%)
  waiting for transfers between devices  15.7 us (32%)
  Pallas kernels  12.9 us (26%)
  local copies, waits for them, and re-layouts  2.35 us (5%)
  between operations  0.85 us (2%)
    ppermute x4, starting transfers between devices, step(): near[k] = lax.ppermute(out, 'dp', pair)  7.96 us
    pallas_call x2, Pallas kernels, own_scores(): call(functools.partial(own_kernel, part, pieces, factor), outs, [SMEM, HB...  6.38 us
    ppermute x4, waiting for transfers between devices, step(): near[k] = lax.ppermute(out, 'dp', pair)  6.15 us
    ppermute x2, waiting for transfers between devices, on_device(): far[k] = lax.ppermute(sent[k], 'dp', ahead)  5.72 us
    ppermute x2, starting transfers between devices, on_device(): far[k] = lax.ppermute(sent[k], 'dp', ahead)  4.65 us
    ppermute x3, starting transfers between devices, send_across(): block[CHUNKS - 1 - k] = lax.ppermute(sent, 'groups', across)  4.54 us
    pallas_call x3, Pallas kernels, pair_scores(): call(functools.partial(pair_kernel, ks, alone, sums is None), floats(doc_...  2.87 us
    unnamed x6, local copies, waits for them, and re-layouts  2.35 us
  transfers between devices with their start and end apart: 15, of which 9 were waited for; matrix products, arithmetic and copies ran while one was open for 0% of the time, Pallas kernels for 21%

profile of v10, /device:TPU:0, one launch (start us, length us, event | category | flops | bytes accessed | tf_op | source)
XLA Modules:
  0.0 49.4 jit_solution(15222336776752871792)
XLA Ops:
  0.0 1.1 %shard_map.46 = (bf16[128,1536]{1,0:T(8,128)(2,1)S(1)}, bf16[128,1536]{1,0:T(8,128)(2,1)S(1)}) custom-call(bf16[128,8192]{1,0:T(8,128)(2,1)} %queries.19), custom_call_target="tpu_custom_call" | custom-call | flops 1024 | tf_op jit(solution)/shard_map/pallas_call | solution.py:229
  1.1 3.1 %collective-permute-start = (bf16[128,1536]{1,0:T(8,128)(2,1)S(1)}, bf16[128,1536]{1,0:T(8,128)(2,1)S(1)}, u32[]{:S(2)}, u32[]{:S(2)}) collective-permute-start(bf16[128,1536]{1,0:T(8,128)(2,1)S(1)} %get-tuple-element.27), channel_id=1, source_target_pairs={{0,4},{2,6},{4,8},{6,10},{8,12},{10,14},{12,0},{14,2},{1,5},{3,7},... | collective-permute-start | bytes 1179656 | tf_op jit(solution)/shard_map/ppermute | solution.py:277
  4.2 1.6 %collective-permute-start.1 = (bf16[128,1536]{1,0:T(8,128)(2,1)S(1)}, bf16[128,1536]{1,0:T(8,128)(2,1)S(1)}, u32[]{:S(2)}, u32[]{:S(2)}) collective-permute-start(bf16[128,1536]{1,0:T(8,128)(2,1)S(1)} %get-tuple-element.22), channel_id=1, source_target_pairs={{0,4},{2,6},{4,8},{6,10},{8,12},{10,14},{12,0},{14,2},{1,5},{3,7},... | collective-permute-start | bytes 1179656 | tf_op jit(solution)/shard_map/ppermute | solution.py:277
  6.4 0.0 copy-start
  6.5 1.6 %copy-done = bf16[128,8192]{1,0:T(8,128)(2,1)S(1)} copy-done((bf16[128,8192]{1,0:T(8,128)(2,1)S(1)}, bf16[128,8192]{1,0:T(8,128)(2,1)}, u32[]{:S(2)}) %copy-start) | copy-done | bytes 2097176
  8.0 0.0 copy-start.2
  8.0 0.8 %copy-done.2 = f32[8192]{0:T(1024)S(1)} copy-done((f32[8192]{0:T(1024)S(1)}, f32[8192]{0:T(1024)}, u32[]{:S(2)}) %copy-start.2) | copy-done | bytes 32792
  8.8 3.2 %shard_map.47 = (f32[320,128]{1,0:T(8,128)S(1)}, f32[320,128]{1,0:T(8,128)S(1)}, bf16[640,4096]{1,0:T(8,128)(2,1)S(1)}, f32[1,8192]{1,0:T(1,128)S(1)}) custom-call(s32[1]{0:T(128)S(6)} %copy.5.counts, bf16[640,8192]{1,0:T(8,128)(2,1)} %documents.3, bf16[128,8192]{1,0:T(8,128)(2,1)S(1)} %copy-done, f32[1,8192]{1,0:T(1,128)S(1)} %bitcast.1), custom_call_target="tpu_custom_call" | custom-call | flops 1600000000 | tf_op jit(solution)/shard_map/pallas_call | solution.py:287
  12.0 4.2 %collective-permute-done.received.refs_1_ = bf16[128,1536]{1,0:T(8,128)(2,1)S(1)} collective-permute-done((bf16[128,1536]{1,0:T(8,128)(2,1)S(1)}, bf16[128,1536]{1,0:T(8,128)(2,1)S(1)}, u32[]{:S(2)}, u32[]{:S(2)}) %collective-permute-start) | collective-permute-done | bytes 393248 | tf_op jit(solution)/shard_map/ppermute | solution.py:277
  16.2 0.0 copy-start.1
  16.2 2.0 %collective-permute-start.4 = (bf16[128,1536]{1,0:T(8,128)(2,1)S(1)}, bf16[128,1536]{1,0:T(8,128)(2,1)S(1)}, u32[]{:S(2)}, u32[]{:S(2)}) collective-permute-start(bf16[128,1536]{1,0:T(8,128)(2,1)S(1)} %shard_map.48.refs_0_), channel_id=1, source_target_pairs={{0,2},{2,0},{4,6},{6,4},{8,10},{10,8},{12,14},{14,12},{1,3},{3,1},... | collective-permute-start | bytes 1179656 | tf_op jit(solution)/shard_map/ppermute | solution.py:246
  18.3 0.1 collective-permute-start.6
  18.3 1.6 %collective-permute-start.5 = (bf16[128,1536]{1,0:T(8,128)(2,1)S(1)}, bf16[128,1536]{1,0:T(8,128)(2,1)S(1)}, u32[]{:S(2)}, u32[]{:S(2)}) collective-permute-start(bf16[128,1536]{1,0:T(8,128)(2,1)S(1)} %collective-permute-done.received.refs_1_), channel_id=1, source_target_pairs={{0,16},{16,0},{1,17},{17,1},{2,18},{18,2},{3,19},{19,3},{4,20},{20... | collective-permute-start | bytes 1179656 | tf_op jit(solution)/shard_map/ppermute | solution.py:270
  19.9 0.0 copy-done.1
  19.9 3.2 %shard_map.50 = (f32[320,128]{1,0:T(8,128)S(1)}, f32[320,128]{1,0:T(8,128)S(1)}, bf16[640,4096]{1,0:T(8,128)(2,1)S(1)}) custom-call(s32[1]{0:T(128)S(6)} %copy.5.counts, bf16[640,8192]{1,0:T(8,128)(2,1)} %documents.3, bf16[128,8192]{1,0:T(8,128)(2,1)S(1)} %copy-done.1, f32[1,8192]{1,0:T(1,128)S(1)} %get-tuple-element.24.refs_0_.inverse, ...), custom_call_target="tpu_custom_call" | custom-call | flops 1600000000 | tf_op jit(solution)/shard_map/pallas_call | solution.py:287
  23.1 1.5 %collective-permute-done.1.received.refs_1_ = bf16[128,1536]{1,0:T(8,128)(2,1)S(1)} collective-permute-done((bf16[128,1536]{1,0:T(8,128)(2,1)S(1)}, bf16[128,1536]{1,0:T(8,128)(2,1)S(1)}, u32[]{:S(2)}, u32[]{:S(2)}) %collective-permute-start.1) | collective-permute-done | bytes 393248 | tf_op jit(solution)/shard_map/ppermute | solution.py:277
  24.7 2.0 %collective-permute-start.3 = (bf16[128,1536]{1,0:T(8,128)(2,1)S(1)}, bf16[128,1536]{1,0:T(8,128)(2,1)S(1)}, u32[]{:S(2)}, u32[]{:S(2)}) collective-permute-start(bf16[128,1536]{1,0:T(8,128)(2,1)S(1)} %shard_map.51.refs_0_), channel_id=1, source_target_pairs={{0,2},{2,0},{4,6},{6,4},{8,10},{10,8},{12,14},{14,12},{1,3},{3,1},... | collective-permute-start | bytes 1179656 | tf_op jit(solution)/shard_map/ppermute | solution.py:246
  26.7 0.1 collective-permute-start.2
  26.7 0.0 collective-permute-done.4.refs_0_
  26.8 1.6 %collective-permute-start.12 = (bf16[128,1536]{1,0:T(8,128)(2,1)S(1)}, bf16[128,1536]{1,0:T(8,128)(2,1)S(1)}, u32[]{:S(2)}, u32[]{:S(2)}) collective-permute-start(bf16[128,1536]{1,0:T(8,128)(2,1)S(1)} %collective-permute-done.4.refs_0_), channel_id=1, source_target_pairs={{0,16},{16,0},{1,17},{17,1},{2,18},{18,2},{3,19},{19,3},{4,20},{20... | collective-permute-start | bytes 1179656 | tf_op jit(solution)/shard_map/ppermute | solution.py:270
  28.3 0.0 collective-permute-done.5.refs_3_
  28.3 0.7 %shard_map.53.refs_0_.refs_2_ = f32[640,256]{1,0:T(8,128)S(1)} custom-call(bf16[640,4096]{1,0:T(8,128)(2,1)S(1)} %get-tuple-element.30.held0, bf16[640,4096]{1,0:T(8,128)(2,1)S(1)} %get-tuple-element.31.held1, f32[1,8192]{1,0:T(1,128)S(1)} %get-tuple-element.24.refs_0_.inverse, bf16[128,1536]{1,0:T(8,128)(2,1)S(1)} %collective-permute-done.4.refs_0_, ...), custom_call_target="tpu_custom_call" | custom-call | flops 1600000000 | tf_op jit(solution)/shard_map/pallas_call | solution.py:260
  29.0 0.9 %collective-permute-done.6.received.refs_1_ = bf16[128,1024]{1,0:T(8,128)(2,1)S(1)} collective-permute-done((bf16[128,1024]{1,0:T(8,128)(2,1)S(1)}, bf16[128,1024]{1,0:T(8,128)(2,1)S(1)}, u32[]{:S(2)}, u32[]{:S(2)}) %collective-permute-start.6) | collective-permute-done | bytes 262176 | tf_op jit(solution)/shard_map/ppermute | solution.py:251
  30.0 2.1 %collective-permute-start.11 = (bf16[128,1024]{1,0:T(8,128)(2,1)S(1)}, bf16[128,1024]{1,0:T(8,128)(2,1)S(1)}, u32[]{:S(2)}, u32[]{:S(2)}) collective-permute-start(bf16[128,1024]{1,0:T(8,128)(2,1)S(1)} %shard_map.54.refs_0_), channel_id=1, source_target_pairs={{0,2},{2,0},{4,6},{6,4},{8,10},{10,8},{12,14},{14,12},{1,3},{3,1},... | collective-permute-start | bytes 786440 | tf_op jit(solution)/shard_map/ppermute | solution.py:246
  32.2 0.1 collective-permute-start.10
  32.2 4.6 %collective-permute-done.3.refs_0_ = bf16[128,1536]{1,0:T(8,128)(2,1)S(1)} collective-permute-done((bf16[128,1536]{1,0:T(8,128)(2,1)S(1)}, bf16[128,1536]{1,0:T(8,128)(2,1)S(1)}, u32[]{:S(2)}, u32[]{:S(2)}) %collective-permute-start.3) | collective-permute-done | bytes 393248 | tf_op jit(solution)/shard_map/ppermute | solution.py:246
  36.8 1.4 %collective-permute-start.9 = (bf16[128,1536]{1,0:T(8,128)(2,1)S(1)}, bf16[128,1536]{1,0:T(8,128)(2,1)S(1)}, u32[]{:S(2)}, u32[]{:S(2)}) collective-permute-start(bf16[128,1536]{1,0:T(8,128)(2,1)S(1)} %collective-permute-done.3.refs_0_), channel_id=1, source_target_pairs={{0,16},{16,0},{1,17},{17,1},{2,18},{18,2},{3,19},{19,3},{4,20},{20... | collective-permute-start | bytes 1179656 | tf_op jit(solution)/shard_map/ppermute | solution.py:270
  38.2 0.7 %shard_map.56.refs_0_.refs_4_ = f32[640,256]{1,0:T(8,128)S(1)} custom-call(bf16[640,4096]{1,0:T(8,128)(2,1)S(1)} %get-tuple-element.30.held0, bf16[640,4096]{1,0:T(8,128)(2,1)S(1)} %get-tuple-element.31.held1, f32[1,8192]{1,0:T(1,128)S(1)} %get-tuple-element.24.refs_0_.inverse, bf16[128,1536]{1,0:T(8,128)(2,1)S(1)} %collective-permute-done.3.refs_0_, ...), custom_call_target="tpu_custom_call" | custom-call | flops 1600000000 | tf_op jit(solution)/shard_map/pallas_call | solution.py:260
  38.9 0.0 collective-permute-done.2.received.refs_5_
  39.0 0.1 shard_map.57.refs_6_
  39.0 1.9 %collective-permute-start.8 = (bf16[128,1024]{1,0:T(8,128)(2,1)S(1)}, bf16[128,1024]{1,0:T(8,128)(2,1)S(1)}, u32[]{:S(2)}, u32[]{:S(2)}) collective-permute-start(bf16[128,1024]{1,0:T(8,128)(2,1)S(1)} %shard_map.57.refs_6_), channel_id=1, source_target_pairs={{0,2},{2,0},{4,6},{6,4},{8,10},{10,8},{12,14},{14,12},{1,3},{3,1},... | collective-permute-start | bytes 786440 | tf_op jit(solution)/shard_map/ppermute | solution.py:246
  40.9 1.5 %collective-permute-done.11.refs_0_ = bf16[128,1024]{1,0:T(8,128)(2,1)S(1)} collective-permute-done((bf16[128,1024]{1,0:T(8,128)(2,1)S(1)}, bf16[128,1024]{1,0:T(8,128)(2,1)S(1)}, u32[]{:S(2)}, u32[]{:S(2)}) %collective-permute-start.11) | collective-permute-done | bytes 262176 | tf_op jit(solution)/shard_map/ppermute | solution.py:246
  42.4 0.0 collective-permute-start.7
  42.4 0.0 collective-permute-done.12.refs_2_
  42.4 1.4 %shard_map.58.sums = f32[640,256]{1,0:T(8,128)S(1)} custom-call(bf16[640,4096]{1,0:T(8,128)(2,1)S(1)} %get-tuple-element.30.held0, bf16[640,4096]{1,0:T(8,128)(2,1)S(1)} %get-tuple-element.31.held1, f32[1,8192]{1,0:T(1,128)S(1)} %get-tuple-element.24.refs_0_.inverse, bf16[128,1024]{1,0:T(8,128)(2,1)S(1)} %collective-permute-done.11.refs_0_, ...), custom_call_target="tpu_custom_call" | custom-call | flops 1600000000 | tf_op jit(solution)/shard_map/pallas_call | solution.py:260
  43.8 0.7 %collective-permute-done.9.near = bf16[128,1536]{1,0:T(8,128)(2,1)S(1)} collective-permute-done((bf16[128,1536]{1,0:T(8,128)(2,1)S(1)}, bf16[128,1536]{1,0:T(8,128)(2,1)S(1)}, u32[]{:S(2)}, u32[]{:S(2)}) %collective-permute-start.9) | collective-permute-done | bytes 393248 | tf_op jit(solution)/shard_map/ppermute | solution.py:270
  44.6 0.0 collective-permute-done.10.far
  44.6 0.7 %shard_map.59 = (f32[640,128]{1,0:T(8,128)S(1)}, f32[320,128]{1,0:T(8,128)S(1)}, f32[320,128]{1,0:T(8,128)S(1)}) custom-call(s32[1]{0:T(128)S(6)} %copy.5.counts, bf16[640,4096]{1,0:T(8,128)(2,1)S(1)} %get-tuple-element.30.held0, bf16[640,4096]{1,0:T(8,128)(2,1)S(1)} %get-tuple-element.31.held1, f32[1,8192]{1,0:T(1,128)S(1)} %get-tuple-element.24.refs_0_.inverse, ...), custom_call_target="tpu_custom_call" | custom-call | flops 1600000000 | tf_op jit(solution)/shard_map/pallas_call | solution.py:318
  45.3 0.1 collective-permute-start.13
  45.4 0.0 collective-permute-done.7.refs_0_.refs_1_
  45.4 0.1 collective-permute-done.8.last
  45.5 1.3 %collective-permute-done.13.refs_1_.refs_5_ = f32[320,128]{1,0:T(8,128)S(1)} collective-permute-done((f32[320,128]{1,0:T(8,128)S(1)}, f32[320,128]{1,0:T(8,128)S(1)}, u32[]{:S(2)}, u32[]{:S(2)}) %collective-permute-start.13) | collective-permute-done | bytes 163872 | tf_op jit(solution)/shard_map/ppermute | solution.py:325
  46.7 0.3 shard_map.60.refs_0_
  47.1 0.2 collective-permute-start.14
  47.3 0.3 shard_map.61.refs_2_
  47.6 0.9 %collective-permute-done.14.refs_3_ = f32[320,128]{1,0:T(8,128)S(1)} collective-permute-done((f32[320,128]{1,0:T(8,128)S(1)}, f32[320,128]{1,0:T(8,128)S(1)}, u32[]{:S(2)}, u32[]{:S(2)}) %collective-permute-start.14) | collective-permute-done | bytes 163872 | tf_op jit(solution)/shard_map/ppermute | solution.py:337
  48.6 0.8 %shard_map.62 = f32[320,384]{1,0:T(8,128)} custom-call(f32[320,128]{1,0:T(8,128)S(1)} %get-tuple-element.28.refs_0_, f32[320,128]{1,0:T(8,128)S(1)} %collective-permute-done.7.refs_0_.refs_1_, f32[320,128]{1,0:T(8,128)S(1)} %shard_map.61.refs_2_, f32[320,128]{1,0:T(8,128)S(1)} %collective-permute-done.14.refs_3_, f32[320,128]{1,0:T(8,128)S(1)} %get-tuple-element.38.refs_4_, ...), custom_call_target="tpu_custom_call" | custom-call | flops 1600000000 | tf_op jit(solution)/shard_map/pallas_call | solution.py:339
  (6 shorter events, 0.2 us)
Async XLA Ops:
  1.1 15.0 %collective-permute-start = (bf16[128,1536]{1,0:T(8,128)(2,1)S(1)}, bf16[128,1536]{1,0:T(8,128)(2,1)S(1)}, u32[]{:S(2)}, u32[]{:S(2)}) collective-permute-start(bf16[128,1536]{1,0:T(8,128)(2,1)S(1)} %get-tuple-element.27), channel_id=1, source_target_pairs={{0,4},{2,6},{4,8},{6,10},{8,12},{10,14},{12,0},{14,2},{1,5},{3,7},... | collective-permute-start | bytes 1179656 | tf_op jit(solution)/shard_map/ppermute | solution.py:277
  4.2 20.4 %collective-permute-start.1 = (bf16[128,1536]{1,0:T(8,128)(2,1)S(1)}, bf16[128,1536]{1,0:T(8,128)(2,1)S(1)}, u32[]{:S(2)}, u32[]{:S(2)}) collective-permute-start(bf16[128,1536]{1,0:T(8,128)(2,1)S(1)} %get-tuple-element.22), channel_id=1, source_target_pairs={{0,4},{2,6},{4,8},{6,10},{8,12},{10,14},{12,0},{14,2},{1,5},{3,7},... | collective-permute-start | bytes 1179656 | tf_op jit(solution)/shard_map/ppermute | solution.py:277
  6.4 1.6 %copy-start = (bf16[128,8192]{1,0:T(8,128)(2,1)S(1)}, bf16[128,8192]{1,0:T(8,128)(2,1)}, u32[]{:S(2)}) copy-start(bf16[128,8192]{1,0:T(8,128)(2,1)} %queries.19) | copy-start | bytes 6291460
  8.0 0.8 %copy-start.2 = (f32[8192]{0:T(1024)S(1)}, f32[8192]{0:T(1024)}, u32[]{:S(2)}) copy-start(f32[8192]{0:T(1024)} %param.7) | copy-start | bytes 98308
  16.2 3.7 %copy-start.1 = (bf16[128,8192]{1,0:T(8,128)(2,1)S(1)}, bf16[128,8192]{1,0:T(8,128)(2,1)}, u32[]{:S(2)}) copy-start(bf16[128,8192]{1,0:T(8,128)(2,1)} %queries.19) | copy-start | bytes 6291460
  16.2 10.5 %collective-permute-start.4 = (bf16[128,1536]{1,0:T(8,128)(2,1)S(1)}, bf16[128,1536]{1,0:T(8,128)(2,1)S(1)}, u32[]{:S(2)}, u32[]{:S(2)}) collective-permute-start(bf16[128,1536]{1,0:T(8,128)(2,1)S(1)} %shard_map.48.refs_0_), channel_id=1, source_target_pairs={{0,2},{2,0},{4,6},{6,4},{8,10},{10,8},{12,14},{14,12},{1,3},{3,1},... | collective-permute-start | bytes 1179656 | tf_op jit(solution)/shard_map/ppermute | solution.py:246
  18.3 11.7 %collective-permute-start.6 = (bf16[128,1024]{1,0:T(8,128)(2,1)S(1)}, bf16[128,1024]{1,0:T(8,128)(2,1)S(1)}, u32[]{:S(2)}, u32[]{:S(2)}) collective-permute-start(bf16[128,1024]{1,0:T(8,128)(2,1)S(1)} %shard_map.49.refs_3_), channel_id=1, source_target_pairs={{0,4},{2,6},{4,8},{6,10},{8,12},{10,14},{12,0},{14,2},{1,5},{3,7},... | collective-permute-start | bytes 786440 | tf_op jit(solution)/shard_map/ppermute | solution.py:251
  18.3 10.0 %collective-permute-start.5 = (bf16[128,1536]{1,0:T(8,128)(2,1)S(1)}, bf16[128,1536]{1,0:T(8,128)(2,1)S(1)}, u32[]{:S(2)}, u32[]{:S(2)}) collective-permute-start(bf16[128,1536]{1,0:T(8,128)(2,1)S(1)} %collective-permute-done.received.refs_1_), channel_id=1, source_target_pairs={{0,16},{16,0},{1,17},{17,1},{2,18},{18,2},{3,19},{19,3},{4,20},{20... | collective-permute-start | bytes 1179656 | tf_op jit(solution)/shard_map/ppermute | solution.py:270
  24.7 12.1 %collective-permute-start.3 = (bf16[128,1536]{1,0:T(8,128)(2,1)S(1)}, bf16[128,1536]{1,0:T(8,128)(2,1)S(1)}, u32[]{:S(2)}, u32[]{:S(2)}) collective-permute-start(bf16[128,1536]{1,0:T(8,128)(2,1)S(1)} %shard_map.51.refs_0_), channel_id=1, source_target_pairs={{0,2},{2,0},{4,6},{6,4},{8,10},{10,8},{12,14},{14,12},{1,3},{3,1},... | collective-permute-start | bytes 1179656 | tf_op jit(solution)/shard_map/ppermute | solution.py:246
  26.7 12.3 %collective-permute-start.2 = (bf16[128,1024]{1,0:T(8,128)(2,1)S(1)}, bf16[128,1024]{1,0:T(8,128)(2,1)S(1)}, u32[]{:S(2)}, u32[]{:S(2)}) collective-permute-start(bf16[128,1024]{1,0:T(8,128)(2,1)S(1)} %shard_map.52.refs_2_), channel_id=1, source_target_pairs={{0,4},{2,6},{4,8},{6,10},{8,12},{10,14},{12,0},{14,2},{1,5},{3,7},... | collective-permute-start | bytes 786440 | tf_op jit(solution)/shard_map/ppermute | solution.py:251
  26.8 15.7 %collective-permute-start.12 = (bf16[128,1536]{1,0:T(8,128)(2,1)S(1)}, bf16[128,1536]{1,0:T(8,128)(2,1)S(1)}, u32[]{:S(2)}, u32[]{:S(2)}) collective-permute-start(bf16[128,1536]{1,0:T(8,128)(2,1)S(1)} %collective-permute-done.4.refs_0_), channel_id=1, source_target_pairs={{0,16},{16,0},{1,17},{17,1},{2,18},{18,2},{3,19},{19,3},{4,20},{20... | collective-permute-start | bytes 1179656 | tf_op jit(solution)/shard_map/ppermute | solution.py:270
  30.0 12.4 %collective-permute-start.11 = (bf16[128,1024]{1,0:T(8,128)(2,1)S(1)}, bf16[128,1024]{1,0:T(8,128)(2,1)S(1)}, u32[]{:S(2)}, u32[]{:S(2)}) collective-permute-start(bf16[128,1024]{1,0:T(8,128)(2,1)S(1)} %shard_map.54.refs_0_), channel_id=1, source_target_pairs={{0,2},{2,0},{4,6},{6,4},{8,10},{10,8},{12,14},{14,12},{1,3},{3,1},... | collective-permute-start | bytes 786440 | tf_op jit(solution)/shard_map/ppermute | solution.py:246
  32.2 12.4 %collective-permute-start.10 = (bf16[128,1536]{1,0:T(8,128)(2,1)S(1)}, bf16[128,1536]{1,0:T(8,128)(2,1)S(1)}, u32[]{:S(2)}, u32[]{:S(2)}) collective-permute-start(bf16[128,1536]{1,0:T(8,128)(2,1)S(1)} %shard_map.55.refs_3_), channel_id=1, source_target_pairs={{0,4},{2,6},{4,8},{6,10},{8,12},{10,14},{12,0},{14,2},{1,5},{3,7},... | collective-permute-start | bytes 1179656 | tf_op jit(solution)/shard_map/ppermute | solution.py:251
  36.8 7.8 %collective-permute-start.9 = (bf16[128,1536]{1,0:T(8,128)(2,1)S(1)}, bf16[128,1536]{1,0:T(8,128)(2,1)S(1)}, u32[]{:S(2)}, u32[]{:S(2)}) collective-permute-start(bf16[128,1536]{1,0:T(8,128)(2,1)S(1)} %collective-permute-done.3.refs_0_), channel_id=1, source_target_pairs={{0,16},{16,0},{1,17},{17,1},{2,18},{18,2},{3,19},{19,3},{4,20},{20... | collective-permute-start | bytes 1179656 | tf_op jit(solution)/shard_map/ppermute | solution.py:270
  39.0 6.4 %collective-permute-start.8 = (bf16[128,1024]{1,0:T(8,128)(2,1)S(1)}, bf16[128,1024]{1,0:T(8,128)(2,1)S(1)}, u32[]{:S(2)}, u32[]{:S(2)}) collective-permute-start(bf16[128,1024]{1,0:T(8,128)(2,1)S(1)} %shard_map.57.refs_6_), channel_id=1, source_target_pairs={{0,2},{2,0},{4,6},{6,4},{8,10},{10,8},{12,14},{14,12},{1,3},{3,1},... | collective-permute-start | bytes 786440 | tf_op jit(solution)/shard_map/ppermute | solution.py:246
  42.4 3.0 %collective-permute-start.7 = (f32[320,128]{1,0:T(8,128)S(1)}, f32[320,128]{1,0:T(8,128)S(1)}, u32[]{:S(2)}, u32[]{:S(2)}) collective-permute-start(f32[320,128]{1,0:T(8,128)S(1)} %get-tuple-element.33.refs_0_), channel_id=1, source_target_pairs={{0,1},{1,0},{2,3},{3,2},{4,5},{5,4},{6,7},{7,6},{8,9},{9,8},{10,11... | collective-permute-start | bytes 491528 | tf_op jit(solution)/shard_map/ppermute | solution.py:316
  45.3 1.5 %collective-permute-start.13 = (f32[320,128]{1,0:T(8,128)S(1)}, f32[320,128]{1,0:T(8,128)S(1)}, u32[]{:S(2)}, u32[]{:S(2)}) collective-permute-start(f32[320,128]{1,0:T(8,128)S(1)} %get-tuple-element.37), channel_id=1, source_target_pairs={{0,1},{1,0},{2,3},{3,2},{4,5},{5,4},{6,7},{7,6},{8,9},{9,8},{10,11... | collective-permute-start | bytes 491528 | tf_op jit(solution)/shard_map/ppermute | solution.py:325
  47.1 1.5 %collective-permute-start.14 = (f32[320,128]{1,0:T(8,128)S(1)}, f32[320,128]{1,0:T(8,128)S(1)}, u32[]{:S(2)}, u32[]{:S(2)}) collective-permute-start(f32[320,128]{1,0:T(8,128)S(1)} %shard_map.60.refs_0_), channel_id=1, source_target_pairs={{0,1},{1,0},{2,3},{3,2},{4,5},{5,4},{6,7},{7,6},{8,9},{9,8},{10,11... | collective-permute-start | bytes 491528 | tf_op jit(solution)/shard_map/ppermute | solution.py:337

commit v11 on v10

--- a/solution.py
+++ b/solution.py
@@ -333,9 +333,9 @@
             [],
         )(counts, *held, inverse, near[3], near_sums, *until)
 
-    theirs_near = near_scores(0, got0, got_far)
+    theirs_near = near_scores(0, got0)
     got_near = lax.ppermute(theirs_near, "layer", across)
-    mine_near = near_scores(1, theirs_near)
+    mine_near = near_scores(1, theirs_near, got_far)
     return call(final_kernel, floats(half, 3 * rows), [VMEM] * 6, VMEM, [])(
         mine0, got0, mine_near, got_near, mine_far, got_far
     )

time: 49.6 us -> 48.4 us (0.976)
  waiting for transfers between devices: 15.7 us -> 14.2 us
    ppermute x1, waiting for transfers between devices: 1.3 us -> 0.47 us  [on_device(): got_far = lax.ppermute(theirs_far, 'layer', across)]
    ppermute x1, waiting for transfers between devices: 0.91 us -> 0.22 us  [on_device(): got_near = lax.ppermute(theirs_near, 'layer', across)]
  transfers between devices with their start and end apart: 15 -> 15, of which waited for: 9 -> 9; matrix products, arithmetic and copies ran while one was open for 0% -> 0% of each run, Pallas kernels for 21% -> 23%
where the time goes in v11:
time: 48.4 us; the launch traced here: 48.1 us
  starting transfers between devices  17.9 us (37%)
  waiting for transfers between devices  14.2 us (29%)
  Pallas kernels  12.9 us (27%)
  local copies, waits for them, and re-layouts  2.35 us (5%)
  between operations  0.85 us (2%)
    ppermute x4, starting transfers between devices, step(): near[k] = lax.ppermute(out, 'dp', pair)  7.96 us
    pallas_call x2, Pallas kernels, own_scores(): call(functools.partial(own_kernel, part, pieces, factor), outs, [SMEM, HB...  6.38 us
    ppermute x4, waiting for transfers between devices, step(): near[k] = lax.ppermute(out, 'dp', pair)  6.15 us
    ppermute x2, waiting for transfers between devices, on_device(): far[k] = lax.ppermute(sent[k], 'dp', ahead)  5.72 us
    ppermute x2, starting transfers between devices, on_device(): far[k] = lax.ppermute(sent[k], 'dp', ahead)  4.65 us
    ppermute x3, starting transfers between devices, send_across(): block[CHUNKS - 1 - k] = lax.ppermute(sent, 'groups', across)  4.54 us
    pallas_call x3, Pallas kernels, pair_scores(): call(functools.partial(pair_kernel, ks, alone, sums is None), floats(doc_...  2.87 us
    unnamed x6, local copies, waits for them, and re-layouts  2.35 us
  transfers between devices with their start and end apart: 15, of which 9 were waited for; matrix products, arithmetic and copies ran while one was open for 0% of the time, Pallas kernels for 23%

profile of v11, /device:TPU:0, one launch (start us, length us, event | category | flops | bytes accessed | tf_op | source)
XLA Modules:
  0.0 48.1 jit_solution(17391961009703927173)
XLA Ops:
  0.0 1.1 %shard_map.46 = (bf16[128,1536]{1,0:T(8,128)(2,1)S(1)}, bf16[128,1536]{1,0:T(8,128)(2,1)S(1)}) custom-call(bf16[128,8192]{1,0:T(8,128)(2,1)} %queries.19), custom_call_target="tpu_custom_call" | custom-call | flops 1024 | tf_op jit(solution)/shard_map/pallas_call | solution.py:229
  1.1 3.1 %collective-permute-start = (bf16[128,1536]{1,0:T(8,128)(2,1)S(1)}, bf16[128,1536]{1,0:T(8,128)(2,1)S(1)}, u32[]{:S(2)}, u32[]{:S(2)}) collective-permute-start(bf16[128,1536]{1,0:T(8,128)(2,1)S(1)} %get-tuple-element.27), channel_id=1, source_target_pairs={{0,4},{2,6},{4,8},{6,10},{8,12},{10,14},{12,0},{14,2},{1,5},{3,7},... | collective-permute-start | bytes 1179656 | tf_op jit(solution)/shard_map/ppermute | solution.py:277
  4.2 1.6 %collective-permute-start.1 = (bf16[128,1536]{1,0:T(8,128)(2,1)S(1)}, bf16[128,1536]{1,0:T(8,128)(2,1)S(1)}, u32[]{:S(2)}, u32[]{:S(2)}) collective-permute-start(bf16[128,1536]{1,0:T(8,128)(2,1)S(1)} %get-tuple-element.22), channel_id=1, source_target_pairs={{0,4},{2,6},{4,8},{6,10},{8,12},{10,14},{12,0},{14,2},{1,5},{3,7},... | collective-permute-start | bytes 1179656 | tf_op jit(solution)/shard_map/ppermute | solution.py:277
  6.4 0.0 copy-start
  6.5 1.6 %copy-done = bf16[128,8192]{1,0:T(8,128)(2,1)S(1)} copy-done((bf16[128,8192]{1,0:T(8,128)(2,1)S(1)}, bf16[128,8192]{1,0:T(8,128)(2,1)}, u32[]{:S(2)}) %copy-start) | copy-done | bytes 2097176
  8.0 0.0 copy-start.2
  8.0 0.8 %copy-done.2 = f32[8192]{0:T(1024)S(1)} copy-done((f32[8192]{0:T(1024)S(1)}, f32[8192]{0:T(1024)}, u32[]{:S(2)}) %copy-start.2) | copy-done | bytes 32792
  8.8 3.2 %shard_map.47 = (f32[320,128]{1,0:T(8,128)S(1)}, f32[320,128]{1,0:T(8,128)S(1)}, bf16[640,4096]{1,0:T(8,128)(2,1)S(1)}, f32[1,8192]{1,0:T(1,128)S(1)}) custom-call(s32[1]{0:T(128)S(6)} %copy.5.counts, bf16[640,8192]{1,0:T(8,128)(2,1)} %documents.3, bf16[128,8192]{1,0:T(8,128)(2,1)S(1)} %copy-done, f32[1,8192]{1,0:T(1,128)S(1)} %bitcast.1), custom_call_target="tpu_custom_call" | custom-call | flops 1600000000 | tf_op jit(solution)/shard_map/pallas_call | solution.py:287
  12.0 4.2 %collective-permute-done.received.refs_1_ = bf16[128,1536]{1,0:T(8,128)(2,1)S(1)} collective-permute-done((bf16[128,1536]{1,0:T(8,128)(2,1)S(1)}, bf16[128,1536]{1,0:T(8,128)(2,1)S(1)}, u32[]{:S(2)}, u32[]{:S(2)}) %collective-permute-start) | collective-permute-done | bytes 393248 | tf_op jit(solution)/shard_map/ppermute | solution.py:277
  16.2 0.0 copy-start.1
  16.2 2.0 %collective-permute-start.4 = (bf16[128,1536]{1,0:T(8,128)(2,1)S(1)}, bf16[128,1536]{1,0:T(8,128)(2,1)S(1)}, u32[]{:S(2)}, u32[]{:S(2)}) collective-permute-start(bf16[128,1536]{1,0:T(8,128)(2,1)S(1)} %shard_map.48.refs_0_), channel_id=1, source_target_pairs={{0,2},{2,0},{4,6},{6,4},{8,10},{10,8},{12,14},{14,12},{1,3},{3,1},... | collective-permute-start | bytes 1179656 | tf_op jit(solution)/shard_map/ppermute | solution.py:246
  18.3 0.1 collective-permute-start.6
  18.3 1.6 %collective-permute-start.5 = (bf16[128,1536]{1,0:T(8,128)(2,1)S(1)}, bf16[128,1536]{1,0:T(8,128)(2,1)S(1)}, u32[]{:S(2)}, u32[]{:S(2)}) collective-permute-start(bf16[128,1536]{1,0:T(8,128)(2,1)S(1)} %collective-permute-done.received.refs_1_), channel_id=1, source_target_pairs={{0,16},{16,0},{1,17},{17,1},{2,18},{18,2},{3,19},{19,3},{4,20},{20... | collective-permute-start | bytes 1179656 | tf_op jit(solution)/shard_map/ppermute | solution.py:270
  19.9 0.0 copy-done.1
  19.9 3.2 %shard_map.50 = (f32[320,128]{1,0:T(8,128)S(1)}, f32[320,128]{1,0:T(8,128)S(1)}, bf16[640,4096]{1,0:T(8,128)(2,1)S(1)}) custom-call(s32[1]{0:T(128)S(6)} %copy.5.counts, bf16[640,8192]{1,0:T(8,128)(2,1)} %documents.3, bf16[128,8192]{1,0:T(8,128)(2,1)S(1)} %copy-done.1, f32[1,8192]{1,0:T(1,128)S(1)} %get-tuple-element.24.refs_0_.inverse, ...), custom_call_target="tpu_custom_call" | custom-call | flops 1600000000 | tf_op jit(solution)/shard_map/pallas_call | solution.py:287
  23.1 1.5 %collective-permute-done.1.received.refs_1_ = bf16[128,1536]{1,0:T(8,128)(2,1)S(1)} collective-permute-done((bf16[128,1536]{1,0:T(8,128)(2,1)S(1)}, bf16[128,1536]{1,0:T(8,128)(2,1)S(1)}, u32[]{:S(2)}, u32[]{:S(2)}) %collective-permute-start.1) | collective-permute-done | bytes 393248 | tf_op jit(solution)/shard_map/ppermute | solution.py:277
  24.7 2.0 %collective-permute-start.3 = (bf16[128,1536]{1,0:T(8,128)(2,1)S(1)}, bf16[128,1536]{1,0:T(8,128)(2,1)S(1)}, u32[]{:S(2)}, u32[]{:S(2)}) collective-permute-start(bf16[128,1536]{1,0:T(8,128)(2,1)S(1)} %shard_map.51.refs_0_), channel_id=1, source_target_pairs={{0,2},{2,0},{4,6},{6,4},{8,10},{10,8},{12,14},{14,12},{1,3},{3,1},... | collective-permute-start | bytes 1179656 | tf_op jit(solution)/shard_map/ppermute | solution.py:246
  26.7 0.1 collective-permute-start.2
  26.7 0.0 collective-permute-done.4.refs_0_
  26.8 1.6 %collective-permute-start.12 = (bf16[128,1536]{1,0:T(8,128)(2,1)S(1)}, bf16[128,1536]{1,0:T(8,128)(2,1)S(1)}, u32[]{:S(2)}, u32[]{:S(2)}) collective-permute-start(bf16[128,1536]{1,0:T(8,128)(2,1)S(1)} %collective-permute-done.4.refs_0_), channel_id=1, source_target_pairs={{0,16},{16,0},{1,17},{17,1},{2,18},{18,2},{3,19},{19,3},{4,20},{20... | collective-permute-start | bytes 1179656 | tf_op jit(solution)/shard_map/ppermute | solution.py:270
  28.3 0.0 collective-permute-done.5.refs_3_
  28.3 0.7 %shard_map.53.refs_0_.refs_2_ = f32[640,256]{1,0:T(8,128)S(1)} custom-call(bf16[640,4096]{1,0:T(8,128)(2,1)S(1)} %get-tuple-element.30.held0, bf16[640,4096]{1,0:T(8,128)(2,1)S(1)} %get-tuple-element.31.held1, f32[1,8192]{1,0:T(1,128)S(1)} %get-tuple-element.24.refs_0_.inverse, bf16[128,1536]{1,0:T(8,128)(2,1)S(1)} %collective-permute-done.4.refs_0_, ...), custom_call_target="tpu_custom_call" | custom-call | flops 1600000000 | tf_op jit(solution)/shard_map/pallas_call | solution.py:260
  29.0 0.9 %collective-permute-done.6.received.refs_1_ = bf16[128,1024]{1,0:T(8,128)(2,1)S(1)} collective-permute-done((bf16[128,1024]{1,0:T(8,128)(2,1)S(1)}, bf16[128,1024]{1,0:T(8,128)(2,1)S(1)}, u32[]{:S(2)}, u32[]{:S(2)}) %collective-permute-start.6) | collective-permute-done | bytes 262176 | tf_op jit(solution)/shard_map/ppermute | solution.py:251
  30.0 2.1 %collective-permute-start.11 = (bf16[128,1024]{1,0:T(8,128)(2,1)S(1)}, bf16[128,1024]{1,0:T(8,128)(2,1)S(1)}, u32[]{:S(2)}, u32[]{:S(2)}) collective-permute-start(bf16[128,1024]{1,0:T(8,128)(2,1)S(1)} %shard_map.54.refs_0_), channel_id=1, source_target_pairs={{0,2},{2,0},{4,6},{6,4},{8,10},{10,8},{12,14},{14,12},{1,3},{3,1},... | collective-permute-start | bytes 786440 | tf_op jit(solution)/shard_map/ppermute | solution.py:246
  32.2 0.1 collective-permute-start.10
  32.2 4.6 %collective-permute-done.3.refs_0_ = bf16[128,1536]{1,0:T(8,128)(2,1)S(1)} collective-permute-done((bf16[128,1536]{1,0:T(8,128)(2,1)S(1)}, bf16[128,1536]{1,0:T(8,128)(2,1)S(1)}, u32[]{:S(2)}, u32[]{:S(2)}) %collective-permute-start.3) | collective-permute-done | bytes 393248 | tf_op jit(solution)/shard_map/ppermute | solution.py:246
  36.8 1.4 %collective-permute-start.9 = (bf16[128,1536]{1,0:T(8,128)(2,1)S(1)}, bf16[128,1536]{1,0:T(8,128)(2,1)S(1)}, u32[]{:S(2)}, u32[]{:S(2)}) collective-permute-start(bf16[128,1536]{1,0:T(8,128)(2,1)S(1)} %collective-permute-done.3.refs_0_), channel_id=1, source_target_pairs={{0,16},{16,0},{1,17},{17,1},{2,18},{18,2},{3,19},{19,3},{4,20},{20... | collective-permute-start | bytes 1179656 | tf_op jit(solution)/shard_map/ppermute | solution.py:270
  38.2 0.7 %shard_map.56.refs_0_.refs_4_ = f32[640,256]{1,0:T(8,128)S(1)} custom-call(bf16[640,4096]{1,0:T(8,128)(2,1)S(1)} %get-tuple-element.30.held0, bf16[640,4096]{1,0:T(8,128)(2,1)S(1)} %get-tuple-element.31.held1, f32[1,8192]{1,0:T(1,128)S(1)} %get-tuple-element.24.refs_0_.inverse, bf16[128,1536]{1,0:T(8,128)(2,1)S(1)} %collective-permute-done.3.refs_0_, ...), custom_call_target="tpu_custom_call" | custom-call | flops 1600000000 | tf_op jit(solution)/shard_map/pallas_call | solution.py:260
  38.9 0.0 collective-permute-done.2.received.refs_5_
  39.0 0.1 shard_map.57.refs_6_
  39.0 1.9 %collective-permute-start.8 = (bf16[128,1024]{1,0:T(8,128)(2,1)S(1)}, bf16[128,1024]{1,0:T(8,128)(2,1)S(1)}, u32[]{:S(2)}, u32[]{:S(2)}) collective-permute-start(bf16[128,1024]{1,0:T(8,128)(2,1)S(1)} %shard_map.57.refs_6_), channel_id=1, source_target_pairs={{0,2},{2,0},{4,6},{6,4},{8,10},{10,8},{12,14},{14,12},{1,3},{3,1},... | collective-permute-start | bytes 786440 | tf_op jit(solution)/shard_map/ppermute | solution.py:246
  40.9 1.5 %collective-permute-done.11.refs_0_ = bf16[128,1024]{1,0:T(8,128)(2,1)S(1)} collective-permute-done((bf16[128,1024]{1,0:T(8,128)(2,1)S(1)}, bf16[128,1024]{1,0:T(8,128)(2,1)S(1)}, u32[]{:S(2)}, u32[]{:S(2)}) %collective-permute-start.11) | collective-permute-done | bytes 262176 | tf_op jit(solution)/shard_map/ppermute | solution.py:246
  42.4 0.0 collective-permute-start.7
  42.4 0.0 collective-permute-done.12.refs_2_
  42.4 1.4 %shard_map.58.sums = f32[640,256]{1,0:T(8,128)S(1)} custom-call(bf16[640,4096]{1,0:T(8,128)(2,1)S(1)} %get-tuple-element.30.held0, bf16[640,4096]{1,0:T(8,128)(2,1)S(1)} %get-tuple-element.31.held1, f32[1,8192]{1,0:T(1,128)S(1)} %get-tuple-element.24.refs_0_.inverse, bf16[128,1024]{1,0:T(8,128)(2,1)S(1)} %collective-permute-done.11.refs_0_, ...), custom_call_target="tpu_custom_call" | custom-call | flops 1600000000 | tf_op jit(solution)/shard_map/pallas_call | solution.py:260
  43.8 0.7 %collective-permute-done.9.near = bf16[128,1536]{1,0:T(8,128)(2,1)S(1)} collective-permute-done((bf16[128,1536]{1,0:T(8,128)(2,1)S(1)}, bf16[128,1536]{1,0:T(8,128)(2,1)S(1)}, u32[]{:S(2)}, u32[]{:S(2)}) %collective-permute-start.9) | collective-permute-done | bytes 393248 | tf_op jit(solution)/shard_map/ppermute | solution.py:270
  44.6 0.0 collective-permute-done.10.far
  44.6 0.7 %shard_map.59 = (f32[640,128]{1,0:T(8,128)S(1)}, f32[320,128]{1,0:T(8,128)S(1)}, f32[320,128]{1,0:T(8,128)S(1)}) custom-call(s32[1]{0:T(128)S(6)} %copy.5.counts, bf16[640,4096]{1,0:T(8,128)(2,1)S(1)} %get-tuple-element.30.held0, bf16[640,4096]{1,0:T(8,128)(2,1)S(1)} %get-tuple-element.31.held1, f32[1,8192]{1,0:T(1,128)S(1)} %get-tuple-element.24.refs_0_.inverse, ...), custom_call_target="tpu_custom_call" | custom-call | flops 1600000000 | tf_op jit(solution)/shard_map/pallas_call | solution.py:318
  45.3 0.1 collective-permute-start.13
  45.4 0.0 collective-permute-done.7.refs_0_.refs_1_
  45.4 0.1 collective-permute-done.8.last
  45.5 0.3 shard_map.60.refs_0_
  45.8 0.5 %collective-permute-start.14 = (f32[320,128]{1,0:T(8,128)S(1)}, f32[320,128]{1,0:T(8,128)S(1)}, u32[]{:S(2)}, u32[]{:S(2)}) collective-permute-start(f32[320,128]{1,0:T(8,128)S(1)} %shard_map.60.refs_0_), channel_id=1, source_target_pairs={{0,1},{1,0},{2,3},{3,2},{4,5},{5,4},{6,7},{7,6},{8,9},{9,8},{10,11... | collective-permute-start | bytes 491528 | tf_op jit(solution)/shard_map/ppermute | solution.py:337
  46.3 0.5 collective-permute-done.13.refs_1_.refs_5_
  46.7 0.3 shard_map.61.refs_2_
  47.1 0.2 collective-permute-done.14.refs_3_
  47.3 0.8 %shard_map.62 = f32[320,384]{1,0:T(8,128)} custom-call(f32[320,128]{1,0:T(8,128)S(1)} %get-tuple-element.28.refs_0_, f32[320,128]{1,0:T(8,128)S(1)} %collective-permute-done.7.refs_0_.refs_1_, f32[320,128]{1,0:T(8,128)S(1)} %shard_map.61.refs_2_, f32[320,128]{1,0:T(8,128)S(1)} %collective-permute-done.14.refs_3_, f32[320,128]{1,0:T(8,128)S(1)} %get-tuple-element.38.refs_4_, ...), custom_call_target="tpu_custom_call" | custom-call | flops 1600000000 | tf_op jit(solution)/shard_map/pallas_call | solution.py:339
  (6 shorter events, 0.2 us)
Async XLA Ops:
  1.1 15.0 %collective-permute-start = (bf16[128,1536]{1,0:T(8,128)(2,1)S(1)}, bf16[128,1536]{1,0:T(8,128)(2,1)S(1)}, u32[]{:S(2)}, u32[]{:S(2)}) collective-permute-start(bf16[128,1536]{1,0:T(8,128)(2,1)S(1)} %get-tuple-element.27), channel_id=1, source_target_pairs={{0,4},{2,6},{4,8},{6,10},{8,12},{10,14},{12,0},{14,2},{1,5},{3,7},... | collective-permute-start | bytes 1179656 | tf_op jit(solution)/shard_map/ppermute | solution.py:277
  4.2 20.4 %collective-permute-start.1 = (bf16[128,1536]{1,0:T(8,128)(2,1)S(1)}, bf16[128,1536]{1,0:T(8,128)(2,1)S(1)}, u32[]{:S(2)}, u32[]{:S(2)}) collective-permute-start(bf16[128,1536]{1,0:T(8,128)(2,1)S(1)} %get-tuple-element.22), channel_id=1, source_target_pairs={{0,4},{2,6},{4,8},{6,10},{8,12},{10,14},{12,0},{14,2},{1,5},{3,7},... | collective-permute-start | bytes 1179656 | tf_op jit(solution)/shard_map/ppermute | solution.py:277
  6.4 1.6 %copy-start = (bf16[128,8192]{1,0:T(8,128)(2,1)S(1)}, bf16[128,8192]{1,0:T(8,128)(2,1)}, u32[]{:S(2)}) copy-start(bf16[128,8192]{1,0:T(8,128)(2,1)} %queries.19) | copy-start | bytes 6291460
  8.0 0.8 %copy-start.2 = (f32[8192]{0:T(1024)S(1)}, f32[8192]{0:T(1024)}, u32[]{:S(2)}) copy-start(f32[8192]{0:T(1024)} %param.7) | copy-start | bytes 98308
  16.2 3.7 %copy-start.1 = (bf16[128,8192]{1,0:T(8,128)(2,1)S(1)}, bf16[128,8192]{1,0:T(8,128)(2,1)}, u32[]{:S(2)}) copy-start(bf16[128,8192]{1,0:T(8,128)(2,1)} %queries.19) | copy-start | bytes 6291460
  16.2 10.5 %collective-permute-start.4 = (bf16[128,1536]{1,0:T(8,128)(2,1)S(1)}, bf16[128,1536]{1,0:T(8,128)(2,1)S(1)}, u32[]{:S(2)}, u32[]{:S(2)}) collective-permute-start(bf16[128,1536]{1,0:T(8,128)(2,1)S(1)} %shard_map.48.refs_0_), channel_id=1, source_target_pairs={{0,2},{2,0},{4,6},{6,4},{8,10},{10,8},{12,14},{14,12},{1,3},{3,1},... | collective-permute-start | bytes 1179656 | tf_op jit(solution)/shard_map/ppermute | solution.py:246
  18.3 11.7 %collective-permute-start.6 = (bf16[128,1024]{1,0:T(8,128)(2,1)S(1)}, bf16[128,1024]{1,0:T(8,128)(2,1)S(1)}, u32[]{:S(2)}, u32[]{:S(2)}) collective-permute-start(bf16[128,1024]{1,0:T(8,128)(2,1)S(1)} %shard_map.49.refs_3_), channel_id=1, source_target_pairs={{0,4},{2,6},{4,8},{6,10},{8,12},{10,14},{12,0},{14,2},{1,5},{3,7},... | collective-permute-start | bytes 786440 | tf_op jit(solution)/shard_map/ppermute | solution.py:251
  18.3 10.0 %collective-permute-start.5 = (bf16[128,1536]{1,0:T(8,128)(2,1)S(1)}, bf16[128,1536]{1,0:T(8,128)(2,1)S(1)}, u32[]{:S(2)}, u32[]{:S(2)}) collective-permute-start(bf16[128,1536]{1,0:T(8,128)(2,1)S(1)} %collective-permute-done.received.refs_1_), channel_id=1, source_target_pairs={{0,16},{16,0},{1,17},{17,1},{2,18},{18,2},{3,19},{19,3},{4,20},{20... | collective-permute-start | bytes 1179656 | tf_op jit(solution)/shard_map/ppermute | solution.py:270
  24.7 12.1 %collective-permute-start.3 = (bf16[128,1536]{1,0:T(8,128)(2,1)S(1)}, bf16[128,1536]{1,0:T(8,128)(2,1)S(1)}, u32[]{:S(2)}, u32[]{:S(2)}) collective-permute-start(bf16[128,1536]{1,0:T(8,128)(2,1)S(1)} %shard_map.51.refs_0_), channel_id=1, source_target_pairs={{0,2},{2,0},{4,6},{6,4},{8,10},{10,8},{12,14},{14,12},{1,3},{3,1},... | collective-permute-start | bytes 1179656 | tf_op jit(solution)/shard_map/ppermute | solution.py:246
  26.7 12.3 %collective-permute-start.2 = (bf16[128,1024]{1,0:T(8,128)(2,1)S(1)}, bf16[128,1024]{1,0:T(8,128)(2,1)S(1)}, u32[]{:S(2)}, u32[]{:S(2)}) collective-permute-start(bf16[128,1024]{1,0:T(8,128)(2,1)S(1)} %shard_map.52.refs_2_), channel_id=1, source_target_pairs={{0,4},{2,6},{4,8},{6,10},{8,12},{10,14},{12,0},{14,2},{1,5},{3,7},... | collective-permute-start | bytes 786440 | tf_op jit(solution)/shard_map/ppermute | solution.py:251
  26.8 15.7 %collective-permute-start.12 = (bf16[128,1536]{1,0:T(8,128)(2,1)S(1)}, bf16[128,1536]{1,0:T(8,128)(2,1)S(1)}, u32[]{:S(2)}, u32[]{:S(2)}) collective-permute-start(bf16[128,1536]{1,0:T(8,128)(2,1)S(1)} %collective-permute-done.4.refs_0_), channel_id=1, source_target_pairs={{0,16},{16,0},{1,17},{17,1},{2,18},{18,2},{3,19},{19,3},{4,20},{20... | collective-permute-start | bytes 1179656 | tf_op jit(solution)/shard_map/ppermute | solution.py:270
  30.0 12.4 %collective-permute-start.11 = (bf16[128,1024]{1,0:T(8,128)(2,1)S(1)}, bf16[128,1024]{1,0:T(8,128)(2,1)S(1)}, u32[]{:S(2)}, u32[]{:S(2)}) collective-permute-start(bf16[128,1024]{1,0:T(8,128)(2,1)S(1)} %shard_map.54.refs_0_), channel_id=1, source_target_pairs={{0,2},{2,0},{4,6},{6,4},{8,10},{10,8},{12,14},{14,12},{1,3},{3,1},... | collective-permute-start | bytes 786440 | tf_op jit(solution)/shard_map/ppermute | solution.py:246
  32.2 12.4 %collective-permute-start.10 = (bf16[128,1536]{1,0:T(8,128)(2,1)S(1)}, bf16[128,1536]{1,0:T(8,128)(2,1)S(1)}, u32[]{:S(2)}, u32[]{:S(2)}) collective-permute-start(bf16[128,1536]{1,0:T(8,128)(2,1)S(1)} %shard_map.55.refs_3_), channel_id=1, source_target_pairs={{0,4},{2,6},{4,8},{6,10},{8,12},{10,14},{12,0},{14,2},{1,5},{3,7},... | collective-permute-start | bytes 1179656 | tf_op jit(solution)/shard_map/ppermute | solution.py:251
  36.8 7.8 %collective-permute-start.9 = (bf16[128,1536]{1,0:T(8,128)(2,1)S(1)}, bf16[128,1536]{1,0:T(8,128)(2,1)S(1)}, u32[]{:S(2)}, u32[]{:S(2)}) collective-permute-start(bf16[128,1536]{1,0:T(8,128)(2,1)S(1)} %collective-permute-done.3.refs_0_), channel_id=1, source_target_pairs={{0,16},{16,0},{1,17},{17,1},{2,18},{18,2},{3,19},{19,3},{4,20},{20... | collective-permute-start | bytes 1179656 | tf_op jit(solution)/shard_map/ppermute | solution.py:270
  39.0 6.4 %collective-permute-start.8 = (bf16[128,1024]{1,0:T(8,128)(2,1)S(1)}, bf16[128,1024]{1,0:T(8,128)(2,1)S(1)}, u32[]{:S(2)}, u32[]{:S(2)}) collective-permute-start(bf16[128,1024]{1,0:T(8,128)(2,1)S(1)} %shard_map.57.refs_6_), channel_id=1, source_target_pairs={{0,2},{2,0},{4,6},{6,4},{8,10},{10,8},{12,14},{14,12},{1,3},{3,1},... | collective-permute-start | bytes 786440 | tf_op jit(solution)/shard_map/ppermute | solution.py:246
  42.4 3.0 %collective-permute-start.7 = (f32[320,128]{1,0:T(8,128)S(1)}, f32[320,128]{1,0:T(8,128)S(1)}, u32[]{:S(2)}, u32[]{:S(2)}) collective-permute-start(f32[320,128]{1,0:T(8,128)S(1)} %get-tuple-element.33.refs_0_), channel_id=1, source_target_pairs={{0,1},{1,0},{2,3},{3,2},{4,5},{5,4},{6,7},{7,6},{8,9},{9,8},{10,11... | collective-permute-start | bytes 491528 | tf_op jit(solution)/shard_map/ppermute | solution.py:316
  45.3 1.5 %collective-permute-start.13 = (f32[320,128]{1,0:T(8,128)S(1)}, f32[320,128]{1,0:T(8,128)S(1)}, u32[]{:S(2)}, u32[]{:S(2)}) collective-permute-start(f32[320,128]{1,0:T(8,128)S(1)} %get-tuple-element.37), channel_id=1, source_target_pairs={{0,1},{1,0},{2,3},{3,2},{4,5},{5,4},{6,7},{7,6},{8,9},{9,8},{10,11... | collective-permute-start | bytes 491528 | tf_op jit(solution)/shard_map/ppermute | solution.py:325
  45.8 1.5 %collective-permute-start.14 = (f32[320,128]{1,0:T(8,128)S(1)}, f32[320,128]{1,0:T(8,128)S(1)}, u32[]{:S(2)}, u32[]{:S(2)}) collective-permute-start(f32[320,128]{1,0:T(8,128)S(1)} %shard_map.60.refs_0_), channel_id=1, source_target_pairs={{0,1},{1,0},{2,3},{3,2},{4,5},{5,4},{6,7},{7,6},{8,9},{9,8},{10,11... | collective-permute-start | bytes 491528 | tf_op jit(solution)/shard_map/ppermute | solution.py:337

commit v12 on v11

--- a/solution.py
+++ b/solution.py
@@ -272,9 +272,10 @@
     far = [None] * CHUNKS
     near = [None] * CHUNKS
 
-    sent = own_chunks(0, 1, space=VMEM, vmem_mib=53, flops=FIRST)
-    for k in range(2):
-        far[k] = lax.ppermute(sent[k], "dp", ahead)
+    sent = own_chunks(0, space=VMEM, vmem_mib=53, flops=FIRST)
+    far[0] = lax.ppermute(sent[0], "dp", ahead)
+    sent += own_chunks(1, until=(sent[0],), space=VMEM)
+    far[1] = lax.ppermute(sent[1], "dp", ahead)
 
     def own_scores(part, *operands, until=()):
         pieces = 4

time: 48.4 us -> 48.3 us (level)
  local copies, waits for them, and re-layouts: 2.35 us -> 1.6 us
  waiting for transfers between devices: 14.2 us -> 14.9 us
    unnamed x6, local copies, waits for them, and re-layouts: 2.35 us -> 1.6 us
    ppermute x2, waiting for transfers between devices: 5.72 us -> 6.41 us  [the longest x1 4.85 us: on_device(): far[0] = lax.ppermute(sent[0], 'dp', ahead)]
    pallas_call x4 -> x5, Pallas kernels: 1.23 us -> 1.3 us  [own_chunks(): call(functools.partial(chunk_kernel, ks), [chunk(k) for k in ks], [ANY] *...]
where the time goes in v12:
time: 48.3 us; the launch traced here: 48.2 us
  starting transfers between devices  17.9 us (37%)
  waiting for transfers between devices  14.9 us (31%)
  Pallas kernels  12.9 us (27%)
  local copies, waits for them, and re-layouts  1.6 us (3%)
  between operations  0.86 us (2%)
    ppermute x4, starting transfers between devices, step(): near[k] = lax.ppermute(out, 'dp', pair)  7.96 us
    pallas_call x2, Pallas kernels, own_scores(): call(functools.partial(own_kernel, part, pieces, factor), outs, [SMEM, HB...  6.33 us
    ppermute x4, waiting for transfers between devices, step(): near[k] = lax.ppermute(out, 'dp', pair)  6.16 us
    ppermute x1, waiting for transfers between devices, on_device(): far[0] = lax.ppermute(sent[0], 'dp', ahead)  4.85 us
    ppermute x3, starting transfers between devices, send_across(): block[CHUNKS - 1 - k] = lax.ppermute(sent, 'groups', across)  4.54 us
    ppermute x1, starting transfers between devices, on_device(): far[0] = lax.ppermute(sent[0], 'dp', ahead)  3.08 us
    pallas_call x3, Pallas kernels, pair_scores(): call(functools.partial(pair_kernel, ks, alone, sums is None), floats(doc_...  2.87 us
    ppermute x1, starting transfers between devices, on_device(): far[1] = lax.ppermute(sent[1], 'dp', ahead)  1.63 us
  transfers between devices with their start and end apart: 15, of which 9 were waited for; matrix products, arithmetic and copies ran while one was open for 0% of the time, Pallas kernels for 23%

profile of v12, /device:TPU:0, one launch (start us, length us, event | category | flops | bytes accessed | tf_op | source)
XLA Modules:
  0.0 48.2 jit_solution(14533961579706759092)
XLA Ops:
  0.0 0.0 copy-start.1
  0.0 0.0 copy-start.2
  0.0 1.2 %shard_map.46.refs_0_ = bf16[128,1536]{1,0:T(8,128)(2,1)S(1)} custom-call(bf16[128,8192]{1,0:T(8,128)(2,1)} %queries.21), custom_call_target="tpu_custom_call" | custom-call | flops 1024 | tf_op jit(solution)/shard_map/pallas_call | solution.py:229
  1.2 3.1 %collective-permute-start = (bf16[128,1536]{1,0:T(8,128)(2,1)S(1)}, bf16[128,1536]{1,0:T(8,128)(2,1)S(1)}, u32[]{:S(2)}, u32[]{:S(2)}) collective-permute-start(bf16[128,1536]{1,0:T(8,128)(2,1)S(1)} %shard_map.46.refs_0_), channel_id=1, source_target_pairs={{0,4},{2,6},{4,8},{6,10},{8,12},{10,14},{12,0},{14,2},{1,5},{3,7},... | collective-permute-start | bytes 1179656 | tf_op jit(solution)/shard_map/ppermute | solution.py:276
  4.2 0.0 copy-start
  4.2 1.6 %copy-done = bf16[128,8192]{1,0:T(8,128)(2,1)S(1)} copy-done((bf16[128,8192]{1,0:T(8,128)(2,1)S(1)}, bf16[128,8192]{1,0:T(8,128)(2,1)}, u32[]{:S(2)}) %copy-start) | copy-done | bytes 2097176
  5.9 1.6 %collective-permute-start.1 = (bf16[128,1536]{1,0:T(8,128)(2,1)S(1)}, bf16[128,1536]{1,0:T(8,128)(2,1)S(1)}, u32[]{:S(2)}, u32[]{:S(2)}) collective-permute-start(bf16[128,1536]{1,0:T(8,128)(2,1)S(1)} %shard_map.47), channel_id=1, source_target_pairs={{0,4},{2,6},{4,8},{6,10},{8,12},{10,14},{12,0},{14,2},{1,5},{3,7},... | collective-permute-start | bytes 1179656 | tf_op jit(solution)/shard_map/ppermute | solution.py:278
  8.2 0.0 copy-done.1
  8.2 0.0 copy-done.2
  8.2 3.2 %shard_map.48 = (f32[320,128]{1,0:T(8,128)S(1)}, f32[320,128]{1,0:T(8,128)S(1)}, bf16[640,4096]{1,0:T(8,128)(2,1)S(1)}, f32[1,8192]{1,0:T(1,128)S(1)}) custom-call(s32[1]{0:T(128)S(6)} %copy.5.counts, bf16[640,8192]{1,0:T(8,128)(2,1)} %documents.3, bf16[128,8192]{1,0:T(8,128)(2,1)S(1)} %copy-done.1, f32[1,8192]{1,0:T(1,128)S(1)} %bitcast.1), custom_call_target="tpu_custom_call" | custom-call | flops 1600000000 | tf_op jit(solution)/shard_map/pallas_call | solution.py:288
  11.4 4.8 %collective-permute-done.received.refs_1_ = bf16[128,1536]{1,0:T(8,128)(2,1)S(1)} collective-permute-done((bf16[128,1536]{1,0:T(8,128)(2,1)S(1)}, bf16[128,1536]{1,0:T(8,128)(2,1)S(1)}, u32[]{:S(2)}, u32[]{:S(2)}) %collective-permute-start) | collective-permute-done | bytes 393248 | tf_op jit(solution)/shard_map/ppermute | solution.py:276
  16.3 2.0 %collective-permute-start.4 = (bf16[128,1536]{1,0:T(8,128)(2,1)S(1)}, bf16[128,1536]{1,0:T(8,128)(2,1)S(1)}, u32[]{:S(2)}, u32[]{:S(2)}) collective-permute-start(bf16[128,1536]{1,0:T(8,128)(2,1)S(1)} %shard_map.49.refs_0_), channel_id=1, source_target_pairs={{0,2},{2,0},{4,6},{6,4},{8,10},{10,8},{12,14},{14,12},{1,3},{3,1},... | collective-permute-start | bytes 1179656 | tf_op jit(solution)/shard_map/ppermute | solution.py:246
  18.3 0.1 collective-permute-start.6
  18.3 1.6 %collective-permute-start.5 = (bf16[128,1536]{1,0:T(8,128)(2,1)S(1)}, bf16[128,1536]{1,0:T(8,128)(2,1)S(1)}, u32[]{:S(2)}, u32[]{:S(2)}) collective-permute-start(bf16[128,1536]{1,0:T(8,128)(2,1)S(1)} %collective-permute-done.received.refs_1_), channel_id=1, source_target_pairs={{0,16},{16,0},{1,17},{17,1},{2,18},{18,2},{3,19},{19,3},{4,20},{20... | collective-permute-start | bytes 1179656 | tf_op jit(solution)/shard_map/ppermute | solution.py:270
  19.9 3.2 %shard_map.51 = (f32[320,128]{1,0:T(8,128)S(1)}, f32[320,128]{1,0:T(8,128)S(1)}, bf16[640,4096]{1,0:T(8,128)(2,1)S(1)}) custom-call(s32[1]{0:T(128)S(6)} %copy.5.counts, bf16[640,8192]{1,0:T(8,128)(2,1)} %documents.3, bf16[128,8192]{1,0:T(8,128)(2,1)S(1)} %copy-done.1, f32[1,8192]{1,0:T(1,128)S(1)} %get-tuple-element.21.refs_0_.inverse, ...), custom_call_target="tpu_custom_call" | custom-call | flops 1600000000 | tf_op jit(solution)/shard_map/pallas_call | solution.py:288
  23.1 1.6 %collective-permute-done.1.received.refs_1_ = bf16[128,1536]{1,0:T(8,128)(2,1)S(1)} collective-permute-done((bf16[128,1536]{1,0:T(8,128)(2,1)S(1)}, bf16[128,1536]{1,0:T(8,128)(2,1)S(1)}, u32[]{:S(2)}, u32[]{:S(2)}) %collective-permute-start.1) | collective-permute-done | bytes 393248 | tf_op jit(solution)/shard_map/ppermute | solution.py:278
  24.7 2.0 %collective-permute-start.3 = (bf16[128,1536]{1,0:T(8,128)(2,1)S(1)}, bf16[128,1536]{1,0:T(8,128)(2,1)S(1)}, u32[]{:S(2)}, u32[]{:S(2)}) collective-permute-start(bf16[128,1536]{1,0:T(8,128)(2,1)S(1)} %shard_map.52.refs_0_), channel_id=1, source_target_pairs={{0,2},{2,0},{4,6},{6,4},{8,10},{10,8},{12,14},{14,12},{1,3},{3,1},... | collective-permute-start | bytes 1179656 | tf_op jit(solution)/shard_map/ppermute | solution.py:246
  26.7 0.1 collective-permute-start.2
  26.8 0.0 collective-permute-done.4.refs_0_
  26.8 1.6 %collective-permute-start.12 = (bf16[128,1536]{1,0:T(8,128)(2,1)S(1)}, bf16[128,1536]{1,0:T(8,128)(2,1)S(1)}, u32[]{:S(2)}, u32[]{:S(2)}) collective-permute-start(bf16[128,1536]{1,0:T(8,128)(2,1)S(1)} %collective-permute-done.4.refs_0_), channel_id=1, source_target_pairs={{0,16},{16,0},{1,17},{17,1},{2,18},{18,2},{3,19},{19,3},{4,20},{20... | collective-permute-start | bytes 1179656 | tf_op jit(solution)/shard_map/ppermute | solution.py:270
  28.3 0.0 collective-permute-done.5.refs_3_
  28.3 0.7 %shard_map.54.refs_0_.refs_2_ = f32[640,256]{1,0:T(8,128)S(1)} custom-call(bf16[640,4096]{1,0:T(8,128)(2,1)S(1)} %get-tuple-element.26.held0, bf16[640,4096]{1,0:T(8,128)(2,1)S(1)} %get-tuple-element.27.held1, f32[1,8192]{1,0:T(1,128)S(1)} %get-tuple-element.21.refs_0_.inverse, bf16[128,1536]{1,0:T(8,128)(2,1)S(1)} %collective-permute-done.4.refs_0_, ...), custom_call_target="tpu_custom_call" | custom-call | flops 1600000000 | tf_op jit(solution)/shard_map/pallas_call | solution.py:260
  29.1 0.9 %collective-permute-done.6.received.refs_1_ = bf16[128,1024]{1,0:T(8,128)(2,1)S(1)} collective-permute-done((bf16[128,1024]{1,0:T(8,128)(2,1)S(1)}, bf16[128,1024]{1,0:T(8,128)(2,1)S(1)}, u32[]{:S(2)}, u32[]{:S(2)}) %collective-permute-start.6) | collective-permute-done | bytes 262176 | tf_op jit(solution)/shard_map/ppermute | solution.py:251
  30.0 2.1 %collective-permute-start.11 = (bf16[128,1024]{1,0:T(8,128)(2,1)S(1)}, bf16[128,1024]{1,0:T(8,128)(2,1)S(1)}, u32[]{:S(2)}, u32[]{:S(2)}) collective-permute-start(bf16[128,1024]{1,0:T(8,128)(2,1)S(1)} %shard_map.55.refs_0_), channel_id=1, source_target_pairs={{0,2},{2,0},{4,6},{6,4},{8,10},{10,8},{12,14},{14,12},{1,3},{3,1},... | collective-permute-start | bytes 786440 | tf_op jit(solution)/shard_map/ppermute | solution.py:246
  32.2 0.1 collective-permute-start.10
  32.2 4.6 %collective-permute-done.3.refs_0_ = bf16[128,1536]{1,0:T(8,128)(2,1)S(1)} collective-permute-done((bf16[128,1536]{1,0:T(8,128)(2,1)S(1)}, bf16[128,1536]{1,0:T(8,128)(2,1)S(1)}, u32[]{:S(2)}, u32[]{:S(2)}) %collective-permute-start.3) | collective-permute-done | bytes 393248 | tf_op jit(solution)/shard_map/ppermute | solution.py:246
  36.8 1.4 %collective-permute-start.9 = (bf16[128,1536]{1,0:T(8,128)(2,1)S(1)}, bf16[128,1536]{1,0:T(8,128)(2,1)S(1)}, u32[]{:S(2)}, u32[]{:S(2)}) collective-permute-start(bf16[128,1536]{1,0:T(8,128)(2,1)S(1)} %collective-permute-done.3.refs_0_), channel_id=1, source_target_pairs={{0,16},{16,0},{1,17},{17,1},{2,18},{18,2},{3,19},{19,3},{4,20},{20... | collective-permute-start | bytes 1179656 | tf_op jit(solution)/shard_map/ppermute | solution.py:270
  38.2 0.7 %shard_map.57.refs_0_.refs_4_ = f32[640,256]{1,0:T(8,128)S(1)} custom-call(bf16[640,4096]{1,0:T(8,128)(2,1)S(1)} %get-tuple-element.26.held0, bf16[640,4096]{1,0:T(8,128)(2,1)S(1)} %get-tuple-element.27.held1, f32[1,8192]{1,0:T(1,128)S(1)} %get-tuple-element.21.refs_0_.inverse, bf16[128,1536]{1,0:T(8,128)(2,1)S(1)} %collective-permute-done.3.refs_0_, ...), custom_call_target="tpu_custom_call" | custom-call | flops 1600000000 | tf_op jit(solution)/shard_map/pallas_call | solution.py:260
  39.0 0.0 collective-permute-done.2.received.refs_5_
  39.0 0.1 shard_map.58.refs_6_
  39.0 1.9 %collective-permute-start.8 = (bf16[128,1024]{1,0:T(8,128)(2,1)S(1)}, bf16[128,1024]{1,0:T(8,128)(2,1)S(1)}, u32[]{:S(2)}, u32[]{:S(2)}) collective-permute-start(bf16[128,1024]{1,0:T(8,128)(2,1)S(1)} %shard_map.58.refs_6_), channel_id=1, source_target_pairs={{0,2},{2,0},{4,6},{6,4},{8,10},{10,8},{12,14},{14,12},{1,3},{3,1},... | collective-permute-start | bytes 786440 | tf_op jit(solution)/shard_map/ppermute | solution.py:246
  40.9 1.5 %collective-permute-done.11.refs_0_ = bf16[128,1024]{1,0:T(8,128)(2,1)S(1)} collective-permute-done((bf16[128,1024]{1,0:T(8,128)(2,1)S(1)}, bf16[128,1024]{1,0:T(8,128)(2,1)S(1)}, u32[]{:S(2)}, u32[]{:S(2)}) %collective-permute-start.11) | collective-permute-done | bytes 262176 | tf_op jit(solution)/shard_map/ppermute | solution.py:246
  42.4 0.0 collective-permute-start.7
  42.4 0.0 collective-permute-done.12.refs_2_
  42.4 1.4 %shard_map.59.sums = f32[640,256]{1,0:T(8,128)S(1)} custom-call(bf16[640,4096]{1,0:T(8,128)(2,1)S(1)} %get-tuple-element.26.held0, bf16[640,4096]{1,0:T(8,128)(2,1)S(1)} %get-tuple-element.27.held1, f32[1,8192]{1,0:T(1,128)S(1)} %get-tuple-element.21.refs_0_.inverse, bf16[128,1024]{1,0:T(8,128)(2,1)S(1)} %collective-permute-done.11.refs_0_, ...), custom_call_target="tpu_custom_call" | custom-call | flops 1600000000 | tf_op jit(solution)/shard_map/pallas_call | solution.py:260
  43.9 0.7 %collective-permute-done.9.near = bf16[128,1536]{1,0:T(8,128)(2,1)S(1)} collective-permute-done((bf16[128,1536]{1,0:T(8,128)(2,1)S(1)}, bf16[128,1536]{1,0:T(8,128)(2,1)S(1)}, u32[]{:S(2)}, u32[]{:S(2)}) %collective-permute-start.9) | collective-permute-done | bytes 393248 | tf_op jit(solution)/shard_map/ppermute | solution.py:270
  44.6 0.0 collective-permute-done.10.far
  44.6 0.7 %shard_map.60 = (f32[640,128]{1,0:T(8,128)S(1)}, f32[320,128]{1,0:T(8,128)S(1)}, f32[320,128]{1,0:T(8,128)S(1)}) custom-call(s32[1]{0:T(128)S(6)} %copy.5.counts, bf16[640,4096]{1,0:T(8,128)(2,1)S(1)} %get-tuple-element.26.held0, bf16[640,4096]{1,0:T(8,128)(2,1)S(1)} %get-tuple-element.27.held1, f32[1,8192]{1,0:T(1,128)S(1)} %get-tuple-element.21.refs_0_.inverse, ...), custom_call_target="tpu_custom_call" | custom-call | flops 1600000000 | tf_op jit(solution)/shard_map/pallas_call | solution.py:319
  45.3 0.1 collective-permute-start.13
  45.4 0.0 collective-permute-done.7.refs_0_.refs_1_
  45.4 0.1 collective-permute-done.8.last
  45.5 0.3 shard_map.61.refs_0_
  45.8 0.5 %collective-permute-start.14 = (f32[320,128]{1,0:T(8,128)S(1)}, f32[320,128]{1,0:T(8,128)S(1)}, u32[]{:S(2)}, u32[]{:S(2)}) collective-permute-start(f32[320,128]{1,0:T(8,128)S(1)} %shard_map.61.refs_0_), channel_id=1, source_target_pairs={{0,1},{1,0},{2,3},{3,2},{4,5},{5,4},{6,7},{7,6},{8,9},{9,8},{10,11... | collective-permute-start | bytes 491528 | tf_op jit(solution)/shard_map/ppermute | solution.py:338
  46.3 0.5 collective-permute-done.13.refs_1_.refs_5_
  46.8 0.3 shard_map.62.refs_2_
  47.1 0.2 collective-permute-done.14.refs_3_
  47.3 0.8 %shard_map.63 = f32[320,384]{1,0:T(8,128)} custom-call(f32[320,128]{1,0:T(8,128)S(1)} %get-tuple-element.24.refs_0_, f32[320,128]{1,0:T(8,128)S(1)} %collective-permute-done.7.refs_0_.refs_1_, f32[320,128]{1,0:T(8,128)S(1)} %shard_map.62.refs_2_, f32[320,128]{1,0:T(8,128)S(1)} %collective-permute-done.14.refs_3_, f32[320,128]{1,0:T(8,128)S(1)} %get-tuple-element.34.refs_4_, ...), custom_call_target="tpu_custom_call" | custom-call | flops 1600000000 | tf_op jit(solution)/shard_map/pallas_call | solution.py:340
  (7 shorter events, 0.3 us)
Async XLA Ops:
  0.0 8.2 %copy-start.1 = (bf16[128,8192]{1,0:T(8,128)(2,1)S(1)}, bf16[128,8192]{1,0:T(8,128)(2,1)}, u32[]{:S(2)}) copy-start(bf16[128,8192]{1,0:T(8,128)(2,1)} %queries.21) | copy-start | bytes 6291460
  0.0 8.2 %copy-start.2 = (f32[8192]{0:T(1024)S(1)}, f32[8192]{0:T(1024)}, u32[]{:S(2)}) copy-start(f32[8192]{0:T(1024)} %param.7) | copy-start | bytes 98308
  1.2 15.0 %collective-permute-start = (bf16[128,1536]{1,0:T(8,128)(2,1)S(1)}, bf16[128,1536]{1,0:T(8,128)(2,1)S(1)}, u32[]{:S(2)}, u32[]{:S(2)}) collective-permute-start(bf16[128,1536]{1,0:T(8,128)(2,1)S(1)} %shard_map.46.refs_0_), channel_id=1, source_target_pairs={{0,4},{2,6},{4,8},{6,10},{8,12},{10,14},{12,0},{14,2},{1,5},{3,7},... | collective-permute-start | bytes 1179656 | tf_op jit(solution)/shard_map/ppermute | solution.py:276
  4.2 1.6 %copy-start = (bf16[128,8192]{1,0:T(8,128)(2,1)S(1)}, bf16[128,8192]{1,0:T(8,128)(2,1)}, u32[]{:S(2)}) copy-start(bf16[128,8192]{1,0:T(8,128)(2,1)} %queries.21) | copy-start | bytes 6291460
  5.9 18.7 %collective-permute-start.1 = (bf16[128,1536]{1,0:T(8,128)(2,1)S(1)}, bf16[128,1536]{1,0:T(8,128)(2,1)S(1)}, u32[]{:S(2)}, u32[]{:S(2)}) collective-permute-start(bf16[128,1536]{1,0:T(8,128)(2,1)S(1)} %shard_map.47), channel_id=1, source_target_pairs={{0,4},{2,6},{4,8},{6,10},{8,12},{10,14},{12,0},{14,2},{1,5},{3,7},... | collective-permute-start | bytes 1179656 | tf_op jit(solution)/shard_map/ppermute | solution.py:278
  16.3 10.5 %collective-permute-start.4 = (bf16[128,1536]{1,0:T(8,128)(2,1)S(1)}, bf16[128,1536]{1,0:T(8,128)(2,1)S(1)}, u32[]{:S(2)}, u32[]{:S(2)}) collective-permute-start(bf16[128,1536]{1,0:T(8,128)(2,1)S(1)} %shard_map.49.refs_0_), channel_id=1, source_target_pairs={{0,2},{2,0},{4,6},{6,4},{8,10},{10,8},{12,14},{14,12},{1,3},{3,1},... | collective-permute-start | bytes 1179656 | tf_op jit(solution)/shard_map/ppermute | solution.py:246
  18.3 11.7 %collective-permute-start.6 = (bf16[128,1024]{1,0:T(8,128)(2,1)S(1)}, bf16[128,1024]{1,0:T(8,128)(2,1)S(1)}, u32[]{:S(2)}, u32[]{:S(2)}) collective-permute-start(bf16[128,1024]{1,0:T(8,128)(2,1)S(1)} %shard_map.50.refs_3_), channel_id=1, source_target_pairs={{0,4},{2,6},{4,8},{6,10},{8,12},{10,14},{12,0},{14,2},{1,5},{3,7},... | collective-permute-start | bytes 786440 | tf_op jit(solution)/shard_map/ppermute | solution.py:251
  18.3 10.0 %collective-permute-start.5 = (bf16[128,1536]{1,0:T(8,128)(2,1)S(1)}, bf16[128,1536]{1,0:T(8,128)(2,1)S(1)}, u32[]{:S(2)}, u32[]{:S(2)}) collective-permute-start(bf16[128,1536]{1,0:T(8,128)(2,1)S(1)} %collective-permute-done.received.refs_1_), channel_id=1, source_target_pairs={{0,16},{16,0},{1,17},{17,1},{2,18},{18,2},{3,19},{19,3},{4,20},{20... | collective-permute-start | bytes 1179656 | tf_op jit(solution)/shard_map/ppermute | solution.py:270
  24.7 12.1 %collective-permute-start.3 = (bf16[128,1536]{1,0:T(8,128)(2,1)S(1)}, bf16[128,1536]{1,0:T(8,128)(2,1)S(1)}, u32[]{:S(2)}, u32[]{:S(2)}) collective-permute-start(bf16[128,1536]{1,0:T(8,128)(2,1)S(1)} %shard_map.52.refs_0_), channel_id=1, source_target_pairs={{0,2},{2,0},{4,6},{6,4},{8,10},{10,8},{12,14},{14,12},{1,3},{3,1},... | collective-permute-start | bytes 1179656 | tf_op jit(solution)/shard_map/ppermute | solution.py:246
  26.7 12.3 %collective-permute-start.2 = (bf16[128,1024]{1,0:T(8,128)(2,1)S(1)}, bf16[128,1024]{1,0:T(8,128)(2,1)S(1)}, u32[]{:S(2)}, u32[]{:S(2)}) collective-permute-start(bf16[128,1024]{1,0:T(8,128)(2,1)S(1)} %shard_map.53.refs_2_), channel_id=1, source_target_pairs={{0,4},{2,6},{4,8},{6,10},{8,12},{10,14},{12,0},{14,2},{1,5},{3,7},... | collective-permute-start | bytes 786440 | tf_op jit(solution)/shard_map/ppermute | solution.py:251
  26.8 15.7 %collective-permute-start.12 = (bf16[128,1536]{1,0:T(8,128)(2,1)S(1)}, bf16[128,1536]{1,0:T(8,128)(2,1)S(1)}, u32[]{:S(2)}, u32[]{:S(2)}) collective-permute-start(bf16[128,1536]{1,0:T(8,128)(2,1)S(1)} %collective-permute-done.4.refs_0_), channel_id=1, source_target_pairs={{0,16},{16,0},{1,17},{17,1},{2,18},{18,2},{3,19},{19,3},{4,20},{20... | collective-permute-start | bytes 1179656 | tf_op jit(solution)/shard_map/ppermute | solution.py:270
  30.0 12.4 %collective-permute-start.11 = (bf16[128,1024]{1,0:T(8,128)(2,1)S(1)}, bf16[128,1024]{1,0:T(8,128)(2,1)S(1)}, u32[]{:S(2)}, u32[]{:S(2)}) collective-permute-start(bf16[128,1024]{1,0:T(8,128)(2,1)S(1)} %shard_map.55.refs_0_), channel_id=1, source_target_pairs={{0,2},{2,0},{4,6},{6,4},{8,10},{10,8},{12,14},{14,12},{1,3},{3,1},... | collective-permute-start | bytes 786440 | tf_op jit(solution)/shard_map/ppermute | solution.py:246
  32.2 12.4 %collective-permute-start.10 = (bf16[128,1536]{1,0:T(8,128)(2,1)S(1)}, bf16[128,1536]{1,0:T(8,128)(2,1)S(1)}, u32[]{:S(2)}, u32[]{:S(2)}) collective-permute-start(bf16[128,1536]{1,0:T(8,128)(2,1)S(1)} %shard_map.56.refs_3_), channel_id=1, source_target_pairs={{0,4},{2,6},{4,8},{6,10},{8,12},{10,14},{12,0},{14,2},{1,5},{3,7},... | collective-permute-start | bytes 1179656 | tf_op jit(solution)/shard_map/ppermute | solution.py:251
  36.8 7.8 %collective-permute-start.9 = (bf16[128,1536]{1,0:T(8,128)(2,1)S(1)}, bf16[128,1536]{1,0:T(8,128)(2,1)S(1)}, u32[]{:S(2)}, u32[]{:S(2)}) collective-permute-start(bf16[128,1536]{1,0:T(8,128)(2,1)S(1)} %collective-permute-done.3.refs_0_), channel_id=1, source_target_pairs={{0,16},{16,0},{1,17},{17,1},{2,18},{18,2},{3,19},{19,3},{4,20},{20... | collective-permute-start | bytes 1179656 | tf_op jit(solution)/shard_map/ppermute | solution.py:270
  39.0 6.4 %collective-permute-start.8 = (bf16[128,1024]{1,0:T(8,128)(2,1)S(1)}, bf16[128,1024]{1,0:T(8,128)(2,1)S(1)}, u32[]{:S(2)}, u32[]{:S(2)}) collective-permute-start(bf16[128,1024]{1,0:T(8,128)(2,1)S(1)} %shard_map.58.refs_6_), channel_id=1, source_target_pairs={{0,2},{2,0},{4,6},{6,4},{8,10},{10,8},{12,14},{14,12},{1,3},{3,1},... | collective-permute-start | bytes 786440 | tf_op jit(solution)/shard_map/ppermute | solution.py:246
  42.4 3.0 %collective-permute-start.7 = (f32[320,128]{1,0:T(8,128)S(1)}, f32[320,128]{1,0:T(8,128)S(1)}, u32[]{:S(2)}, u32[]{:S(2)}) collective-permute-start(f32[320,128]{1,0:T(8,128)S(1)} %get-tuple-element.29.refs_0_), channel_id=1, source_target_pairs={{0,1},{1,0},{2,3},{3,2},{4,5},{5,4},{6,7},{7,6},{8,9},{9,8},{10,11... | collective-permute-start | bytes 491528 | tf_op jit(solution)/shard_map/ppermute | solution.py:317
  45.3 1.5 %collective-permute-start.13 = (f32[320,128]{1,0:T(8,128)S(1)}, f32[320,128]{1,0:T(8,128)S(1)}, u32[]{:S(2)}, u32[]{:S(2)}) collective-permute-start(f32[320,128]{1,0:T(8,128)S(1)} %get-tuple-element.33), channel_id=1, source_target_pairs={{0,1},{1,0},{2,3},{3,2},{4,5},{5,4},{6,7},{7,6},{8,9},{9,8},{10,11... | collective-permute-start | bytes 491528 | tf_op jit(solution)/shard_map/ppermute | solution.py:326
  45.8 1.5 %collective-permute-start.14 = (f32[320,128]{1,0:T(8,128)S(1)}, f32[320,128]{1,0:T(8,128)S(1)}, u32[]{:S(2)}, u32[]{:S(2)}) collective-permute-start(f32[320,128]{1,0:T(8,128)S(1)} %shard_map.61.refs_0_), channel_id=1, source_target_pairs={{0,1},{1,0},{2,3},{3,2},{4,5},{5,4},{6,7},{7,6},{8,9},{9,8},{10,11... | collective-permute-start | bytes 491528 | tf_op jit(solution)/shard_map/ppermute | solution.py:338
